TPU v7x, 32 devices: a whole 2x2x4 slice. The times are simulated.
32 devices in a mesh: ctx: 4 (over y, x), mp: 8 (over z, core).
Axes of the slice: x: 2, y: 2, z: 4, core: 2. Of those that a mesh axis runs over, the one named last changes fastest.
Arguments:
- activations: bfloat16 [4096, 4096], P('ctx', 'mp'), may hold values from -36 to 36
- norm_gain: float32 [4096], P('mp'), may hold values from 0.1 to 1.9
- w_in: bfloat16 [4096, 3, 4096], P('ctx', None, 'mp'), may hold values from -0.09375 to 0.09375
- tail_rows: bfloat16 [3, 4096, 2], P(None, 'mp'), may hold values from -4 to 4
- short_filter: float32 [3, 3, 4096], P(None, None, 'mp'), may hold values from -3 to 3
- decay_rate: float32 [4096, 16], P('mp'), may hold values from 4.8828125e-05 to 0.08, as said below
- residue: float32 [4096, 16], P('mp'), may hold values from -1.5 to 1.5
- skip_gain: float32 [4096], P('mp'), may hold values from -4 to 4
- state_in: float32 [4096, 16], P('mp'), may hold values from -4 to 4
- w_out: bfloat16 [4096, 4096], P('mp', 'ctx'), may hold values from -0.125 to 0.125
Outputs:
- block_out: bfloat16 [4096, 4096], P('ctx', 'mp')
- state_out: float32 [4096, 16], P('mp')
Inputs may be any that keep to these rules, and one draw needn't show every extreme that they name: `decay_rate`: every rate lies between 0.2/4096 and 0.08; any share of the modes may be slow (below 2/4096) or fast.
All inputs are finite; a program needn't handle non-finite values.
Results may differ from a plain program's by a relative error of at most 0.03.
Values may be sent and summed in bfloat16 or wider, within the bound.
No kernel may reach another device: no remote copies, remote signals or barrier semaphores. Data moves between devices by JAX's collectives and lax.ppermute only.
A program may use at most 128 MiB of HBM per device.

v0:
```python
import functools

import jax
import jax.numpy as jnp
from jax import lax
from jax.experimental import pallas as pl
from jax.experimental.pallas import tpu as pltpu
from jax.sharding import PartitionSpec as P

LANES = 128
SEGMENTS = 8
f32 = jnp.float32
bf16 = jnp.bfloat16


def swap_route(size, bit):
    return [(i, i ^ bit) for i in range(size)]


def gathered_blocks(block):
    size = lax.axis_size("ctx")
    me = lax.axis_index("ctx")
    rows = block.shape[0]
    if size != 4:
        whole = lax.all_gather(block, "ctx", axis=0)
        return [(i, 0, whole[i]) for i in range(size)]
    half = rows // 2
    by_x = lax.ppermute(block, "ctx", swap_route(size, 1))
    by_y = lax.ppermute(block, "ctx", swap_route(size, 2))
    far_top = lax.ppermute(by_y[:half], "ctx", swap_route(size, 1))
    far_bottom = lax.ppermute(by_x[half:], "ctx", swap_route(size, 2))
    return [
        (me, 0, block),
        (me ^ 1, 0, by_x),
        (me ^ 2, 0, by_y),
        (me ^ 3, 0, far_top),
        (me ^ 3, half, far_bottom),
    ]


def shifted_start(ref, tail_ref, back, segment):
    last = ref[pl.ds(segment - back, SEGMENTS, stride=segment), :]
    rolled = pltpu.roll(last, 1, 0)
    first = lax.broadcasted_iota(jnp.int32, rolled.shape, 0) == 0
    return jnp.where(first, jnp.broadcast_to(tail_ref[2 - back : 3 - back, :], rolled.shape), rolled)


def wide(row):
    return jnp.broadcast_to(row, (SEGMENTS, row.shape[1]))


def local_kernel(
    segment, modes, k_ref, v_ref, tail_k_ref, tail_v_ref, taps_k_ref, taps_v_ref, lam_ref, weight_ref,
    scale_ref, skip_ref, reach_ref, resp_ref, ends_ref, last_ref,
):
    lam = [wide(lam_ref[n : n + 1, :]) for n in range(modes)]
    weight = [wide(weight_ref[n : n + 1, :]) for n in range(modes)]
    tk = [wide(taps_k_ref[i : i + 1, :]) for i in range(3)]
    tv = [wide(taps_v_ref[i : i + 1, :]) for i in range(3)]
    skip = wide(skip_ref[...])
    zero = jnp.zeros((SEGMENTS, LANES), f32)

    def step(t, carry):
        k1, k2, v1, v2, state = carry
        at = pl.ds(t, SEGMENTS, stride=segment)
        k = k_ref[at, :]
        v = v_ref[at, :]
        u = (tk[0] * k + tk[1] * k1 + tk[2] * k2) * (tv[0] * v + tv[1] * v1 + tv[2] * v2)
        sums = [skip * u, zero, zero, zero]
        moved = []
        for n in range(modes):
            s = lam[n] * state[n] + u
            moved.append(s)
            sums[n % 4] = sums[n % 4] + weight[n] * s
        resp_ref[at, :] = (sums[0] + sums[1]) + (sums[2] + sums[3])
        return (k, k1, v, v1, tuple(moved))

    carry = (
        shifted_start(k_ref, tail_k_ref, 1, segment),
        shifted_start(k_ref, tail_k_ref, 2, segment),
        shifted_start(v_ref, tail_v_ref, 1, segment),
        shifted_start(v_ref, tail_v_ref, 2, segment),
        (zero,) * modes,
    )
    state = lax.fori_loop(0, segment, step, carry, unroll=4)[4]
    for n in range(modes):
        end = wide(scale_ref[n : n + 1, :]) * state[n]
        rows = slice(n * SEGMENTS, (n + 1) * SEGMENTS)
        ends_ref[rows, :] = end
        last_ref[n : n + 1, :] = jnp.sum(end * reach_ref[rows, :], axis=0, keepdims=True)


def gate_kernel(
    segment, modes, parts, q_ref, tail_q_ref, taps_q_ref, lam_ref, hop_ref, residue_ref, resp_ref, ends_ref,
    states_ref, shares_ref, gated_ref, enter_ref, wide_ref,
):
    now = shares_ref[0:modes, :] * states_ref[0:modes, :]
    for i in range(1, parts):
        rows = slice(i * modes, (i + 1) * modes)
        now = now + shares_ref[rows, :] * states_ref[rows, :]
    hop = hop_ref[...]
    for s in range(SEGMENTS):
        at = pl.ds(s, modes, stride=SEGMENTS)
        enter_ref[at, :] = now
        now = hop * now + ends_ref[at, :]
    lam = [wide(lam_ref[n : n + 1, :]) for n in range(modes)]
    taps = [wide(taps_q_ref[i : i + 1, :]) for i in range(3)]
    carried = tuple(
        wide(residue_ref[n : n + 1, :]) * lam[n] * enter_ref[n * SEGMENTS : (n + 1) * SEGMENTS, :]
        for n in range(modes)
    )

    def step(t, carry):
        q1, q2, carried = carry
        at = pl.ds(t, SEGMENTS, stride=segment)
        q = q_ref[at, :]
        sums = [resp_ref[at, :], carried[0], carried[1], carried[2]]
        for n in range(3, modes):
            sums[n % 4] = sums[n % 4] + carried[n]
        response = (sums[0] + sums[1]) + (sums[2] + sums[3])
        wide_ref[at, :] = (taps[0] * q + taps[1] * q1 + taps[2] * q2) * response
        return (q, q1, tuple(lam[n] * carried[n] for n in range(modes)))

    start = (shifted_start(q_ref, tail_q_ref, 1, segment), shifted_start(q_ref, tail_q_ref, 2, segment), carried)
    lax.fori_loop(0, segment, step, start, unroll=4)
    gated_ref[...] = wide_ref[...].astype(gated_ref.dtype)


def column(rows, first):
    return pl.BlockSpec((rows, LANES), lambda c: (0, first + c))


def local_filter(projected, tails, taps, tables):
    tokens, width = projected.shape
    blocks = width // 3 // LANES
    modes = tables["lam"].shape[0]
    flops = tokens * width // 3 * modes * 4
    return pl.pallas_call(
        functools.partial(local_kernel, tokens // SEGMENTS, modes),
        grid=(blocks,),
        in_specs=[
            column(tokens, blocks),
            column(tokens, 2 * blocks),
            column(2, blocks),
            column(2, 2 * blocks),
            column(3, blocks),
            column(3, 2 * blocks),
            column(modes, 0),
            column(modes, 0),
            column(modes, 0),
            column(1, 0),
            column(modes * SEGMENTS, 0),
        ],
        out_specs=[column(tokens, 0), column(modes * SEGMENTS, 0), column(modes, 0)],
        out_shape=[
            jax.ShapeDtypeStruct((tokens, width // 3), f32),
            jax.ShapeDtypeStruct((modes * SEGMENTS, width // 3), f32),
            jax.ShapeDtypeStruct((modes, width // 3), f32),
        ],
        cost_estimate=pl.CostEstimate(flops=flops, bytes_accessed=tokens * width * 4, transcendentals=0),
        compiler_params=pltpu.CompilerParams(vmem_limit_bytes=32 * 2**20),
        name="local_filter",
    )(
        projected, projected, tails, tails, taps, taps, tables["lam"], tables["weight"], tables["scale"],
        tables["skip"], tables["reach"],
    )


def gated_signal(projected, tails, taps, tables, response, ends, states):
    tokens, width = projected.shape
    blocks = width // 3 // LANES
    modes = tables["lam"].shape[0]
    parts = states.shape[0] // modes
    flops = tokens * width // 3 * modes * 2
    return pl.pallas_call(
        functools.partial(gate_kernel, tokens // SEGMENTS, modes, parts),
        grid=(blocks,),
        in_specs=[
            column(tokens, 0),
            column(2, 0),
            column(3, 0),
            column(modes, 0),
            column(modes, 0),
            column(modes, 0),
            column(tokens, 0),
            column(modes * SEGMENTS, 0),
            column(parts * modes, 0),
            column(parts * modes, 0),
        ],
        out_specs=column(tokens, 0),
        out_shape=jax.ShapeDtypeStruct((tokens, width // 3), bf16),
        scratch_shapes=[pltpu.VMEM((modes * SEGMENTS, LANES), f32), pltpu.VMEM((tokens, LANES), f32)],
        cost_estimate=pl.CostEstimate(flops=flops, bytes_accessed=tokens * width * 3, transcendentals=0),
        compiler_params=pltpu.CompilerParams(vmem_limit_bytes=32 * 2**20),
        name="gated_signal",
    )(
        projected, tails, taps, tables["lam"], tables["hop"], tables["residue"], response, ends, states,
        tables["shares"],
    )


def filter_tables(decay_rate, residue, skip_gain, tokens):
    me = lax.axis_index("ctx")
    size = lax.axis_size("ctx")
    rate = decay_rate.T
    modes, channels = rate.shape
    scale = jnp.sqrt(-jnp.expm1(-2.0 * rate))
    segment = tokens // SEGMENTS
    ahead = (SEGMENTS - 1 - jnp.arange(SEGMENTS, dtype=f32)) * segment
    reach = jnp.exp(-rate[:, None, :] * ahead[None, :, None]).reshape(modes * SEGMENTS, channels)
    index = jnp.arange(size)
    gap = (me - 1 - index).astype(f32) * tokens
    shares = jnp.where(
        (index < me)[:, None, None], jnp.exp(-rate[None] * jnp.maximum(gap, 0.0)[:, None, None]), 0.0
    )
    first = jnp.exp(-rate * (me * tokens).astype(f32))[None]
    final_gap = (size - 1 - index).astype(f32) * tokens
    final = jnp.exp(-rate[None] * final_gap[:, None, None])
    final_first = jnp.exp(-rate * (size * tokens))[None]
    return {
        "lam": jnp.exp(-rate),
        "hop": jnp.exp(-rate * segment),
        "weight": residue.T * scale,
        "residue": residue.T,
        "scale": scale,
        "skip": skip_gain[None, :],
        "reach": reach,
        "shares": jnp.concatenate([shares, first]).reshape((size + 1) * modes, channels),
        "final": jnp.concatenate([final, final_first]),
    }


def cut(tables, start, stop):
    return {name: table[..., start:stop] for name, table in tables.items()}


def local(
    activations,
    norm_gain,
    w_in,
    tail_rows,
    short_filter,
    decay_rate,
    residue,
    skip_gain,
    state_in,
    w_out,
):
    tokens, features = activations.shape
    channels = w_in.shape[2]
    mp = lax.axis_size("mp")
    ctx = lax.axis_size("ctx")
    me = lax.axis_index("ctx")
    model_width = features * mp
    groups = 2 if channels % (2 * LANES) == 0 else 1
    share = channels // groups
    act_float = activations.astype(f32)
    scaled = (act_float * norm_gain[None, :]).astype(bf16)
    everything = lax.all_gather(scaled, "mp", axis=0)
    squares = lax.psum(jnp.sum(act_float * act_float, axis=1), "mp")
    inverse = lax.rsqrt(squares / model_width + 1e-06)[:, None]
    per_block = mp // ctx
    by_block = everything.reshape(ctx, per_block, tokens, features)

    def project(blocks):
        total = None
        for owner, first, rows in blocks:
            for i in range(0, rows.shape[0], features):
                source = lax.dynamic_index_in_dim(by_block, owner, 0, False)[(first + i) // features]
                part = lax.dot_general(
                    source, rows[i : i + features], (((1,), (0,)), ((), ())), preferred_element_type=f32
                )
                total = part if total is None else total + part
        return total * inverse

    tables = filter_tables(decay_rate, residue, skip_gain, tokens)
    start_state = state_in.T
    taps_all = short_filter
    tails_all = tail_rows.transpose(2, 0, 1).astype(f32)
    pieces = [w_in[:, :, g * share : (g + 1) * share].reshape(-1, 3 * share) for g in range(groups)]
    arriving = [gathered_blocks(piece) for piece in pieces]
    outputs = []
    finals = []
    for g in range(groups):
        span = slice(g * share, (g + 1) * share)
        own = cut(tables, g * share, (g + 1) * share)
        taps = taps_all[:, :, span].reshape(3, 3 * share)
        projected = project(arriving[g])
        behind = lax.ppermute(projected[-2:], "ctx", [(i, i + 1) for i in range(ctx - 1)])
        tails = jnp.where(me == 0, tails_all[:, :, span].reshape(2, 3 * share), behind)
        response, ends, last = local_filter(projected, tails, taps, own)
        lasts = lax.all_gather(last, "ctx", axis=0)
        states = jnp.concatenate([lasts, start_state[None, :, span]])
        finals.append(jnp.sum(own["final"] * states, axis=0))
        outputs.append(
            gated_signal(projected, tails, taps, own, response, ends, states.reshape(-1, share))
        )
    state_out = jnp.concatenate(finals, axis=1).T
    gated = jnp.concatenate(outputs, axis=1)
    panel = lax.all_gather(w_out, "ctx", axis=1, tiled=True)
    partial = lax.dot_general(panel, gated, (((0,), (1,)), ((), ())), preferred_element_type=f32)
    branch = lax.psum_scatter(partial.astype(bf16), "mp", scatter_dimension=0, tiled=True).astype(f32).T
    return ((act_float + branch).astype(bf16), state_out)


def solution(mesh):
    placed = (
        P("ctx", "mp"),
        P("mp"),
        P("ctx", None, "mp"),
        P(None, "mp", None),
        P(None, None, "mp"),
        P("mp", None),
        P("mp", None),
        P("mp"),
        P("mp", None),
        P("mp", "ctx"),
    )
    return jax.shard_map(
        local,
        mesh=mesh,
        in_specs=placed,
        out_specs=(P("ctx", "mp"), P("mp", None)),
        check_vma=False,
    )
```

profile of v0, /device:TPU:1, one launch (start us, length us, event | category | flops | bytes accessed | tf_op | source)
XLA Modules:
  0.0 296.0 jit_solution(1733291619504356648)
XLA Ops:
  7.2 0.0 all-gather.8.cloned.1.call-start
  7.2 2.6 fusion.1
  9.9 0.0 all-gather.8.cloned.1.call-update
  9.9 0.0 all-gather.6.cloned.1.call-start
  10.0 1.9 fusion.55
  11.8 2.6 copy.20
  14.4 2.0 collective-permute-start
  16.5 1.2 collective-permute-start.1
  17.7 2.6 copy.23
  20.3 0.3 collective-permute-start.5
  20.6 0.0 all-gather.6.cloned.1.call-update
  20.6 0.0 reduce-scatter.2.cloned.1.call-start
  20.7 1.8 fusion.54
  22.5 0.0 copy-start.9
  22.5 2.5 copy.19
  25.0 1.4 copy.18
  26.4 15.5 %psum.7 = f32[1024]{0:T(1024)S(1)} all-reduce(f32[1024]{0:T(1024)S(1)} %get-tuple-element.22), channel_id=1, replica_groups=mesh['ctx'=4,'mp'=8] {'mp'}, use_global_device_ids=true, to_apply=%region_1.0 | all-reduce | flops 1024 | bytes 8192 | tf_op jit(solution)/shard_map/psum | solution.py:260
  42.1 0.1 mul.141
  42.2 1.2 copy.22
  43.4 0.3 copy.21
  43.7 0.1 exponential_bitcast_fusion
  43.8 0.1 multiply_exponential_fusion
  44.0 0.1 fusion.26
  44.1 7.6 %collective-permute-done.1 = bf16[1024,768]{0,1:T(8,128)(2,1)} collective-permute-done((bf16[1024,768]{0,1:T(8,128)(2,1)}, bf16[1024,768]{0,1:T(8,128)(2,1)}, u32[]{:S(2)}, u32[]{:S(2)}) %collective-permute-start.1) | collective-permute-done | bytes 1572896 | tf_op jit(solution)/shard_map/ppermute | solution.py:29
  51.7 2.1 slice.234
  53.8 0.4 collective-permute-start.2
  54.2 2.2 slice.233
  56.4 1.1 collective-permute-start.3
  57.5 28.0 %collective-permute-done.6 = bf16[1024,768]{0,1:T(8,128)(2,1)} collective-permute-done((bf16[1024,768]{0,1:T(8,128)(2,1)}, bf16[1024,768]{0,1:T(8,128)(2,1)}, u32[]{:S(2)}, u32[]{:S(2)}) %collective-permute-start.6) | collective-permute-done | bytes 1572896 | tf_op jit(solution)/shard_map/ppermute | solution.py:29
  85.4 2.1 slice.249
  87.5 0.4 collective-permute-start.7
  87.9 2.1 slice.248
  90.0 1.1 collective-permute-start.8
  91.1 3.9 %all-gather.8.cloned.1.call-done = bf16[8192,512]{1,0:T(8,128)(2,1)} async-done(((bf16[1024,512]{1,0:T(8,128)(2,1)}), bf16[8192,512]{1,0:T(8,128)(2,1)}) %all-gather.8.cloned.1.call-update) | async-done | bytes 8388624 | tf_op jit(solution)/shard_map/all_gather | solution.py:259
  95.0 2.4 fusion.7
  97.4 4.2 %fusion.15 = f32[1024,768]{1,0:T(8,128)} fusion(bf16[512,768]{0,1:T(8,128)(2,1)S(1)} %bitcast.130, bf16[4,2,1024,512]{3,2,1,0:T(8,128)(2,1)} %bitcast.112, s32[]{:T(128)S(6)} %select_n.41, s32[]{:T(128)S(6)} %add.102), kind=kOutput, calls=%fused_computation.29 | convolution fusion | flops 805306368 | bytes 4980744 | tf_op jit(solution)/shard_map/dot_general | solution.py:270
  101.6 4.0 %fusion.19 = f32[1024,768]{1,0:T(8,128)} fusion(bf16[4,2,1024,512]{3,2,1,0:T(8,128)(2,1)S(1)} %bitcast.113, s32[]{:T(128)S(6)} %select_n.43, s32[]{:T(128)S(6)} %add.102, bf16[1024,768]{0,1:T(8,128)(2,1)} %collective-permute-done.1), kind=kOutput, calls=%fused_computation.33 | convolution fusion | flops 805306368 | bytes 4980744 | tf_op jit(solution)/shard_map/dot_general | solution.py:270
  105.6 2.1 fusion.11
  107.8 3.9 %fusion.17 = f32[1024,768]{1,0:T(8,128)} fusion(bf16[4,2,1024,512]{3,2,1,0:T(8,128)(2,1)S(1)} %bitcast.115, s32[]{:T(128)S(6)} %select_n.42, s32[]{:T(128)S(6)} %add.102, bf16[1024,768]{0,1:T(8,128)(2,1)} %collective-permute-done), kind=kOutput, calls=%fused_computation.31 | convolution fusion | flops 805306368 | bytes 4980744 | tf_op jit(solution)/shard_map/dot_general | solution.py:270
  111.7 2.1 fusion.9
  113.8 3.8 %fusion.13 = f32[1024,768]{1,0:T(8,128)} fusion(bf16[512,768]{0,1:T(8,128)(2,1)} %collective-permute-done.2, bf16[4,2,1024,512]{3,2,1,0:T(8,128)(2,1)S(1)} %bitcast.117, s32[]{:T(128)S(6)} %select_n.44), kind=kOutput, calls=%fused_computation.27 | convolution fusion | flops 805306368 | bytes 4980740 | tf_op jit(solution)/shard_map/dot_general | solution.py:270
  117.6 6.4 %add_multiply_fusion.1.k_ref.v_ref.q_ref = f32[1024,768]{1,0:T(8,128)S(1)} fusion(f32[1024,768]{1,0:T(8,128)} %fusion.13, f32[1024,768]{1,0:T(8,128)} %fusion.19, f32[1024,768]{1,0:T(8,128)S(1)} %fusion.11, f32[1024,768]{1,0:T(8,128)} %fusion.17, f32[1024,768]{1,0:T(8,128)S(1)} %fusion.9, f32[1024,768]{1,0:T(8,128)S(1)} %fusion.7, f32[1024,768]{1,0:T(8,128)} %fusion.15, ...), kind=kOutput, calls=%fused_computation.2 | convolution fusion | flops 811597824 | bytes 27004936 | tf_op jit(solution)/shard_map/dot_general | solution.py:270
  124.1 3.3 %collective-permute-start.4 = (f32[2,768]{1,0:T(2,128)S(1)}, f32[2,768]{1,0:T(2,128)S(1)}, u32[]{:S(2)}, u32[]{:S(2)}) collective-permute-start(f32[2,768]{1,0:T(2,128)S(1)} %slice.237), channel_id=1, source_target_pairs={{0,8},{8,16},{16,24},{1,9},{9,17},{17,25},{2,10},{10,18},{18,26},{... | collective-permute-start | bytes 18440 | tf_op jit(solution)/shard_map/ppermute | solution.py:289
  127.4 2.6 fusion.14
  130.0 1.0 fusion.6
  131.0 3.9 %fusion.16 = f32[1024,768]{1,0:T(8,128)} fusion(bf16[4,2,1024,512]{3,2,1,0:T(8,128)(2,1)S(1)} %bitcast.121, s32[]{:T(128)S(6)} %select_n.42, s32[]{:T(128)S(6)} %add.102, bf16[1024,768]{0,1:T(8,128)(2,1)} %collective-permute-done.5), kind=kOutput, calls=%fused_computation.30 | convolution fusion | flops 805306368 | bytes 4980744 | tf_op jit(solution)/shard_map/dot_general | solution.py:270
  135.0 4.1 %fusion.18 = f32[1024,768]{1,0:T(8,128)} fusion(bf16[4,2,1024,512]{3,2,1,0:T(8,128)(2,1)S(1)} %bitcast.122, s32[]{:T(128)S(6)} %select_n.43, s32[]{:T(128)S(6)} %add.102, bf16[1024,768]{0,1:T(8,128)(2,1)} %collective-permute-done.6), kind=kOutput, calls=%fused_computation.32 | convolution fusion | flops 805306368 | bytes 4980744 | tf_op jit(solution)/shard_map/dot_general | solution.py:270
  139.1 2.1 fusion.10
  141.2 3.9 %fusion.8 = f32[1024,768]{1,0:T(8,128)} fusion(bf16[4,2,1024,512]{3,2,1,0:T(8,128)(2,1)S(1)} %bitcast.124, s32[]{:T(128)S(6)} %select_n.42, bf16[1024,768]{0,1:T(8,128)(2,1)} %collective-permute-done.5), kind=kOutput, calls=%fused_computation.22 | convolution fusion | flops 805306368 | bytes 4980740 | tf_op jit(solution)/shard_map/dot_general | solution.py:270
  145.1 3.8 %fusion.12 = f32[1024,768]{1,0:T(8,128)} fusion(bf16[512,768]{0,1:T(8,128)(2,1)} %collective-permute-done.7, bf16[4,2,1024,512]{3,2,1,0:T(8,128)(2,1)S(1)} %bitcast.125, s32[]{:T(128)S(6)} %select_n.44), kind=kOutput, calls=%fused_computation.26 | convolution fusion | flops 805306368 | bytes 4980740 | tf_op jit(solution)/shard_map/dot_general | solution.py:270
  148.9 7.3 %add_multiply_fusion.k_ref.v_ref.q_ref = f32[1024,768]{1,0:T(8,128)S(1)} fusion(f32[1024,768]{1,0:T(8,128)} %fusion.12, f32[1024,768]{1,0:T(8,128)} %fusion.18, f32[1024,768]{1,0:T(8,128)S(1)} %fusion.10, f32[1024,768]{1,0:T(8,128)} %fusion.16, f32[1024,768]{1,0:T(8,128)} %fusion.8, f32[1024,768]{1,0:T(8,128)S(1)} %fusion.6, f32[1024,768]{1,0:T(8,128)} %fusion.14, ...), kind=kOutput, calls=%fused_computation.1 | convolution fusion | flops 811597824 | bytes 27004936 | tf_op jit(solution)/shard_map/dot_general | solution.py:270
  156.2 3.1 %collective-permute-start.9 = (f32[2,768]{1,0:T(2,128)S(1)}, f32[2,768]{1,0:T(2,128)S(1)}, u32[]{:S(2)}, u32[]{:S(2)}) collective-permute-start(f32[2,768]{1,0:T(2,128)S(1)} %slice.252), channel_id=1, source_target_pairs={{0,8},{8,16},{16,24},{1,9},{9,17},{17,25},{2,10},{10,18},{18,26},{... | collective-permute-start | bytes 18440 | tf_op jit(solution)/shard_map/ppermute | solution.py:289
  159.3 5.1 %local_filter.2 = (f32[1024,256]{1,0:T(8,128)S(1)}, f32[128,256]{1,0:T(8,128)S(1)}, f32[16,256]{1,0:T(8,128)S(1)}) custom-call(f32[1024,768]{1,0:T(8,128)S(1)} %add_multiply_fusion.1.k_ref.v_ref.q_ref, f32[1024,768]{1,0:T(8,128)S(1)} %add_multiply_fusion.1.k_ref.v_ref.q_ref, f32[2,768]{1,0:T(2,128)S(1)} %broadcast_select_fusion.1.tail_k_ref.tail_v_ref.tail_q_ref, ...), custom_call_target="tpu_custom_call" | custom-call | flops 16777216 | bytes 3145728 | tf_op jit(solution)/shard_map/local_filter/pallas_call | solution.py:138
  164.5 5.1 %local_filter.3 = (f32[1024,256]{1,0:T(8,128)S(1)}, f32[128,256]{1,0:T(8,128)S(1)}, f32[16,256]{1,0:T(8,128)S(1)}) custom-call(f32[1024,768]{1,0:T(8,128)S(1)} %add_multiply_fusion.k_ref.v_ref.q_ref, f32[1024,768]{1,0:T(8,128)S(1)} %add_multiply_fusion.k_ref.v_ref.q_ref, f32[2,768]{1,0:T(2,128)S(1)} %broadcast_select_fusion.tail_k_ref.tail_v_ref.tail_q_ref, ...), custom_call_target="tpu_custom_call" | custom-call | flops 16777216 | bytes 3145728 | tf_op jit(solution)/shard_map/local_filter/pallas_call | solution.py:138
  169.6 6.2 %all-gather.1 = f32[64,256]{1,0:T(8,128)S(1)} all-gather(f32[16,256]{1,0:T(8,128)S(1)} %get-tuple-element.10), channel_id=3, replica_groups=mesh['ctx'=4,'mp'=8] {'ctx'}, dimensions={0}, use_global_device_ids=true | all-gather | bytes 81920 | tf_op jit(solution)/shard_map/all_gather | solution.py:292
  175.8 5.4 %all-gather.2 = f32[64,256]{1,0:T(8,128)S(1)} all-gather(f32[16,256]{1,0:T(8,128)S(1)} %get-tuple-element.13), channel_id=4, replica_groups=mesh['ctx'=4,'mp'=8] {'ctx'}, dimensions={0}, use_global_device_ids=true | all-gather | bytes 81920 | tf_op jit(solution)/shard_map/all_gather | solution.py:292
  181.2 3.0 %gated_signal.2 = bf16[1024,256]{1,0:T(8,128)(2,1)S(1)} custom-call(f32[1024,768]{1,0:T(8,128)S(1)} %add_multiply_fusion.1.k_ref.v_ref.q_ref, f32[2,768]{1,0:T(2,128)S(1)} %broadcast_select_fusion.1.tail_k_ref.tail_v_ref.tail_q_ref, f32[3,768]{1,0:T(4,128)S(1)} %bitcast.110, f32[16,256]{1,0:T(8,128)S(1)} %get-tuple-element.60.lam_ref, ...), custom_call_target="tpu_custom_call" | custom-call | flops 8388608 | bytes 2359296 | tf_op jit(solution)/shard_map/gated_signal/pallas_call | solution.py:175
  184.2 3.0 %gated_signal.3 = bf16[1024,256]{1,0:T(8,128)(2,1)S(1)} custom-call(f32[1024,768]{1,0:T(8,128)S(1)} %add_multiply_fusion.k_ref.v_ref.q_ref, f32[2,768]{1,0:T(2,128)S(1)} %broadcast_select_fusion.tail_k_ref.tail_v_ref.tail_q_ref, f32[3,768]{1,0:T(4,128)S(1)} %bitcast.107, f32[16,256]{1,0:T(8,128)S(1)} %get-tuple-element.59.lam_ref, ...), custom_call_target="tpu_custom_call" | custom-call | flops 8388608 | bytes 2359296 | tf_op jit(solution)/shard_map/gated_signal/pallas_call | solution.py:175
  187.2 0.0 all-gather.6.cloned.1.call-done
  187.2 9.0 %convert_bitcast_fusion = bf16[4096,1024]{0,1:T(8,128)(2,1)} fusion(bf16[512,4096]{1,0:T(8,128)(2,1)} %all-gather.6.cloned.1.call-done, bf16[1024,256]{1,0:T(8,128)(2,1)S(1)} %gated_signal.3, bf16[1024,256]{1,0:T(8,128)(2,1)S(1)} %gated_signal.2), kind=kOutput, calls=%fused_computation | convolution fusion | flops 4301258752 | bytes 13631488 | tf_op jit(solution)/shard_map/dot_general | solution.py:301
  196.2 0.0 reduce-scatter.2.cloned.1.call-update
  196.2 0.6 maximum_bitcast_fusion
  196.9 90.1 %reduce-scatter.2.cloned.1.call-done = bf16[512,1024]{0,1:T(8,128)(2,1)} async-done(((bf16[4096,1024]{0,1:T(8,128)(2,1)}), bf16[512,1024]{0,1:T(8,128)(2,1)}) %reduce-scatter.2.cloned.1.call-update) | async-done | bytes 1048592 | tf_op jit(solution)/shard_map/reduce_scatter | solution.py:302
  287.0 2.5 fusion.2
  (58 shorter events, 0.3 us)
Async XLA Ops:
  7.2 2.8 copy-start.1
  7.2 87.9 %all-gather.8.cloned.1.call-start = ((), (), s32[]{:S(2)}) async-start(), calls=%async_computation.3 | async-start | bytes 9437184 | tf_op jit(solution)/shard_map/all_gather | solution.py:259
  9.9 177.3 %all-gather.6.cloned.1.call-start = ((), (), s32[]{:S(2)}) async-start(), calls=%async_computation.1 | async-start | bytes 5242880 | tf_op jit(solution)/shard_map/all_gather | solution.py:300
  14.4 39.8 %collective-permute-start = (bf16[1024,768]{0,1:T(8,128)(2,1)}, bf16[1024,768]{0,1:T(8,128)(2,1)}, u32[]{:S(2)}, u32[]{:S(2)}) collective-permute-start(bf16[1024,768]{0,1:T(8,128)(2,1)} %bitcast.133), channel_id=1, source_target_pairs={{0,8},{8,0},{16,24},{24,16},{1,9},{9,1},{17,25},{25,17},{2,10},{10... | collective-permute-start | bytes 4718600 | tf_op jit(solution)/shard_map/ppermute | solution.py:28
  16.5 35.3 %collective-permute-start.1 = (bf16[1024,768]{0,1:T(8,128)(2,1)}, bf16[1024,768]{0,1:T(8,128)(2,1)}, u32[]{:S(2)}, u32[]{:S(2)}) collective-permute-start(bf16[1024,768]{0,1:T(8,128)(2,1)} %bitcast.134), channel_id=1, source_target_pairs={{0,16},{8,24},{16,0},{24,8},{1,17},{9,25},{17,1},{25,9},{2,18},{10... | collective-permute-start | bytes 4718600 | tf_op jit(solution)/shard_map/ppermute | solution.py:29
  20.3 67.6 %collective-permute-start.5 = (bf16[1024,768]{0,1:T(8,128)(2,1)}, bf16[1024,768]{0,1:T(8,128)(2,1)}, u32[]{:S(2)}, u32[]{:S(2)}) collective-permute-start(bf16[1024,768]{0,1:T(8,128)(2,1)} %bitcast.131), channel_id=1, source_target_pairs={{0,8},{8,0},{16,24},{24,16},{1,9},{9,1},{17,25},{25,17},{2,10},{10... | collective-permute-start | bytes 4718600 | tf_op jit(solution)/shard_map/ppermute | solution.py:28
  20.6 64.9 %collective-permute-start.6 = (bf16[1024,768]{0,1:T(8,128)(2,1)}, bf16[1024,768]{0,1:T(8,128)(2,1)}, u32[]{:S(2)}, u32[]{:S(2)}) collective-permute-start(bf16[1024,768]{0,1:T(8,128)(2,1)} %bitcast.132), channel_id=1, source_target_pairs={{0,16},{8,24},{16,0},{24,8},{1,17},{9,25},{17,1},{25,9},{2,18},{10... | collective-permute-start | bytes 4718600 | tf_op jit(solution)/shard_map/ppermute | solution.py:29
  20.6 266.4 %reduce-scatter.2.cloned.1.call-start = ((), (), s32[]{:S(2)}) async-start(), calls=%async_computation.2 | async-start | bytes 9437184 | tf_op jit(solution)/shard_map/reduce_scatter | solution.py:302
  22.5 19.5 %copy-start.11 = (bf16[3,512,2]{1,2,0:T(2,128)(2,1)S(1)}, bf16[3,512,2]{1,2,0:T(2,128)(2,1)}, u32[]{:S(2)}) copy-start(bf16[3,512,2]{1,2,0:T(2,128)(2,1)} %param.13) | copy-start | bytes 18436
  22.5 19.5 %copy-start.7 = (f32[512,16]{0,1:T(8,128)S(1)}, f32[512,16]{0,1:T(8,128)}, u32[]{:S(2)}) copy-start(f32[512,16]{0,1:T(8,128)} %param.15) | copy-start | bytes 98308
  22.5 19.7 %copy-start.10 = (f32[3,3,512]{2,1,0:T(4,128)S(1)}, f32[3,3,512]{2,1,0:T(4,128)}, u32[]{:S(2)}) copy-start(f32[3,3,512]{2,1,0:T(4,128)} %param.14) | copy-start | bytes 55300
  22.5 19.7 %copy-start.4 = (bf16[512,3,256]{2,0,1:T(8,128)(2,1)S(1)}, bf16[512,3,256]{2,0,1:T(8,128)(2,1)}, u32[]{:S(2)}) copy-start(bf16[512,3,256]{2,0,1:T(8,128)(2,1)} %get-tuple-element.17) | copy-start | bytes 2359300
  22.5 20.9 %copy-start.3 = (bf16[512,3,256]{2,0,1:T(8,128)(2,1)S(1)}, bf16[512,3,256]{2,0,1:T(8,128)(2,1)}, u32[]{:S(2)}) copy-start(bf16[512,3,256]{2,0,1:T(8,128)(2,1)} %get-tuple-element.18) | copy-start | bytes 2359300
  22.5 21.2 %copy-start.9 = (f32[512,16]{0,1:T(8,128)S(1)}, f32[512,16]{0,1:T(8,128)}, u32[]{:S(2)}) copy-start(f32[512,16]{0,1:T(8,128)} %param.18) | copy-start | bytes 98308
  22.5 21.2 %copy-start.8 = (f32[512,16]{0,1:T(8,128)S(1)}, f32[512,16]{0,1:T(8,128)}, u32[]{:S(2)}) copy-start(f32[512,16]{0,1:T(8,128)} %param.16) | copy-start | bytes 98308
  25.0 18.9 %copy-start.12 = (f32[512]{0:T(512)S(1)}, f32[512]{0:T(512)}, u32[]{:S(2)}) copy-start(f32[512]{0:T(512)} %param.17) | copy-start | bytes 6148
  53.8 60.0 %collective-permute-start.2 = (bf16[512,768]{0,1:T(8,128)(2,1)}, bf16[512,768]{0,1:T(8,128)(2,1)}, u32[]{:S(2)}, u32[]{:S(2)}) collective-permute-start(bf16[512,768]{0,1:T(8,128)(2,1)} %slice.234), channel_id=1, source_target_pairs={{0,8},{8,0},{16,24},{24,16},{1,9},{9,1},{17,25},{25,17},{2,10},{10... | collective-permute-start | bytes 2359304 | tf_op jit(solution)/shard_map/ppermute | solution.py:30
  56.4 61.3 %collective-permute-start.3 = (bf16[512,768]{0,1:T(8,128)(2,1)}, bf16[512,768]{0,1:T(8,128)(2,1)}, u32[]{:S(2)}, u32[]{:S(2)}) collective-permute-start(bf16[512,768]{0,1:T(8,128)(2,1)} %slice.233), channel_id=1, source_target_pairs={{0,16},{8,24},{16,0},{24,8},{1,17},{9,25},{17,1},{25,9},{2,18},{10... | collective-permute-start | bytes 2359304 | tf_op jit(solution)/shard_map/ppermute | solution.py:31
  87.5 9.9 %copy-start.6 = (bf16[512,3,256]{0,2,1:T(8,128)(2,1)S(1)}, bf16[512,3,256]{0,2,1:T(8,128)(2,1)}, u32[]{:S(2)}) copy-start(bf16[512,3,256]{0,2,1:T(8,128)(2,1)} %copy.19) | copy-start | bytes 2359300
  87.5 57.6 %collective-permute-start.7 = (bf16[512,768]{0,1:T(8,128)(2,1)}, bf16[512,768]{0,1:T(8,128)(2,1)}, u32[]{:S(2)}, u32[]{:S(2)}) collective-permute-start(bf16[512,768]{0,1:T(8,128)(2,1)} %slice.249), channel_id=1, source_target_pairs={{0,8},{8,0},{16,24},{24,16},{1,9},{9,1},{17,25},{25,17},{2,10},{10... | collective-permute-start | bytes 2359304 | tf_op jit(solution)/shard_map/ppermute | solution.py:30
  90.0 58.9 %collective-permute-start.8 = (bf16[512,768]{0,1:T(8,128)(2,1)}, bf16[512,768]{0,1:T(8,128)(2,1)}, u32[]{:S(2)}, u32[]{:S(2)}) collective-permute-start(bf16[512,768]{0,1:T(8,128)(2,1)} %slice.248), channel_id=1, source_target_pairs={{0,16},{8,24},{16,0},{24,8},{1,17},{9,25},{17,1},{25,9},{2,18},{10... | collective-permute-start | bytes 2359304 | tf_op jit(solution)/shard_map/ppermute | solution.py:31
  95.0 6.6 %copy-start = (bf16[8192,512]{1,0:T(8,128)(2,1)S(1)}, bf16[8192,512]{1,0:T(8,128)(2,1)}, u32[]{:S(2)}) copy-start(bf16[8192,512]{1,0:T(8,128)(2,1)} %all-gather.8.cloned.1.call-done) | copy-start | bytes 25165828
  117.6 9.8 %copy-start.5 = (bf16[512,3,256]{0,2,1:T(8,128)(2,1)S(1)}, bf16[512,3,256]{0,2,1:T(8,128)(2,1)}, u32[]{:S(2)}) copy-start(bf16[512,3,256]{0,2,1:T(8,128)(2,1)} %copy.22) | copy-start | bytes 2359300
  124.1 35.2 %collective-permute-start.4 = (f32[2,768]{1,0:T(2,128)S(1)}, f32[2,768]{1,0:T(2,128)S(1)}, u32[]{:S(2)}, u32[]{:S(2)}) collective-permute-start(f32[2,768]{1,0:T(2,128)S(1)} %slice.237), channel_id=1, source_target_pairs={{0,8},{8,16},{16,24},{1,9},{9,17},{17,25},{2,10},{10,18},{18,26},{... | collective-permute-start | bytes 18440 | tf_op jit(solution)/shard_map/ppermute | solution.py:289
  156.2 8.2 %collective-permute-start.9 = (f32[2,768]{1,0:T(2,128)S(1)}, f32[2,768]{1,0:T(2,128)S(1)}, u32[]{:S(2)}, u32[]{:S(2)}) collective-permute-start(f32[2,768]{1,0:T(2,128)S(1)} %slice.252), channel_id=1, source_target_pairs={{0,8},{8,16},{16,24},{1,9},{9,17},{17,25},{2,10},{10,18},{18,26},{... | collective-permute-start | bytes 18440 | tf_op jit(solution)/shard_map/ppermute | solution.py:289
  196.2 90.8 %copy-start.2 = (bf16[1024,512]{1,0:T(8,128)(2,1)S(1)}, bf16[1024,512]{1,0:T(8,128)(2,1)}, u32[]{:S(2)}) copy-start(bf16[1024,512]{1,0:T(8,128)(2,1)} %param.10) | copy-start | bytes 3145732
Sparse Core Ops, SparseCore 0:
  10.2 84.8 all-gather.7
  96.9 62.2 all-gather.5
  196.4 90.5 reduce-scatter.1
where the time goes:
time: 300 us; the launch traced here: 296 us
  waiting for transfers between devices  130 us (43%)
  matrix products  66.7 us (22%)
  blocking collectives  27.1 us (9%)
  local copies, waits for them, and re-layouts  22.8 us (8%)
  Pallas kernels  16.2 us (5%)
  between operations  14.2 us (5%)
  starting transfers between devices  13.1 us (4%)
  other arithmetic  6.14 us (2%)
    reduce_scatter x1, waiting for transfers between devices, local(): lax.psum_scatter(partial.astype(bf16), 'mp', scatter_dimension=0, tiled=T...  90.1 us
    dot_general x16, matrix products, project(): lax.dot_general(source, rows[i:i + features], (((1,), (0,)), ((), ())), p...  57.7 us
    ppermute x2, waiting for transfers between devices, gathered_blocks(): by_y = lax.ppermute(block, 'ctx', swap_route(size, 2))  35.6 us
    psum x1, blocking collectives, local(): squares = lax.psum(jnp.sum(act_float * act_float, axis=1), 'mp')  15.5 us
    all_gather x2, blocking collectives, local(): lasts = lax.all_gather(last, 'ctx', axis=0)  11.6 us
    unnamed x35, local copies, waits for them, and re-layouts  10.6 us
    pallas_call x2, Pallas kernels, local_filter(): pl.pallas_call(functools.partial(local_kernel, tokens // SEGMENTS, modes)...  10.2 us
    slice x5, local copies, waits for them, and re-layouts, project(): rows[i:i + features]  10.2 us
  transfers between devices with their start and end apart: 13, of which 4 were waited for; matrix products, arithmetic and copies ran while one was open for 28% of the time, Pallas kernels for 5%

commit v1 on v0

--- a/solution.py
+++ b/solution.py
@@ -1,4 +1,5 @@
 import functools
+import math
 
 import jax
 import jax.numpy as jnp
@@ -199,6 +200,129 @@
     )
 
 
+def project_kernel(chunks, order_ref, all_ref, *refs):
+    pieces, inverse_ref, out_ref = refs[:-2], refs[-2], refs[-1]
+    features = all_ref.shape[2]
+    total = None
+    for n, (piece, first) in enumerate(chunks):
+        part = jnp.dot(
+            all_ref[order_ref[n]], pieces[piece][first : first + features, :], preferred_element_type=f32
+        )
+        total = part if total is None else total + part
+    out_ref[...] = total * inverse_ref[...]
+
+
+def project(everything, blocks, inverse):
+    mp, tokens, features = everything.shape
+    per_block = mp // lax.axis_size("ctx")
+    width = blocks[0][2].shape[1]
+    chunks, order = [], []
+    for n, (owner, first, rows) in enumerate(blocks):
+        for i in range(0, rows.shape[0], features):
+            chunks.append((n, i))
+            order.append(owner * per_block + (first + i) // features)
+    tile = math.gcd(tokens, 256)
+    whole = [pl.BlockSpec(rows.shape, lambda m, order: (0, 0)) for _, _, rows in blocks]
+    return pl.pallas_call(
+        functools.partial(project_kernel, chunks),
+        grid_spec=pltpu.PrefetchScalarGridSpec(
+            num_scalar_prefetch=1,
+            grid=(tokens // tile,),
+            in_specs=[
+                pl.BlockSpec((mp, tile, features), lambda m, order: (0, m, 0)),
+                *whole,
+                pl.BlockSpec((tile, 1), lambda m, order: (m, 0)),
+            ],
+            out_specs=pl.BlockSpec((tile, width), lambda m, order: (m, 0)),
+        ),
+        out_shape=jax.ShapeDtypeStruct((tokens, width), f32),
+        cost_estimate=pl.CostEstimate(
+            flops=2 * tokens * width * mp * features, bytes_accessed=2 * mp * features * (tokens + width), transcendentals=0
+        ),
+        compiler_params=pltpu.CompilerParams(vmem_limit_bytes=40 * 2**20),
+        name="project",
+    )(jnp.stack([jnp.asarray(o, jnp.int32) for o in order]), everything, *[rows for _, _, rows in blocks], inverse)
+
+
+def output_kernel(order_ref, gated_ref, panel_ref, base_ref, out_ref):
+    total = base_ref[...].astype(f32)
+    for x in range(panel_ref.shape[0]):
+        total = total + jnp.dot(gated_ref[order_ref[x]], panel_ref[x], preferred_element_type=f32)
+    out_ref[...] = total.astype(out_ref.dtype)
+
+
+def add_outputs(gated, panel, group, order, base, dtype):
+    mp, tokens, share = gated.shape
+    columns = panel.shape[2]
+    tile = math.gcd(tokens, 256)
+    return pl.pallas_call(
+        output_kernel,
+        grid_spec=pltpu.PrefetchScalarGridSpec(
+            num_scalar_prefetch=1,
+            grid=(tokens // tile,),
+            in_specs=[
+                pl.BlockSpec((mp, tile, share), lambda m, order: (0, m, 0)),
+                pl.BlockSpec((mp, share, columns), lambda m, order: (0, group, 0)),
+                pl.BlockSpec((tile, columns), lambda m, order: (m, 0)),
+            ],
+            out_specs=pl.BlockSpec((tile, columns), lambda m, order: (m, 0)),
+        ),
+        out_shape=jax.ShapeDtypeStruct((tokens, columns), dtype),
+        cost_estimate=pl.CostEstimate(
+            flops=2 * tokens * columns * mp * share, bytes_accessed=2 * mp * share * (tokens + columns), transcendentals=0
+        ),
+        compiler_params=pltpu.CompilerParams(vmem_limit_bytes=40 * 2**20),
+        name="add_outputs",
+    )(order, gated, panel, base)
+
+
+def exchange(rows, axis, masks):
+    size = lax.axis_size(axis)
+    return [
+        rows[n] if mask == 0 else lax.ppermute(rows[n], axis, swap_route(size, mask)) for n, mask in enumerate(masks)
+    ]
+
+
+def output_panel(w_out, after):
+    channels, wide_columns = w_out.shape
+    ctx, mp = lax.axis_size("ctx"), lax.axis_size("mp")
+    me, place = lax.axis_index("ctx"), lax.axis_index("mp")
+    part, per = channels // ctx, mp // ctx
+    columns = wide_columns // per
+    if (ctx, mp) != (4, 8):
+        rows = lax.all_to_all(w_out.reshape(ctx, part, wide_columns), "ctx", 0, 0)
+        rows = rows.reshape(ctx, part, per, columns).swapaxes(1, 2).reshape(mp, part, columns)
+        rows = lax.all_to_all(rows, "mp", 0, 0)
+        panel = lax.all_gather(rows, "ctx", axis=1).reshape(mp, channels, columns)
+        return panel, jnp.arange(mp, dtype=jnp.int32)
+    mine = w_out.reshape(ctx, part, wide_columns)
+    sent = [lax.dynamic_index_in_dim(mine, me ^ d, 0, False) for d in range(ctx)]
+    by_owner = jnp.stack(exchange(sent, "ctx", range(ctx)))
+    by_owner = lax.optimization_barrier((by_owner, after))[0]
+    chip, core = place // per, place % per
+    sent = [lax.dynamic_index_in_dim(by_owner, (chip ^ d) ^ me, 0, False) for d in range(mp // per)]
+    rows = jnp.stack(exchange(sent, "mp", range(0, mp, per)))
+    keep = lax.dynamic_slice_in_dim(rows, core * columns, columns, 2)
+    give = lax.dynamic_slice_in_dim(rows, (core ^ 1) * columns, columns, 2)
+    rows = jnp.stack([keep, lax.ppermute(give, "mp", swap_route(mp, 1))], axis=1).reshape(mp, 1, part, columns)
+    panel = jnp.zeros((mp, ctx, part, columns), w_out.dtype)
+    for owner, first, block in gathered_blocks(rows):
+        panel = lax.dynamic_update_slice(panel, block, (first, owner, 0, 0))
+    return panel.reshape(mp, channels, columns), place ^ jnp.arange(mp, dtype=jnp.int32)
+
+
+def end_states(last):
+    size = lax.axis_size("ctx")
+    if size != 4:
+        return lax.all_gather(last, "ctx", axis=0)
+    return jnp.stack(exchange([last] * size, "ctx", range(size)))
+
+
+def ctx_order():
+    size = lax.axis_size("ctx")
+    return lax.axis_index("ctx") ^ jnp.arange(size) if size == 4 else jnp.arange(size)
+
+
 def filter_tables(decay_rate, residue, skip_gain, tokens):
     me = lax.axis_index("ctx")
     size = lax.axis_size("ctx")
@@ -208,7 +332,7 @@
     segment = tokens // SEGMENTS
     ahead = (SEGMENTS - 1 - jnp.arange(SEGMENTS, dtype=f32)) * segment
     reach = jnp.exp(-rate[:, None, :] * ahead[None, :, None]).reshape(modes * SEGMENTS, channels)
-    index = jnp.arange(size)
+    index = ctx_order()
     gap = (me - 1 - index).astype(f32) * tokens
     shares = jnp.where(
         (index < me)[:, None, None], jnp.exp(-rate[None] * jnp.maximum(gap, 0.0)[:, None, None]), 0.0
@@ -259,48 +383,29 @@
     everything = lax.all_gather(scaled, "mp", axis=0)
     squares = lax.psum(jnp.sum(act_float * act_float, axis=1), "mp")
     inverse = lax.rsqrt(squares / model_width + 1e-06)[:, None]
-    per_block = mp // ctx
-    by_block = everything.reshape(ctx, per_block, tokens, features)
-
-    def project(blocks):
-        total = None
-        for owner, first, rows in blocks:
-            for i in range(0, rows.shape[0], features):
-                source = lax.dynamic_index_in_dim(by_block, owner, 0, False)[(first + i) // features]
-                part = lax.dot_general(
-                    source, rows[i : i + features], (((1,), (0,)), ((), ())), preferred_element_type=f32
-                )
-                total = part if total is None else total + part
-        return total * inverse
-
     tables = filter_tables(decay_rate, residue, skip_gain, tokens)
     start_state = state_in.T
     taps_all = short_filter
     tails_all = tail_rows.transpose(2, 0, 1).astype(f32)
     pieces = [w_in[:, :, g * share : (g + 1) * share].reshape(-1, 3 * share) for g in range(groups)]
     arriving = [gathered_blocks(piece) for piece in pieces]
-    outputs = []
+    panel, order = output_panel(w_out, everything[0, :16, :LANES])
+    total = activations
     finals = []
     for g in range(groups):
         span = slice(g * share, (g + 1) * share)
         own = cut(tables, g * share, (g + 1) * share)
         taps = taps_all[:, :, span].reshape(3, 3 * share)
-        projected = project(arriving[g])
+        projected = project(everything, arriving[g], inverse)
         behind = lax.ppermute(projected[-2:], "ctx", [(i, i + 1) for i in range(ctx - 1)])
         tails = jnp.where(me == 0, tails_all[:, :, span].reshape(2, 3 * share), behind)
         response, ends, last = local_filter(projected, tails, taps, own)
-        lasts = lax.all_gather(last, "ctx", axis=0)
-        states = jnp.concatenate([lasts, start_state[None, :, span]])
+        states = jnp.concatenate([end_states(last), start_state[None, :, span]])
         finals.append(jnp.sum(own["final"] * states, axis=0))
-        outputs.append(
-            gated_signal(projected, tails, taps, own, response, ends, states.reshape(-1, share))
-        )
-    state_out = jnp.concatenate(finals, axis=1).T
-    gated = jnp.concatenate(outputs, axis=1)
-    panel = lax.all_gather(w_out, "ctx", axis=1, tiled=True)
-    partial = lax.dot_general(panel, gated, (((0,), (1,)), ((), ())), preferred_element_type=f32)
-    branch = lax.psum_scatter(partial.astype(bf16), "mp", scatter_dimension=0, tiled=True).astype(f32).T
-    return ((act_float + branch).astype(bf16), state_out)
+        gated = gated_signal(projected, tails, taps, own, response, ends, states.reshape(-1, share))
+        gated = lax.all_gather(gated, "mp", axis=0)
+        total = add_outputs(gated, panel, g, order, total, f32 if g < groups - 1 else bf16)
+    return (total, jnp.concatenate(finals, axis=1).T)
 
 
 def solution(mesh):

time: 300 us -> 304 us (1.013)
  matrix products: 66.7 us -> 0 us
  Pallas kernels: 16.2 us -> 46 us
  starting transfers between devices: 13.1 us -> 38 us
  local copies, waits for them, and re-layouts: 22.8 us -> 47.6 us
  blocking collectives: 27.1 us -> 15.5 us
  waiting for transfers between devices: 130 us -> 134 us
    reduce_scatter x1 -> x0, waiting for transfers between devices: 90.1 us -> none  [local(): lax.psum_scatter(partial.astype(bf16), 'mp', scatter_dimension=0, tiled=T...]
    dot_general x17 -> x0, matrix products: 66.7 us -> none  [the longest x16 57.7 us: project(): lax.dot_general(source, rows[i:i + features], (((1,), (0,)), ((), ())), p...]
    ppermute x0 -> x13, waiting for transfers between devices: none -> 42 us  [the longest x12 40.4 us: exchange(): lax.ppermute(rows[n], axis, swap_route(size, mask))]
    pallas_call x0 -> x4, Pallas kernels: none -> 29.8 us  [the longest x2 21.4 us: project(): pl.pallas_call(functools.partial(project_kernel, chunks), grid_spec=pltpu...]
    ppermute x2 -> x3, waiting for transfers between devices: 0.01 us -> 23 us  [gathered_blocks(): far_top = lax.ppermute(by_y[:half], 'ctx', swap_route(size, 1))]
    ppermute x2 -> x3, waiting for transfers between devices: 35.6 us -> 56.9 us  [gathered_blocks(): by_y = lax.ppermute(block, 'ctx', swap_route(size, 2))]
    ppermute x0 -> x13, starting transfers between devices: none -> 19.7 us  [the longest x12 11.7 us: exchange(): lax.ppermute(rows[n], axis, swap_route(size, mask))]
    unnamed x35 -> x87, local copies, waits for them, and re-layouts: 10.6 us -> 26.3 us
  transfers between devices with their start and end apart: 13 -> 30, of which waited for: 4 -> 13; matrix products, arithmetic and copies ran while one was open for 28% -> 10% of each run, Pallas kernels for 5% -> 11%
where the time goes in v1:
time: 304 us; the launch traced here: 301 us
  waiting for transfers between devices  134 us (44%)
  local copies, waits for them, and re-layouts  47.6 us (16%)
  Pallas kernels  46 us (15%)
  starting transfers between devices  38 us (12%)
  blocking collectives  15.5 us (5%)
  between operations  14.3 us (5%)
  other arithmetic  5.85 us (2%)
    ppermute x3, waiting for transfers between devices, gathered_blocks(): by_y = lax.ppermute(block, 'ctx', swap_route(size, 2))  56.9 us
    ppermute x12, waiting for transfers between devices, exchange(): lax.ppermute(rows[n], axis, swap_route(size, mask))  40.4 us
    unnamed x87, local copies, waits for them, and re-layouts  26.3 us
    ppermute x3, waiting for transfers between devices, gathered_blocks(): far_top = lax.ppermute(by_y[:half], 'ctx', swap_route(size, 1))  23 us
    pallas_call x2, Pallas kernels, project(): pl.pallas_call(functools.partial(project_kernel, chunks), grid_spec=pltpu...  21.4 us
    psum x1, blocking collectives, local(): squares = lax.psum(jnp.sum(act_float * act_float, axis=1), 'mp')  15.5 us
    all_gather x2, waiting for transfers between devices, local(): gated = lax.all_gather(gated, 'mp', axis=0)  12.1 us
    ppermute x12, starting transfers between devices, exchange(): lax.ppermute(rows[n], axis, swap_route(size, mask))  11.7 us
  transfers between devices with their start and end apart: 30, of which 13 were waited for; matrix products, arithmetic and copies ran while one was open for 10% of the time, Pallas kernels for 11%

profile of v1, /device:TPU:1, one launch (start us, length us, event | category | flops | bytes accessed | tf_op | source)
XLA Modules:
  0.0 301.2 jit_solution(13122649142775891698)
XLA Ops:
  7.2 2.5 fusion.1
  9.8 3.3 %fusion.10 = (bf16[1024,3,256]{2,0,1:T(8,128)(2,1)S(1)}, bf16[1024,3,256]{2,0,1:T(8,128)(2,1)}) fusion(bf16[1024,3,512]{2,0,1:T(8,128)(2,1)} %param.12), kind=kLoop, calls=%fused_computation.67 | loop fusion | bytes 6291456 | tf_op jit(solution)/shard_map/slice | solution.py:390
  13.0 0.9 copy.27
  14.6 2.1 collective-permute-start.20
  16.8 1.2 collective-permute-start.19
  18.0 2.7 copy.26
  20.7 1.8 copy.18.refs_0_
  22.9 15.5 %psum.7 = f32[1024]{0:T(1024)S(1)} all-reduce(f32[1024]{0:T(1024)S(1)} %get-tuple-element.28), channel_id=1, replica_groups=mesh['ctx'=4,'mp'=8] {'mp'}, use_global_device_ids=true, to_apply=%region_1.0 | all-reduce | flops 1024 | bytes 8192 | tf_op jit(solution)/shard_map/psum | solution.py:384
  38.4 1.1 copy.19.refs_5_
  40.8 0.8 multiply_exponential_fusion
  44.2 6.8 %collective-permute-done.20.refs_2_ = bf16[1024,768]{1,0:T(8,128)(2,1)} collective-permute-done((bf16[1024,768]{1,0:T(8,128)(2,1)S(1)}, bf16[1024,768]{1,0:T(8,128)(2,1)}, u32[]{:S(2)}, u32[]{:S(2)}) %collective-permute-start.20) | collective-permute-done | bytes 1572896 | tf_op jit(solution)/shard_map/ppermute | solution.py:30
  51.0 2.1 slice.152
  53.0 1.1 collective-permute-start.21
  54.2 2.1 slice.153
  56.2 1.2 collective-permute-start.22
  57.8 26.9 %collective-permute-done.1.refs_2_ = bf16[1024,768]{1,0:T(8,128)(2,1)} collective-permute-done((bf16[1024,768]{1,0:T(8,128)(2,1)S(1)}, bf16[1024,768]{1,0:T(8,128)(2,1)}, u32[]{:S(2)}, u32[]{:S(2)}) %collective-permute-start.1) | collective-permute-done | bytes 1572896 | tf_op jit(solution)/shard_map/ppermute | solution.py:30
  84.7 2.1 slice.137
  86.8 1.1 collective-permute-start.2
  87.9 1.2 slice.138
  89.1 1.3 collective-permute-start.3
  91.0 11.4 %collective-permute-done.21.refs_3_ = bf16[512,768]{1,0:T(8,128)(2,1)} collective-permute-done((bf16[512,768]{1,0:T(8,128)(2,1)}, bf16[512,768]{1,0:T(8,128)(2,1)}, u32[]{:S(2)}, u32[]{:S(2)}) %collective-permute-start.21) | collective-permute-done | bytes 786464 | tf_op jit(solution)/shard_map/ppermute | solution.py:31
  102.4 1.0 copy-done.14
  103.4 10.8 %project.3.k_ref.v_ref.q_ref = f32[1024,768]{1,0:T(8,128)S(1)} custom-call(s32[8]{0:T(128)S(1)} %stack.103.order_ref, bf16[8,1024,512]{2,1,0:T(8,128)(2,1)} %bitcast.135, bf16[1024,768]{1,0:T(8,128)(2,1)S(1)} %copy.24.refs_0_, bf16[1024,768]{1,0:T(8,128)(2,1)} %collective-permute-done.19.refs_1_, bf16[1024,768]{1,0:T(8,128)(2,1)} %collective-permute-done.20.refs_2_, ...), custom_call_target="tpu_custom_call" | custom-call | flops 6442450944 | bytes 14680064 | tf_op jit(solution)/shard_map/project/pallas_call | solution.py:226
  114.8 3.1 %collective-permute-start.23 = (f32[2,768]{1,0:T(2,128)}, f32[2,768]{1,0:T(2,128)S(1)}, u32[]{:S(2)}, u32[]{:S(2)}) collective-permute-start(f32[2,768]{1,0:T(2,128)} %slice.155), channel_id=1, source_target_pairs={{0,8},{8,16},{16,24},{1,9},{9,17},{17,25},{2,10},{10,18},{18,26},{... | collective-permute-start | bytes 18440 | tf_op jit(solution)/shard_map/ppermute | solution.py:400
  117.9 1.3 collective-permute-done.2.refs_3_
  119.2 0.9 copy-done.26
  120.1 1.1 copy-done.27
  121.2 10.6 %project.2.k_ref.v_ref.q_ref = f32[1024,768]{1,0:T(8,128)S(1)} custom-call(s32[8]{0:T(128)S(1)} %stack.103.order_ref, bf16[8,1024,512]{2,1,0:T(8,128)(2,1)} %bitcast.136, bf16[1024,768]{1,0:T(8,128)(2,1)S(1)} %copy-done.11, bf16[1024,768]{1,0:T(8,128)(2,1)} %collective-permute-done.refs_1_, bf16[1024,768]{1,0:T(8,128)(2,1)} %collective-permute-done.1.refs_2_, ...), custom_call_target="tpu_custom_call" | custom-call | flops 6442450944 | bytes 14680064 | tf_op jit(solution)/shard_map/project/pallas_call | solution.py:226
  132.5 3.7 %collective-permute-start.4 = (f32[2,768]{1,0:T(2,128)}, f32[2,768]{1,0:T(2,128)}, u32[]{:S(2)}, u32[]{:S(2)}) collective-permute-start(f32[2,768]{1,0:T(2,128)} %slice.140), channel_id=1, source_target_pairs={{0,8},{8,16},{16,24},{1,9},{9,17},{17,25},{2,10},{10,18},{18,26},{... | collective-permute-start | bytes 18440 | tf_op jit(solution)/shard_map/ppermute | solution.py:400
  140.4 5.1 %local_filter.2 = (f32[1024,256]{1,0:T(8,128)S(1)}, f32[128,256]{1,0:T(8,128)S(1)}, f32[16,256]{1,0:T(8,128)S(1)}) custom-call(f32[1024,768]{1,0:T(8,128)S(1)} %project.2.k_ref.v_ref.q_ref, f32[1024,768]{1,0:T(8,128)S(1)} %project.2.k_ref.v_ref.q_ref, f32[2,768]{1,0:T(2,128)S(1)} %get-tuple-element.62.tail_k_ref.tail_v_ref.tail_q_ref, ...), custom_call_target="tpu_custom_call" | custom-call | flops 16777216 | bytes 3145728 | tf_op jit(solution)/shard_map/local_filter/pallas_call | solution.py:139
  145.5 1.0 copy-done.12
  146.9 2.2 collective-permute-start.7
  149.1 5.1 %local_filter.3 = (f32[1024,256]{1,0:T(8,128)S(1)}, f32[128,256]{1,0:T(8,128)S(1)}, f32[16,256]{1,0:T(8,128)S(1)}) custom-call(f32[1024,768]{1,0:T(8,128)S(1)} %copy-done.4, f32[1024,768]{1,0:T(8,128)S(1)} %copy-done.4, f32[2,768]{1,0:T(2,128)S(1)} %get-tuple-element.61.tail_k_ref.tail_v_ref.tail_q_ref, ...), custom_call_target="tpu_custom_call" | custom-call | flops 16777216 | bytes 3145728 | tf_op jit(solution)/shard_map/local_filter/pallas_call | solution.py:139
  154.8 2.2 collective-permute-start.26
  157.1 1.2 collective-permute-done.26
  158.4 3.0 gated_signal.3
  161.4 0.8 copy-done.8
  162.5 1.2 copy-done.13
  163.7 0.9 copy-done.17
  164.6 3.0 gated_signal.2
  167.6 0.8 copy-done.9
  168.4 1.3 constant_dynamic-slice_fusion.2
  169.7 1.3 collective-permute-start.8
  171.0 1.2 collective-permute-start.9
  172.4 2.6 collective-permute-done.8
  175.0 4.4 %collective-permute-done.9 = bf16[128,1024]{1,0:T(8,128)(2,1)S(1)} collective-permute-done((bf16[128,1024]{1,0:T(8,128)(2,1)S(1)}, bf16[128,1024]{1,0:T(8,128)(2,1)S(1)}, u32[]{:S(2)}, u32[]{:S(2)}) %collective-permute-start.9) | collective-permute-done | bytes 262176 | tf_op jit(solution)/shard_map/ppermute | solution.py:282
  179.6 1.3 collective-permute-start.11
  180.9 2.3 collective-permute-start.12
  183.2 21.3 %collective-permute-done.11 = bf16[128,1024]{1,0:T(8,128)(2,1)S(1)} collective-permute-done((bf16[128,1024]{1,0:T(8,128)(2,1)S(1)}, bf16[128,1024]{1,0:T(8,128)(2,1)S(1)}, u32[]{:S(2)}, u32[]{:S(2)}) %collective-permute-start.11) | collective-permute-done | bytes 262176 | tf_op jit(solution)/shard_map/ppermute | solution.py:282
  204.6 10.8 %collective-permute-done.13 = bf16[128,1024]{1,0:T(8,128)(2,1)S(1)} collective-permute-done((bf16[128,1024]{1,0:T(8,128)(2,1)S(1)}, bf16[128,1024]{1,0:T(8,128)(2,1)S(1)}, u32[]{:S(2)}, u32[]{:S(2)}) %collective-permute-start.13) | collective-permute-done | bytes 262176 | tf_op jit(solution)/shard_map/ppermute | solution.py:282
  215.6 8.1 %collective-permute-start.14 = (bf16[4,128,512]{2,1,0:T(8,128)(2,1)S(1)}, bf16[4,128,512]{2,1,0:T(8,128)(2,1)S(1)}, u32[]{:S(2)}, u32[]{:S(2)}) collective-permute-start(bf16[4,128,512]{2,1,0:T(8,128)(2,1)S(1)} %get-tuple-element.19), channel_id=1, source_target_pairs={{0,1},{1,0},{2,3},{3,2},{4,5},{5,4},{6,7},{7,6},{8,9},{9,8},{10,11... | collective-permute-start | bytes 1572872 | tf_op jit(solution)/shard_map/ppermute | solution.py:307
  223.7 1.5 collective-permute-done.14
  226.0 0.7 collective-permute-start.15
  226.8 23.2 %collective-permute-done.16 = bf16[8,1,128,512]{3,2,1,0:T(8,128)(2,1)S(1)} collective-permute-done((bf16[8,1,128,512]{3,2,1,0:T(8,128)(2,1)S(1)}, bf16[8,1,128,512]{3,2,1,0:T(8,128)(2,1)S(1)}, u32[]{:S(2)}, u32[]{:S(2)}) %collective-permute-start.16) | collective-permute-done | bytes 1048608 | tf_op jit(solution)/shard_map/ppermute | solution.py:30
  250.5 0.9 collective-permute-start.18
  252.2 10.3 %collective-permute-done.17 = bf16[4,1,128,512]{3,2,1,0:T(8,128)(2,1)S(1)} collective-permute-done((bf16[4,1,128,512]{3,2,1,0:T(8,128)(2,1)S(1)}, bf16[4,1,128,512]{3,2,1,0:T(8,128)(2,1)S(1)}, u32[]{:S(2)}, u32[]{:S(2)}) %collective-permute-start.17) | collective-permute-done | bytes 524320 | tf_op jit(solution)/shard_map/ppermute | solution.py:31
  262.6 2.1 copy-done
  265.4 2.2 copy-done.1
  267.6 2.2 copy-done.6
  269.8 3.9 %add_outputs.2.base_ref = f32[1024,512]{1,0:T(8,128)S(1)} custom-call(s32[8]{0:T(128)S(1)} %iota_xor_fusion.1.order_ref, bf16[8,1024,256]{2,1,0:T(8,128)(2,1)S(1)} %bitcast.105, bf16[8,512,512]{2,1,0:T(8,128)(2,1)S(1)} %bitcast.103, bf16[1024,512]{1,0:T(8,128)(2,1)S(1)} %copy-done.5), custom_call_target="tpu_custom_call" | custom-call | flops 2147483648 | bytes 6291456 | tf_op jit(solution)/shard_map/add_outputs/pallas_call | solution.py:258
  273.7 12.1 %all-gather.9.cloned.1.call-done = bf16[8192,256]{1,0:T(8,128)(2,1)} async-done(((bf16[1024,256]{1,0:T(8,128)(2,1)}), bf16[8192,256]{1,0:T(8,128)(2,1)}) %all-gather.9.cloned.1.call-update) | async-done | bytes 4194320 | tf_op jit(solution)/shard_map/all_gather | solution.py:406
  285.7 2.2 copy-done.2
  287.9 2.2 copy-done.7
  290.1 4.6 %add_outputs.3 = bf16[1024,512]{1,0:T(8,128)(2,1)} custom-call(s32[8]{0:T(128)S(1)} %iota_xor_fusion.1.order_ref, bf16[8,1024,256]{2,1,0:T(8,128)(2,1)S(1)} %bitcast.106, bf16[8,512,512]{2,1,0:T(8,128)(2,1)S(1)} %bitcast.104, f32[1024,512]{1,0:T(8,128)S(1)} %add_outputs.2.base_ref), custom_call_target="tpu_custom_call" | custom-call | flops 2147483648 | bytes 6291456 | tf_op jit(solution)/shard_map/add_outputs/pallas_call | solution.py:258
  (147 shorter events, 16.3 us)
Async XLA Ops:
  7.2 95.2 %all-gather.7.cloned.1.call-start = ((), (), s32[]{:S(2)}) async-start(), calls=%async_computation | async-start | bytes 9437184 | tf_op jit(solution)/shard_map/all_gather | solution.py:383
  9.7 255.7 %all-gather.11.cloned.1.call-start = ((), (), s32[]{:S(2)}) async-start(), calls=%async_computation.2 | async-start | bytes 4718592 | tf_op jit(solution)/shard_map/all_gather | solution.py:406
  14.6 36.4 %collective-permute-start.20 = (bf16[1024,768]{1,0:T(8,128)(2,1)S(1)}, bf16[1024,768]{1,0:T(8,128)(2,1)}, u32[]{:S(2)}, u32[]{:S(2)}) collective-permute-start(bf16[1024,768]{1,0:T(8,128)(2,1)S(1)} %copy.24.refs_0_), channel_id=1, source_target_pairs={{0,16},{8,24},{16,0},{24,8},{1,17},{9,25},{17,1},{25,9},{2,18},{10... | collective-permute-start | bytes 4718600 | tf_op jit(solution)/shard_map/ppermute | solution.py:30
  16.8 37.4 %collective-permute-start.19 = (bf16[1024,768]{1,0:T(8,128)(2,1)S(1)}, bf16[1024,768]{1,0:T(8,128)(2,1)}, u32[]{:S(2)}, u32[]{:S(2)}) collective-permute-start(bf16[1024,768]{1,0:T(8,128)(2,1)S(1)} %copy.24.refs_0_), channel_id=1, source_target_pairs={{0,8},{8,0},{16,24},{24,16},{1,9},{9,1},{17,25},{25,17},{2,10},{10... | collective-permute-start | bytes 4718600 | tf_op jit(solution)/shard_map/ppermute | solution.py:29
  18.0 21.5 %copy-start.35 = (bf16[3,512,2]{1,2,0:T(2,128)(2,1)S(1)}, bf16[3,512,2]{1,2,0:T(2,128)(2,1)}, u32[]{:S(2)}) copy-start(bf16[3,512,2]{1,2,0:T(2,128)(2,1)} %param.13) | copy-start | bytes 18436
  18.0 21.6 %copy-start.33 = (f32[3,3,512]{2,1,0:T(4,128)S(1)}, f32[3,3,512]{2,1,0:T(4,128)}, u32[]{:S(2)}) copy-start(f32[3,3,512]{2,1,0:T(4,128)} %param.14) | copy-start | bytes 55300
  18.0 22.2 %copy-start.29 = (f32[512,16]{0,1:T(8,128)S(1)}, f32[512,16]{0,1:T(8,128)}, u32[]{:S(2)}) copy-start(f32[512,16]{0,1:T(8,128)} %param.15) | copy-start | bytes 98308
  18.0 22.2 %copy-start.30 = (f32[512,16]{0,1:T(8,128)S(1)}, f32[512,16]{0,1:T(8,128)}, u32[]{:S(2)}) copy-start(f32[512,16]{0,1:T(8,128)} %param.16) | copy-start | bytes 98308
  22.5 64.3 %copy-start.10 = (bf16[1024,768]{1,0:T(8,128)(2,1)}, bf16[1024,768]{1,0:T(8,128)(2,1)S(1)}, u32[]{:S(2)}) copy-start(bf16[1024,768]{1,0:T(8,128)(2,1)S(1)} %copy.18.refs_0_) | copy-start | bytes 4718596
  22.5 62.2 %collective-permute-start.1 = (bf16[1024,768]{1,0:T(8,128)(2,1)S(1)}, bf16[1024,768]{1,0:T(8,128)(2,1)}, u32[]{:S(2)}, u32[]{:S(2)}) collective-permute-start(bf16[1024,768]{1,0:T(8,128)(2,1)S(1)} %copy.18.refs_0_), channel_id=1, source_target_pairs={{0,16},{8,24},{16,0},{24,8},{1,17},{9,25},{17,1},{25,9},{2,18},{10... | collective-permute-start | bytes 4718600 | tf_op jit(solution)/shard_map/ppermute | solution.py:30
  22.8 65.1 %collective-permute-start = (bf16[1024,768]{1,0:T(8,128)(2,1)S(1)}, bf16[1024,768]{1,0:T(8,128)(2,1)}, u32[]{:S(2)}, u32[]{:S(2)}) collective-permute-start(bf16[1024,768]{1,0:T(8,128)(2,1)S(1)} %copy.18.refs_0_), channel_id=1, source_target_pairs={{0,8},{8,0},{16,24},{24,16},{1,9},{9,1},{17,25},{25,17},{2,10},{10... | collective-permute-start | bytes 4718600 | tf_op jit(solution)/shard_map/ppermute | solution.py:29
  53.0 49.3 %collective-permute-start.21 = (bf16[512,768]{1,0:T(8,128)(2,1)}, bf16[512,768]{1,0:T(8,128)(2,1)}, u32[]{:S(2)}, u32[]{:S(2)}) collective-permute-start(bf16[512,768]{1,0:T(8,128)(2,1)} %slice.152), channel_id=1, source_target_pairs={{0,8},{8,0},{16,24},{24,16},{1,9},{9,1},{17,25},{25,17},{2,10},{10... | collective-permute-start | bytes 2359304 | tf_op jit(solution)/shard_map/ppermute | solution.py:31
  56.2 46.1 %collective-permute-start.22 = (bf16[512,768]{1,0:T(8,128)(2,1)}, bf16[512,768]{1,0:T(8,128)(2,1)}, u32[]{:S(2)}, u32[]{:S(2)}) collective-permute-start(bf16[512,768]{1,0:T(8,128)(2,1)} %slice.153), channel_id=1, source_target_pairs={{0,16},{8,24},{16,0},{24,8},{1,17},{9,25},{17,1},{25,9},{2,18},{10... | collective-permute-start | bytes 2359304 | tf_op jit(solution)/shard_map/ppermute | solution.py:32
  86.8 32.5 %collective-permute-start.2 = (bf16[512,768]{1,0:T(8,128)(2,1)}, bf16[512,768]{1,0:T(8,128)(2,1)}, u32[]{:S(2)}, u32[]{:S(2)}) collective-permute-start(bf16[512,768]{1,0:T(8,128)(2,1)} %slice.137), channel_id=1, source_target_pairs={{0,8},{8,0},{16,24},{24,16},{1,9},{9,1},{17,25},{25,17},{2,10},{10... | collective-permute-start | bytes 2359304 | tf_op jit(solution)/shard_map/ppermute | solution.py:31
  89.1 30.1 %collective-permute-start.3 = (bf16[512,768]{1,0:T(8,128)(2,1)S(1)}, bf16[512,768]{1,0:T(8,128)(2,1)S(1)}, u32[]{:S(2)}, u32[]{:S(2)}) collective-permute-start(bf16[512,768]{1,0:T(8,128)(2,1)S(1)} %slice.138), channel_id=1, source_target_pairs={{0,16},{8,24},{16,0},{24,8},{1,17},{9,25},{17,1},{25,9},{2,18},{10... | collective-permute-start | bytes 2359304 | tf_op jit(solution)/shard_map/ppermute | solution.py:32
  102.4 1.0 copy-start.14
  103.4 16.7 %copy-start.11 = (bf16[1024,768]{1,0:T(8,128)(2,1)S(1)}, bf16[1024,768]{1,0:T(8,128)(2,1)}, u32[]{:S(2)}) copy-start(bf16[1024,768]{1,0:T(8,128)(2,1)} %copy-done.10) | copy-start | bytes 4718596
  114.2 17.7 %copy-start.3 = (f32[1024,768]{1,0:T(8,128)}, f32[1024,768]{1,0:T(8,128)S(1)}, u32[]{:S(2)}) copy-start(f32[1024,768]{1,0:T(8,128)S(1)} %project.3.k_ref.v_ref.q_ref) | copy-start | bytes 9437188
  114.2 22.0 %copy-start.36 = (f32[512]{0:T(512)S(1)}, f32[512]{0:T(512)}, u32[]{:S(2)}) copy-start(f32[512]{0:T(512)} %param.17) | copy-start | bytes 6148
  114.8 22.8 %collective-permute-start.23 = (f32[2,768]{1,0:T(2,128)}, f32[2,768]{1,0:T(2,128)S(1)}, u32[]{:S(2)}, u32[]{:S(2)}) collective-permute-start(f32[2,768]{1,0:T(2,128)} %slice.155), channel_id=1, source_target_pairs={{0,8},{8,16},{16,24},{1,9},{9,17},{17,25},{2,10},{10,18},{18,26},{... | collective-permute-start | bytes 18440 | tf_op jit(solution)/shard_map/ppermute | solution.py:400
  119.2 0.9 copy-start.26
  120.1 1.1 copy-start.27
  132.5 5.1 %collective-permute-start.4 = (f32[2,768]{1,0:T(2,128)}, f32[2,768]{1,0:T(2,128)}, u32[]{:S(2)}, u32[]{:S(2)}) collective-permute-start(f32[2,768]{1,0:T(2,128)} %slice.140), channel_id=1, source_target_pairs={{0,8},{8,16},{16,24},{1,9},{9,17},{17,25},{2,10},{10,18},{18,26},{... | collective-permute-start | bytes 18440 | tf_op jit(solution)/shard_map/ppermute | solution.py:400
  140.3 8.7 %copy-start.4 = (f32[1024,768]{1,0:T(8,128)S(1)}, f32[1024,768]{1,0:T(8,128)}, u32[]{:S(2)}) copy-start(f32[1024,768]{1,0:T(8,128)} %copy-done.3) | copy-start | bytes 9437188
  140.3 8.7 %copy-start.22 = (f32[16,256]{1,0:T(8,128)S(1)}, f32[16,256]{1,0:T(8,128)}, u32[]{:S(2)}) copy-start(f32[16,256]{1,0:T(8,128)} %get-tuple-element.45.weight_ref) | copy-start | bytes 49156
  140.3 8.7 %copy-start.23 = (f32[16,256]{1,0:T(8,128)S(1)}, f32[16,256]{1,0:T(8,128)}, u32[]{:S(2)}) copy-start(f32[16,256]{1,0:T(8,128)} %get-tuple-element.43.scale_ref) | copy-start | bytes 49156
  145.4 1.0 copy-start.12
  146.4 7.8 %copy-start.16 = (f32[128,256]{1,0:T(8,128)}, f32[128,256]{1,0:T(8,128)S(1)}, u32[]{:S(2)}) copy-start(f32[128,256]{1,0:T(8,128)S(1)} %get-tuple-element.9.ends_ref) | copy-start | bytes 393220
  146.4 8.4 %collective-permute-start.5 = (f32[16,256]{1,0:T(8,128)S(1)}, f32[16,256]{1,0:T(8,128)S(1)}, u32[]{:S(2)}, u32[]{:S(2)}) collective-permute-start(f32[16,256]{1,0:T(8,128)S(1)} %get-tuple-element.10), channel_id=1, source_target_pairs={{0,8},{8,0},{16,24},{24,16},{1,9},{9,1},{17,25},{25,17},{2,10},{10... | collective-permute-start | bytes 49160 | tf_op jit(solution)/shard_map/ppermute | solution.py:282
  146.6 10.4 %collective-permute-start.6 = (f32[16,256]{1,0:T(8,128)S(1)}, f32[16,256]{1,0:T(8,128)S(1)}, u32[]{:S(2)}, u32[]{:S(2)}) collective-permute-start(f32[16,256]{1,0:T(8,128)S(1)} %get-tuple-element.10), channel_id=1, source_target_pairs={{0,16},{8,24},{16,0},{24,8},{1,17},{9,25},{17,1},{25,9},{2,18},{10... | collective-permute-start | bytes 49160 | tf_op jit(solution)/shard_map/ppermute | solution.py:282
  146.9 10.1 %collective-permute-start.7 = (f32[16,256]{1,0:T(8,128)S(1)}, f32[16,256]{1,0:T(8,128)S(1)}, u32[]{:S(2)}, u32[]{:S(2)}) collective-permute-start(f32[16,256]{1,0:T(8,128)S(1)} %get-tuple-element.10), channel_id=1, source_target_pairs={{0,24},{8,16},{16,8},{24,0},{1,25},{9,17},{17,9},{25,1},{2,26},{10... | collective-permute-start | bytes 49160 | tf_op jit(solution)/shard_map/ppermute | solution.py:282
  149.1 9.2 %copy-start.32 = (f32[512,16]{0,1:T(8,128)S(1)}, f32[512,16]{0,1:T(8,128)}, u32[]{:S(2)}) copy-start(f32[512,16]{0,1:T(8,128)} %param.18) | copy-start | bytes 98308
  149.1 9.2 %copy-start.15 = (f32[80,256]{1,0:T(8,128)S(1)}, f32[80,256]{1,0:T(8,128)}, u32[]{:S(2)}) copy-start(f32[80,256]{1,0:T(8,128)} %get-tuple-element.32.shares_ref) | copy-start | bytes 245764
  149.1 9.2 %copy-start.19 = (f32[16,256]{1,0:T(8,128)S(1)}, f32[16,256]{1,0:T(8,128)}, u32[]{:S(2)}) copy-start(f32[16,256]{1,0:T(8,128)} %get-tuple-element.47.residue_ref) | copy-start | bytes 49156
  149.1 9.2 %copy-start.21 = (f32[16,256]{1,0:T(8,128)S(1)}, f32[16,256]{1,0:T(8,128)}, u32[]{:S(2)}) copy-start(f32[16,256]{1,0:T(8,128)} %get-tuple-element.64.hop_ref) | copy-start | bytes 49156
  154.2 8.2 %copy-start.18 = (f32[16,256]{1,0:T(8,128)S(1)}, f32[16,256]{1,0:T(8,128)}, u32[]{:S(2)}) copy-start(f32[16,256]{1,0:T(8,128)} %get-tuple-element.48.residue_ref) | copy-start | bytes 49156
  154.2 8.2 %copy-start.20 = (f32[16,256]{1,0:T(8,128)S(1)}, f32[16,256]{1,0:T(8,128)}, u32[]{:S(2)}) copy-start(f32[16,256]{1,0:T(8,128)} %get-tuple-element.63.hop_ref) | copy-start | bytes 49156
  154.3 2.8 collective-permute-start.24
  154.5 2.6 collective-permute-start.25
  154.8 3.5 %collective-permute-start.26 = (f32[16,256]{1,0:T(8,128)S(1)}, f32[16,256]{1,0:T(8,128)S(1)}, u32[]{:S(2)}, u32[]{:S(2)}) collective-permute-start(f32[16,256]{1,0:T(8,128)S(1)} %get-tuple-element.13), channel_id=1, source_target_pairs={{0,24},{8,16},{16,8},{24,0},{1,25},{9,17},{17,9},{25,1},{2,26},{10... | collective-permute-start | bytes 49160 | tf_op jit(solution)/shard_map/ppermute | solution.py:282
  161.3 0.8 copy-start.8
  162.2 123.5 %all-gather.9.cloned.1.call-start = ((), (), s32[]{:S(2)}) async-start(), calls=%async_computation.1 | async-start | bytes 4718592 | tf_op jit(solution)/shard_map/all_gather | solution.py:406
  162.4 1.2 copy-start.13
  163.7 0.9 copy-start.17
  167.6 0.8 copy-start.9
  169.7 5.3 %collective-permute-start.8 = (bf16[128,1024]{1,0:T(8,128)(2,1)S(1)}, bf16[128,1024]{1,0:T(8,128)(2,1)S(1)}, u32[]{:S(2)}, u32[]{:S(2)}) collective-permute-start(bf16[128,1024]{1,0:T(8,128)(2,1)S(1)} %get-tuple-element.27), channel_id=1, source_target_pairs={{0,8},{8,0},{16,24},{24,16},{1,9},{9,1},{17,25},{25,17},{2,10},{10... | collective-permute-start | bytes 786440 | tf_op jit(solution)/shard_map/ppermute | solution.py:282
  171.0 8.4 %collective-permute-start.9 = (bf16[128,1024]{1,0:T(8,128)(2,1)S(1)}, bf16[128,1024]{1,0:T(8,128)(2,1)S(1)}, u32[]{:S(2)}, u32[]{:S(2)}) collective-permute-start(bf16[128,1024]{1,0:T(8,128)(2,1)S(1)} %get-tuple-element.26), channel_id=1, source_target_pairs={{0,16},{8,24},{16,0},{24,8},{1,17},{9,25},{17,1},{25,9},{2,18},{10... | collective-permute-start | bytes 786440 | tf_op jit(solution)/shard_map/ppermute | solution.py:282
  172.2 7.2 %collective-permute-start.10 = (bf16[128,1024]{1,0:T(8,128)(2,1)S(1)}, bf16[128,1024]{1,0:T(8,128)(2,1)S(1)}, u32[]{:S(2)}, u32[]{:S(2)}) collective-permute-start(bf16[128,1024]{1,0:T(8,128)(2,1)S(1)} %get-tuple-element.25), channel_id=1, source_target_pairs={{0,24},{8,16},{16,8},{24,0},{1,25},{9,17},{17,9},{25,1},{2,26},{10... | collective-permute-start | bytes 786440 | tf_op jit(solution)/shard_map/ppermute | solution.py:282
  179.6 25.0 %collective-permute-start.11 = (bf16[128,1024]{1,0:T(8,128)(2,1)S(1)}, bf16[128,1024]{1,0:T(8,128)(2,1)S(1)}, u32[]{:S(2)}, u32[]{:S(2)}) collective-permute-start(bf16[128,1024]{1,0:T(8,128)(2,1)S(1)} %get-tuple-element.23), channel_id=1, source_target_pairs={{0,2},{1,3},{2,0},{3,1},{4,6},{5,7},{6,4},{7,5},{8,10},{9,11},{10,... | collective-permute-start | bytes 786440 | tf_op jit(solution)/shard_map/ppermute | solution.py:282
  180.9 23.7 %collective-permute-start.12 = (bf16[128,1024]{1,0:T(8,128)(2,1)S(1)}, bf16[128,1024]{1,0:T(8,128)(2,1)S(1)}, u32[]{:S(2)}, u32[]{:S(2)}) collective-permute-start(bf16[128,1024]{1,0:T(8,128)(2,1)S(1)} %get-tuple-element.22), channel_id=1, source_target_pairs={{0,4},{1,5},{2,6},{3,7},{4,0},{5,1},{6,2},{7,3},{8,12},{9,13},{10,... | collective-permute-start | bytes 786440 | tf_op jit(solution)/shard_map/ppermute | solution.py:282
  183.2 32.2 %collective-permute-start.13 = (bf16[128,1024]{1,0:T(8,128)(2,1)S(1)}, bf16[128,1024]{1,0:T(8,128)(2,1)S(1)}, u32[]{:S(2)}, u32[]{:S(2)}) collective-permute-start(bf16[128,1024]{1,0:T(8,128)(2,1)S(1)} %get-tuple-element.21), channel_id=1, source_target_pairs={{0,6},{1,7},{2,4},{3,5},{4,2},{5,3},{6,0},{7,1},{8,14},{9,15},{10,... | collective-permute-start | bytes 786440 | tf_op jit(solution)/shard_map/ppermute | solution.py:282
  215.6 9.6 %collective-permute-start.14 = (bf16[4,128,512]{2,1,0:T(8,128)(2,1)S(1)}, bf16[4,128,512]{2,1,0:T(8,128)(2,1)S(1)}, u32[]{:S(2)}, u32[]{:S(2)}) collective-permute-start(bf16[4,128,512]{2,1,0:T(8,128)(2,1)S(1)} %get-tuple-element.19), channel_id=1, source_target_pairs={{0,1},{1,0},{2,3},{3,2},{4,5},{5,4},{6,7},{7,6},{8,9},{9,8},{10,11... | collective-permute-start | bytes 1572872 | tf_op jit(solution)/shard_map/ppermute | solution.py:307
  225.4 24.5 %collective-permute-start.16 = (bf16[8,1,128,512]{3,2,1,0:T(8,128)(2,1)S(1)}, bf16[8,1,128,512]{3,2,1,0:T(8,128)(2,1)S(1)}, u32[]{:S(2)}, u32[]{:S(2)}) collective-permute-start(bf16[8,1,128,512]{3,2,1,0:T(8,128)(2,1)S(1)} %bitcast.117), channel_id=1, source_target_pairs={{0,16},{8,24},{16,0},{24,8},{1,17},{9,25},{17,1},{25,9},{2,18},{10... | collective-permute-start | bytes 3145736 | tf_op jit(solution)/shard_map/ppermute | solution.py:30
  226.0 24.4 %collective-permute-start.15 = (bf16[8,1,128,512]{3,2,1,0:T(8,128)(2,1)S(1)}, bf16[8,1,128,512]{3,2,1,0:T(8,128)(2,1)S(1)}, u32[]{:S(2)}, u32[]{:S(2)}) collective-permute-start(bf16[8,1,128,512]{3,2,1,0:T(8,128)(2,1)S(1)} %bitcast.118), channel_id=1, source_target_pairs={{0,8},{8,0},{16,24},{24,16},{1,9},{9,1},{17,25},{25,17},{2,10},{10... | collective-permute-start | bytes 3145736 | tf_op jit(solution)/shard_map/ppermute | solution.py:29
  250.0 12.5 %collective-permute-start.17 = (bf16[4,1,128,512]{3,2,1,0:T(8,128)(2,1)S(1)}, bf16[4,1,128,512]{3,2,1,0:T(8,128)(2,1)S(1)}, u32[]{:S(2)}, u32[]{:S(2)}) collective-permute-start(bf16[4,1,128,512]{3,2,1,0:T(8,128)(2,1)S(1)} %slice.150), channel_id=1, source_target_pairs={{0,8},{8,0},{16,24},{24,16},{1,9},{9,1},{17,25},{25,17},{2,10},{10... | collective-permute-start | bytes 1572872 | tf_op jit(solution)/shard_map/ppermute | solution.py:31
  250.5 12.1 %collective-permute-start.18 = (bf16[4,1,128,512]{3,2,1,0:T(8,128)(2,1)S(1)}, bf16[4,1,128,512]{3,2,1,0:T(8,128)(2,1)S(1)}, u32[]{:S(2)}, u32[]{:S(2)}) collective-permute-start(bf16[4,1,128,512]{3,2,1,0:T(8,128)(2,1)S(1)} %slice.151), channel_id=1, source_target_pairs={{0,16},{8,24},{16,0},{24,8},{1,17},{9,25},{17,1},{25,9},{2,18},{10... | collective-permute-start | bytes 1572872 | tf_op jit(solution)/shard_map/ppermute | solution.py:32
  251.9 12.8 %copy-start.28 = (f32[4,16,512]{2,1,0:T(8,128)S(1)}, f32[4,16,512]{2,1,0:T(8,128)}, u32[]{:S(2)}) copy-start(f32[4,16,512]{2,1,0:T(8,128)} %get-tuple-element.39) | copy-start | bytes 393220
  252.0 12.8 %copy-start.31 = (f32[1,16,512]{2,1,0:T(8,128)S(1)}, f32[1,16,512]{2,1,0:T(8,128)}, u32[]{:S(2)}) copy-start(f32[1,16,512]{2,1,0:T(8,128)} %get-tuple-element.34) | copy-start | bytes 98308
  252.0 13.4 %copy-start.5 = (bf16[1024,512]{1,0:T(8,128)(2,1)S(1)}, bf16[1024,512]{1,0:T(8,128)(2,1)}, u32[]{:S(2)}) copy-start(bf16[1024,512]{1,0:T(8,128)(2,1)} %base_ref.1) | copy-start | bytes 3145732
  262.6 2.1 copy-start
  265.4 2.2 copy-start.1
  267.6 2.2 copy-start.6
  285.7 2.2 copy-start.2
  287.9 2.2 copy-start.7
  (3 other events, 2.0 us)
Sparse Core Ops, SparseCore 0:
  10.2 84.8 all-gather.6
  162.3 75.2 all-gather.10
  239.8 45.8 all-gather.8

commit v2 on v0

--- a/solution.py
+++ b/solution.py
@@ -1,4 +1,5 @@
 import functools
+import math
 
 import jax
 import jax.numpy as jnp
@@ -9,6 +10,7 @@
 
 LANES = 128
 SEGMENTS = 8
+TAIL = 16
 f32 = jnp.float32
 bf16 = jnp.bfloat16
 
@@ -17,25 +19,26 @@
     return [(i, i ^ bit) for i in range(size)]
 
 
-def gathered_blocks(block):
-    size = lax.axis_size("ctx")
-    me = lax.axis_index("ctx")
-    rows = block.shape[0]
-    if size != 4:
-        whole = lax.all_gather(block, "ctx", axis=0)
-        return [(i, 0, whole[i]) for i in range(size)]
-    half = rows // 2
-    by_x = lax.ppermute(block, "ctx", swap_route(size, 1))
-    by_y = lax.ppermute(block, "ctx", swap_route(size, 2))
-    far_top = lax.ppermute(by_y[:half], "ctx", swap_route(size, 1))
-    far_bottom = lax.ppermute(by_x[half:], "ctx", swap_route(size, 2))
-    return [
-        (me, 0, block),
-        (me ^ 1, 0, by_x),
-        (me ^ 2, 0, by_y),
-        (me ^ 3, 0, far_top),
-        (me ^ 3, half, far_bottom),
-    ]
+def tie(values, *after):
+    return lax.optimization_barrier((values, after))[0]
+
+
+def corner(array):
+    return array[(slice(0, 1),) * (array.ndim - 2) + (slice(0, 16), slice(0, LANES))]
+
+
+def near_blocks(top, bottom):
+    along_x, along_y = swap_route(4, 1), swap_route(4, 2)
+    return (
+        lax.ppermute(top, "ctx", along_y),
+        lax.ppermute(bottom, "ctx", along_x),
+        lax.ppermute(top, "ctx", along_x),
+        lax.ppermute(bottom, "ctx", along_y),
+    )
+
+
+def far_blocks(y_top, x_bottom):
+    return lax.ppermute(y_top, "ctx", swap_route(4, 1)), lax.ppermute(x_bottom, "ctx", swap_route(4, 2))
 
 
 def shifted_start(ref, tail_ref, back, segment):
@@ -199,6 +202,141 @@
     )
 
 
+def project_kernel(tails_at, offsets, slot_ref, *refs):
+    count, blocks = len(offsets), len(refs) - 6 - len(offsets) - len(set(t for t, _ in tails_at))
+    tail_refs = dict(zip(sorted(set(t for t, _ in tails_at)), refs[count:]))
+    all_refs = refs[:count]
+    block_refs = refs[count + len(tail_refs) : count + len(tail_refs) + blocks]
+    inverse_ref, tail_inverse_ref, out_ref, tail_out_ref, held_ref, arrived = refs[-6:]
+
+    def total(first_rows):
+        result = None
+        for n in range(count):
+            rows = all_refs[n][...]
+            if first_rows:
+                which, at = tails_at[n]
+                rows = jnp.concatenate([tail_refs[which][at : at + TAIL, :], rows], axis=0)
+            weights = held_ref[slot_ref[n], offsets[n] : offsets[n] + rows.shape[1], :]
+            part = jnp.dot(rows, weights, preferred_element_type=f32)
+            result = part if result is None else result + part
+        return result
+
+    @pl.when(pl.program_id(0) == 0)
+    def _():
+        copies = [
+            pltpu.make_async_copy(block_refs[n], held_ref.at[n], arrived.at[n]) for n in range(blocks)
+        ]
+        for copy in copies:
+            copy.start()
+        for copy in copies:
+            copy.wait()
+        result = total(True)
+        tail_out_ref[...] = result[:TAIL] * tail_inverse_ref[...]
+        out_ref[...] = result[TAIL:] * inverse_ref[...]
+
+    @pl.when(pl.program_id(0) > 0)
+    def _():
+        out_ref[...] = total(False) * inverse_ref[...]
+
+
+def project(pieces, tails_at, blocks, slots, offsets, inverse, tail_inverse):
+    tokens = inverse.shape[0]
+    depth, width = blocks[0].shape
+    tile = math.gcd(tokens, 256)
+    tail_block = tokens // (2 * TAIL)
+    carriers = sorted(set(t for t, _ in tails_at))
+    features = sum(piece.shape[1] for piece in pieces)
+    return pl.pallas_call(
+        functools.partial(project_kernel, tails_at, offsets),
+        grid_spec=pltpu.PrefetchScalarGridSpec(
+            num_scalar_prefetch=1,
+            grid=(tokens // tile,),
+            in_specs=[
+                *[pl.BlockSpec((tile, piece.shape[1]), lambda m, slots: (m, 0)) for piece in pieces],
+                *[pl.BlockSpec((2 * TAIL, pieces[t].shape[1]), lambda m, slots: (tail_block, 0)) for t in carriers],
+                *[pl.BlockSpec(memory_space=pl.ANY) for _ in blocks],
+                pl.BlockSpec((tile, 1), lambda m, slots: (m, 0)),
+                pl.BlockSpec((TAIL, 1), lambda m, slots: (0, 0)),
+            ],
+            out_specs=[
+                pl.BlockSpec((tile, width), lambda m, slots: (m, 0)),
+                pl.BlockSpec((TAIL, width), lambda m, slots: (0, 0)),
+            ],
+            scratch_shapes=[
+                pltpu.VMEM((len(blocks), depth, width), bf16),
+                pltpu.SemaphoreType.DMA((len(blocks),)),
+            ],
+        ),
+        out_shape=[jax.ShapeDtypeStruct((tokens, width), f32), jax.ShapeDtypeStruct((TAIL, width), f32)],
+        cost_estimate=pl.CostEstimate(
+            flops=2 * tokens * width * features, bytes_accessed=2 * features * (tokens + width), transcendentals=0
+        ),
+        compiler_params=pltpu.CompilerParams(vmem_limit_bytes=40 * 2**20),
+        name="project",
+    )(slots, *pieces, *[pieces[t] for t in carriers], *blocks, inverse, tail_inverse)
+
+
+def output_kernel(count, order_ref, half_ref, *refs):
+    gated_refs, panel_ref, base_refs, out_ref = refs[:count], refs[count], refs[count + 1 : -1], refs[-1]
+    total = None
+    for n in range(count):
+        part = jnp.dot(gated_refs[n][...], panel_ref[order_ref[n]], preferred_element_type=f32)
+        total = part if total is None else total + part
+    for base_ref in base_refs:
+        total = total + base_ref[...].astype(f32)
+    out_ref[...] = total.astype(out_ref.dtype)
+
+
+def add_outputs(gated, order, panel, group, half, bases, dtype):
+    tokens, share = gated[0].shape
+    chips, columns = panel.shape[0], panel.shape[2] // 2
+    tile = math.gcd(tokens, 256)
+    return pl.pallas_call(
+        functools.partial(output_kernel, len(gated)),
+        grid_spec=pltpu.PrefetchScalarGridSpec(
+            num_scalar_prefetch=2,
+            grid=(tokens // tile,),
+            in_specs=[
+                *[pl.BlockSpec((tile, share), lambda m, order, half: (m, 0)) for _ in gated],
+                pl.BlockSpec((chips, share, columns), lambda m, order, half: (0, group, half[0])),
+                *[pl.BlockSpec((tile, columns), lambda m, order, half: (m, 0)) for _ in bases],
+            ],
+            out_specs=pl.BlockSpec((tile, columns), lambda m, order, half: (m, 0)),
+        ),
+        out_shape=jax.ShapeDtypeStruct((tokens, columns), dtype),
+        cost_estimate=pl.CostEstimate(
+            flops=2 * tokens * columns * len(gated) * share, bytes_accessed=4 * tokens * columns, transcendentals=0
+        ),
+        compiler_params=pltpu.CompilerParams(vmem_limit_bytes=40 * 2**20),
+        name="add_outputs",
+    )(order, half, *gated, panel, *bases)
+
+
+def exchange(rows, axis, masks):
+    size = lax.axis_size(axis)
+    return [
+        rows[n] if mask == 0 else lax.ppermute(rows[n], axis, swap_route(size, mask)) for n, mask in enumerate(masks)
+    ]
+
+
+def ring(block, rounds):
+    size = lax.axis_size("mp")
+    blocks = [block]
+    for _ in range(rounds):
+        blocks.append(lax.ppermute(blocks[-1], "mp", [(i, (i + 2) % size) for i in range(size)]))
+    return blocks
+
+
+def core_swap(block):
+    return lax.ppermute(block, "mp", swap_route(lax.axis_size("mp"), 1))
+
+
+def ctx_order():
+    size = lax.axis_size("ctx")
+    index = jnp.arange(size)
+    return lax.axis_index("ctx") ^ index if (size, lax.axis_size("mp")) == (4, 8) else index
+
+
 def filter_tables(decay_rate, residue, skip_gain, tokens):
     me = lax.axis_index("ctx")
     size = lax.axis_size("ctx")
@@ -208,7 +346,7 @@
     segment = tokens // SEGMENTS
     ahead = (SEGMENTS - 1 - jnp.arange(SEGMENTS, dtype=f32)) * segment
     reach = jnp.exp(-rate[:, None, :] * ahead[None, :, None]).reshape(modes * SEGMENTS, channels)
-    index = jnp.arange(size)
+    index = ctx_order()
     gap = (me - 1 - index).astype(f32) * tokens
     shares = jnp.where(
         (index < me)[:, None, None], jnp.exp(-rate[None] * jnp.maximum(gap, 0.0)[:, None, None]), 0.0
@@ -254,53 +392,124 @@
     model_width = features * mp
     groups = 2 if channels % (2 * LANES) == 0 else 1
     share = channels // groups
+    half = w_in.shape[0] // 2
+    here = lax.axis_index("mp")
+    chips = mp // 2
+    chip, core = here // 2, here % 2
+    special = (ctx, mp) == (4, 8)
+
+    behind = lax.ppermute(activations[-TAIL:], "ctx", [(i, i + 1) for i in range(ctx - 1)])
+    w_parts = [
+        [w_in[top : top + half, :, g * share : (g + 1) * share].reshape(half, 3 * share) for top in (0, half)]
+        for g in range(groups)
+    ]
     act_float = activations.astype(f32)
+    tail_float = behind.astype(f32)
     scaled = (act_float * norm_gain[None, :]).astype(bf16)
-    everything = lax.all_gather(scaled, "mp", axis=0)
-    squares = lax.psum(jnp.sum(act_float * act_float, axis=1), "mp")
-    inverse = lax.rsqrt(squares / model_width + 1e-06)[:, None]
-    per_block = mp // ctx
-    by_block = everything.reshape(ctx, per_block, tokens, features)
-
-    def project(blocks):
-        total = None
-        for owner, first, rows in blocks:
-            for i in range(0, rows.shape[0], features):
-                source = lax.dynamic_index_in_dim(by_block, owner, 0, False)[(first + i) // features]
-                part = lax.dot_general(
-                    source, rows[i : i + features], (((1,), (0,)), ((), ())), preferred_element_type=f32
-                )
-                total = part if total is None else total + part
-        return total * inverse
-
+    scaled_tail = (tail_float * norm_gain[None, :]).astype(bf16)
+    squares = jnp.concatenate([jnp.sum(tail_float * tail_float, axis=1), jnp.sum(act_float * act_float, axis=1)])
     tables = filter_tables(decay_rate, residue, skip_gain, tokens)
     start_state = state_in.T
-    taps_all = short_filter
-    tails_all = tail_rows.transpose(2, 0, 1).astype(f32)
-    pieces = [w_in[:, :, g * share : (g + 1) * share].reshape(-1, 3 * share) for g in range(groups)]
-    arriving = [gathered_blocks(piece) for piece in pieces]
-    outputs = []
+    tails_in = tail_rows.transpose(2, 0, 1).astype(f32)
+
+    if special:
+        part = features // 2
+        first = scaled[:, :part]
+        second = jnp.concatenate([scaled[:, part:], scaled_tail[:, :part], scaled_tail[:, part:]])
+        near = [near_blocks(*w_parts[0])]
+        first, second = ring(first, chips - 1), ring(second, chips - 1)
+        other_first, other_second = [core_swap(p) for p in first], [core_swap(p) for p in second]
+        pieces = first + second + other_first + other_second
+        tails_at = [(n % 4 + 4 + 8 * (n // 8), TAIL * (n // 4 % 2)) for n in range(16)]
+        offsets = [part * (n // 4 % 2) for n in range(16)]
+        slots = jnp.stack([2 * (me ^ ((chip - n % 4) % chips)) + (core ^ (n // 8)) for n in range(16)])
+        squares = squares[None] + core_swap(squares[None])
+        squares = sum(exchange([squares] * chips, "mp", range(0, mp, 2)))[0]
+        mine = w_out.reshape(ctx, channels // ctx, -1)
+        mine = tie(mine, corner(near[0][0]), corner(near[0][1]))
+        sent = [lax.dynamic_index_in_dim(mine, me ^ d, 0, False) for d in range(ctx)]
+        by_owner = jnp.stack(exchange(sent, "ctx", range(ctx)))
+        by_owner = tie(by_owner, corner(second[2]))
+        sent = [lax.dynamic_index_in_dim(by_owner, (chip ^ d) ^ me, 0, False) for d in range(chips)]
+        my_rows = jnp.stack(exchange(sent, "mp", range(0, mp, 2)))
+    else:
+        extended = jnp.concatenate([scaled, scaled_tail, scaled_tail])
+        everything = lax.all_gather(extended, "mp", axis=0)
+        pieces = [everything[n] for n in range(mp)]
+        tails_at = [(n, 0) for n in range(mp)]
+        offsets = [n * features % half for n in range(mp)]
+        slots = jnp.asarray([n * features // half for n in range(mp)])
+        squares = lax.psum(squares, "mp")
+        groups_of_core = [[i for i in range(mp) if i % 2 == c] for c in range(2)]
+        rows = lax.all_to_all(w_out.reshape(ctx, channels // ctx, -1), "ctx", 0, 0)
+        rows = rows.reshape(ctx, channels // ctx, chips // ctx, -1).swapaxes(1, 2)
+        rows = rows.reshape(chips, channels // ctx, -1)
+        rows = lax.all_to_all(rows, "mp", 0, 0, axis_index_groups=groups_of_core)
+        panel = lax.all_gather(rows, "ctx", axis=1).reshape(chips, channels, -1)
+
+    inverse = lax.rsqrt(squares / model_width + 1e-06)[:, None]
+    inverse, tail_inverse = inverse[TAIL:], inverse[:TAIL]
+    slots = slots.astype(jnp.int32)
     finals = []
+    rings = []
+    after_states = None
     for g in range(groups):
         span = slice(g * share, (g + 1) * share)
         own = cut(tables, g * share, (g + 1) * share)
-        taps = taps_all[:, :, span].reshape(3, 3 * share)
-        projected = project(arriving[g])
-        behind = lax.ppermute(projected[-2:], "ctx", [(i, i + 1) for i in range(ctx - 1)])
-        tails = jnp.where(me == 0, tails_all[:, :, span].reshape(2, 3 * share), behind)
+        taps = short_filter[:, :, span].reshape(3, 3 * share)
+        if special:
+            if g > 0:
+                near.append(near_blocks(*tie(w_parts[g], corner(near[g - 1][2]), corner(near[g - 1][3]))))
+            y_top, x_bottom, x_top, y_bottom = near[g]
+            far_top, far_bottom = far_blocks(*(tie((y_top, x_bottom), after_states) if g > 0 else (y_top, x_bottom)))
+            blocks = [*w_parts[g], x_top, x_bottom, y_top, y_bottom, far_top, far_bottom]
+        else:
+            gathered = [lax.all_gather(p, "ctx", axis=0) for p in w_parts[g]]
+            blocks = [gathered[n % 2][n // 2] for n in range(2 * ctx)]
+        projected, before = project(pieces, tails_at, blocks, slots, offsets, inverse, tail_inverse)
+        tails = jnp.where(me == 0, tails_in[:, :, span].reshape(2, 3 * share), before[TAIL - 2 :])
         response, ends, last = local_filter(projected, tails, taps, own)
-        lasts = lax.all_gather(last, "ctx", axis=0)
+        if special:
+            lasts = jnp.stack(exchange([last] * ctx, "ctx", range(ctx)))
+            after_states = lasts[:, :8, :LANES]
+        else:
+            lasts = lax.all_gather(last, "ctx", axis=0)
         states = jnp.concatenate([lasts, start_state[None, :, span]])
         finals.append(jnp.sum(own["final"] * states, axis=0))
-        outputs.append(
-            gated_signal(projected, tails, taps, own, response, ends, states.reshape(-1, share))
-        )
-    state_out = jnp.concatenate(finals, axis=1).T
-    gated = jnp.concatenate(outputs, axis=1)
-    panel = lax.all_gather(w_out, "ctx", axis=1, tiled=True)
-    partial = lax.dot_general(panel, gated, (((0,), (1,)), ((), ())), preferred_element_type=f32)
-    branch = lax.psum_scatter(partial.astype(bf16), "mp", scatter_dimension=0, tiled=True).astype(f32).T
-    return ((act_float + branch).astype(bf16), state_out)
+        gated = gated_signal(projected, tails, taps, own, response, ends, states.reshape(-1, share))
+        if special:
+            rings.append(ring(gated, chips - 1))
+        else:
+            gathered = lax.all_gather(gated, "mp", axis=0, axis_index_groups=groups_of_core)
+            rings.append([gathered[n] for n in range(chips)])
+
+    if special:
+        top, bottom = tie((my_rows[: chips // 2], my_rows[chips // 2 :]), after_states)
+        y_top, x_bottom, x_top, y_bottom = near_blocks(top, bottom)
+        far_top, far_bottom = far_blocks(y_top, x_bottom)
+        panel = jnp.zeros((chips, ctx, *my_rows.shape[1:]), bf16)
+        arrived = [
+            (0, top, bottom), (1, x_top, x_bottom), (2, y_top, y_bottom), (3, far_top, far_bottom),
+        ]
+        for d, upper, lower in arrived:
+            panel = lax.dynamic_update_slice(panel, upper[:, None], (0, me ^ d, 0, 0))
+            panel = lax.dynamic_update_slice(panel, lower[:, None], (chips // 2, me ^ d, 0, 0))
+        panel = panel.reshape(chips, channels, -1)
+        order = jnp.stack([((chip - n) % chips) ^ chip for n in range(chips)])
+    else:
+        order = jnp.arange(chips)
+    order = order.astype(jnp.int32)
+    mine, other = core[None].astype(jnp.int32), (1 - core)[None].astype(jnp.int32)
+    kept, given = [activations], []
+    for g in range(groups):
+        final = g == groups - 1
+        steps = [slice(0, chips - 1), slice(chips - 1, chips)] if final else [slice(0, chips)]
+        for n, step in enumerate(steps):
+            dtype = bf16 if final and n == len(steps) - 1 else f32
+            given = [add_outputs(rings[g][step], order[step], panel, g, other, given, dtype)]
+            kept = [add_outputs(rings[g][step], order[step], panel, g, mine, kept, f32)]
+    total = (kept[0] + core_swap(given[0]).astype(f32)).astype(bf16)
+    return (total, jnp.concatenate(finals, axis=1).T)
 
 
 def solution(mesh):

time: 300 us -> 317 us (1.057)
  matrix products: 66.7 us -> 0 us
  starting transfers between devices: 13.1 us -> 59.7 us
  Pallas kernels: 16.2 us -> 56.2 us
  local copies, waits for them, and re-layouts: 22.8 us -> 57.6 us
  blocking collectives: 27.1 us -> 0 us
  between operations: 14.2 us -> 1.47 us
  other arithmetic: 6.14 us -> 14.6 us
  waiting for transfers between devices: 130 us -> 125 us
    reduce_scatter x1 -> x0, waiting for transfers between devices: 90.1 us -> none  [local(): lax.psum_scatter(partial.astype(bf16), 'mp', scatter_dimension=0, tiled=T...]
    ppermute x10 -> x56, waiting for transfers between devices: 35.6 us -> 125 us  [the longest x12 63.2 us: ring(): lax.ppermute(blocks[-1], 'mp', [(i, (i + 2) % size) for i in range(size)])]
    dot_general x17 -> x0, matrix products: 66.7 us -> none  [the longest x16 57.7 us: project(): lax.dot_general(source, rows[i:i + features], (((1,), (0,)), ((), ())), p...]
    ppermute x10 -> x56, starting transfers between devices: 13 us -> 59.7 us  [the longest x15 19.1 us: exchange(): lax.ppermute(rows[n], axis, swap_route(size, mask))]
    pallas_call x0 -> x8, Pallas kernels: none -> 39.5 us  [the longest x2 25.3 us: project(): pl.pallas_call(functools.partial(project_kernel, tails_at, offsets), grid...]
    unnamed x35 -> x129, local copies, waits for them, and re-layouts: 10.6 us -> 26.2 us
    psum x1 -> x0, blocking collectives: 15.5 us -> none  [local(): squares = lax.psum(jnp.sum(act_float * act_float, axis=1), 'mp')]
    all_gather x2 -> x0, blocking collectives: 11.6 us -> none  [local(): lasts = lax.all_gather(last, 'ctx', axis=0)]
  transfers between devices with their start and end apart: 13 -> 56, of which waited for: 4 -> 17; matrix products, arithmetic and copies ran while one was open for 28% -> 16% of each run, Pallas kernels for 5% -> 18%
where the time goes in v2:
time: 317 us; the launch traced here: 315 us
  waiting for transfers between devices  125 us (39%)
  starting transfers between devices  59.7 us (19%)
  local copies, waits for them, and re-layouts  57.6 us (18%)
  Pallas kernels  56.2 us (18%)
  other arithmetic  14.6 us (5%)
    ppermute x12, waiting for transfers between devices, ring(): lax.ppermute(blocks[-1], 'mp', [(i, (i + 2) % size) for i in range(size)])  63.2 us
    ppermute x15, waiting for transfers between devices, exchange(): lax.ppermute(rows[n], axis, swap_route(size, mask))  34.7 us
    unnamed x129, local copies, waits for them, and re-layouts  26.2 us
    pallas_call x2, Pallas kernels, project(): pl.pallas_call(functools.partial(project_kernel, tails_at, offsets), grid...  25.3 us
    ppermute x15, starting transfers between devices, exchange(): lax.ppermute(rows[n], axis, swap_route(size, mask))  19.1 us
    ppermute x10, starting transfers between devices, core_swap(): return lax.ppermute(block, 'mp', swap_route(lax.axis_size('mp'), 1))  16.4 us
    pallas_call x6, Pallas kernels, add_outputs(): pl.pallas_call(functools.partial(output_kernel, len(gated)), grid_spec=pl...  14.2 us
    ppermute x3, waiting for transfers between devices, near_blocks(): lax.ppermute(top, 'ctx', along_x)  13.5 us
  transfers between devices with their start and end apart: 56, of which 17 were waited for; matrix products, arithmetic and copies ran while one was open for 16% of the time, Pallas kernels for 18%

profile of v2, /device:TPU:1, one launch (start us, length us, event | category | flops | bytes accessed | tf_op | source)
XLA Modules:
  0.0 314.9 jit_solution(1069396231537816043)
XLA Ops:
  0.6 1.7 fusion.1
  3.2 2.1 collective-permute-start
  7.0 3.1 collective-permute-start.3
  11.1 1.2 collective-permute-start.31
  12.4 3.3 %fusion.12 = (bf16[512,3,256]{2,0,1:T(8,128)(2,1)S(1)}, bf16[512,3,256]{2,0,1:T(8,128)(2,1)S(1)}, bf16[512,3,256]{2,0,1:T(8,128)(2,1)}, bf16[512,3,256]{2,0,1:T(8,128)(2,1)}) fusion(bf16[1024,3,512]{2,0,1:T(8,128)(2,1)} %param.12), kind=kLoop, calls=%fused_computation.78 | loop fusion | bytes 6291456 | tf_op jit(solution)/shard_map/slice | solution.py:403
  20.9 1.4 copy.46.refs_24_
  23.5 1.4 copy.47.refs_25_
  25.0 1.7 collective-permute-start.33
  26.7 1.4 collective-permute-start.22
  29.2 4.7 %collective-permute-done.33 = bf16[128,1024]{1,0:T(8,128)(2,1)S(1)} collective-permute-done((bf16[128,1024]{1,0:T(8,128)(2,1)S(1)}, bf16[128,1024]{1,0:T(8,128)(2,1)S(1)}, u32[]{:S(2)}, u32[]{:S(2)}) %collective-permute-start.33) | collective-permute-done | bytes 262176 | tf_op jit(solution)/shard_map/ppermute | solution.py:318
  33.9 2.0 collective-permute-start.24
  38.5 2.2 collective-permute-start.36
  40.7 1.8 collective-permute-start.45
  43.9 25.6 %collective-permute-done.35 = bf16[128,1024]{1,0:T(8,128)(2,1)S(1)} collective-permute-done((bf16[128,1024]{1,0:T(8,128)(2,1)S(1)}, bf16[128,1024]{1,0:T(8,128)(2,1)S(1)}, u32[]{:S(2)}, u32[]{:S(2)}) %collective-permute-start.35) | collective-permute-done | bytes 262176 | tf_op jit(solution)/shard_map/ppermute | solution.py:318
  69.5 1.4 collective-permute-start.11
  71.0 4.5 %collective-permute-start.34 = (bf16[128,1024]{1,0:T(8,128)(2,1)}, bf16[128,1024]{1,0:T(8,128)(2,1)}, u32[]{:S(2)}, u32[]{:S(2)}) collective-permute-start(bf16[128,1024]{1,0:T(8,128)(2,1)} %get-tuple-element.42), channel_id=1, source_target_pairs={{0,2},{1,3},{2,0},{3,1},{4,6},{5,7},{6,4},{7,5},{8,10},{9,11},{10,... | collective-permute-start | bytes 786440 | tf_op jit(solution)/shard_map/ppermute | solution.py:318
  76.4 2.3 copy.50
  78.7 2.3 copy.51
  81.0 2.3 copy.27
  83.3 2.3 copy.26
  86.2 1.7 collective-permute-start.43
  88.3 1.2 collective-permute-start.16
  91.3 13.5 %collective-permute-done.43.refs_26_ = bf16[512,768]{1,0:T(8,128)(2,1)S(1)} collective-permute-done((bf16[512,768]{1,0:T(8,128)(2,1)S(1)}, bf16[512,768]{1,0:T(8,128)(2,1)S(1)}, u32[]{:S(2)}, u32[]{:S(2)}) %collective-permute-start.43) | collective-permute-done | bytes 786464 | tf_op jit(solution)/shard_map/ppermute | solution.py:35
  107.3 1.4 copy.30.refs_24_
  108.7 1.4 copy.31.refs_25_
  110.8 2.8 collective-permute-start.8
  113.5 8.1 %collective-permute-done.16.refs_27_ = bf16[512,768]{1,0:T(8,128)(2,1)} collective-permute-done((bf16[512,768]{1,0:T(8,128)(2,1)}, bf16[512,768]{1,0:T(8,128)(2,1)}, u32[]{:S(2)}, u32[]{:S(2)}) %collective-permute-start.16) | collective-permute-done | bytes 786464 | tf_op jit(solution)/shard_map/ppermute | solution.py:34
  121.6 1.8 collective-permute-start.12
  130.0 1.2 collective-permute-start.48
  131.2 7.9 %collective-permute-done.2.refs_3_ = bf16[1024,256]{1,0:T(8,128)(2,1)} collective-permute-done((bf16[1024,256]{1,0:T(8,128)(2,1)}, bf16[1024,256]{1,0:T(8,128)(2,1)}, u32[]{:S(2)}, u32[]{:S(2)}) %collective-permute-start.2) | collective-permute-done | bytes 524320 | tf_op jit(solution)/shard_map/ppermute | solution.py:326
  141.8 8.8 %collective-permute-done.6.refs_7_.refs_19_ = bf16[1056,256]{1,0:T(8,128)(2,1)} collective-permute-done((bf16[1056,256]{1,0:T(8,128)(2,1)}, bf16[1056,256]{1,0:T(8,128)(2,1)}, u32[]{:S(2)}, u32[]{:S(2)}) %collective-permute-start.6) | collective-permute-done | bytes 540704 | tf_op jit(solution)/shard_map/ppermute | solution.py:326
  152.6 1.2 slice_bitcast_fusion.5
  154.5 1.5 collective-permute-start.15
  156.2 1.2 collective-permute-start.19
  157.6 1.9 pad_maximum_fusion.3
  159.4 1.9 pad_maximum_fusion.2
  161.3 1.4 collective-permute-start.37
  171.7 12.9 %project.3 = (f32[1024,768]{1,0:T(8,128)}, f32[16,768]{1,0:T(8,128)S(1)}) custom-call(s32[16]{0:T(128)S(1)} %copy-done.25, bf16[1024,256]{1,0:T(8,128)(2,1)S(1)} %copy-done.10, bf16[1024,256]{1,0:T(8,128)(2,1)S(1)} %copy-done.31, bf16[1024,256]{1,0:T(8,128)(2,1)} %collective-permute-done.1.refs_2_, bf16[1024,256]{1,0:T(8,128)(2,1)} %collective-permute-done.2.refs_3_, ...), custom_call_target="tpu_custom_call" | custom-call | flops 6442450944 | bytes 14680064 | tf_op jit(solution)/shard_map/project/pallas_call | solution.py:249
  185.0 1.2 collective-permute-start.38
  186.2 4.6 %collective-permute-done.19.refs_30_ = bf16[512,768]{1,0:T(8,128)(2,1)S(1)} collective-permute-done((bf16[512,768]{1,0:T(8,128)(2,1)}, bf16[512,768]{1,0:T(8,128)(2,1)S(1)}, u32[]{:S(2)}, u32[]{:S(2)}) %collective-permute-start.19) | collective-permute-done | bytes 786464 | tf_op jit(solution)/shard_map/ppermute | solution.py:41
  190.8 1.3 collective-permute-done.20.refs_31_
  192.9 12.4 %project.2 = (f32[1024,768]{1,0:T(8,128)}, f32[16,768]{1,0:T(8,128)S(1)}) custom-call(s32[16]{0:T(128)S(1)} %copy-done.25, bf16[1024,256]{1,0:T(8,128)(2,1)S(1)} %copy-done.10, bf16[1024,256]{1,0:T(8,128)(2,1)S(1)} %copy-done.31, bf16[1024,256]{1,0:T(8,128)(2,1)} %collective-permute-done.1.refs_2_, bf16[1024,256]{1,0:T(8,128)(2,1)} %collective-permute-done.2.refs_3_, ...), custom_call_target="tpu_custom_call" | custom-call | flops 6442450944 | bytes 14680064 | tf_op jit(solution)/shard_map/project/pallas_call | solution.py:249
  205.4 2.0 copy-done.1
  207.4 5.1 %local_filter.2 = (f32[1024,256]{1,0:T(8,128)S(1)}, f32[128,256]{1,0:T(8,128)S(1)}, f32[16,256]{1,0:T(8,128)S(1)}) custom-call(f32[1024,768]{1,0:T(8,128)S(1)} %copy-done.1, f32[1024,768]{1,0:T(8,128)S(1)} %copy-done.1, f32[2,768]{1,0:T(2,128)S(1)} %get-tuple-element.88.tail_k_ref.tail_v_ref.tail_q_ref, ...), custom_call_target="tpu_custom_call" | custom-call | flops 16777216 | bytes 3145728 | tf_op jit(solution)/shard_map/local_filter/pallas_call | solution.py:141
  214.5 1.2 collective-permute-start.26
  215.7 5.1 %local_filter.3 = (f32[1024,256]{1,0:T(8,128)S(1)}, f32[128,256]{1,0:T(8,128)S(1)}, f32[16,256]{1,0:T(8,128)S(1)}) custom-call(f32[1024,768]{1,0:T(8,128)S(1)} %copy-done, f32[1024,768]{1,0:T(8,128)S(1)} %copy-done, f32[2,768]{1,0:T(2,128)S(1)} %get-tuple-element.87.tail_k_ref.tail_v_ref.tail_q_ref, ...), custom_call_target="tpu_custom_call" | custom-call | flops 16777216 | bytes 3145728 | tf_op jit(solution)/shard_map/local_filter/pallas_call | solution.py:141
  220.9 1.3 collective-permute-start.27
  222.4 2.1 collective-permute-done.27
  225.9 1.4 collective-permute-done.50
  228.3 3.6 %gated_signal.3.refs_0_ = bf16[1024,256]{1,0:T(8,128)(2,1)} custom-call(f32[1024,768]{1,0:T(8,128)S(1)} %copy-done, f32[2,768]{1,0:T(2,128)S(1)} %get-tuple-element.87.tail_k_ref.tail_v_ref.tail_q_ref, f32[3,768]{1,0:T(4,128)S(1)} %bitcast.148, f32[16,256]{1,0:T(8,128)S(1)} %get-tuple-element.92.lam_ref, f32[16,256]{1,0:T(8,128)S(1)} %copy-done.17, ...), custom_call_target="tpu_custom_call" | custom-call | flops 8388608 | bytes 2359296 | tf_op jit(solution)/shard_map/gated_signal/pallas_call | solution.py:178
  232.0 1.2 copy-done.5
  234.1 3.0 gated_signal.2.refs_0_
  239.9 1.2 collective-permute-start.40
  243.7 10.0 %collective-permute-done.28.refs_1_ = bf16[1024,256]{1,0:T(8,128)(2,1)S(1)} collective-permute-done((bf16[1024,256]{1,0:T(8,128)(2,1)S(1)}, bf16[1024,256]{1,0:T(8,128)(2,1)S(1)}, u32[]{:S(2)}, u32[]{:S(2)}) %collective-permute-start.28) | collective-permute-done | bytes 524320 | tf_op jit(solution)/shard_map/ppermute | solution.py:326
  255.9 9.1 %collective-permute-done.53.refs_2_ = bf16[1024,256]{1,0:T(8,128)(2,1)S(1)} collective-permute-done((bf16[1024,256]{1,0:T(8,128)(2,1)}, bf16[1024,256]{1,0:T(8,128)(2,1)S(1)}, u32[]{:S(2)}, u32[]{:S(2)}) %collective-permute-start.53) | collective-permute-done | bytes 524320 | tf_op jit(solution)/shard_map/ppermute | solution.py:326
  265.0 11.2 %collective-permute-done.29.refs_2_ = bf16[1024,256]{1,0:T(8,128)(2,1)S(1)} collective-permute-done((bf16[1024,256]{1,0:T(8,128)(2,1)S(1)}, bf16[1024,256]{1,0:T(8,128)(2,1)S(1)}, u32[]{:S(2)}, u32[]{:S(2)}) %collective-permute-start.29) | collective-permute-done | bytes 524320 | tf_op jit(solution)/shard_map/ppermute | solution.py:326
  276.3 11.1 %collective-permute-done.54.refs_3_ = bf16[1024,256]{1,0:T(8,128)(2,1)S(1)} collective-permute-done((bf16[1024,256]{1,0:T(8,128)(2,1)S(1)}, bf16[1024,256]{1,0:T(8,128)(2,1)S(1)}, u32[]{:S(2)}, u32[]{:S(2)}) %collective-permute-start.54) | collective-permute-done | bytes 524320 | tf_op jit(solution)/shard_map/ppermute | solution.py:326
  287.4 3.9 %add_outputs.9.refs_4_ = f32[1024,512]{1,0:T(8,128)S(1)} custom-call(s32[4]{0:T(128)S(1)} %pad_add_fusion.1.order_ref, s32[1]{0:T(128)} %bitcast.70.half_ref, bf16[1024,256]{1,0:T(8,128)(2,1)} %gated_signal.3.refs_0_, bf16[1024,256]{1,0:T(8,128)(2,1)} %collective-permute-done.52.refs_1_, bf16[1024,256]{1,0:T(8,128)(2,1)S(1)} %collective-permute-done.53.refs_2_, ...), custom_call_target="tpu_custom_call" | custom-call | flops 1073741824 | bytes 2097152 | tf_op jit(solution)/shard_map/add_outputs/pallas_call | solution.py:294
  291.3 2.2 add_outputs.10.refs_2_
  293.5 5.1 %collective-permute-done.30.refs_0_ = bf16[1024,256]{1,0:T(8,128)(2,1)S(1)} collective-permute-done((bf16[1024,256]{1,0:T(8,128)(2,1)S(1)}, bf16[1024,256]{1,0:T(8,128)(2,1)S(1)}, u32[]{:S(2)}, u32[]{:S(2)}) %collective-permute-start.30) | collective-permute-done | bytes 524320 | tf_op jit(solution)/shard_map/ppermute | solution.py:326
  299.7 6.1 %collective-permute-start.55 = (bf16[1024,512]{1,0:T(8,128)(2,1)S(1)}, bf16[1024,512]{1,0:T(8,128)(2,1)S(1)}, u32[]{:S(2)}, u32[]{:S(2)}) collective-permute-start(bf16[1024,512]{1,0:T(8,128)(2,1)S(1)} %add_outputs.11), channel_id=1, source_target_pairs={{0,1},{1,0},{2,3},{3,2},{4,5},{5,4},{6,7},{7,6},{8,9},{9,8},{10,11... | collective-permute-start | bytes 3145736 | tf_op jit(solution)/shard_map/ppermute | solution.py:331
  306.4 3.9 %add_outputs.6.refs_4_ = f32[1024,512]{1,0:T(8,128)S(1)} custom-call(s32[4]{0:T(128)S(1)} %pad_add_fusion.1.order_ref, s32[1]{0:T(128)} %bitcast.1.half_ref, bf16[1024,256]{1,0:T(8,128)(2,1)} %gated_signal.3.refs_0_, bf16[1024,256]{1,0:T(8,128)(2,1)} %collective-permute-done.52.refs_1_, bf16[1024,256]{1,0:T(8,128)(2,1)S(1)} %collective-permute-done.53.refs_2_, ...), custom_call_target="tpu_custom_call" | custom-call | flops 1073741824 | bytes 2097152 | tf_op jit(solution)/shard_map/add_outputs/pallas_call | solution.py:294
  310.3 2.2 add_outputs.7.refs_2_
  313.6 1.3 add_convert_fusion
  (251 shorter events, 60.4 us)
Async XLA Ops:
  3.2 40.4 %collective-permute-start = (bf16[1024,256]{1,0:T(8,128)(2,1)S(1)}, bf16[1024,256]{1,0:T(8,128)(2,1)S(1)}, u32[]{:S(2)}, u32[]{:S(2)}) collective-permute-start(bf16[1024,256]{1,0:T(8,128)(2,1)S(1)} %get-tuple-element.51.refs_0_), channel_id=1, source_target_pairs={{0,2},{1,3},{2,4},{3,5},{4,6},{5,7},{6,0},{7,1},{8,10},{9,11},{10,... | collective-permute-start | bytes 1572872 | tf_op jit(solution)/shard_map/ppermute | solution.py:326
  5.3 38.6 %collective-permute-start.7 = (bf16[1024,256]{1,0:T(8,128)(2,1)S(1)}, bf16[1024,256]{1,0:T(8,128)(2,1)}, u32[]{:S(2)}, u32[]{:S(2)}) collective-permute-start(bf16[1024,256]{1,0:T(8,128)(2,1)S(1)} %get-tuple-element.51.refs_0_), channel_id=1, source_target_pairs={{0,1},{1,0},{2,3},{3,2},{4,5},{5,4},{6,7},{7,6},{8,9},{9,8},{10,11... | collective-permute-start | bytes 1572872 | tf_op jit(solution)/shard_map/ppermute | solution.py:331
  7.0 11.4 %collective-permute-start.3 = (bf16[16,512]{1,0:T(8,128)(2,1)S(1)}, bf16[16,512]{1,0:T(8,128)(2,1)S(1)}, u32[]{:S(2)}, u32[]{:S(2)}) collective-permute-start(bf16[16,512]{1,0:T(8,128)(2,1)S(1)} %slice.135), channel_id=1, source_target_pairs={{0,8},{8,16},{16,24},{1,9},{9,17},{17,25},{2,10},{10,18},{18,26},{... | collective-permute-start | bytes 49160 | tf_op jit(solution)/shard_map/ppermute | solution.py:401
  11.1 15.6 %collective-permute-start.31 = (bf16[128,1024]{1,0:T(8,128)(2,1)}, bf16[128,1024]{1,0:T(8,128)(2,1)}, u32[]{:S(2)}, u32[]{:S(2)}) collective-permute-start(bf16[128,1024]{1,0:T(8,128)(2,1)} %get-tuple-element.47), channel_id=1, source_target_pairs={{0,8},{8,0},{16,24},{24,16},{1,9},{9,1},{17,25},{25,17},{2,10},{10... | collective-permute-start | bytes 786440 | tf_op jit(solution)/shard_map/ppermute | solution.py:318
  12.3 15.8 %collective-permute-start.32 = (bf16[128,1024]{1,0:T(8,128)(2,1)}, bf16[128,1024]{1,0:T(8,128)(2,1)}, u32[]{:S(2)}, u32[]{:S(2)}) collective-permute-start(bf16[128,1024]{1,0:T(8,128)(2,1)} %get-tuple-element.46), channel_id=1, source_target_pairs={{0,16},{8,24},{16,0},{24,8},{1,17},{9,25},{17,1},{25,9},{2,18},{10... | collective-permute-start | bytes 786440 | tf_op jit(solution)/shard_map/ppermute | solution.py:318
  18.6 6.4 %collective-permute-start.21 = (f32[1,1040]{1,0:T(1,128)S(1)}, f32[1,1040]{1,0:T(1,128)S(1)}, u32[]{:S(2)}, u32[]{:S(2)}) collective-permute-start(f32[1,1040]{1,0:T(1,128)S(1)} %broadcast_in_dim.75), channel_id=1, source_target_pairs={{0,1},{1,0},{2,3},{3,2},{4,5},{5,4},{6,7},{7,6},{8,9},{9,8},{10,11... | collective-permute-start | bytes 12488 | tf_op jit(solution)/shard_map/ppermute | solution.py:331
  25.0 8.9 %collective-permute-start.33 = (bf16[128,1024]{1,0:T(8,128)(2,1)S(1)}, bf16[128,1024]{1,0:T(8,128)(2,1)S(1)}, u32[]{:S(2)}, u32[]{:S(2)}) collective-permute-start(bf16[128,1024]{1,0:T(8,128)(2,1)S(1)} %get-tuple-element.45), channel_id=1, source_target_pairs={{0,24},{8,16},{16,8},{24,0},{1,25},{9,17},{17,9},{25,1},{2,26},{10... | collective-permute-start | bytes 786440 | tf_op jit(solution)/shard_map/ppermute | solution.py:318
  26.7 11.2 %collective-permute-start.22 = (f32[1,1040]{1,0:T(1,128)S(1)}, f32[1,1040]{1,0:T(1,128)S(1)}, u32[]{:S(2)}, u32[]{:S(2)}) collective-permute-start(f32[1,1040]{1,0:T(1,128)S(1)} %reshape_add_fusion), channel_id=1, source_target_pairs={{0,2},{1,3},{2,0},{3,1},{4,6},{5,7},{6,4},{7,5},{8,10},{9,11},{10,... | collective-permute-start | bytes 12488 | tf_op jit(solution)/shard_map/ppermute | solution.py:318
  28.1 10.4 %collective-permute-start.23 = (f32[1,1040]{1,0:T(1,128)S(1)}, f32[1,1040]{1,0:T(1,128)S(1)}, u32[]{:S(2)}, u32[]{:S(2)}) collective-permute-start(f32[1,1040]{1,0:T(1,128)S(1)} %reshape_add_fusion), channel_id=1, source_target_pairs={{0,4},{1,5},{2,6},{3,7},{4,0},{5,1},{6,2},{7,3},{8,12},{9,13},{10,... | collective-permute-start | bytes 12488 | tf_op jit(solution)/shard_map/ppermute | solution.py:318
  33.9 6.9 %collective-permute-start.24 = (f32[1,1040]{1,0:T(1,128)S(1)}, f32[1,1040]{1,0:T(1,128)S(1)}, u32[]{:S(2)}, u32[]{:S(2)}) collective-permute-start(f32[1,1040]{1,0:T(1,128)S(1)} %reshape_add_fusion), channel_id=1, source_target_pairs={{0,6},{1,7},{2,4},{3,5},{4,2},{5,3},{6,0},{7,1},{8,14},{9,15},{10,... | collective-permute-start | bytes 12488 | tf_op jit(solution)/shard_map/ppermute | solution.py:318
  37.9 50.1 %copy-start.46 = (f32[3,3,512]{2,1,0:T(4,128)S(1)}, f32[3,3,512]{2,1,0:T(4,128)}, u32[]{:S(2)}) copy-start(f32[3,3,512]{2,1,0:T(4,128)} %param.14) | copy-start | bytes 55300
  37.9 51.7 %copy-start.51 = (bf16[3,512,2]{1,2,0:T(2,128)(2,1)S(1)}, bf16[3,512,2]{1,2,0:T(2,128)(2,1)}, u32[]{:S(2)}) copy-start(bf16[3,512,2]{1,2,0:T(2,128)(2,1)} %param.13) | copy-start | bytes 18436
  37.9 52.5 %copy-start.39 = (f32[16,512]{1,0:T(8,128)S(1)}, f32[16,512]{1,0:T(8,128)}, u32[]{:S(2)}) copy-start(f32[16,512]{1,0:T(8,128)} %copy-done.38) | copy-start | bytes 98308
  37.9 31.6 %collective-permute-start.35 = (bf16[128,1024]{1,0:T(8,128)(2,1)S(1)}, bf16[128,1024]{1,0:T(8,128)(2,1)S(1)}, u32[]{:S(2)}, u32[]{:S(2)}) collective-permute-start(bf16[128,1024]{1,0:T(8,128)(2,1)S(1)} %get-tuple-element.40), channel_id=1, source_target_pairs={{0,4},{1,5},{2,6},{3,7},{4,0},{5,1},{6,2},{7,3},{8,12},{9,13},{10,... | collective-permute-start | bytes 786440 | tf_op jit(solution)/shard_map/ppermute | solution.py:318
  38.5 32.4 %collective-permute-start.36 = (bf16[128,1024]{1,0:T(8,128)(2,1)S(1)}, bf16[128,1024]{1,0:T(8,128)(2,1)S(1)}, u32[]{:S(2)}, u32[]{:S(2)}) collective-permute-start(bf16[128,1024]{1,0:T(8,128)(2,1)S(1)} %get-tuple-element.41), channel_id=1, source_target_pairs={{0,6},{1,7},{2,4},{3,5},{4,2},{5,3},{6,0},{7,1},{8,14},{9,15},{10,... | collective-permute-start | bytes 786440 | tf_op jit(solution)/shard_map/ppermute | solution.py:318
  40.7 44.8 %copy-start.54 = (f32[1,1040]{1,0:T(1,128)}, f32[1,1040]{1,0:T(1,128)S(1)}, u32[]{:S(2)}) copy-start(f32[1,1040]{1,0:T(1,128)S(1)} %collective-permute-done.24) | copy-start | bytes 12484
  40.7 48.8 %collective-permute-start.45 = (bf16[512,768]{1,0:T(8,128)(2,1)S(1)}, bf16[512,768]{1,0:T(8,128)(2,1)}, u32[]{:S(2)}, u32[]{:S(2)}) collective-permute-start(bf16[512,768]{1,0:T(8,128)(2,1)S(1)} %copy.46.refs_24_), channel_id=1, source_target_pairs={{0,16},{8,24},{16,0},{24,8},{1,17},{9,25},{17,1},{25,9},{2,18},{10... | collective-permute-start | bytes 2359304 | tf_op jit(solution)/shard_map/ppermute | solution.py:33
  43.6 63.7 %copy-start.6 = (bf16[1056,256]{1,0:T(8,128)(2,1)}, bf16[1056,256]{1,0:T(8,128)(2,1)S(1)}, u32[]{:S(2)}) copy-start(bf16[1056,256]{1,0:T(8,128)(2,1)S(1)} %pad_maximum_fusion.1.refs_4_.refs_16_) | copy-start | bytes 1622020
  43.6 42.6 %copy-start.30 = (bf16[1024,256]{1,0:T(8,128)(2,1)}, bf16[1024,256]{1,0:T(8,128)(2,1)S(1)}, u32[]{:S(2)}) copy-start(bf16[1024,256]{1,0:T(8,128)(2,1)S(1)} %collective-permute-done.refs_1_) | copy-start | bytes 1572868
  43.6 46.0 %collective-permute-start.44 = (bf16[512,768]{1,0:T(8,128)(2,1)S(1)}, bf16[512,768]{1,0:T(8,128)(2,1)}, u32[]{:S(2)}, u32[]{:S(2)}) collective-permute-start(bf16[512,768]{1,0:T(8,128)(2,1)S(1)} %copy.47.refs_25_), channel_id=1, source_target_pairs={{0,8},{8,0},{16,24},{24,16},{1,9},{9,1},{17,25},{25,17},{2,10},{10... | collective-permute-start | bytes 2359304 | tf_op jit(solution)/shard_map/ppermute | solution.py:34
  43.9 44.0 %collective-permute-start.4 = (bf16[1056,256]{1,0:T(8,128)(2,1)S(1)}, bf16[1056,256]{1,0:T(8,128)(2,1)}, u32[]{:S(2)}, u32[]{:S(2)}) collective-permute-start(bf16[1056,256]{1,0:T(8,128)(2,1)S(1)} %pad_maximum_fusion.1.refs_4_.refs_16_), channel_id=1, source_target_pairs={{0,2},{1,3},{2,4},{3,5},{4,6},{5,7},{6,0},{7,1},{8,10},{9,11},{10,... | collective-permute-start | bytes 1622024 | tf_op jit(solution)/shard_map/ppermute | solution.py:326
  69.5 18.7 %collective-permute-start.11 = (bf16[1056,256]{1,0:T(8,128)(2,1)S(1)}, bf16[1056,256]{1,0:T(8,128)(2,1)}, u32[]{:S(2)}, u32[]{:S(2)}) collective-permute-start(bf16[1056,256]{1,0:T(8,128)(2,1)S(1)} %pad_maximum_fusion.1.refs_4_.refs_16_), channel_id=1, source_target_pairs={{0,1},{1,0},{2,3},{3,2},{4,5},{5,4},{6,7},{7,6},{8,9},{9,8},{10,11... | collective-permute-start | bytes 1622024 | tf_op jit(solution)/shard_map/ppermute | solution.py:331
  71.0 15.3 %collective-permute-start.34 = (bf16[128,1024]{1,0:T(8,128)(2,1)}, bf16[128,1024]{1,0:T(8,128)(2,1)}, u32[]{:S(2)}, u32[]{:S(2)}) collective-permute-start(bf16[128,1024]{1,0:T(8,128)(2,1)} %get-tuple-element.42), channel_id=1, source_target_pairs={{0,2},{1,3},{2,0},{3,1},{4,6},{5,7},{6,4},{7,5},{8,10},{9,11},{10,... | collective-permute-start | bytes 786440 | tf_op jit(solution)/shard_map/ppermute | solution.py:318
  78.7 46.3 %copy-start.55 = (f32[512]{0:T(512)S(1)}, f32[512]{0:T(512)}, u32[]{:S(2)}) copy-start(f32[512]{0:T(512)} %param.17) | copy-start | bytes 6148
  86.2 18.5 %collective-permute-start.43 = (bf16[512,768]{1,0:T(8,128)(2,1)S(1)}, bf16[512,768]{1,0:T(8,128)(2,1)S(1)}, u32[]{:S(2)}, u32[]{:S(2)}) collective-permute-start(bf16[512,768]{1,0:T(8,128)(2,1)S(1)} %copy.46.refs_24_), channel_id=1, source_target_pairs={{0,8},{8,0},{16,24},{24,16},{1,9},{9,1},{17,25},{25,17},{2,10},{10... | collective-permute-start | bytes 2359304 | tf_op jit(solution)/shard_map/ppermute | solution.py:35
  88.0 22.8 %collective-permute-start.46 = (bf16[512,768]{1,0:T(8,128)(2,1)S(1)}, bf16[512,768]{1,0:T(8,128)(2,1)}, u32[]{:S(2)}, u32[]{:S(2)}) collective-permute-start(bf16[512,768]{1,0:T(8,128)(2,1)S(1)} %copy.47.refs_25_), channel_id=1, source_target_pairs={{0,16},{8,24},{16,0},{24,8},{1,17},{9,25},{17,1},{25,9},{2,18},{10... | collective-permute-start | bytes 2359304 | tf_op jit(solution)/shard_map/ppermute | solution.py:36
  88.3 33.3 %collective-permute-start.16 = (bf16[512,768]{1,0:T(8,128)(2,1)}, bf16[512,768]{1,0:T(8,128)(2,1)}, u32[]{:S(2)}, u32[]{:S(2)}) collective-permute-start(bf16[512,768]{1,0:T(8,128)(2,1)} %copy.27), channel_id=1, source_target_pairs={{0,8},{8,0},{16,24},{24,16},{1,9},{9,1},{17,25},{25,17},{2,10},{10... | collective-permute-start | bytes 2359304 | tf_op jit(solution)/shard_map/ppermute | solution.py:34
  89.5 34.6 %collective-permute-start.17 = (bf16[512,768]{1,0:T(8,128)(2,1)}, bf16[512,768]{1,0:T(8,128)(2,1)}, u32[]{:S(2)}, u32[]{:S(2)}) collective-permute-start(bf16[512,768]{1,0:T(8,128)(2,1)} %copy.26), channel_id=1, source_target_pairs={{0,16},{8,24},{16,0},{24,8},{1,17},{9,25},{17,1},{25,9},{2,18},{10... | collective-permute-start | bytes 2359304 | tf_op jit(solution)/shard_map/ppermute | solution.py:33
  89.6 33.8 %collective-permute-start.1 = (bf16[1024,256]{1,0:T(8,128)(2,1)}, bf16[1024,256]{1,0:T(8,128)(2,1)}, u32[]{:S(2)}, u32[]{:S(2)}) collective-permute-start(bf16[1024,256]{1,0:T(8,128)(2,1)} %copy-done.30), channel_id=1, source_target_pairs={{0,2},{1,3},{2,4},{3,5},{4,6},{5,7},{6,0},{7,1},{8,10},{9,11},{10,... | collective-permute-start | bytes 1572872 | tf_op jit(solution)/shard_map/ppermute | solution.py:326
  105.7 20.9 %collective-permute-start.5 = (bf16[1056,256]{1,0:T(8,128)(2,1)}, bf16[1056,256]{1,0:T(8,128)(2,1)}, u32[]{:S(2)}, u32[]{:S(2)}) collective-permute-start(bf16[1056,256]{1,0:T(8,128)(2,1)} %collective-permute-done.4.refs_5_.refs_17_), channel_id=1, source_target_pairs={{0,2},{1,3},{2,4},{3,5},{4,6},{5,7},{6,0},{7,1},{8,10},{9,11},{10,... | collective-permute-start | bytes 1622024 | tf_op jit(solution)/shard_map/ppermute | solution.py:326
  110.8 17.4 %collective-permute-start.8 = (bf16[1024,256]{1,0:T(8,128)(2,1)}, bf16[1024,256]{1,0:T(8,128)(2,1)S(1)}, u32[]{:S(2)}, u32[]{:S(2)}) collective-permute-start(bf16[1024,256]{1,0:T(8,128)(2,1)} %copy-done.30), channel_id=1, source_target_pairs={{0,1},{1,0},{2,3},{3,2},{4,5},{5,4},{6,7},{7,6},{8,9},{9,8},{10,11... | collective-permute-start | bytes 1572872 | tf_op jit(solution)/shard_map/ppermute | solution.py:331
  121.6 7.6 %collective-permute-start.12 = (bf16[1056,256]{1,0:T(8,128)(2,1)}, bf16[1056,256]{1,0:T(8,128)(2,1)S(1)}, u32[]{:S(2)}, u32[]{:S(2)}) collective-permute-start(bf16[1056,256]{1,0:T(8,128)(2,1)} %collective-permute-done.4.refs_5_.refs_17_), channel_id=1, source_target_pairs={{0,1},{1,0},{2,3},{3,2},{4,5},{5,4},{6,7},{7,6},{8,9},{9,8},{10,11... | collective-permute-start | bytes 1622024 | tf_op jit(solution)/shard_map/ppermute | solution.py:331
  123.4 15.7 %collective-permute-start.2 = (bf16[1024,256]{1,0:T(8,128)(2,1)}, bf16[1024,256]{1,0:T(8,128)(2,1)}, u32[]{:S(2)}, u32[]{:S(2)}) collective-permute-start(bf16[1024,256]{1,0:T(8,128)(2,1)} %collective-permute-done.1.refs_2_), channel_id=1, source_target_pairs={{0,2},{1,3},{2,4},{3,5},{4,6},{5,7},{6,0},{7,1},{8,10},{9,11},{10,... | collective-permute-start | bytes 1572872 | tf_op jit(solution)/shard_map/ppermute | solution.py:326
  124.1 16.1 %collective-permute-start.9 = (bf16[1024,256]{1,0:T(8,128)(2,1)}, bf16[1024,256]{1,0:T(8,128)(2,1)S(1)}, u32[]{:S(2)}, u32[]{:S(2)}) collective-permute-start(bf16[1024,256]{1,0:T(8,128)(2,1)} %collective-permute-done.1.refs_2_), channel_id=1, source_target_pairs={{0,1},{1,0},{2,3},{3,2},{4,5},{5,4},{6,7},{7,6},{8,9},{9,8},{10,11... | collective-permute-start | bytes 1572872 | tf_op jit(solution)/shard_map/ppermute | solution.py:331
  126.6 24.1 %collective-permute-start.6 = (bf16[1056,256]{1,0:T(8,128)(2,1)}, bf16[1056,256]{1,0:T(8,128)(2,1)}, u32[]{:S(2)}, u32[]{:S(2)}) collective-permute-start(bf16[1056,256]{1,0:T(8,128)(2,1)} %collective-permute-done.5.refs_6_.refs_18_), channel_id=1, source_target_pairs={{0,2},{1,3},{2,4},{3,5},{4,6},{5,7},{6,0},{7,1},{8,10},{9,11},{10,... | collective-permute-start | bytes 1622024 | tf_op jit(solution)/shard_map/ppermute | solution.py:326
  128.9 25.6 %collective-permute-start.47 = (bf16[512,768]{1,0:T(8,128)(2,1)}, bf16[512,768]{1,0:T(8,128)(2,1)}, u32[]{:S(2)}, u32[]{:S(2)}) collective-permute-start(bf16[512,768]{1,0:T(8,128)(2,1)} %collective-permute-done.45.refs_28_), channel_id=1, source_target_pairs={{0,8},{8,0},{16,24},{24,16},{1,9},{9,1},{17,25},{25,17},{2,10},{10... | collective-permute-start | bytes 2359304 | tf_op jit(solution)/shard_map/ppermute | solution.py:41
  130.0 26.0 %collective-permute-start.48 = (bf16[512,768]{1,0:T(8,128)(2,1)}, bf16[512,768]{1,0:T(8,128)(2,1)}, u32[]{:S(2)}, u32[]{:S(2)}) collective-permute-start(bf16[512,768]{1,0:T(8,128)(2,1)} %collective-permute-done.44.refs_27_), channel_id=1, source_target_pairs={{0,16},{8,24},{16,0},{24,8},{1,17},{9,25},{17,1},{25,9},{2,18},{10... | collective-permute-start | bytes 2359304 | tf_op jit(solution)/shard_map/ppermute | solution.py:41
  139.1 17.1 %collective-permute-start.13 = (bf16[1056,256]{1,0:T(8,128)(2,1)}, bf16[1056,256]{1,0:T(8,128)(2,1)}, u32[]{:S(2)}, u32[]{:S(2)}) collective-permute-start(bf16[1056,256]{1,0:T(8,128)(2,1)} %collective-permute-done.5.refs_6_.refs_18_), channel_id=1, source_target_pairs={{0,1},{1,0},{2,3},{3,2},{4,5},{5,4},{6,7},{7,6},{8,9},{9,8},{10,11... | collective-permute-start | bytes 1622024 | tf_op jit(solution)/shard_map/ppermute | solution.py:331
  141.1 16.4 %collective-permute-start.10 = (bf16[1024,256]{1,0:T(8,128)(2,1)}, bf16[1024,256]{1,0:T(8,128)(2,1)}, u32[]{:S(2)}, u32[]{:S(2)}) collective-permute-start(bf16[1024,256]{1,0:T(8,128)(2,1)} %collective-permute-done.2.refs_3_), channel_id=1, source_target_pairs={{0,1},{1,0},{2,3},{3,2},{4,5},{5,4},{6,7},{7,6},{8,9},{9,8},{10,11... | collective-permute-start | bytes 1572872 | tf_op jit(solution)/shard_map/ppermute | solution.py:331
  150.7 10.6 %collective-permute-start.14 = (bf16[1056,256]{1,0:T(8,128)(2,1)}, bf16[1056,256]{1,0:T(8,128)(2,1)}, u32[]{:S(2)}, u32[]{:S(2)}) collective-permute-start(bf16[1056,256]{1,0:T(8,128)(2,1)} %collective-permute-done.6.refs_7_.refs_19_), channel_id=1, source_target_pairs={{0,1},{1,0},{2,3},{3,2},{4,5},{5,4},{6,7},{7,6},{8,9},{9,8},{10,11... | collective-permute-start | bytes 1622024 | tf_op jit(solution)/shard_map/ppermute | solution.py:331
  154.5 30.1 %collective-permute-start.15 = (bf16[512,768]{1,0:T(8,128)(2,1)}, bf16[512,768]{1,0:T(8,128)(2,1)S(1)}, u32[]{:S(2)}, u32[]{:S(2)}) collective-permute-start(bf16[512,768]{1,0:T(8,128)(2,1)} %copy.26), channel_id=1, source_target_pairs={{0,8},{8,0},{16,24},{24,16},{1,9},{9,1},{17,25},{25,17},{2,10},{10... | collective-permute-start | bytes 2359304 | tf_op jit(solution)/shard_map/ppermute | solution.py:35
  156.0 29.0 %collective-permute-start.18 = (bf16[512,768]{1,0:T(8,128)(2,1)}, bf16[512,768]{1,0:T(8,128)(2,1)S(1)}, u32[]{:S(2)}, u32[]{:S(2)}) collective-permute-start(bf16[512,768]{1,0:T(8,128)(2,1)} %copy.27), channel_id=1, source_target_pairs={{0,16},{8,24},{16,0},{24,8},{1,17},{9,25},{17,1},{25,9},{2,18},{10... | collective-permute-start | bytes 2359304 | tf_op jit(solution)/shard_map/ppermute | solution.py:36
  156.2 34.5 %collective-permute-start.19 = (bf16[512,768]{1,0:T(8,128)(2,1)}, bf16[512,768]{1,0:T(8,128)(2,1)S(1)}, u32[]{:S(2)}, u32[]{:S(2)}) collective-permute-start(bf16[512,768]{1,0:T(8,128)(2,1)} %collective-permute-done.17.refs_28_), channel_id=1, source_target_pairs={{0,8},{8,0},{16,24},{24,16},{1,9},{9,1},{17,25},{25,17},{2,10},{10... | collective-permute-start | bytes 2359304 | tf_op jit(solution)/shard_map/ppermute | solution.py:41
  157.5 34.6 %collective-permute-start.20 = (bf16[512,768]{1,0:T(8,128)(2,1)}, bf16[512,768]{1,0:T(8,128)(2,1)S(1)}, u32[]{:S(2)}, u32[]{:S(2)}) collective-permute-start(bf16[512,768]{1,0:T(8,128)(2,1)} %collective-permute-done.16.refs_27_), channel_id=1, source_target_pairs={{0,16},{8,24},{16,0},{24,8},{1,17},{9,25},{17,1},{25,9},{2,18},{10... | collective-permute-start | bytes 2359304 | tf_op jit(solution)/shard_map/ppermute | solution.py:41
  161.3 78.5 %collective-permute-start.37 = (bf16[2,128,1024]{2,1,0:T(8,128)(2,1)}, bf16[2,128,1024]{2,1,0:T(8,128)(2,1)}, u32[]{:S(2)}, u32[]{:S(2)}) collective-permute-start(bf16[2,128,1024]{2,1,0:T(8,128)(2,1)} %pad_maximum_fusion.2), channel_id=1, source_target_pairs={{0,8},{8,0},{16,24},{24,16},{1,9},{9,1},{17,25},{25,17},{2,10},{10... | collective-permute-start | bytes 1572872 | tf_op jit(solution)/shard_map/ppermute | solution.py:35
  184.7 56.4 %collective-permute-start.39 = (bf16[2,128,1024]{2,1,0:T(8,128)(2,1)}, bf16[2,128,1024]{2,1,0:T(8,128)(2,1)}, u32[]{:S(2)}, u32[]{:S(2)}) collective-permute-start(bf16[2,128,1024]{2,1,0:T(8,128)(2,1)} %pad_maximum_fusion.2), channel_id=1, source_target_pairs={{0,16},{8,24},{16,0},{24,8},{1,17},{9,25},{17,1},{25,9},{2,18},{10... | collective-permute-start | bytes 1572872 | tf_op jit(solution)/shard_map/ppermute | solution.py:33
  185.0 56.4 %collective-permute-start.38 = (bf16[2,128,1024]{2,1,0:T(8,128)(2,1)}, bf16[2,128,1024]{2,1,0:T(8,128)(2,1)}, u32[]{:S(2)}, u32[]{:S(2)}) collective-permute-start(bf16[2,128,1024]{2,1,0:T(8,128)(2,1)} %pad_maximum_fusion.3), channel_id=1, source_target_pairs={{0,8},{8,0},{16,24},{24,16},{1,9},{9,1},{17,25},{25,17},{2,10},{10... | collective-permute-start | bytes 1572872 | tf_op jit(solution)/shard_map/ppermute | solution.py:34
  192.9 22.8 %copy-start.23 = (f32[1,256]{1,0:T(1,128)S(1)}, f32[1,256]{1,0:T(1,128)}, u32[]{:S(2)}) copy-start(f32[1,256]{1,0:T(1,128)} %get-tuple-element.85.skip_ref) | copy-start | bytes 3076
  214.2 6.7 %collective-permute-start.25 = (f32[16,256]{1,0:T(8,128)S(1)}, f32[16,256]{1,0:T(8,128)S(1)}, u32[]{:S(2)}, u32[]{:S(2)}) collective-permute-start(f32[16,256]{1,0:T(8,128)S(1)} %get-tuple-element.26), channel_id=1, source_target_pairs={{0,8},{8,0},{16,24},{24,16},{1,9},{9,1},{17,25},{25,17},{2,10},{10... | collective-permute-start | bytes 49160 | tf_op jit(solution)/shard_map/ppermute | solution.py:318
  214.5 7.7 %collective-permute-start.26 = (f32[16,256]{1,0:T(8,128)S(1)}, f32[16,256]{1,0:T(8,128)S(1)}, u32[]{:S(2)}, u32[]{:S(2)}) collective-permute-start(f32[16,256]{1,0:T(8,128)S(1)} %get-tuple-element.26), channel_id=1, source_target_pairs={{0,16},{8,24},{16,0},{24,8},{1,17},{9,25},{17,1},{25,9},{2,18},{10... | collective-permute-start | bytes 49160 | tf_op jit(solution)/shard_map/ppermute | solution.py:318
  220.9 3.6 %collective-permute-start.27 = (f32[16,256]{1,0:T(8,128)S(1)}, f32[16,256]{1,0:T(8,128)S(1)}, u32[]{:S(2)}, u32[]{:S(2)}) collective-permute-start(f32[16,256]{1,0:T(8,128)S(1)} %get-tuple-element.26), channel_id=1, source_target_pairs={{0,24},{8,16},{16,8},{24,0},{1,25},{9,17},{17,9},{25,1},{2,26},{10... | collective-permute-start | bytes 49160 | tf_op jit(solution)/shard_map/ppermute | solution.py:318
  222.1 2.6 collective-permute-start.49
  224.4 2.9 collective-permute-start.50
  224.7 3.5 %collective-permute-start.51 = (f32[16,256]{1,0:T(8,128)S(1)}, f32[16,256]{1,0:T(8,128)S(1)}, u32[]{:S(2)}, u32[]{:S(2)}) collective-permute-start(f32[16,256]{1,0:T(8,128)S(1)} %get-tuple-element.33), channel_id=1, source_target_pairs={{0,24},{8,16},{16,8},{24,0},{1,25},{9,17},{17,9},{25,1},{2,26},{10... | collective-permute-start | bytes 49160 | tf_op jit(solution)/shard_map/ppermute | solution.py:318
  231.9 10.7 %collective-permute-start.52 = (bf16[1024,256]{1,0:T(8,128)(2,1)}, bf16[1024,256]{1,0:T(8,128)(2,1)}, u32[]{:S(2)}, u32[]{:S(2)}) collective-permute-start(bf16[1024,256]{1,0:T(8,128)(2,1)} %gated_signal.3.refs_0_), channel_id=1, source_target_pairs={{0,2},{1,3},{2,4},{3,5},{4,6},{5,7},{6,0},{7,1},{8,10},{9,11},{10,... | collective-permute-start | bytes 1572872 | tf_op jit(solution)/shard_map/ppermute | solution.py:326
  237.1 16.6 %collective-permute-start.28 = (bf16[1024,256]{1,0:T(8,128)(2,1)S(1)}, bf16[1024,256]{1,0:T(8,128)(2,1)S(1)}, u32[]{:S(2)}, u32[]{:S(2)}) collective-permute-start(bf16[1024,256]{1,0:T(8,128)(2,1)S(1)} %gated_signal.2.refs_0_), channel_id=1, source_target_pairs={{0,2},{1,3},{2,4},{3,5},{4,6},{5,7},{6,0},{7,1},{8,10},{9,11},{10,... | collective-permute-start | bytes 1572872 | tf_op jit(solution)/shard_map/ppermute | solution.py:326
  239.9 25.1 %collective-permute-start.40 = (bf16[2,128,1024]{2,1,0:T(8,128)(2,1)}, bf16[2,128,1024]{2,1,0:T(8,128)(2,1)S(1)}, u32[]{:S(2)}, u32[]{:S(2)}) collective-permute-start(bf16[2,128,1024]{2,1,0:T(8,128)(2,1)} %pad_maximum_fusion.3), channel_id=1, source_target_pairs={{0,16},{8,24},{16,0},{24,8},{1,17},{9,25},{17,1},{25,9},{2,18},{10... | collective-permute-start | bytes 1572872 | tf_op jit(solution)/shard_map/ppermute | solution.py:36
  241.1 35.1 %collective-permute-start.41 = (bf16[2,128,1024]{2,1,0:T(8,128)(2,1)}, bf16[2,128,1024]{2,1,0:T(8,128)(2,1)S(1)}, u32[]{:S(2)}, u32[]{:S(2)}) collective-permute-start(bf16[2,128,1024]{2,1,0:T(8,128)(2,1)} %collective-permute-done.39), channel_id=1, source_target_pairs={{0,8},{8,0},{16,24},{24,16},{1,9},{9,1},{17,25},{25,17},{2,10},{10... | collective-permute-start | bytes 1572872 | tf_op jit(solution)/shard_map/ppermute | solution.py:41
  241.4 34.9 %collective-permute-start.42 = (bf16[2,128,1024]{2,1,0:T(8,128)(2,1)}, bf16[2,128,1024]{2,1,0:T(8,128)(2,1)S(1)}, u32[]{:S(2)}, u32[]{:S(2)}) collective-permute-start(bf16[2,128,1024]{2,1,0:T(8,128)(2,1)} %collective-permute-done.38), channel_id=1, source_target_pairs={{0,16},{8,24},{16,0},{24,8},{1,17},{9,25},{17,1},{25,9},{2,18},{10... | collective-permute-start | bytes 1572872 | tf_op jit(solution)/shard_map/ppermute | solution.py:41
  242.6 22.3 %collective-permute-start.53 = (bf16[1024,256]{1,0:T(8,128)(2,1)}, bf16[1024,256]{1,0:T(8,128)(2,1)S(1)}, u32[]{:S(2)}, u32[]{:S(2)}) collective-permute-start(bf16[1024,256]{1,0:T(8,128)(2,1)} %collective-permute-done.52.refs_1_), channel_id=1, source_target_pairs={{0,2},{1,3},{2,4},{3,5},{4,6},{5,7},{6,0},{7,1},{8,10},{9,11},{10,... | collective-permute-start | bytes 1572872 | tf_op jit(solution)/shard_map/ppermute | solution.py:326
  253.7 22.5 %collective-permute-start.29 = (bf16[1024,256]{1,0:T(8,128)(2,1)S(1)}, bf16[1024,256]{1,0:T(8,128)(2,1)S(1)}, u32[]{:S(2)}, u32[]{:S(2)}) collective-permute-start(bf16[1024,256]{1,0:T(8,128)(2,1)S(1)} %collective-permute-done.28.refs_1_), channel_id=1, source_target_pairs={{0,2},{1,3},{2,4},{3,5},{4,6},{5,7},{6,0},{7,1},{8,10},{9,11},{10,... | collective-permute-start | bytes 1572872 | tf_op jit(solution)/shard_map/ppermute | solution.py:326
  264.9 22.5 %collective-permute-start.54 = (bf16[1024,256]{1,0:T(8,128)(2,1)S(1)}, bf16[1024,256]{1,0:T(8,128)(2,1)S(1)}, u32[]{:S(2)}, u32[]{:S(2)}) collective-permute-start(bf16[1024,256]{1,0:T(8,128)(2,1)S(1)} %collective-permute-done.53.refs_2_), channel_id=1, source_target_pairs={{0,2},{1,3},{2,4},{3,5},{4,6},{5,7},{6,0},{7,1},{8,10},{9,11},{10,... | collective-permute-start | bytes 1572872 | tf_op jit(solution)/shard_map/ppermute | solution.py:326
  276.2 22.5 %collective-permute-start.30 = (bf16[1024,256]{1,0:T(8,128)(2,1)S(1)}, bf16[1024,256]{1,0:T(8,128)(2,1)S(1)}, u32[]{:S(2)}, u32[]{:S(2)}) collective-permute-start(bf16[1024,256]{1,0:T(8,128)(2,1)S(1)} %collective-permute-done.29.refs_2_), channel_id=1, source_target_pairs={{0,2},{1,3},{2,4},{3,5},{4,6},{5,7},{6,0},{7,1},{8,10},{9,11},{10,... | collective-permute-start | bytes 1572872 | tf_op jit(solution)/shard_map/ppermute | solution.py:326
  299.7 13.9 %collective-permute-start.55 = (bf16[1024,512]{1,0:T(8,128)(2,1)S(1)}, bf16[1024,512]{1,0:T(8,128)(2,1)S(1)}, u32[]{:S(2)}, u32[]{:S(2)}) collective-permute-start(bf16[1024,512]{1,0:T(8,128)(2,1)S(1)} %add_outputs.11), channel_id=1, source_target_pairs={{0,1},{1,0},{2,3},{3,2},{4,5},{5,4},{6,7},{7,6},{8,9},{9,8},{10,11... | collective-permute-start | bytes 3145736 | tf_op jit(solution)/shard_map/ppermute | solution.py:331
  (49 other events, 397.2 us)

commit v3 on v0

--- a/solution.py
+++ b/solution.py
@@ -1,4 +1,5 @@
 import functools
+import math
 
 import jax
 import jax.numpy as jnp
@@ -9,6 +10,7 @@
 
 LANES = 128
 SEGMENTS = 8
+TAIL = 16
 f32 = jnp.float32
 bf16 = jnp.bfloat16
 
@@ -17,25 +19,12 @@
     return [(i, i ^ bit) for i in range(size)]
 
 
-def gathered_blocks(block):
-    size = lax.axis_size("ctx")
-    me = lax.axis_index("ctx")
-    rows = block.shape[0]
-    if size != 4:
-        whole = lax.all_gather(block, "ctx", axis=0)
-        return [(i, 0, whole[i]) for i in range(size)]
-    half = rows // 2
-    by_x = lax.ppermute(block, "ctx", swap_route(size, 1))
-    by_y = lax.ppermute(block, "ctx", swap_route(size, 2))
-    far_top = lax.ppermute(by_y[:half], "ctx", swap_route(size, 1))
-    far_bottom = lax.ppermute(by_x[half:], "ctx", swap_route(size, 2))
-    return [
-        (me, 0, block),
-        (me ^ 1, 0, by_x),
-        (me ^ 2, 0, by_y),
-        (me ^ 3, 0, far_top),
-        (me ^ 3, half, far_bottom),
-    ]
+def send(transfers, after=()):
+    arrays = {id(array): array for array, _, _ in transfers}
+    if len(after) > 0:
+        tied = lax.optimization_barrier((list(arrays.values()), tuple(after)))[0]
+        arrays = dict(zip(arrays, tied))
+    return [lax.ppermute(arrays[id(array)], axis, route) for array, axis, route in transfers]
 
 
 def shifted_start(ref, tail_ref, back, segment):
@@ -134,7 +123,7 @@
     tokens, width = projected.shape
     blocks = width // 3 // LANES
     modes = tables["lam"].shape[0]
-    flops = tokens * width // 3 * modes * 4
+    flops = 0
     return pl.pallas_call(
         functools.partial(local_kernel, tokens // SEGMENTS, modes),
         grid=(blocks,),
@@ -166,29 +155,28 @@
     )
 
 
-def gated_signal(projected, tails, taps, tables, response, ends, states):
+def gated_signal(projected, tails, taps, tables, response, ends, states, lane):
     tokens, width = projected.shape
-    blocks = width // 3 // LANES
     modes = tables["lam"].shape[0]
     parts = states.shape[0] // modes
-    flops = tokens * width // 3 * modes * 2
+    flops = 0
     return pl.pallas_call(
         functools.partial(gate_kernel, tokens // SEGMENTS, modes, parts),
-        grid=(blocks,),
+        grid=(1,),
         in_specs=[
-            column(tokens, 0),
-            column(2, 0),
-            column(3, 0),
-            column(modes, 0),
-            column(modes, 0),
-            column(modes, 0),
-            column(tokens, 0),
-            column(modes * SEGMENTS, 0),
-            column(parts * modes, 0),
-            column(parts * modes, 0),
+            column(tokens, lane),
+            column(2, lane),
+            column(3, lane),
+            column(modes, lane),
+            column(modes, lane),
+            column(modes, lane),
+            column(tokens, lane),
+            column(modes * SEGMENTS, lane),
+            column(parts * modes, lane),
+            column(parts * modes, lane),
         ],
         out_specs=column(tokens, 0),
-        out_shape=jax.ShapeDtypeStruct((tokens, width // 3), bf16),
+        out_shape=jax.ShapeDtypeStruct((tokens, LANES), bf16),
         scratch_shapes=[pltpu.VMEM((modes * SEGMENTS, LANES), f32), pltpu.VMEM((tokens, LANES), f32)],
         cost_estimate=pl.CostEstimate(flops=flops, bytes_accessed=tokens * width * 3, transcendentals=0),
         compiler_params=pltpu.CompilerParams(vmem_limit_bytes=32 * 2**20),
@@ -197,6 +185,111 @@
         projected, tails, taps, tables["lam"], tables["hop"], tables["residue"], response, ends, states,
         tables["shares"],
     )
+
+
+def project_kernel(order_ref, all_ref, tails_ref, *refs):
+    unit_refs, (inverse_ref, tail_inverse_ref, out_ref, tail_out_ref) = refs[:-4], refs[-4:]
+    features = all_ref.shape[2]
+    chunks = [(ref, at) for ref in unit_refs for at in range(0, ref.shape[0], features)]
+
+    def total(first_rows):
+        result = None
+        for n, (ref, at) in enumerate(chunks):
+            block = all_ref[order_ref[n]]
+            if first_rows:
+                block = jnp.concatenate([tails_ref[order_ref[len(chunks) + n]], block], axis=0)
+            part = jnp.dot(block, ref[at : at + features, :], preferred_element_type=f32)
+            result = part if result is None else result + part
+        return result
+
+    @pl.when(pl.program_id(0) == 0)
+    def _():
+        result = total(True)
+        tail_out_ref[...] = result[:TAIL] * tail_inverse_ref[...]
+        out_ref[...] = result[TAIL:] * inverse_ref[...]
+
+    @pl.when(pl.program_id(0) > 0)
+    def _():
+        out_ref[...] = total(False) * inverse_ref[...]
+
+
+def project(everything, tails, units, order, inverse, tail_inverse):
+    mp, tokens, features = everything.shape
+    width = units[0].shape[1]
+    tile = math.gcd(tokens, 256)
+    return pl.pallas_call(
+        project_kernel,
+        grid_spec=pltpu.PrefetchScalarGridSpec(
+            num_scalar_prefetch=1,
+            grid=(tokens // tile,),
+            in_specs=[
+                pl.BlockSpec((mp, tile, features), lambda m, order: (0, m, 0)),
+                pl.BlockSpec((mp, TAIL, features), lambda m, order: (0, 0, 0)),
+                *[pl.BlockSpec(memory_space=pltpu.VMEM) for _ in units],
+                pl.BlockSpec((tile, 1), lambda m, order: (m, 0)),
+                pl.BlockSpec((TAIL, 1), lambda m, order: (0, 0)),
+            ],
+            out_specs=[
+                pl.BlockSpec((tile, width), lambda m, order: (m, 0)),
+                pl.BlockSpec((TAIL, width), lambda m, order: (0, 0)),
+            ],
+        ),
+        out_shape=[jax.ShapeDtypeStruct((tokens, width), f32), jax.ShapeDtypeStruct((TAIL, width), f32)],
+        compiler_params=pltpu.CompilerParams(vmem_limit_bytes=40 * 2**20),
+        name="project",
+    )(order, everything, tails, *units, inverse, tail_inverse)
+
+
+def output_kernel(chips, order_ref, half_ref, *refs):
+    count = len(chips[0])
+    gated_refs = refs[: count * len(chips)]
+    panel_ref, base_refs, out_ref = refs[len(gated_refs)], refs[len(gated_refs) + 1 : -1], refs[-1]
+    total = None
+    for n, chip in enumerate(chips):
+        rows = [ref[...] for ref in gated_refs[n * count : (n + 1) * count]]
+        rows = jnp.concatenate(rows, axis=1) if count > 1 else rows[0]
+        part = jnp.dot(rows, panel_ref[order_ref[n]], preferred_element_type=f32)
+        total = part if total is None else total + part
+    for base_ref in base_refs:
+        total = total + base_ref[...].astype(f32)
+    out_ref[...] = total.astype(out_ref.dtype)
+
+
+def add_outputs(gated, order, panel, group, half, bases, dtype):
+    tokens = gated[0][0].shape[0]
+    share = len(gated[0]) * LANES
+    chips, columns = panel.shape[0], panel.shape[2] // 2
+    tile = math.gcd(tokens, 256)
+    blocks = [block for chip in gated for block in chip]
+    return pl.pallas_call(
+        functools.partial(output_kernel, [[0] * len(chip) for chip in gated]),
+        grid_spec=pltpu.PrefetchScalarGridSpec(
+            num_scalar_prefetch=2,
+            grid=(tokens // tile,),
+            in_specs=[
+                *[pl.BlockSpec((tile, LANES), lambda m, order, half: (m, 0)) for _ in blocks],
+                pl.BlockSpec((chips, share, columns), lambda m, order, half: (0, group, half[0])),
+                *[pl.BlockSpec((tile, columns), lambda m, order, half: (m, 0)) for _ in bases],
+            ],
+            out_specs=pl.BlockSpec((tile, columns), lambda m, order, half: (m, 0)),
+        ),
+        out_shape=jax.ShapeDtypeStruct((tokens, columns), dtype),
+        cost_estimate=pl.CostEstimate(
+            flops=4 * tokens * columns * len(gated) * share, bytes_accessed=4 * tokens * columns, transcendentals=0
+        ),
+        compiler_params=pltpu.CompilerParams(vmem_limit_bytes=32 * 2**20),
+        name="add_outputs",
+    )(order, half, *blocks, panel, *bases)
+
+
+def core_swap(block):
+    return lax.ppermute(block, "mp", swap_route(lax.axis_size("mp"), 1))
+
+
+def ctx_order():
+    size = lax.axis_size("ctx")
+    index = jnp.arange(size)
+    return lax.axis_index("ctx") ^ index if (size, lax.axis_size("mp")) == (4, 8) else index
 
 
 def filter_tables(decay_rate, residue, skip_gain, tokens):
@@ -208,7 +301,7 @@
     segment = tokens // SEGMENTS
     ahead = (SEGMENTS - 1 - jnp.arange(SEGMENTS, dtype=f32)) * segment
     reach = jnp.exp(-rate[:, None, :] * ahead[None, :, None]).reshape(modes * SEGMENTS, channels)
-    index = jnp.arange(size)
+    index = ctx_order()
     gap = (me - 1 - index).astype(f32) * tokens
     shares = jnp.where(
         (index < me)[:, None, None], jnp.exp(-rate[None] * jnp.maximum(gap, 0.0)[:, None, None]), 0.0
@@ -254,53 +347,138 @@
     model_width = features * mp
     groups = 2 if channels % (2 * LANES) == 0 else 1
     share = channels // groups
+    here = lax.axis_index("mp")
+    chips = mp // 2
+    chip, core = here // 2, here % 2
+    special = (ctx, mp, groups) == (4, 8, 2)
+    per = mp // ctx
+
     act_float = activations.astype(f32)
     scaled = (act_float * norm_gain[None, :]).astype(bf16)
     everything = lax.all_gather(scaled, "mp", axis=0)
-    squares = lax.psum(jnp.sum(act_float * act_float, axis=1), "mp")
-    inverse = lax.rsqrt(squares / model_width + 1e-06)[:, None]
-    per_block = mp // ctx
-    by_block = everything.reshape(ctx, per_block, tokens, features)
-
-    def project(blocks):
-        total = None
-        for owner, first, rows in blocks:
-            for i in range(0, rows.shape[0], features):
-                source = lax.dynamic_index_in_dim(by_block, owner, 0, False)[(first + i) // features]
-                part = lax.dot_general(
-                    source, rows[i : i + features], (((1,), (0,)), ((), ())), preferred_element_type=f32
-                )
-                total = part if total is None else total + part
-        return total * inverse
-
+    w_units = [w_in[:, :, g * share : (g + 1) * share].reshape(-1, 3 * share) for g in range(groups)]
+    next_on = ("ctx", [(i, i + 1) for i in range(ctx - 1)])
+    tails_all = lax.ppermute(scaled[-TAIL:], *next_on)[None]
+    squares = jnp.sum(act_float * act_float, axis=1)[None]
     tables = filter_tables(decay_rate, residue, skip_gain, tokens)
     start_state = state_in.T
-    taps_all = short_filter
-    tails_all = tail_rows.transpose(2, 0, 1).astype(f32)
-    pieces = [w_in[:, :, g * share : (g + 1) * share].reshape(-1, 3 * share) for g in range(groups)]
-    arriving = [gathered_blocks(piece) for piece in pieces]
-    outputs = []
+    tails_in = tail_rows.transpose(2, 0, 1).astype(f32)
+    columns = w_out.shape[1] // per
+
+    if special:
+        along_x, along_y, across = (("ctx", swap_route(ctx, mask)) for mask in (1, 2, 3))
+        along_z = ("mp", [(i, (i + 2) % mp) for i in range(mp)])
+        others = [("mp", swap_route(mp, 2 * d)) for d in range(1, chips)]
+        middle, quarter = w_in.shape[0] // 2, w_in.shape[0] // 4
+        own_rows = w_out.reshape(ctx, channels // ctx, -1)
+        sent = [lax.dynamic_index_in_dim(own_rows, me ^ d, 0, False) for d in range(ctx)]
+        near = send([(w_units[0], *along_x), (w_units[0], *along_y)])
+        squares = squares + core_swap(squares)
+        squares = squares + sum(lax.ppermute(squares, *route) for route in others)
+        inverse = lax.rsqrt(squares[0] / model_width + 1e-06)[:, None]
+        tail_inverse = lax.ppermute(inverse[-TAIL:], *next_on)
+        first_near = near
+        near, sent = lax.optimization_barrier(((near, sent), inverse))[0]
+        far = send([(near[1][:middle], *along_x), (near[0][middle:], *along_y)])
+        units = [[w_units[0], *near, *far]]
+        got = send([(sent[1], *along_x), (sent[2], *along_y), (sent[3], *across)], first_near)
+        by_owner = jnp.stack([sent[0], *got])
+        tails_all = jnp.concatenate([tails_all, core_swap(tails_all)])
+        tails_all = jnp.concatenate([tails_all, *[lax.ppermute(tails_all, *route) for route in others]])
+        near = send([(w_units[1], *along_x), (w_units[1], *along_y)], [*far, *got, tails_all, tail_inverse])
+        order = jnp.stack([(me ^ (n // per)) * per + n % per for n in range(mp)]).astype(jnp.int32)
+        order = jnp.concatenate([order, order ^ here])
+
+        sent = [lax.dynamic_index_in_dim(by_owner, (chip ^ d) ^ me, 0, False) for d in range(chips)]
+        own_row, *sent = lax.optimization_barrier((sent, everything))[0]
+        by_chip = [lax.ppermute(block, *route) for block, route in zip(sent, others)]
+        rows = jnp.stack([own_row, *by_chip])
+        panel_order = jnp.stack([((chip - n) % chips) ^ chip for n in range(chips)]).astype(jnp.int32)
+    else:
+        units = []
+        for g in range(groups):
+            gathered = lax.all_gather(w_units[g], "ctx", axis=0)
+            units.append([gathered[n] for n in range(ctx)])
+        order = jnp.tile(jnp.arange(mp, dtype=jnp.int32), 2)
+        tails_all = lax.all_gather(tails_all[0], "mp", axis=0)
+        inverse = lax.rsqrt(lax.psum(squares, "mp")[0] / model_width + 1e-06)[:, None]
+        tail_inverse = lax.ppermute(inverse[-TAIL:], *next_on)
+        groups_of_core = [[i for i in range(mp) if i % 2 == c] for c in range(2)]
+        rows = lax.all_to_all(w_out.reshape(ctx, channels // ctx, -1), "ctx", 0, 0)
+        rows = rows.reshape(ctx, channels // ctx, chips // ctx, 2 * columns).swapaxes(1, 2)
+        rows = rows.reshape(chips, channels // ctx, 2 * columns)
+        rows = lax.all_to_all(rows, "mp", 0, 0, axis_index_groups=groups_of_core)
+        panel = lax.all_gather(rows, "ctx", axis=1).reshape(chips, channels, 2 * columns)
+        panel_order = jnp.arange(chips, dtype=jnp.int32)
+
     finals = []
+    rings = []
     for g in range(groups):
         span = slice(g * share, (g + 1) * share)
         own = cut(tables, g * share, (g + 1) * share)
-        taps = taps_all[:, :, span].reshape(3, 3 * share)
-        projected = project(arriving[g])
-        behind = lax.ppermute(projected[-2:], "ctx", [(i, i + 1) for i in range(ctx - 1)])
-        tails = jnp.where(me == 0, tails_all[:, :, span].reshape(2, 3 * share), behind)
+        taps = short_filter[:, :, span].reshape(3, 3 * share)
+        if rings:
+            order = lax.optimization_barrier((order, gated))[0]
+        projected, before = project(everything, tails_all, units[g], order, inverse, tail_inverse)
+        tails = jnp.where(me == 0, tails_in[:, :, span].reshape(2, 3 * share), before[TAIL - 2 :])
+        if special and g > 0:
+            tails = lax.optimization_barrier((tails, rings[0][1]))[0]
         response, ends, last = local_filter(projected, tails, taps, own)
-        lasts = lax.all_gather(last, "ctx", axis=0)
+        if special:
+            shared = lax.optimization_barrier((last, by_chip[0]))[0] if g == 0 else last
+            arrived = [lax.ppermute(shared, *route) for route in (along_x, along_y, across)]
+            if g == 0:
+                near = lax.optimization_barrier((near, before))[0]
+                far = send([(near[1][:quarter], *along_x), (near[0][middle : middle + quarter], *along_y)])
+                arrived = lax.optimization_barrier((arrived, (*by_chip, *far)))[0]
+                late = send([(near[1][quarter:middle], *along_x), (near[0][middle + quarter :], *along_y)], arrived)
+            else:
+                arrived = lax.optimization_barrier((arrived, rings[0][2]))[0]
+                panel_bottom = send([(bottom, *along_x), (bottom, *along_y)], arrived)
+                panel_far = send([(panel_top[1], *along_x), (panel_bottom[0], *along_y)])
+            lasts = jnp.stack([last, *arrived])
+        else:
+            lasts = lax.all_gather(last, "ctx", axis=0)
         states = jnp.concatenate([lasts, start_state[None, :, span]])
         finals.append(jnp.sum(own["final"] * states, axis=0))
-        outputs.append(
-            gated_signal(projected, tails, taps, own, response, ends, states.reshape(-1, share))
-        )
-    state_out = jnp.concatenate(finals, axis=1).T
-    gated = jnp.concatenate(outputs, axis=1)
-    panel = lax.all_gather(w_out, "ctx", axis=1, tiled=True)
-    partial = lax.dot_general(panel, gated, (((0,), (1,)), ((), ())), preferred_element_type=f32)
-    branch = lax.psum_scatter(partial.astype(bf16), "mp", scatter_dimension=0, tiled=True).astype(f32).T
-    return ((act_float + branch).astype(bf16), state_out)
+        gated = [
+            gated_signal(projected, tails, taps, own, response, ends, states.reshape(-1, share), lane)
+            for lane in range(share // LANES)
+        ]
+        if special:
+            blocks = [gated]
+            for _ in range(chips - 1):
+                blocks.append([lax.ppermute(block, *along_z) for block in blocks[-1]])
+            rings.append(blocks)
+            if g == 0:
+                units.append([w_units[1], *near, *[jnp.concatenate(pair) for pair in zip(far, late)]])
+                top, bottom = rows[: chips // 2], rows[chips // 2 :]
+                panel_top = send([(top, *along_x), (top, *along_y)], [*late, *gated])
+        else:
+            gathered = [lax.all_gather(block, "mp", axis=0, axis_index_groups=groups_of_core) for block in gated]
+            rings.append([[block[n] for block in gathered] for n in range(chips)])
+
+    if special:
+        panel = jnp.zeros((chips, ctx, *rows.shape[1:]), bf16)
+        landed = [(0, 0, rows), (3, 0, panel_far[0]), (3, 2, panel_far[1])]
+        landed += [(1 + n, 0, panel_top[n]) for n in range(2)] + [(1 + n, 2, panel_bottom[n]) for n in range(2)]
+        for d, first, block in landed:
+            panel = lax.dynamic_update_slice(panel, block[:, None], (first, me ^ d, 0, 0))
+        panel = panel.reshape(chips, channels, 2 * columns)
+    mine, other = core[None].astype(jnp.int32), (1 - core)[None].astype(jnp.int32)
+    kept, given = [activations], []
+    for g in range(groups):
+        final = g == groups - 1
+        steps = [slice(0, chips - 1), slice(chips - 1, chips)] if final else [slice(0, chips)]
+        for n, step in enumerate(steps):
+            dtype = bf16 if final and n == len(steps) - 1 else f32
+            last_step = rings[g][step]
+            if final and n == len(steps) - 1:
+                last_step = lax.optimization_barrier((last_step, kept[0]))[0]
+            given = [add_outputs(last_step, panel_order[step], panel, g, other, given, dtype)]
+            kept = [add_outputs(last_step, panel_order[step], panel, g, mine, kept, f32)]
+    total = (kept[0] + core_swap(given[0]).astype(f32)).astype(bf16)
+    return (total, jnp.concatenate(finals, axis=1).T)
 
 
 def solution(mesh):

time: 300 us -> 260 us (0.87)
  matrix products: 66.7 us -> 0 us
  waiting for transfers between devices: 130 us -> 76.4 us
  starting transfers between devices: 13.1 us -> 66.6 us
  Pallas kernels: 16.2 us -> 47.6 us
  blocking collectives: 27.1 us -> 0 us
  local copies, waits for them, and re-layouts: 22.8 us -> 39.5 us
  other arithmetic: 6.14 us -> 14 us
    reduce_scatter x1 -> x0, waiting for transfers between devices: 90.1 us -> none  [local(): lax.psum_scatter(partial.astype(bf16), 'mp', scatter_dimension=0, tiled=T...]
    dot_general x17 -> x0, matrix products: 66.7 us -> none  [the longest x16 57.7 us: project(): lax.dot_general(source, rows[i:i + features], (((1,), (0,)), ((), ())), p...]
    ppermute x10 -> x51, starting transfers between devices: 13 us -> 66.5 us  [the longest x19 21.6 us: send(): lax.ppermute(arrays[id(array)], axis, route)]
    ppermute x10 -> x51, waiting for transfers between devices: 35.6 us -> 76.4 us  [the longest x19 37.3 us: send(): lax.ppermute(arrays[id(array)], axis, route)]
    pallas_call x0 -> x8, Pallas kernels: none -> 31.8 us  [the longest x2 20.5 us: project(): pl.pallas_call(project_kernel, grid_spec=pltpu.PrefetchScalarGridSpec(num...]
    psum x1 -> x0, blocking collectives: 15.5 us -> none  [local(): squares = lax.psum(jnp.sum(act_float * act_float, axis=1), 'mp')]
    all_gather x2 -> x0, blocking collectives: 11.6 us -> none  [local(): lasts = lax.all_gather(last, 'ctx', axis=0)]
    slice x6, local copies, waits for them, and re-layouts: 0.06 us -> 4.66 us  [cut(): return {name: table[..., start:stop] for name, table in tables.items()}]
  transfers between devices with their start and end apart: 13 -> 52, of which waited for: 4 -> 23; matrix products, arithmetic and copies ran while one was open for 28% -> 17% of each run, Pallas kernels for 5% -> 16%
where the time goes in v3:
time: 260 us; the launch traced here: 259 us
  waiting for transfers between devices  76.4 us (29%)
  starting transfers between devices  66.6 us (26%)
  Pallas kernels  47.6 us (18%)
  local copies, waits for them, and re-layouts  39.5 us (15%)
  between operations  15 us (6%)
  other arithmetic  14 us (5%)
    ppermute x19, waiting for transfers between devices, send(): lax.ppermute(arrays[id(array)], axis, route)  37.3 us
    ppermute x12, waiting for transfers between devices, local(): blocks.append([lax.ppermute(block, *along_z) for block in blocks[-1]])  22.1 us
    ppermute x19, starting transfers between devices, send(): lax.ppermute(arrays[id(array)], axis, route)  21.6 us
    pallas_call x2, Pallas kernels, project(): pl.pallas_call(project_kernel, grid_spec=pltpu.PrefetchScalarGridSpec(num...  20.5 us
    ppermute x3, starting transfers between devices, core_swap(): return lax.ppermute(block, 'mp', swap_route(lax.axis_size('mp'), 1))  14.6 us
    ppermute x1, waiting for transfers between devices, local(): tails_all = lax.ppermute(scaled[-TAIL:], *next_on)[None]  12.2 us
    pallas_call x6, Pallas kernels, add_outputs(): pl.pallas_call(functools.partial(output_kernel, [[0] * len(chip) for chip...  11.3 us
    pallas_call x2, Pallas kernels, local_filter(): pl.pallas_call(functools.partial(local_kernel, tokens // SEGMENTS, modes)...  10.2 us
  transfers between devices with their start and end apart: 52, of which 23 were waited for; matrix products, arithmetic and copies ran while one was open for 17% of the time, Pallas kernels for 16%

profile of v3, /device:TPU:1, one launch (start us, length us, event | category | flops | bytes accessed | tf_op | source)
XLA Modules:
  0.0 259.0 jit_solution(13490213649156722854)
XLA Ops:
  7.2 2.5 fusion.1
  9.7 3.3 %fusion.11 = (bf16[1024,3,256]{2,0,1:T(8,128)(2,1)}, bf16[1024,3,256]{2,0,1:T(8,128)(2,1)S(1)}) fusion(bf16[1024,3,512]{2,0,1:T(8,128)(2,1)} %param.12), kind=kLoop, calls=%fused_computation.80 | loop fusion | bytes 6291456 | tf_op jit(solution)/shard_map/slice | solution.py:359
  14.7 2.1 collective-permute-start.5
  16.8 1.2 collective-permute-start.6
  18.1 1.2 collective-permute-start.7
  23.4 3.4 %collective-permute-start.10 = (f32[1,1024]{1,0:T(1,128)S(1)}, f32[1,1024]{1,0:T(1,128)S(1)}, u32[]{:S(2)}, u32[]{:S(2)}) collective-permute-start(f32[1,1024]{1,0:T(1,128)S(1)} %add.105), channel_id=1, source_target_pairs={{0,6},{1,7},{2,4},{3,5},{4,2},{5,3},{6,0},{7,1},{8,14},{9,15},{10,... | collective-permute-start | bytes 12296 | tf_op jit(solution)/shard_map/ppermute | solution.py:377
  27.1 2.2 dynamic-slice_bitcast_fusion.4
  30.0 2.6 copy.39
  32.6 2.1 collective-permute-start
  35.0 3.1 %collective-permute-start.13 = (f32[16,1]{1,0:T(8,128)S(1)}, f32[16,1]{1,0:T(8,128)S(1)}, u32[]{:S(2)}, u32[]{:S(2)}) collective-permute-start(f32[16,1]{1,0:T(8,128)S(1)} %copy.24), channel_id=1, source_target_pairs={{0,8},{8,16},{16,24},{1,9},{9,17},{17,25},{2,10},{10,18},{18,26},{... | collective-permute-start | bytes 200 | tf_op jit(solution)/shard_map/ppermute | solution.py:379
  38.0 12.2 %collective-permute-done = bf16[16,512]{1,0:T(8,128)(2,1)S(1)} collective-permute-done((bf16[16,512]{1,0:T(8,128)(2,1)S(1)}, bf16[16,512]{1,0:T(8,128)(2,1)S(1)}, u32[]{:S(2)}, u32[]{:S(2)}) %collective-permute-start) | collective-permute-done | bytes 16416 | tf_op jit(solution)/shard_map/ppermute | solution.py:361
  50.2 1.6 collective-permute-start.1
  51.9 1.8 slice.121
  53.6 2.3 collective-permute-start.11
  56.0 1.3 collective-permute-start.12
  57.3 1.4 collective-permute-start.2
  58.6 2.3 collective-permute-start.3
  61.2 2.4 collective-permute-start.16
  63.9 1.8 collective-permute-start.15
  67.3 11.9 %collective-permute-done.16 = bf16[128,1024]{1,0:T(8,128)(2,1)S(1)} collective-permute-done((bf16[128,1024]{1,0:T(8,128)(2,1)}, bf16[128,1024]{1,0:T(8,128)(2,1)S(1)}, u32[]{:S(2)}, u32[]{:S(2)}) %collective-permute-start.16) | collective-permute-done | bytes 262176 | tf_op jit(solution)/shard_map/ppermute | solution.py:27
  79.2 7.0 %collective-permute-done.15 = bf16[128,1024]{1,0:T(8,128)(2,1)S(1)} collective-permute-done((bf16[128,1024]{1,0:T(8,128)(2,1)}, bf16[128,1024]{1,0:T(8,128)(2,1)S(1)}, u32[]{:S(2)}, u32[]{:S(2)}) %collective-permute-start.15) | collective-permute-done | bytes 262176 | tf_op jit(solution)/shard_map/ppermute | solution.py:27
  88.2 2.6 %copy.28 = bf16[1024,768]{1,0:T(8,128)(2,1)} copy(bf16[1024,768]{0,1:T(8,128)(2,1)} %bitcast.162) | data formatting | bytes 3145728 | tf_op jit(solution)/shard_map/optimization_barrier | solution.py:25
  90.9 1.2 collective-permute-start.24
  93.3 1.4 fusion.17
  98.6 1.4 pad_maximum_fusion
  101.0 1.3 collective-permute-start.17
  102.3 2.3 collective-permute-start.21
  104.6 1.4 copy-done.2
  107.1 10.0 %project.2 = (f32[1024,768]{1,0:T(8,128)S(1)}, f32[16,768]{1,0:T(8,128)S(1)}) custom-call(s32[16]{0:T(128)S(1)} %concatenate.35.order_ref, bf16[8,1024,512]{2,1,0:T(8,128)(2,1)} %bitcast.160, bf16[8,16,512]{2,1,0:T(8,128)(2,1)S(1)} %constant_dynamic-update-slice_fusion.tails_ref, bf16[1024,768]{1,0:T(8,128)(2,1)S(1)} %copy.25.refs_0_, ...), custom_call_target="tpu_custom_call" | custom-call | tf_op jit(solution)/shard_map/project/pallas_call | solution.py:220
  117.8 8.2 %collective-permute-done.23.refs_1_ = bf16[1024,768]{1,0:T(8,128)(2,1)} collective-permute-done((bf16[1024,768]{1,0:T(8,128)(2,1)}, bf16[1024,768]{1,0:T(8,128)(2,1)}, u32[]{:S(2)}, u32[]{:S(2)}) %collective-permute-start.23) | collective-permute-done | bytes 1572896 | tf_op jit(solution)/shard_map/ppermute | solution.py:27
  126.0 1.9 fusion.13
  129.1 1.9 fusion.12
  131.0 1.2 collective-permute-start.26
  132.2 5.1 %local_filter.2 = (f32[1024,256]{1,0:T(8,128)S(1)}, f32[128,256]{1,0:T(8,128)S(1)}, f32[16,256]{1,0:T(8,128)S(1)}) custom-call(f32[1024,768]{1,0:T(8,128)S(1)} %get-tuple-element.45.k_ref.v_ref.q_ref, f32[1024,768]{1,0:T(8,128)S(1)} %get-tuple-element.45.k_ref.v_ref.q_ref, f32[2,768]{1,0:T(2,128)S(1)} %slice_select_fusion.1.tail_k_ref.tail_v_ref.tail_q_ref, ...), custom_call_target="tpu_custom_call" | custom-call | bytes 3145728 | tf_op jit(solution)/shard_map/local_filter/pallas_call | solution.py:127
  138.0 2.1 collective-permute-start.20
  142.8 1.4 gated_signal.4.refs_0_
  144.2 1.3 collective-permute-start.29
  145.6 1.4 gated_signal.5.refs_1_
  147.0 1.4 collective-permute-start.30
  148.4 1.2 collective-permute-start.28
  149.6 1.7 copy.30.refs_0_
  153.2 1.3 pad_maximum_fusion.4
  154.5 1.4 collective-permute-start.34
  158.3 10.5 %project.3 = (f32[1024,768]{1,0:T(8,128)S(1)}, f32[16,768]{1,0:T(8,128)S(1)}) custom-call(s32[16]{0:T(128)S(1)} %concatenate.35.order_ref, bf16[8,1024,512]{2,1,0:T(8,128)(2,1)} %bitcast.161, bf16[8,16,512]{2,1,0:T(8,128)(2,1)S(1)} %copy-done.11, bf16[1024,768]{1,0:T(8,128)(2,1)S(1)} %copy.30.refs_0_, bf16[1024,768]{1,0:T(8,128)(2,1)} %collective-permute-done.23.refs_1_, ...), custom_call_target="tpu_custom_call" | custom-call | tf_op jit(solution)/shard_map/project/pallas_call | solution.py:220
  168.8 5.1 %local_filter.3 = (f32[1024,256]{1,0:T(8,128)S(1)}, f32[128,256]{1,0:T(8,128)S(1)}, f32[16,256]{1,0:T(8,128)S(1)}) custom-call(f32[1024,768]{1,0:T(8,128)S(1)} %get-tuple-element.70.k_ref.v_ref.q_ref, f32[1024,768]{1,0:T(8,128)S(1)} %get-tuple-element.70.k_ref.v_ref.q_ref, f32[2,768]{1,0:T(2,128)S(1)} %slice_select_fusion.tail_k_ref.tail_v_ref.tail_q_ref, ...), custom_call_target="tpu_custom_call" | custom-call | bytes 3145728 | tf_op jit(solution)/shard_map/local_filter/pallas_call | solution.py:127
  175.0 1.7 collective-permute-start.33
  179.3 5.8 %collective-permute-done.42 = bf16[2,128,1024]{2,1,0:T(8,128)(2,1)} collective-permute-done((bf16[2,128,1024]{2,1,0:T(8,128)(2,1)S(1)}, bf16[2,128,1024]{2,1,0:T(8,128)(2,1)}, u32[]{:S(2)}, u32[]{:S(2)}) %collective-permute-start.42) | collective-permute-done | bytes 524320 | tf_op jit(solution)/shard_map/ppermute | solution.py:27
  185.8 1.4 gated_signal.6.refs_0_
  187.3 1.4 gated_signal.7.refs_1_
  189.5 1.3 collective-permute-start.39
  192.9 2.8 %collective-permute-done.36.refs_2_ = bf16[1024,128]{1,0:T(8,128)(2,1)S(1)} collective-permute-done((bf16[1024,128]{1,0:T(8,128)(2,1)S(1)}, bf16[1024,128]{1,0:T(8,128)(2,1)S(1)}, u32[]{:S(2)}, u32[]{:S(2)}) %collective-permute-start.36) | collective-permute-done | bytes 262176 | tf_op jit(solution)/shard_map/ppermute | solution.py:451
  196.0 2.5 collective-permute-done.39.refs_3_
  200.3 1.5 collective-permute-start.48
  203.0 4.4 %collective-permute-done.46 = bf16[2,128,1024]{2,1,0:T(8,128)(2,1)S(1)} collective-permute-done((bf16[2,128,1024]{2,1,0:T(8,128)(2,1)}, bf16[2,128,1024]{2,1,0:T(8,128)(2,1)S(1)}, u32[]{:S(2)}, u32[]{:S(2)}) %collective-permute-start.46) | collective-permute-done | bytes 524320 | tf_op jit(solution)/shard_map/ppermute | solution.py:27
  208.4 5.6 %collective-permute-done.40.refs_5_ = bf16[1024,128]{1,0:T(8,128)(2,1)S(1)} collective-permute-done((bf16[1024,128]{1,0:T(8,128)(2,1)S(1)}, bf16[1024,128]{1,0:T(8,128)(2,1)S(1)}, u32[]{:S(2)}, u32[]{:S(2)}) %collective-permute-start.40) | collective-permute-done | bytes 262176 | tf_op jit(solution)/shard_map/ppermute | solution.py:451
  216.8 2.8 %collective-permute-done.49.refs_7_ = bf16[1024,128]{1,0:T(8,128)(2,1)S(1)} collective-permute-done((bf16[1024,128]{1,0:T(8,128)(2,1)S(1)}, bf16[1024,128]{1,0:T(8,128)(2,1)S(1)}, u32[]{:S(2)}, u32[]{:S(2)}) %collective-permute-start.49) | collective-permute-done | bytes 262176 | tf_op jit(solution)/shard_map/ppermute | solution.py:451
  219.6 2.4 add_outputs.6.refs_7_
  222.1 2.2 add_outputs.7.refs_3_
  224.2 1.2 collective-permute-done.38.refs_0_
  225.5 5.6 %collective-permute-done.41.refs_1_ = bf16[1024,128]{1,0:T(8,128)(2,1)S(1)} collective-permute-done((bf16[1024,128]{1,0:T(8,128)(2,1)S(1)}, bf16[1024,128]{1,0:T(8,128)(2,1)S(1)}, u32[]{:S(2)}, u32[]{:S(2)}) %collective-permute-start.41) | collective-permute-done | bytes 262176 | tf_op jit(solution)/shard_map/ppermute | solution.py:451
  231.1 2.4 add_outputs.9.refs_7_
  233.5 2.2 add_outputs.10.refs_3_
  236.8 11.7 %collective-permute-start.50 = (bf16[1024,512]{1,0:T(8,128)(2,1)S(1)}, bf16[1024,512]{1,0:T(8,128)(2,1)S(1)}, u32[]{:S(2)}, u32[]{:S(2)}) collective-permute-start(bf16[1024,512]{1,0:T(8,128)(2,1)S(1)} %add_outputs.11), channel_id=1, source_target_pairs={{0,1},{1,0},{2,3},{3,2},{4,5},{5,4},{6,7},{7,6},{8,9},{9,8},{10,11... | collective-permute-start | bytes 3145736 | tf_op jit(solution)/shard_map/ppermute | solution.py:286
  250.8 1.3 add_convert_fusion
  (232 shorter events, 45.2 us)
Async XLA Ops:
  7.2 93.8 %all-gather.3.cloned.1.call-start = ((), (), s32[]{:S(2)}) async-start(), calls=%async_computation | async-start | bytes 9437184 | tf_op jit(solution)/shard_map/all_gather | solution.py:358
  14.7 37.2 %collective-permute-start.5 = (bf16[1024,768]{1,0:T(8,128)(2,1)S(1)}, bf16[1024,768]{1,0:T(8,128)(2,1)S(1)}, u32[]{:S(2)}, u32[]{:S(2)}) collective-permute-start(bf16[1024,768]{1,0:T(8,128)(2,1)S(1)} %copy.25.refs_0_), channel_id=1, source_target_pairs={{0,8},{8,0},{16,24},{24,16},{1,9},{9,1},{17,25},{25,17},{2,10},{10... | collective-permute-start | bytes 4718600 | tf_op jit(solution)/shard_map/ppermute | solution.py:27
  16.8 35.1 %collective-permute-start.6 = (bf16[1024,768]{1,0:T(8,128)(2,1)S(1)}, bf16[1024,768]{1,0:T(8,128)(2,1)}, u32[]{:S(2)}, u32[]{:S(2)}) collective-permute-start(bf16[1024,768]{1,0:T(8,128)(2,1)S(1)} %copy.25.refs_0_), channel_id=1, source_target_pairs={{0,16},{8,24},{16,0},{24,8},{1,17},{9,25},{17,1},{25,9},{2,18},{10... | collective-permute-start | bytes 4718600 | tf_op jit(solution)/shard_map/ppermute | solution.py:27
  18.1 5.3 %collective-permute-start.7 = (f32[1,1024]{1,0:T(1,128)S(1)}, f32[1,1024]{1,0:T(1,128)S(1)}, u32[]{:S(2)}, u32[]{:S(2)}) collective-permute-start(f32[1,1024]{1,0:T(1,128)S(1)} %bitcast.187), channel_id=1, source_target_pairs={{0,1},{1,0},{2,3},{3,2},{4,5},{5,4},{6,7},{7,6},{8,9},{9,8},{10,11... | collective-permute-start | bytes 12296 | tf_op jit(solution)/shard_map/ppermute | solution.py:286
  23.4 9.2 %collective-permute-start.10 = (f32[1,1024]{1,0:T(1,128)S(1)}, f32[1,1024]{1,0:T(1,128)S(1)}, u32[]{:S(2)}, u32[]{:S(2)}) collective-permute-start(f32[1,1024]{1,0:T(1,128)S(1)} %add.105), channel_id=1, source_target_pairs={{0,6},{1,7},{2,4},{3,5},{4,2},{5,3},{6,0},{7,1},{8,14},{9,15},{10,... | collective-permute-start | bytes 12296 | tf_op jit(solution)/shard_map/ppermute | solution.py:377
  26.8 8.0 %collective-permute-start.8 = (f32[1,1024]{1,0:T(1,128)S(1)}, f32[1,1024]{1,0:T(1,128)S(1)}, u32[]{:S(2)}, u32[]{:S(2)}) collective-permute-start(f32[1,1024]{1,0:T(1,128)S(1)} %add.105), channel_id=1, source_target_pairs={{0,2},{1,3},{2,0},{3,1},{4,6},{5,7},{6,4},{7,5},{8,10},{9,11},{10,... | collective-permute-start | bytes 12296 | tf_op jit(solution)/shard_map/ppermute | solution.py:377
  26.8 8.0 %collective-permute-start.9 = (f32[1,1024]{1,0:T(1,128)S(1)}, f32[1,1024]{1,0:T(1,128)S(1)}, u32[]{:S(2)}, u32[]{:S(2)}) collective-permute-start(f32[1,1024]{1,0:T(1,128)S(1)} %add.105), channel_id=1, source_target_pairs={{0,4},{1,5},{2,6},{3,7},{4,0},{5,1},{6,2},{7,3},{8,12},{9,13},{10,... | collective-permute-start | bytes 12296 | tf_op jit(solution)/shard_map/ppermute | solution.py:377
  32.6 17.6 %collective-permute-start = (bf16[16,512]{1,0:T(8,128)(2,1)S(1)}, bf16[16,512]{1,0:T(8,128)(2,1)S(1)}, u32[]{:S(2)}, u32[]{:S(2)}) collective-permute-start(bf16[16,512]{1,0:T(8,128)(2,1)S(1)} %slice.156), channel_id=1, source_target_pairs={{0,8},{8,16},{16,24},{1,9},{9,17},{17,25},{2,10},{10,18},{18,26},{... | collective-permute-start | bytes 49160 | tf_op jit(solution)/shard_map/ppermute | solution.py:361
  34.8 21.2 %copy-start.46 = (f32[1,1024]{1,0:T(1,128)}, f32[1,1024]{1,0:T(1,128)S(1)}, u32[]{:S(2)}) copy-start(f32[1,1024]{1,0:T(1,128)S(1)} %add_rsqrt_fusion) | copy-start | bytes 12292
  35.0 26.0 %collective-permute-start.13 = (f32[16,1]{1,0:T(8,128)S(1)}, f32[16,1]{1,0:T(8,128)S(1)}, u32[]{:S(2)}, u32[]{:S(2)}) collective-permute-start(f32[16,1]{1,0:T(8,128)S(1)} %copy.24), channel_id=1, source_target_pairs={{0,8},{8,16},{16,24},{1,9},{9,17},{17,25},{2,10},{10,18},{18,26},{... | collective-permute-start | bytes 200 | tf_op jit(solution)/shard_map/ppermute | solution.py:379
  50.2 7.0 %collective-permute-start.1 = (bf16[1,16,512]{2,1,0:T(8,128)(2,1)S(1)}, bf16[1,16,512]{2,1,0:T(8,128)(2,1)S(1)}, u32[]{:S(2)}, u32[]{:S(2)}) collective-permute-start(bf16[1,16,512]{2,1,0:T(8,128)(2,1)S(1)} %bitcast.180), channel_id=1, source_target_pairs={{0,1},{1,0},{2,3},{3,2},{4,5},{5,4},{6,7},{7,6},{8,9},{9,8},{10,11... | collective-permute-start | bytes 49160 | tf_op jit(solution)/shard_map/ppermute | solution.py:286
  51.9 38.9 %copy-start.1 = (bf16[1024,768]{1,0:T(8,128)(2,1)}, bf16[1024,768]{1,0:T(8,128)(2,1)S(1)}, u32[]{:S(2)}) copy-start(bf16[1024,768]{1,0:T(8,128)(2,1)S(1)} %collective-permute-done.5.refs_1_) | copy-start | bytes 4718596
  53.6 32.6 %collective-permute-start.11 = (bf16[512,768]{1,0:T(8,128)(2,1)S(1)}, bf16[512,768]{1,0:T(8,128)(2,1)S(1)}, u32[]{:S(2)}, u32[]{:S(2)}) collective-permute-start(bf16[512,768]{1,0:T(8,128)(2,1)S(1)} %slice.121), channel_id=1, source_target_pairs={{0,8},{8,0},{16,24},{24,16},{1,9},{9,1},{17,25},{25,17},{2,10},{10... | collective-permute-start | bytes 2359304 | tf_op jit(solution)/shard_map/ppermute | solution.py:27
  56.0 31.2 %collective-permute-start.12 = (bf16[512,768]{1,0:T(8,128)(2,1)S(1)}, bf16[512,768]{1,0:T(8,128)(2,1)S(1)}, u32[]{:S(2)}, u32[]{:S(2)}) collective-permute-start(bf16[512,768]{1,0:T(8,128)(2,1)S(1)} %slice.122), channel_id=1, source_target_pairs={{0,16},{8,24},{16,0},{24,8},{1,17},{9,25},{17,1},{25,9},{2,18},{10... | collective-permute-start | bytes 2359304 | tf_op jit(solution)/shard_map/ppermute | solution.py:27
  57.3 3.9 %collective-permute-start.2 = (bf16[2,16,512]{2,1,0:T(8,128)(2,1)S(1)}, bf16[2,16,512]{2,1,0:T(8,128)(2,1)S(1)}, u32[]{:S(2)}, u32[]{:S(2)}) collective-permute-start(bf16[2,16,512]{2,1,0:T(8,128)(2,1)S(1)} %pad_maximum_fusion.7), channel_id=1, source_target_pairs={{0,2},{1,3},{2,0},{3,1},{4,6},{5,7},{6,4},{7,5},{8,10},{9,11},{10,... | collective-permute-start | bytes 98312 | tf_op jit(solution)/shard_map/ppermute | solution.py:387
  58.6 5.2 %collective-permute-start.3 = (bf16[2,16,512]{2,1,0:T(8,128)(2,1)S(1)}, bf16[2,16,512]{2,1,0:T(8,128)(2,1)S(1)}, u32[]{:S(2)}, u32[]{:S(2)}) collective-permute-start(bf16[2,16,512]{2,1,0:T(8,128)(2,1)S(1)} %pad_maximum_fusion.7), channel_id=1, source_target_pairs={{0,4},{1,5},{2,6},{3,7},{4,0},{5,1},{6,2},{7,3},{8,12},{9,13},{10,... | collective-permute-start | bytes 98312 | tf_op jit(solution)/shard_map/ppermute | solution.py:387
  61.0 43.6 %copy-start.15 = (f32[16,1]{1,0:T(8,128)}, f32[16,1]{1,0:T(8,128)S(1)}, u32[]{:S(2)}) copy-start(f32[16,1]{1,0:T(8,128)S(1)} %collective-permute-done.13.refs_6_) | copy-start | bytes 196
  61.0 5.3 %collective-permute-start.4 = (bf16[2,16,512]{2,1,0:T(8,128)(2,1)S(1)}, bf16[2,16,512]{2,1,0:T(8,128)(2,1)S(1)}, u32[]{:S(2)}, u32[]{:S(2)}) collective-permute-start(bf16[2,16,512]{2,1,0:T(8,128)(2,1)S(1)} %pad_maximum_fusion.7), channel_id=1, source_target_pairs={{0,6},{1,7},{2,4},{3,5},{4,2},{5,3},{6,0},{7,1},{8,14},{9,15},{10,... | collective-permute-start | bytes 98312 | tf_op jit(solution)/shard_map/ppermute | solution.py:387
  61.2 18.0 %collective-permute-start.16 = (bf16[128,1024]{1,0:T(8,128)(2,1)}, bf16[128,1024]{1,0:T(8,128)(2,1)S(1)}, u32[]{:S(2)}, u32[]{:S(2)}) collective-permute-start(bf16[128,1024]{1,0:T(8,128)(2,1)} %get-tuple-element.56), channel_id=1, source_target_pairs={{0,24},{8,16},{16,8},{24,0},{1,25},{9,17},{17,9},{25,1},{2,26},{10... | collective-permute-start | bytes 786440 | tf_op jit(solution)/shard_map/ppermute | solution.py:27
  63.9 22.3 %collective-permute-start.15 = (bf16[128,1024]{1,0:T(8,128)(2,1)}, bf16[128,1024]{1,0:T(8,128)(2,1)S(1)}, u32[]{:S(2)}, u32[]{:S(2)}) collective-permute-start(bf16[128,1024]{1,0:T(8,128)(2,1)} %get-tuple-element.55), channel_id=1, source_target_pairs={{0,16},{8,24},{16,0},{24,8},{1,17},{9,25},{17,1},{25,9},{2,18},{10... | collective-permute-start | bytes 786440 | tf_op jit(solution)/shard_map/ppermute | solution.py:27
  66.2 20.0 %collective-permute-start.14 = (bf16[128,1024]{1,0:T(8,128)(2,1)}, bf16[128,1024]{1,0:T(8,128)(2,1)S(1)}, u32[]{:S(2)}, u32[]{:S(2)}) collective-permute-start(bf16[128,1024]{1,0:T(8,128)(2,1)} %get-tuple-element.54), channel_id=1, source_target_pairs={{0,8},{8,0},{16,24},{24,16},{1,9},{9,1},{17,25},{25,17},{2,10},{10... | collective-permute-start | bytes 786440 | tf_op jit(solution)/shard_map/ppermute | solution.py:27
  90.8 35.2 %collective-permute-start.23 = (bf16[1024,768]{1,0:T(8,128)(2,1)}, bf16[1024,768]{1,0:T(8,128)(2,1)}, u32[]{:S(2)}, u32[]{:S(2)}) collective-permute-start(bf16[1024,768]{1,0:T(8,128)(2,1)} %copy.28), channel_id=1, source_target_pairs={{0,8},{8,0},{16,24},{24,16},{1,9},{9,1},{17,25},{25,17},{2,10},{10... | collective-permute-start | bytes 4718600 | tf_op jit(solution)/shard_map/ppermute | solution.py:27
  90.9 35.1 %collective-permute-start.24 = (bf16[1024,768]{1,0:T(8,128)(2,1)}, bf16[1024,768]{1,0:T(8,128)(2,1)}, u32[]{:S(2)}, u32[]{:S(2)}) collective-permute-start(bf16[1024,768]{1,0:T(8,128)(2,1)} %copy.28), channel_id=1, source_target_pairs={{0,16},{8,24},{16,0},{24,8},{1,17},{9,25},{17,1},{25,9},{2,18},{10... | collective-permute-start | bytes 4718600 | tf_op jit(solution)/shard_map/ppermute | solution.py:27
  101.0 36.4 %collective-permute-start.17 = (bf16[128,1024]{1,0:T(8,128)(2,1)}, bf16[128,1024]{1,0:T(8,128)(2,1)S(1)}, u32[]{:S(2)}, u32[]{:S(2)}) collective-permute-start(bf16[128,1024]{1,0:T(8,128)(2,1)} %get-tuple-element.57), channel_id=1, source_target_pairs={{0,2},{1,3},{2,0},{3,1},{4,6},{5,7},{6,4},{7,5},{8,10},{9,11},{10,... | collective-permute-start | bytes 786440 | tf_op jit(solution)/shard_map/ppermute | solution.py:394
  102.3 35.5 %collective-permute-start.21 = (bf16[128,1024]{1,0:T(8,128)(2,1)}, bf16[128,1024]{1,0:T(8,128)(2,1)S(1)}, u32[]{:S(2)}, u32[]{:S(2)}) collective-permute-start(bf16[128,1024]{1,0:T(8,128)(2,1)} %get-tuple-element.59), channel_id=1, source_target_pairs={{0,4},{1,5},{2,6},{3,7},{4,0},{5,1},{6,2},{7,3},{8,12},{9,13},{10,... | collective-permute-start | bytes 786440 | tf_op jit(solution)/shard_map/ppermute | solution.py:394
  104.6 33.4 %collective-permute-start.22 = (bf16[128,1024]{1,0:T(8,128)(2,1)}, bf16[128,1024]{1,0:T(8,128)(2,1)S(1)}, u32[]{:S(2)}, u32[]{:S(2)}) collective-permute-start(bf16[128,1024]{1,0:T(8,128)(2,1)} %get-tuple-element.60), channel_id=1, source_target_pairs={{0,6},{1,7},{2,4},{3,5},{4,2},{5,3},{6,0},{7,1},{8,14},{9,15},{10,... | collective-permute-start | bytes 786440 | tf_op jit(solution)/shard_map/ppermute | solution.py:394
  117.8 14.4 %copy-start.45 = (f32[2,3,256]{2,0,1:T(2,128)S(1)}, f32[2,3,256]{2,0,1:T(2,128)}, u32[]{:S(2)}) copy-start(f32[2,3,256]{2,0,1:T(2,128)} %get-tuple-element.128) | copy-start | bytes 18436
  127.9 13.7 %collective-permute-start.25 = (bf16[256,768]{1,0:T(8,128)(2,1)S(1)}, bf16[256,768]{1,0:T(8,128)(2,1)S(1)}, u32[]{:S(2)}, u32[]{:S(2)}) collective-permute-start(bf16[256,768]{1,0:T(8,128)(2,1)S(1)} %get-tuple-element.91), channel_id=1, source_target_pairs={{0,8},{8,0},{16,24},{24,16},{1,9},{9,1},{17,25},{25,17},{2,10},{10... | collective-permute-start | bytes 1179656 | tf_op jit(solution)/shard_map/ppermute | solution.py:27
  131.0 10.6 %collective-permute-start.26 = (bf16[256,768]{1,0:T(8,128)(2,1)S(1)}, bf16[256,768]{1,0:T(8,128)(2,1)S(1)}, u32[]{:S(2)}, u32[]{:S(2)}) collective-permute-start(bf16[256,768]{1,0:T(8,128)(2,1)S(1)} %get-tuple-element.89), channel_id=1, source_target_pairs={{0,16},{8,24},{16,0},{24,8},{1,17},{9,25},{17,1},{25,9},{2,18},{10... | collective-permute-start | bytes 1179656 | tf_op jit(solution)/shard_map/ppermute | solution.py:27
  137.4 2.9 %collective-permute-start.18 = (f32[16,256]{1,0:T(8,128)S(1)}, f32[16,256]{1,0:T(8,128)S(1)}, u32[]{:S(2)}, u32[]{:S(2)}) collective-permute-start(f32[16,256]{1,0:T(8,128)S(1)} %get-tuple-element.58), channel_id=1, source_target_pairs={{0,8},{8,0},{16,24},{24,16},{1,9},{9,1},{17,25},{25,17},{2,10},{10... | collective-permute-start | bytes 49160 | tf_op jit(solution)/shard_map/ppermute | solution.py:429
  137.7 3.1 %collective-permute-start.19 = (f32[16,256]{1,0:T(8,128)S(1)}, f32[16,256]{1,0:T(8,128)S(1)}, u32[]{:S(2)}, u32[]{:S(2)}) collective-permute-start(f32[16,256]{1,0:T(8,128)S(1)} %get-tuple-element.58), channel_id=1, source_target_pairs={{0,16},{8,24},{16,0},{24,8},{1,17},{9,25},{17,1},{25,9},{2,18},{10... | collective-permute-start | bytes 49160 | tf_op jit(solution)/shard_map/ppermute | solution.py:429
  138.0 3.6 %collective-permute-start.20 = (f32[16,256]{1,0:T(8,128)S(1)}, f32[16,256]{1,0:T(8,128)S(1)}, u32[]{:S(2)}, u32[]{:S(2)}) collective-permute-start(f32[16,256]{1,0:T(8,128)S(1)} %get-tuple-element.58), channel_id=1, source_target_pairs={{0,24},{8,16},{16,8},{24,0},{1,25},{9,17},{17,9},{25,1},{2,26},{10... | collective-permute-start | bytes 49160 | tf_op jit(solution)/shard_map/ppermute | solution.py:429
  141.6 14.5 %collective-permute-start.27 = (bf16[256,768]{1,0:T(8,128)(2,1)}, bf16[256,768]{1,0:T(8,128)(2,1)}, u32[]{:S(2)}, u32[]{:S(2)}) collective-permute-start(bf16[256,768]{1,0:T(8,128)(2,1)} %get-tuple-element.68), channel_id=1, source_target_pairs={{0,8},{8,0},{16,24},{24,16},{1,9},{9,1},{17,25},{25,17},{2,10},{10... | collective-permute-start | bytes 1179656 | tf_op jit(solution)/shard_map/ppermute | solution.py:27
  144.2 10.3 %collective-permute-start.29 = (bf16[1024,128]{1,0:T(8,128)(2,1)S(1)}, bf16[1024,128]{1,0:T(8,128)(2,1)S(1)}, u32[]{:S(2)}, u32[]{:S(2)}) collective-permute-start(bf16[1024,128]{1,0:T(8,128)(2,1)S(1)} %gated_signal.4.refs_0_), channel_id=1, source_target_pairs={{0,2},{1,3},{2,4},{3,5},{4,6},{5,7},{6,0},{7,1},{8,10},{9,11},{10,... | collective-permute-start | bytes 786440 | tf_op jit(solution)/shard_map/ppermute | solution.py:451
  147.0 8.9 %collective-permute-start.30 = (bf16[1024,128]{1,0:T(8,128)(2,1)S(1)}, bf16[1024,128]{1,0:T(8,128)(2,1)S(1)}, u32[]{:S(2)}, u32[]{:S(2)}) collective-permute-start(bf16[1024,128]{1,0:T(8,128)(2,1)S(1)} %gated_signal.5.refs_1_), channel_id=1, source_target_pairs={{0,2},{1,3},{2,4},{3,5},{4,6},{5,7},{6,0},{7,1},{8,10},{9,11},{10,... | collective-permute-start | bytes 786440 | tf_op jit(solution)/shard_map/ppermute | solution.py:451
  148.4 8.8 %collective-permute-start.28 = (bf16[256,768]{1,0:T(8,128)(2,1)}, bf16[256,768]{1,0:T(8,128)(2,1)}, u32[]{:S(2)}, u32[]{:S(2)}) collective-permute-start(bf16[256,768]{1,0:T(8,128)(2,1)} %get-tuple-element.69), channel_id=1, source_target_pairs={{0,16},{8,24},{16,0},{24,8},{1,17},{9,25},{17,1},{25,9},{2,18},{10... | collective-permute-start | bytes 1179656 | tf_op jit(solution)/shard_map/ppermute | solution.py:27
  153.1 23.6 %copy-start.28 = (bf16[2,128,1024]{2,1,0:T(8,128)(2,1)}, bf16[2,128,1024]{2,1,0:T(8,128)(2,1)S(1)}, u32[]{:S(2)}) copy-start(bf16[2,128,1024]{2,1,0:T(8,128)(2,1)S(1)} %pad_maximum_fusion.3) | copy-start | bytes 1572868
  154.5 24.1 %copy-start.26 = (bf16[2,128,1024]{2,1,0:T(8,128)(2,1)}, bf16[2,128,1024]{2,1,0:T(8,128)(2,1)S(1)}, u32[]{:S(2)}) copy-start(bf16[2,128,1024]{2,1,0:T(8,128)(2,1)S(1)} %pad_maximum_fusion.4) | copy-start | bytes 1572868
  154.5 24.0 %collective-permute-start.34 = (bf16[1024,128]{1,0:T(8,128)(2,1)S(1)}, bf16[1024,128]{1,0:T(8,128)(2,1)S(1)}, u32[]{:S(2)}, u32[]{:S(2)}) collective-permute-start(bf16[1024,128]{1,0:T(8,128)(2,1)S(1)} %collective-permute-done.29.refs_2_), channel_id=1, source_target_pairs={{0,2},{1,3},{2,4},{3,5},{4,6},{5,7},{6,0},{7,1},{8,10},{9,11},{10,... | collective-permute-start | bytes 786440 | tf_op jit(solution)/shard_map/ppermute | solution.py:451
  155.8 22.7 %collective-permute-start.35 = (bf16[1024,128]{1,0:T(8,128)(2,1)S(1)}, bf16[1024,128]{1,0:T(8,128)(2,1)S(1)}, u32[]{:S(2)}, u32[]{:S(2)}) collective-permute-start(bf16[1024,128]{1,0:T(8,128)(2,1)S(1)} %collective-permute-done.30.refs_3_), channel_id=1, source_target_pairs={{0,2},{1,3},{2,4},{3,5},{4,6},{5,7},{6,0},{7,1},{8,10},{9,11},{10,... | collective-permute-start | bytes 786440 | tf_op jit(solution)/shard_map/ppermute | solution.py:451
  168.8 17.0 %copy-start.42 = (f32[512,16]{0,1:T(8,128)S(1)}, f32[512,16]{0,1:T(8,128)}, u32[]{:S(2)}) copy-start(f32[512,16]{0,1:T(8,128)} %param.18) | copy-start | bytes 98308
  168.8 17.0 %copy-start.9 = (f32[80,256]{1,0:T(8,128)S(1)}, f32[80,256]{1,0:T(8,128)}, u32[]{:S(2)}) copy-start(f32[80,256]{1,0:T(8,128)} %get-tuple-element.104.shares_ref) | copy-start | bytes 245764
  174.0 2.7 %collective-permute-start.31 = (f32[16,256]{1,0:T(8,128)S(1)}, f32[16,256]{1,0:T(8,128)S(1)}, u32[]{:S(2)}, u32[]{:S(2)}) collective-permute-start(f32[16,256]{1,0:T(8,128)S(1)} %get-tuple-element.75), channel_id=1, source_target_pairs={{0,8},{8,0},{16,24},{24,16},{1,9},{9,1},{17,25},{25,17},{2,10},{10... | collective-permute-start | bytes 49160 | tf_op jit(solution)/shard_map/ppermute | solution.py:429
  174.8 2.6 collective-permute-start.32
  175.0 3.5 %collective-permute-start.33 = (f32[16,256]{1,0:T(8,128)S(1)}, f32[16,256]{1,0:T(8,128)S(1)}, u32[]{:S(2)}, u32[]{:S(2)}) collective-permute-start(f32[16,256]{1,0:T(8,128)S(1)} %get-tuple-element.75), channel_id=1, source_target_pairs={{0,24},{8,16},{16,8},{24,0},{1,25},{9,17},{17,9},{25,1},{2,26},{10... | collective-permute-start | bytes 49160 | tf_op jit(solution)/shard_map/ppermute | solution.py:429
  176.7 8.4 %collective-permute-start.42 = (bf16[2,128,1024]{2,1,0:T(8,128)(2,1)S(1)}, bf16[2,128,1024]{2,1,0:T(8,128)(2,1)}, u32[]{:S(2)}, u32[]{:S(2)}) collective-permute-start(bf16[2,128,1024]{2,1,0:T(8,128)(2,1)S(1)} %pad_maximum_fusion.3), channel_id=1, source_target_pairs={{0,16},{8,24},{16,0},{24,8},{1,17},{9,25},{17,1},{25,9},{2,18},{10... | collective-permute-start | bytes 1572872 | tf_op jit(solution)/shard_map/ppermute | solution.py:27
  178.5 12.3 %collective-permute-start.44 = (bf16[2,128,1024]{2,1,0:T(8,128)(2,1)S(1)}, bf16[2,128,1024]{2,1,0:T(8,128)(2,1)}, u32[]{:S(2)}, u32[]{:S(2)}) collective-permute-start(bf16[2,128,1024]{2,1,0:T(8,128)(2,1)S(1)} %pad_maximum_fusion.4), channel_id=1, source_target_pairs={{0,8},{8,0},{16,24},{24,16},{1,9},{9,1},{17,25},{25,17},{2,10},{10... | collective-permute-start | bytes 1572872 | tf_op jit(solution)/shard_map/ppermute | solution.py:27
  185.1 13.5 %collective-permute-start.43 = (bf16[2,128,1024]{2,1,0:T(8,128)(2,1)}, bf16[2,128,1024]{2,1,0:T(8,128)(2,1)}, u32[]{:S(2)}, u32[]{:S(2)}) collective-permute-start(bf16[2,128,1024]{2,1,0:T(8,128)(2,1)} %collective-permute-done.42), channel_id=1, source_target_pairs={{0,8},{8,0},{16,24},{24,16},{1,9},{9,1},{17,25},{25,17},{2,10},{10... | collective-permute-start | bytes 1572872 | tf_op jit(solution)/shard_map/ppermute | solution.py:27
  188.7 7.1 %collective-permute-start.36 = (bf16[1024,128]{1,0:T(8,128)(2,1)S(1)}, bf16[1024,128]{1,0:T(8,128)(2,1)S(1)}, u32[]{:S(2)}, u32[]{:S(2)}) collective-permute-start(bf16[1024,128]{1,0:T(8,128)(2,1)S(1)} %gated_signal.6.refs_0_), channel_id=1, source_target_pairs={{0,2},{1,3},{2,4},{3,5},{4,6},{5,7},{6,0},{7,1},{8,10},{9,11},{10,... | collective-permute-start | bytes 786440 | tf_op jit(solution)/shard_map/ppermute | solution.py:451
  189.5 9.0 %collective-permute-start.39 = (bf16[1024,128]{1,0:T(8,128)(2,1)S(1)}, bf16[1024,128]{1,0:T(8,128)(2,1)S(1)}, u32[]{:S(2)}, u32[]{:S(2)}) collective-permute-start(bf16[1024,128]{1,0:T(8,128)(2,1)S(1)} %gated_signal.7.refs_1_), channel_id=1, source_target_pairs={{0,2},{1,3},{2,4},{3,5},{4,6},{5,7},{6,0},{7,1},{8,10},{9,11},{10,... | collective-permute-start | bytes 786440 | tf_op jit(solution)/shard_map/ppermute | solution.py:451
  190.8 9.5 %collective-permute-start.45 = (bf16[2,128,1024]{2,1,0:T(8,128)(2,1)}, bf16[2,128,1024]{2,1,0:T(8,128)(2,1)}, u32[]{:S(2)}, u32[]{:S(2)}) collective-permute-start(bf16[2,128,1024]{2,1,0:T(8,128)(2,1)} %collective-permute-done.44), channel_id=1, source_target_pairs={{0,16},{8,24},{16,0},{24,8},{1,17},{9,25},{17,1},{25,9},{2,18},{10... | collective-permute-start | bytes 1572872 | tf_op jit(solution)/shard_map/ppermute | solution.py:27
  191.4 16.0 %collective-permute-start.46 = (bf16[2,128,1024]{2,1,0:T(8,128)(2,1)}, bf16[2,128,1024]{2,1,0:T(8,128)(2,1)S(1)}, u32[]{:S(2)}, u32[]{:S(2)}) collective-permute-start(bf16[2,128,1024]{2,1,0:T(8,128)(2,1)} %copy-done.28), channel_id=1, source_target_pairs={{0,8},{8,0},{16,24},{24,16},{1,9},{9,1},{17,25},{25,17},{2,10},{10... | collective-permute-start | bytes 1572872 | tf_op jit(solution)/shard_map/ppermute | solution.py:27
  192.8 14.6 %copy-start.4 = (bf16[1024,128]{1,0:T(8,128)(2,1)S(1)}, bf16[1024,128]{1,0:T(8,128)(2,1)}, u32[]{:S(2)}) copy-start(bf16[1024,128]{1,0:T(8,128)(2,1)} %copy-done.3) | copy-start | bytes 786436
  195.7 20.5 %collective-permute-start.47 = (bf16[2,128,1024]{2,1,0:T(8,128)(2,1)S(1)}, bf16[2,128,1024]{2,1,0:T(8,128)(2,1)S(1)}, u32[]{:S(2)}, u32[]{:S(2)}) collective-permute-start(bf16[2,128,1024]{2,1,0:T(8,128)(2,1)S(1)} %copy-done.27), channel_id=1, source_target_pairs={{0,16},{8,24},{16,0},{24,8},{1,17},{9,25},{17,1},{25,9},{2,18},{10... | collective-permute-start | bytes 1572872 | tf_op jit(solution)/shard_map/ppermute | solution.py:27
  198.6 9.9 %collective-permute-start.37 = (bf16[1024,128]{1,0:T(8,128)(2,1)S(1)}, bf16[1024,128]{1,0:T(8,128)(2,1)S(1)}, u32[]{:S(2)}, u32[]{:S(2)}) collective-permute-start(bf16[1024,128]{1,0:T(8,128)(2,1)S(1)} %collective-permute-done.36.refs_2_), channel_id=1, source_target_pairs={{0,2},{1,3},{2,4},{3,5},{4,6},{5,7},{6,0},{7,1},{8,10},{9,11},{10,... | collective-permute-start | bytes 786440 | tf_op jit(solution)/shard_map/ppermute | solution.py:451
  198.6 15.5 %collective-permute-start.40 = (bf16[1024,128]{1,0:T(8,128)(2,1)S(1)}, bf16[1024,128]{1,0:T(8,128)(2,1)S(1)}, u32[]{:S(2)}, u32[]{:S(2)}) collective-permute-start(bf16[1024,128]{1,0:T(8,128)(2,1)S(1)} %collective-permute-done.39.refs_3_), channel_id=1, source_target_pairs={{0,2},{1,3},{2,4},{3,5},{4,6},{5,7},{6,0},{7,1},{8,10},{9,11},{10,... | collective-permute-start | bytes 786440 | tf_op jit(solution)/shard_map/ppermute | solution.py:451
  200.3 16.5 %collective-permute-start.48 = (bf16[1024,128]{1,0:T(8,128)(2,1)S(1)}, bf16[1024,128]{1,0:T(8,128)(2,1)S(1)}, u32[]{:S(2)}, u32[]{:S(2)}) collective-permute-start(bf16[1024,128]{1,0:T(8,128)(2,1)S(1)} %collective-permute-done.34.refs_4_), channel_id=1, source_target_pairs={{0,2},{1,3},{2,4},{3,5},{4,6},{5,7},{6,0},{7,1},{8,10},{9,11},{10,... | collective-permute-start | bytes 786440 | tf_op jit(solution)/shard_map/ppermute | solution.py:451
  203.0 16.7 %copy-start = (bf16[1024,512]{1,0:T(8,128)(2,1)S(1)}, bf16[1024,512]{1,0:T(8,128)(2,1)}, u32[]{:S(2)}) copy-start(bf16[1024,512]{1,0:T(8,128)(2,1)} %refs_9_.1) | copy-start | bytes 3145732
  207.4 12.2 %collective-permute-start.49 = (bf16[1024,128]{1,0:T(8,128)(2,1)S(1)}, bf16[1024,128]{1,0:T(8,128)(2,1)S(1)}, u32[]{:S(2)}, u32[]{:S(2)}) collective-permute-start(bf16[1024,128]{1,0:T(8,128)(2,1)S(1)} %copy-done.4), channel_id=1, source_target_pairs={{0,2},{1,3},{2,4},{3,5},{4,6},{5,7},{6,0},{7,1},{8,10},{9,11},{10,... | collective-permute-start | bytes 786440 | tf_op jit(solution)/shard_map/ppermute | solution.py:451
  208.4 17.0 %collective-permute-start.38 = (bf16[1024,128]{1,0:T(8,128)(2,1)S(1)}, bf16[1024,128]{1,0:T(8,128)(2,1)S(1)}, u32[]{:S(2)}, u32[]{:S(2)}) collective-permute-start(bf16[1024,128]{1,0:T(8,128)(2,1)S(1)} %collective-permute-done.37.refs_4_), channel_id=1, source_target_pairs={{0,2},{1,3},{2,4},{3,5},{4,6},{5,7},{6,0},{7,1},{8,10},{9,11},{10,... | collective-permute-start | bytes 786440 | tf_op jit(solution)/shard_map/ppermute | solution.py:451
  214.1 17.0 %collective-permute-start.41 = (bf16[1024,128]{1,0:T(8,128)(2,1)S(1)}, bf16[1024,128]{1,0:T(8,128)(2,1)S(1)}, u32[]{:S(2)}, u32[]{:S(2)}) collective-permute-start(bf16[1024,128]{1,0:T(8,128)(2,1)S(1)} %collective-permute-done.40.refs_5_), channel_id=1, source_target_pairs={{0,2},{1,3},{2,4},{3,5},{4,6},{5,7},{6,0},{7,1},{8,10},{9,11},{10,... | collective-permute-start | bytes 786440 | tf_op jit(solution)/shard_map/ppermute | solution.py:451
  235.7 12.8 %copy-start.29 = (f32[4,16,512]{2,1,0:T(8,128)S(1)}, f32[4,16,512]{2,1,0:T(8,128)}, u32[]{:S(2)}) copy-start(f32[4,16,512]{2,1,0:T(8,128)} %get-tuple-element.111) | copy-start | bytes 393220
  235.7 12.8 %copy-start.40 = (f32[1,16,512]{2,1,0:T(8,128)S(1)}, f32[1,16,512]{2,1,0:T(8,128)}, u32[]{:S(2)}) copy-start(f32[1,16,512]{2,1,0:T(8,128)} %get-tuple-element.106) | copy-start | bytes 98308
  236.8 14.0 %collective-permute-start.50 = (bf16[1024,512]{1,0:T(8,128)(2,1)S(1)}, bf16[1024,512]{1,0:T(8,128)(2,1)S(1)}, u32[]{:S(2)}, u32[]{:S(2)}) collective-permute-start(bf16[1024,512]{1,0:T(8,128)(2,1)S(1)} %add_outputs.11), channel_id=1, source_target_pairs={{0,1},{1,0},{2,3},{3,2},{4,5},{5,4},{6,7},{7,6},{8,9},{9,8},{10,11... | collective-permute-start | bytes 3145736 | tf_op jit(solution)/shard_map/ppermute | solution.py:286
  (37 other events, 192.1 us)
Sparse Core Ops, SparseCore 0:
  10.2 87.6 all-gather.2

commit v4 on v3

--- a/solution.py
+++ b/solution.py
@@ -187,18 +187,18 @@
     )
 
 
-def project_kernel(order_ref, all_ref, tails_ref, *refs):
+def project_kernel(chunks, order_ref, all_ref, tails_ref, *refs):
     unit_refs, (inverse_ref, tail_inverse_ref, out_ref, tail_out_ref) = refs[:-4], refs[-4:]
-    features = all_ref.shape[2]
-    chunks = [(ref, at) for ref in unit_refs for at in range(0, ref.shape[0], features)]
+    blocks = tails_ref.shape[0]
 
     def total(first_rows):
         result = None
-        for n, (ref, at) in enumerate(chunks):
-            block = all_ref[order_ref[n]]
+        for unit, at, n, first, rows in chunks:
+            block = all_ref[order_ref[n], :, first : first + rows]
             if first_rows:
-                block = jnp.concatenate([tails_ref[order_ref[len(chunks) + n]], block], axis=0)
-            part = jnp.dot(block, ref[at : at + features, :], preferred_element_type=f32)
+                tail = tails_ref[order_ref[blocks + n], :, first : first + rows]
+                block = jnp.concatenate([tail, block], axis=0)
+            part = jnp.dot(block, unit_refs[unit][at : at + rows, :], preferred_element_type=f32)
             result = part if result is None else result + part
         return result
 
@@ -217,8 +217,15 @@
     mp, tokens, features = everything.shape
     width = units[0].shape[1]
     tile = math.gcd(tokens, 256)
+    chunks, row = [], 0
+    for n, unit in enumerate(units):
+        at = 0
+        while at < unit.shape[0]:
+            rows = min(features - row % features, unit.shape[0] - at)
+            chunks.append((n, at, row // features, row % features, rows))
+            at, row = at + rows, row + rows
     return pl.pallas_call(
-        project_kernel,
+        functools.partial(project_kernel, chunks),
         grid_spec=pltpu.PrefetchScalarGridSpec(
             num_scalar_prefetch=1,
             grid=(tokens // tile,),
@@ -369,7 +376,7 @@
         along_x, along_y, across = (("ctx", swap_route(ctx, mask)) for mask in (1, 2, 3))
         along_z = ("mp", [(i, (i + 2) % mp) for i in range(mp)])
         others = [("mp", swap_route(mp, 2 * d)) for d in range(1, chips)]
-        middle, quarter = w_in.shape[0] // 2, w_in.shape[0] // 4
+        middle = w_in.shape[0] // 2
         own_rows = w_out.reshape(ctx, channels // ctx, -1)
         sent = [lax.dynamic_index_in_dim(own_rows, me ^ d, 0, False) for d in range(ctx)]
         near = send([(w_units[0], *along_x), (w_units[0], *along_y)])
@@ -385,12 +392,13 @@
         by_owner = jnp.stack([sent[0], *got])
         tails_all = jnp.concatenate([tails_all, core_swap(tails_all)])
         tails_all = jnp.concatenate([tails_all, *[lax.ppermute(tails_all, *route) for route in others]])
-        near = send([(w_units[1], *along_x), (w_units[1], *along_y)], [*far, *got, tails_all, tail_inverse])
+        w_second = lax.optimization_barrier((w_units[1], (*far, *got, tails_all, tail_inverse)))[0]
+        near = send([(w_second, *along_x), (w_second, *along_y)])
         order = jnp.stack([(me ^ (n // per)) * per + n % per for n in range(mp)]).astype(jnp.int32)
         order = jnp.concatenate([order, order ^ here])
 
         sent = [lax.dynamic_index_in_dim(by_owner, (chip ^ d) ^ me, 0, False) for d in range(chips)]
-        own_row, *sent = lax.optimization_barrier((sent, everything))[0]
+        own_row, *sent = sent
         by_chip = [lax.ppermute(block, *route) for block, route in zip(sent, others)]
         rows = jnp.stack([own_row, *by_chip])
         panel_order = jnp.stack([((chip - n) % chips) ^ chip for n in range(chips)]).astype(jnp.int32)
@@ -420,22 +428,22 @@
         if rings:
             order = lax.optimization_barrier((order, gated))[0]
         projected, before = project(everything, tails_all, units[g], order, inverse, tail_inverse)
+        if special and g > 0:
+            rings[0].append(send([(block, *along_z) for block in rings[0][-1]], [before]))
         tails = jnp.where(me == 0, tails_in[:, :, span].reshape(2, 3 * share), before[TAIL - 2 :])
         if special and g > 0:
             tails = lax.optimization_barrier((tails, rings[0][1]))[0]
         response, ends, last = local_filter(projected, tails, taps, own)
         if special:
-            shared = lax.optimization_barrier((last, by_chip[0]))[0] if g == 0 else last
+            shared = lax.optimization_barrier((last, by_chip[0] if g == 0 else rings[0][2]))[0]
             arrived = [lax.ppermute(shared, *route) for route in (along_x, along_y, across)]
             if g == 0:
-                near = lax.optimization_barrier((near, before))[0]
-                far = send([(near[1][:quarter], *along_x), (near[0][middle : middle + quarter], *along_y)])
-                arrived = lax.optimization_barrier((arrived, (*by_chip, *far)))[0]
-                late = send([(near[1][quarter:middle], *along_x), (near[0][middle + quarter :], *along_y)], arrived)
+                near = lax.optimization_barrier((near, arrived))[0]
+                arrived = lax.optimization_barrier((arrived, by_chip))[0]
+                far = send([(near[1][:middle], *along_x), (near[0][middle:], *along_y)])
             else:
-                arrived = lax.optimization_barrier((arrived, rings[0][2]))[0]
+                arrived = lax.optimization_barrier((arrived, rings[0][3]))[0]
                 panel_bottom = send([(bottom, *along_x), (bottom, *along_y)], arrived)
-                panel_far = send([(panel_top[1], *along_x), (panel_bottom[0], *along_y)])
             lasts = jnp.stack([last, *arrived])
         else:
             lasts = lax.all_gather(last, "ctx", axis=0)
@@ -447,13 +455,15 @@
         ]
         if special:
             blocks = [gated]
-            for _ in range(chips - 1):
+            for _ in range(chips - 2 if g == 0 else chips - 1):
                 blocks.append([lax.ppermute(block, *along_z) for block in blocks[-1]])
             rings.append(blocks)
             if g == 0:
-                units.append([w_units[1], *near, *[jnp.concatenate(pair) for pair in zip(far, late)]])
+                units.append([w_second, *near, *far])
                 top, bottom = rows[: chips // 2], rows[chips // 2 :]
-                panel_top = send([(top, *along_x), (top, *along_y)], [*late, *gated])
+                panel_top = send([(top, *along_x), (top, *along_y)], gated)
+            else:
+                panel_far = send([(panel_top[1], *along_x), (panel_bottom[0], *along_y)], blocks[1])
         else:
             gathered = [lax.all_gather(block, "mp", axis=0, axis_index_groups=groups_of_core) for block in gated]
             rings.append([[block[n] for block in gathered] for n in range(chips)])
@@ -474,7 +484,7 @@
             dtype = bf16 if final and n == len(steps) - 1 else f32
             last_step = rings[g][step]
             if final and n == len(steps) - 1:
-                last_step = lax.optimization_barrier((last_step, kept[0]))[0]
+                last_step = lax.optimization_barrier((last_step, (kept[0], given[0])))[0]
             given = [add_outputs(last_step, panel_order[step], panel, g, other, given, dtype)]
             kept = [add_outputs(last_step, panel_order[step], panel, g, mine, kept, f32)]
     total = (kept[0] + core_swap(given[0]).astype(f32)).astype(bf16)

time: 260 us -> 243 us (0.935)
  waiting for transfers between devices: 76.4 us -> 60.6 us
  starting transfers between devices: 66.6 us -> 69.7 us
  other arithmetic: 14 us -> 11.1 us
    ppermute x19, waiting for transfers between devices: 37.3 us -> 19.6 us  [send(): lax.ppermute(arrays[id(array)], axis, route)]
    ppermute x3, starting transfers between devices: 14.6 us -> 20.4 us  [core_swap(): return lax.ppermute(block, 'mp', swap_route(lax.axis_size('mp'), 1))]
    unnamed x115 -> x127, local copies, waits for them, and re-layouts: 10.1 us -> 14.2 us
    slice x2 -> x0, local copies, waits for them, and re-layouts: 3.82 us -> none  [the longest x1 1.91 us: local(): near[1][quarter:middle]]
    ppermute x12 -> x10, waiting for transfers between devices: 22.1 us -> 24 us  [local(): blocks.append([lax.ppermute(block, *along_z) for block in blocks[-1]])]
    ppermute x12 -> x10, starting transfers between devices: 8.73 us -> 7.2 us  [local(): blocks.append([lax.ppermute(block, *along_z) for block in blocks[-1]])]
  transfers between devices with their start and end apart: 52 -> 50, of which waited for: 23 -> 19; matrix products, arithmetic and copies ran while one was open for 17% -> 14% of each run, Pallas kernels for 16% -> 19%
where the time goes in v4:
time: 243 us; the launch traced here: 242 us
  starting transfers between devices  69.7 us (29%)
  waiting for transfers between devices  60.6 us (25%)
  Pallas kernels  47.6 us (20%)
  local copies, waits for them, and re-layouts  37.9 us (16%)
  between operations  15 us (6%)
  other arithmetic  11.1 us (5%)
    ppermute x10, waiting for transfers between devices, local(): blocks.append([lax.ppermute(block, *along_z) for block in blocks[-1]])  24 us
    pallas_call x2, Pallas kernels, project(): pl.pallas_call(functools.partial(project_kernel, chunks), grid_spec=pltpu...  20.5 us
    ppermute x3, starting transfers between devices, core_swap(): return lax.ppermute(block, 'mp', swap_route(lax.axis_size('mp'), 1))  20.4 us
    ppermute x19, starting transfers between devices, send(): lax.ppermute(arrays[id(array)], axis, route)  20.2 us
    ppermute x19, waiting for transfers between devices, send(): lax.ppermute(arrays[id(array)], axis, route)  19.6 us
    unnamed x127, local copies, waits for them, and re-layouts  14.2 us
    pallas_call x6, Pallas kernels, add_outputs(): pl.pallas_call(functools.partial(output_kernel, [[0] * len(chip) for chip...  11.3 us
    ppermute x1, waiting for transfers between devices, local(): tails_all = lax.ppermute(scaled[-TAIL:], *next_on)[None]  11.3 us
  transfers between devices with their start and end apart: 50, of which 19 were waited for; matrix products, arithmetic and copies ran while one was open for 14% of the time, Pallas kernels for 19%

profile of v4, /device:TPU:1, one launch (start us, length us, event | category | flops | bytes accessed | tf_op | source)
XLA Modules:
  0.0 241.8 jit_solution(11200532146007269239)
XLA Ops:
  7.2 2.5 %fusion.1 = (f32[1024]{0:T(1024)S(1)}, bf16[1024,512]{1,0:T(8,128)(2,1)}) fusion(bf16[1024,512]{1,0:T(8,128)(2,1)} %refs_9_.1, f32[512]{0:T(512)} %param.11), kind=kLoop, calls=%fused_computation.3 | loop fusion | flops 2620416 | bytes 2103296 | tf_op jit(solution)/shard_map/reduce_sum | solution.py:369
  9.7 3.3 %fusion.11 = (bf16[1024,3,256]{2,0,1:T(8,128)(2,1)}, bf16[1024,3,256]{2,0,1:T(8,128)(2,1)S(1)}) fusion(bf16[1024,3,512]{2,0,1:T(8,128)(2,1)} %param.12), kind=kLoop, calls=%fused_computation.78 | loop fusion | bytes 6291456 | tf_op jit(solution)/shard_map/slice | solution.py:366
  14.7 2.1 collective-permute-start.5
  16.8 1.2 collective-permute-start.6
  18.0 1.2 collective-permute-start.7
  25.5 3.4 %collective-permute-start.10 = (f32[1,1024]{1,0:T(1,128)S(1)}, f32[1,1024]{1,0:T(1,128)S(1)}, u32[]{:S(2)}, u32[]{:S(2)}) collective-permute-start(f32[1,1024]{1,0:T(1,128)S(1)} %add.105), channel_id=1, source_target_pairs={{0,6},{1,7},{2,4},{3,5},{4,2},{5,3},{6,0},{7,1},{8,14},{9,15},{10,... | collective-permute-start | bytes 12296 | tf_op jit(solution)/shard_map/ppermute | solution.py:384
  30.1 2.6 %copy.39 = bf16[1024,3,256]{0,2,1:T(8,128)(2,1)} copy(bf16[1024,3,256]{2,0,1:T(8,128)(2,1)} %get-tuple-element.84) | data formatting | bytes 3145728
  33.4 2.1 collective-permute-start
  35.8 3.2 %collective-permute-start.13 = (f32[16,1]{1,0:T(8,128)S(1)}, f32[16,1]{1,0:T(8,128)S(1)}, u32[]{:S(2)}, u32[]{:S(2)}) collective-permute-start(f32[16,1]{1,0:T(8,128)S(1)} %copy.24), channel_id=1, source_target_pairs={{0,8},{8,16},{16,24},{1,9},{9,17},{17,25},{2,10},{10,18},{18,26},{... | collective-permute-start | bytes 200 | tf_op jit(solution)/shard_map/ppermute | solution.py:386
  39.0 11.3 %collective-permute-done = bf16[16,512]{1,0:T(8,128)(2,1)S(1)} collective-permute-done((bf16[16,512]{1,0:T(8,128)(2,1)S(1)}, bf16[16,512]{1,0:T(8,128)(2,1)S(1)}, u32[]{:S(2)}, u32[]{:S(2)}) %collective-permute-start) | collective-permute-done | bytes 16416 | tf_op jit(solution)/shard_map/ppermute | solution.py:368
  50.2 1.6 collective-permute-start.1
  51.9 1.8 slice.115
  53.6 2.3 collective-permute-start.11
  55.9 1.3 collective-permute-start.12
  57.3 1.4 collective-permute-start.2
  58.6 2.3 collective-permute-start.3
  61.2 2.4 %collective-permute-start.16 = (bf16[128,1024]{1,0:T(8,128)(2,1)S(1)}, bf16[128,1024]{1,0:T(8,128)(2,1)S(1)}, u32[]{:S(2)}, u32[]{:S(2)}) collective-permute-start(bf16[128,1024]{1,0:T(8,128)(2,1)S(1)} %copy-done.39), channel_id=1, source_target_pairs={{0,24},{8,16},{16,8},{24,0},{1,25},{9,17},{17,9},{25,1},{2,26},{10... | collective-permute-start | bytes 786440 | tf_op jit(solution)/shard_map/ppermute | solution.py:27
  63.8 1.9 collective-permute-start.15
  67.3 11.8 %collective-permute-done.16 = bf16[128,1024]{1,0:T(8,128)(2,1)S(1)} collective-permute-done((bf16[128,1024]{1,0:T(8,128)(2,1)S(1)}, bf16[128,1024]{1,0:T(8,128)(2,1)S(1)}, u32[]{:S(2)}, u32[]{:S(2)}) %collective-permute-start.16) | collective-permute-done | bytes 262176 | tf_op jit(solution)/shard_map/ppermute | solution.py:27
  79.2 7.0 %collective-permute-done.15 = bf16[128,1024]{1,0:T(8,128)(2,1)S(1)} collective-permute-done((bf16[128,1024]{1,0:T(8,128)(2,1)S(1)}, bf16[128,1024]{1,0:T(8,128)(2,1)S(1)}, u32[]{:S(2)}, u32[]{:S(2)}) %collective-permute-start.15) | collective-permute-done | bytes 262176 | tf_op jit(solution)/shard_map/ppermute | solution.py:27
  88.2 1.7 copy.30.refs_0_
  90.1 1.2 collective-permute-start.24
  92.7 1.3 pad_maximum_fusion
  95.0 1.4 collective-permute-start.17
  96.4 2.2 collective-permute-start.21
  99.5 1.7 copy.26.refs_5_
  102.2 1.4 copy-done.3
  103.6 1.1 copy-done.9
  104.8 1.1 copy-done.11
  106.6 10.0 %project.2 = (f32[1024,768]{1,0:T(8,128)S(1)}, f32[16,768]{1,0:T(8,128)S(1)}) custom-call(s32[16]{0:T(128)S(1)} %concatenate.29.order_ref, bf16[8,1024,512]{2,1,0:T(8,128)(2,1)} %bitcast.157, bf16[8,16,512]{2,1,0:T(8,128)(2,1)S(1)} %constant_dynamic-update-slice_fusion.tails_ref, bf16[1024,768]{1,0:T(8,128)(2,1)S(1)} %copy.25.refs_0_, ...), custom_call_target="tpu_custom_call" | custom-call | tf_op jit(solution)/shard_map/project/pallas_call | solution.py:227
  117.3 5.1 %local_filter.2 = (f32[1024,256]{1,0:T(8,128)S(1)}, f32[128,256]{1,0:T(8,128)S(1)}, f32[16,256]{1,0:T(8,128)S(1)}) custom-call(f32[1024,768]{1,0:T(8,128)S(1)} %get-tuple-element.44.k_ref.v_ref.q_ref, f32[1024,768]{1,0:T(8,128)S(1)} %get-tuple-element.44.k_ref.v_ref.q_ref, f32[2,768]{1,0:T(2,128)S(1)} %slice_select_fusion.1.tail_k_ref.tail_v_ref.tail_q_ref, ...), custom_call_target="tpu_custom_call" | custom-call | bytes 3145728 | tf_op jit(solution)/shard_map/local_filter/pallas_call | solution.py:127
  122.5 1.4 collective-permute-start.18
  127.6 1.2 slice.132
  129.1 1.2 slice.133
  130.3 1.3 collective-permute-start.26
  131.7 1.4 gated_signal.4.refs_0_
  133.5 1.4 gated_signal.5.refs_1_
  135.0 1.2 collective-permute-start.28
  136.2 4.0 %collective-permute-done.27.refs_2_ = bf16[1024,128]{1,0:T(8,128)(2,1)S(1)} collective-permute-done((bf16[1024,128]{1,0:T(8,128)(2,1)S(1)}, bf16[1024,128]{1,0:T(8,128)(2,1)S(1)}, u32[]{:S(2)}, u32[]{:S(2)}) %collective-permute-start.27) | collective-permute-done | bytes 262176 | tf_op jit(solution)/shard_map/ppermute | solution.py:459
  140.2 3.7 %collective-permute-done.28.refs_3_ = bf16[1024,128]{1,0:T(8,128)(2,1)S(1)} collective-permute-done((bf16[1024,128]{1,0:T(8,128)(2,1)S(1)}, bf16[1024,128]{1,0:T(8,128)(2,1)S(1)}, u32[]{:S(2)}, u32[]{:S(2)}) %collective-permute-start.28) | collective-permute-done | bytes 262176 | tf_op jit(solution)/shard_map/ppermute | solution.py:459
  144.9 1.3 pad_maximum_fusion.2
  146.3 10.5 %project.3 = (f32[1024,768]{1,0:T(8,128)S(1)}, f32[16,768]{1,0:T(8,128)S(1)}) custom-call(s32[16]{0:T(128)S(1)} %concatenate.29.order_ref, bf16[8,1024,512]{2,1,0:T(8,128)(2,1)} %bitcast.158, bf16[8,16,512]{2,1,0:T(8,128)(2,1)S(1)} %copy-done.14, bf16[1024,768]{1,0:T(8,128)(2,1)S(1)} %copy.30.refs_0_, bf16[1024,768]{1,0:T(8,128)(2,1)} %collective-permute-done.23.refs_1_, ...), custom_call_target="tpu_custom_call" | custom-call | tf_op jit(solution)/shard_map/project/pallas_call | solution.py:227
  156.8 1.3 collective-permute-start.34
  158.7 5.1 %local_filter.3 = (f32[1024,256]{1,0:T(8,128)S(1)}, f32[128,256]{1,0:T(8,128)S(1)}, f32[16,256]{1,0:T(8,128)S(1)}) custom-call(f32[1024,768]{1,0:T(8,128)S(1)} %get-tuple-element.64.k_ref.v_ref.q_ref, f32[1024,768]{1,0:T(8,128)S(1)} %get-tuple-element.64.k_ref.v_ref.q_ref, f32[2,768]{1,0:T(2,128)S(1)} %slice_select_fusion.tail_k_ref.tail_v_ref.tail_q_ref, ...), custom_call_target="tpu_custom_call" | custom-call | bytes 3145728 | tf_op jit(solution)/shard_map/local_filter/pallas_call | solution.py:127
  163.8 1.3 collective-permute-start.31
  165.4 1.2 collective-permute-start.33
  169.4 1.4 gated_signal.6.refs_0_
  170.8 1.4 gated_signal.7.refs_1_
  172.2 2.0 collective-permute-start.36
  174.9 4.6 %collective-permute-done.36.refs_2_ = bf16[1024,128]{1,0:T(8,128)(2,1)S(1)} collective-permute-done((bf16[1024,128]{1,0:T(8,128)(2,1)S(1)}, bf16[1024,128]{1,0:T(8,128)(2,1)S(1)}, u32[]{:S(2)}, u32[]{:S(2)}) %collective-permute-start.36) | collective-permute-done | bytes 262176 | tf_op jit(solution)/shard_map/ppermute | solution.py:459
  179.5 2.8 %collective-permute-done.39.refs_3_ = bf16[1024,128]{1,0:T(8,128)(2,1)S(1)} collective-permute-done((bf16[1024,128]{1,0:T(8,128)(2,1)S(1)}, bf16[1024,128]{1,0:T(8,128)(2,1)S(1)}, u32[]{:S(2)}, u32[]{:S(2)}) %collective-permute-start.39) | collective-permute-done | bytes 262176 | tf_op jit(solution)/shard_map/ppermute | solution.py:459
  183.1 1.2 collective-permute-start.44
  184.3 1.9 collective-permute-start.40
  187.6 1.3 fusion.2
  188.9 3.8 %collective-permute-done.37.refs_4_ = bf16[1024,128]{1,0:T(8,128)(2,1)S(1)} collective-permute-done((bf16[1024,128]{1,0:T(8,128)(2,1)S(1)}, bf16[1024,128]{1,0:T(8,128)(2,1)S(1)}, u32[]{:S(2)}, u32[]{:S(2)}) %collective-permute-start.37) | collective-permute-done | bytes 262176 | tf_op jit(solution)/shard_map/ppermute | solution.py:459
  193.2 5.1 %collective-permute-done.40.refs_5_ = bf16[1024,128]{1,0:T(8,128)(2,1)S(1)} collective-permute-done((bf16[1024,128]{1,0:T(8,128)(2,1)S(1)}, bf16[1024,128]{1,0:T(8,128)(2,1)S(1)}, u32[]{:S(2)}, u32[]{:S(2)}) %collective-permute-start.40) | collective-permute-done | bytes 262176 | tf_op jit(solution)/shard_map/ppermute | solution.py:459
  198.3 1.5 collective-permute-start.41
  202.1 1.2 bitcast_dynamic-update-slice_fusion.1
  203.4 2.4 %add_outputs.6.refs_7_ = f32[1024,512]{1,0:T(8,128)S(1)} custom-call(s32[4]{0:T(128)S(1)} %pad_add_fusion.1.order_ref, s32[1]{0:T(128)} %bitcast.1.half_ref, bf16[1024,128]{1,0:T(8,128)(2,1)S(1)} %gated_signal.4.refs_0_, bf16[1024,128]{1,0:T(8,128)(2,1)S(1)} %gated_signal.5.refs_1_, bf16[1024,128]{1,0:T(8,128)(2,1)S(1)} %collective-permute-done.27.refs_2_, ...), custom_call_target="tpu_custom_call" | custom-call | flops 2147483648 | bytes 2097152 | tf_op jit(solution)/shard_map/add_outputs/pallas_call | solution.py:271
  205.9 2.4 %add_outputs.8.refs_7_ = f32[1024,512]{1,0:T(8,128)S(1)} custom-call(s32[4]{0:T(128)S(1)} %pad_add_fusion.1.order_ref, s32[1]{0:T(128)} %bitcast.72.half_ref, bf16[1024,128]{1,0:T(8,128)(2,1)S(1)} %gated_signal.4.refs_0_, bf16[1024,128]{1,0:T(8,128)(2,1)S(1)} %gated_signal.5.refs_1_, bf16[1024,128]{1,0:T(8,128)(2,1)S(1)} %collective-permute-done.27.refs_2_, ...), custom_call_target="tpu_custom_call" | custom-call | flops 2147483648 | bytes 2097152 | tf_op jit(solution)/shard_map/add_outputs/pallas_call | solution.py:271
  208.3 2.2 add_outputs.7.refs_3_
  210.5 2.2 add_outputs.9.refs_3_
  213.8 17.5 %collective-permute-start.48 = (bf16[1024,512]{1,0:T(8,128)(2,1)S(1)}, bf16[1024,512]{1,0:T(8,128)(2,1)S(1)}, u32[]{:S(2)}, u32[]{:S(2)}) collective-permute-start(bf16[1024,512]{1,0:T(8,128)(2,1)S(1)} %add_outputs.11), channel_id=1, source_target_pairs={{0,1},{1,0},{2,3},{3,2},{4,5},{5,4},{6,7},{7,6},{8,9},{9,8},{10,11... | collective-permute-start | bytes 3145736 | tf_op jit(solution)/shard_map/ppermute | solution.py:293
  233.6 1.3 add_convert_fusion
  (237 shorter events, 37.8 us)
Async XLA Ops:
  7.2 94.0 %all-gather.3.cloned.1.call-start = ((), (), s32[]{:S(2)}) async-start(), calls=%async_computation | async-start | bytes 9437184 | tf_op jit(solution)/shard_map/all_gather | solution.py:365
  14.7 37.2 %collective-permute-start.5 = (bf16[1024,768]{1,0:T(8,128)(2,1)S(1)}, bf16[1024,768]{1,0:T(8,128)(2,1)S(1)}, u32[]{:S(2)}, u32[]{:S(2)}) collective-permute-start(bf16[1024,768]{1,0:T(8,128)(2,1)S(1)} %copy.25.refs_0_), channel_id=1, source_target_pairs={{0,8},{8,0},{16,24},{24,16},{1,9},{9,1},{17,25},{25,17},{2,10},{10... | collective-permute-start | bytes 4718600 | tf_op jit(solution)/shard_map/ppermute | solution.py:27
  16.8 35.1 %collective-permute-start.6 = (bf16[1024,768]{1,0:T(8,128)(2,1)S(1)}, bf16[1024,768]{1,0:T(8,128)(2,1)}, u32[]{:S(2)}, u32[]{:S(2)}) collective-permute-start(bf16[1024,768]{1,0:T(8,128)(2,1)S(1)} %copy.25.refs_0_), channel_id=1, source_target_pairs={{0,16},{8,24},{16,0},{24,8},{1,17},{9,25},{17,1},{25,9},{2,18},{10... | collective-permute-start | bytes 4718600 | tf_op jit(solution)/shard_map/ppermute | solution.py:27
  18.0 7.5 %collective-permute-start.7 = (f32[1,1024]{1,0:T(1,128)S(1)}, f32[1,1024]{1,0:T(1,128)S(1)}, u32[]{:S(2)}, u32[]{:S(2)}) collective-permute-start(f32[1,1024]{1,0:T(1,128)S(1)} %bitcast.175), channel_id=1, source_target_pairs={{0,1},{1,0},{2,3},{3,2},{4,5},{5,4},{6,7},{7,6},{8,9},{9,8},{10,11... | collective-permute-start | bytes 12296 | tf_op jit(solution)/shard_map/ppermute | solution.py:293
  25.5 7.9 %collective-permute-start.10 = (f32[1,1024]{1,0:T(1,128)S(1)}, f32[1,1024]{1,0:T(1,128)S(1)}, u32[]{:S(2)}, u32[]{:S(2)}) collective-permute-start(f32[1,1024]{1,0:T(1,128)S(1)} %add.105), channel_id=1, source_target_pairs={{0,6},{1,7},{2,4},{3,5},{4,2},{5,3},{6,0},{7,1},{8,14},{9,15},{10,... | collective-permute-start | bytes 12296 | tf_op jit(solution)/shard_map/ppermute | solution.py:384
  28.9 6.6 %collective-permute-start.8 = (f32[1,1024]{1,0:T(1,128)S(1)}, f32[1,1024]{1,0:T(1,128)S(1)}, u32[]{:S(2)}, u32[]{:S(2)}) collective-permute-start(f32[1,1024]{1,0:T(1,128)S(1)} %add.105), channel_id=1, source_target_pairs={{0,2},{1,3},{2,0},{3,1},{4,6},{5,7},{6,4},{7,5},{8,10},{9,11},{10,... | collective-permute-start | bytes 12296 | tf_op jit(solution)/shard_map/ppermute | solution.py:384
  28.9 6.7 %collective-permute-start.9 = (f32[1,1024]{1,0:T(1,128)S(1)}, f32[1,1024]{1,0:T(1,128)S(1)}, u32[]{:S(2)}, u32[]{:S(2)}) collective-permute-start(f32[1,1024]{1,0:T(1,128)S(1)} %add.105), channel_id=1, source_target_pairs={{0,4},{1,5},{2,6},{3,7},{4,0},{5,1},{6,2},{7,3},{8,12},{9,13},{10,... | collective-permute-start | bytes 12296 | tf_op jit(solution)/shard_map/ppermute | solution.py:384
  33.4 16.8 %collective-permute-start = (bf16[16,512]{1,0:T(8,128)(2,1)S(1)}, bf16[16,512]{1,0:T(8,128)(2,1)S(1)}, u32[]{:S(2)}, u32[]{:S(2)}) collective-permute-start(bf16[16,512]{1,0:T(8,128)(2,1)S(1)} %slice.148), channel_id=1, source_target_pairs={{0,8},{8,16},{16,24},{1,9},{9,17},{17,25},{2,10},{10,18},{18,26},{... | collective-permute-start | bytes 49160 | tf_op jit(solution)/shard_map/ppermute | solution.py:368
  35.6 54.3 %copy-start.51 = (f32[1,1024]{1,0:T(1,128)}, f32[1,1024]{1,0:T(1,128)S(1)}, u32[]{:S(2)}) copy-start(f32[1,1024]{1,0:T(1,128)S(1)} %add_rsqrt_fusion) | copy-start | bytes 12292
  35.8 25.4 %copy-start.39 = (bf16[128,1024]{1,0:T(8,128)(2,1)S(1)}, bf16[128,1024]{1,0:T(8,128)(2,1)}, u32[]{:S(2)}) copy-start(bf16[128,1024]{1,0:T(8,128)(2,1)} %get-tuple-element.55) | copy-start | bytes 786436
  35.8 28.1 %copy-start.38 = (bf16[128,1024]{1,0:T(8,128)(2,1)S(1)}, bf16[128,1024]{1,0:T(8,128)(2,1)}, u32[]{:S(2)}) copy-start(bf16[128,1024]{1,0:T(8,128)(2,1)} %get-tuple-element.54) | copy-start | bytes 786436
  35.8 30.5 %copy-start.37 = (bf16[128,1024]{1,0:T(8,128)(2,1)S(1)}, bf16[128,1024]{1,0:T(8,128)(2,1)}, u32[]{:S(2)}) copy-start(bf16[128,1024]{1,0:T(8,128)(2,1)} %get-tuple-element.53) | copy-start | bytes 786436
  35.8 25.2 %collective-permute-start.13 = (f32[16,1]{1,0:T(8,128)S(1)}, f32[16,1]{1,0:T(8,128)S(1)}, u32[]{:S(2)}, u32[]{:S(2)}) collective-permute-start(f32[16,1]{1,0:T(8,128)S(1)} %copy.24), channel_id=1, source_target_pairs={{0,8},{8,16},{16,24},{1,9},{9,17},{17,25},{2,10},{10,18},{18,26},{... | collective-permute-start | bytes 200 | tf_op jit(solution)/shard_map/ppermute | solution.py:386
  50.2 7.0 %collective-permute-start.1 = (bf16[1,16,512]{2,1,0:T(8,128)(2,1)S(1)}, bf16[1,16,512]{2,1,0:T(8,128)(2,1)S(1)}, u32[]{:S(2)}, u32[]{:S(2)}) collective-permute-start(bf16[1,16,512]{2,1,0:T(8,128)(2,1)S(1)} %bitcast.168), channel_id=1, source_target_pairs={{0,1},{1,0},{2,3},{3,2},{4,5},{5,4},{6,7},{7,6},{8,9},{9,8},{10,11... | collective-permute-start | bytes 49160 | tf_op jit(solution)/shard_map/ppermute | solution.py:293
  51.9 35.3 %copy-start.2 = (bf16[1024,768]{1,0:T(8,128)(2,1)}, bf16[1024,768]{1,0:T(8,128)(2,1)S(1)}, u32[]{:S(2)}) copy-start(bf16[1024,768]{1,0:T(8,128)(2,1)S(1)} %collective-permute-done.5.refs_1_) | copy-start | bytes 4718596
  53.6 32.6 %collective-permute-start.11 = (bf16[512,768]{1,0:T(8,128)(2,1)S(1)}, bf16[512,768]{1,0:T(8,128)(2,1)S(1)}, u32[]{:S(2)}, u32[]{:S(2)}) collective-permute-start(bf16[512,768]{1,0:T(8,128)(2,1)S(1)} %slice.115), channel_id=1, source_target_pairs={{0,8},{8,0},{16,24},{24,16},{1,9},{9,1},{17,25},{25,17},{2,10},{10... | collective-permute-start | bytes 2359304 | tf_op jit(solution)/shard_map/ppermute | solution.py:27
  55.9 35.4 %copy-start.53 = (f32[512]{0:T(512)S(1)}, f32[512]{0:T(512)}, u32[]{:S(2)}) copy-start(f32[512]{0:T(512)} %param.17) | copy-start | bytes 6148
  55.9 31.2 %collective-permute-start.12 = (bf16[512,768]{1,0:T(8,128)(2,1)S(1)}, bf16[512,768]{1,0:T(8,128)(2,1)S(1)}, u32[]{:S(2)}, u32[]{:S(2)}) collective-permute-start(bf16[512,768]{1,0:T(8,128)(2,1)S(1)} %slice.116), channel_id=1, source_target_pairs={{0,16},{8,24},{16,0},{24,8},{1,17},{9,25},{17,1},{25,9},{2,18},{10... | collective-permute-start | bytes 2359304 | tf_op jit(solution)/shard_map/ppermute | solution.py:27
  57.3 3.9 %collective-permute-start.2 = (bf16[2,16,512]{2,1,0:T(8,128)(2,1)S(1)}, bf16[2,16,512]{2,1,0:T(8,128)(2,1)S(1)}, u32[]{:S(2)}, u32[]{:S(2)}) collective-permute-start(bf16[2,16,512]{2,1,0:T(8,128)(2,1)S(1)} %pad_maximum_fusion.5), channel_id=1, source_target_pairs={{0,2},{1,3},{2,0},{3,1},{4,6},{5,7},{6,4},{7,5},{8,10},{9,11},{10,... | collective-permute-start | bytes 98312 | tf_op jit(solution)/shard_map/ppermute | solution.py:394
  58.6 5.2 %collective-permute-start.3 = (bf16[2,16,512]{2,1,0:T(8,128)(2,1)S(1)}, bf16[2,16,512]{2,1,0:T(8,128)(2,1)S(1)}, u32[]{:S(2)}, u32[]{:S(2)}) collective-permute-start(bf16[2,16,512]{2,1,0:T(8,128)(2,1)S(1)} %pad_maximum_fusion.5), channel_id=1, source_target_pairs={{0,4},{1,5},{2,6},{3,7},{4,0},{5,1},{6,2},{7,3},{8,12},{9,13},{10,... | collective-permute-start | bytes 98312 | tf_op jit(solution)/shard_map/ppermute | solution.py:394
  61.0 31.0 %copy-start.23 = (f32[16,1]{1,0:T(8,128)}, f32[16,1]{1,0:T(8,128)S(1)}, u32[]{:S(2)}) copy-start(f32[16,1]{1,0:T(8,128)S(1)} %collective-permute-done.13.refs_6_) | copy-start | bytes 196
  61.0 5.3 %collective-permute-start.4 = (bf16[2,16,512]{2,1,0:T(8,128)(2,1)S(1)}, bf16[2,16,512]{2,1,0:T(8,128)(2,1)S(1)}, u32[]{:S(2)}, u32[]{:S(2)}) collective-permute-start(bf16[2,16,512]{2,1,0:T(8,128)(2,1)S(1)} %pad_maximum_fusion.5), channel_id=1, source_target_pairs={{0,6},{1,7},{2,4},{3,5},{4,2},{5,3},{6,0},{7,1},{8,14},{9,15},{10,... | collective-permute-start | bytes 98312 | tf_op jit(solution)/shard_map/ppermute | solution.py:394
  61.2 18.0 %collective-permute-start.16 = (bf16[128,1024]{1,0:T(8,128)(2,1)S(1)}, bf16[128,1024]{1,0:T(8,128)(2,1)S(1)}, u32[]{:S(2)}, u32[]{:S(2)}) collective-permute-start(bf16[128,1024]{1,0:T(8,128)(2,1)S(1)} %copy-done.39), channel_id=1, source_target_pairs={{0,24},{8,16},{16,8},{24,0},{1,25},{9,17},{17,9},{25,1},{2,26},{10... | collective-permute-start | bytes 786440 | tf_op jit(solution)/shard_map/ppermute | solution.py:27
  63.8 22.4 %collective-permute-start.15 = (bf16[128,1024]{1,0:T(8,128)(2,1)S(1)}, bf16[128,1024]{1,0:T(8,128)(2,1)S(1)}, u32[]{:S(2)}, u32[]{:S(2)}) collective-permute-start(bf16[128,1024]{1,0:T(8,128)(2,1)S(1)} %copy-done.38), channel_id=1, source_target_pairs={{0,16},{8,24},{16,0},{24,8},{1,17},{9,25},{17,1},{25,9},{2,18},{10... | collective-permute-start | bytes 786440 | tf_op jit(solution)/shard_map/ppermute | solution.py:27
  66.2 20.0 %collective-permute-start.14 = (bf16[128,1024]{1,0:T(8,128)(2,1)S(1)}, bf16[128,1024]{1,0:T(8,128)(2,1)S(1)}, u32[]{:S(2)}, u32[]{:S(2)}) collective-permute-start(bf16[128,1024]{1,0:T(8,128)(2,1)S(1)} %copy-done.37), channel_id=1, source_target_pairs={{0,8},{8,0},{16,24},{24,16},{1,9},{9,1},{17,25},{25,17},{2,10},{10... | collective-permute-start | bytes 786440 | tf_op jit(solution)/shard_map/ppermute | solution.py:27
  89.9 37.8 %collective-permute-start.23 = (bf16[1024,768]{1,0:T(8,128)(2,1)S(1)}, bf16[1024,768]{1,0:T(8,128)(2,1)}, u32[]{:S(2)}, u32[]{:S(2)}) collective-permute-start(bf16[1024,768]{1,0:T(8,128)(2,1)S(1)} %copy.30.refs_0_), channel_id=1, source_target_pairs={{0,8},{8,0},{16,24},{24,16},{1,9},{9,1},{17,25},{25,17},{2,10},{10... | collective-permute-start | bytes 4718600 | tf_op jit(solution)/shard_map/ppermute | solution.py:27
  90.1 37.6 %collective-permute-start.24 = (bf16[1024,768]{1,0:T(8,128)(2,1)S(1)}, bf16[1024,768]{1,0:T(8,128)(2,1)}, u32[]{:S(2)}, u32[]{:S(2)}) collective-permute-start(bf16[1024,768]{1,0:T(8,128)(2,1)S(1)} %copy.30.refs_0_), channel_id=1, source_target_pairs={{0,16},{8,24},{16,0},{24,8},{1,17},{9,25},{17,1},{25,9},{2,18},{10... | collective-permute-start | bytes 4718600 | tf_op jit(solution)/shard_map/ppermute | solution.py:27
  95.0 27.5 %collective-permute-start.17 = (bf16[128,1024]{1,0:T(8,128)(2,1)}, bf16[128,1024]{1,0:T(8,128)(2,1)}, u32[]{:S(2)}, u32[]{:S(2)}) collective-permute-start(bf16[128,1024]{1,0:T(8,128)(2,1)} %get-tuple-element.89), channel_id=1, source_target_pairs={{0,2},{1,3},{2,0},{3,1},{4,6},{5,7},{6,4},{7,5},{8,10},{9,11},{10,... | collective-permute-start | bytes 786440 | tf_op jit(solution)/shard_map/ppermute | solution.py:402
  96.4 27.5 %collective-permute-start.21 = (bf16[128,1024]{1,0:T(8,128)(2,1)}, bf16[128,1024]{1,0:T(8,128)(2,1)}, u32[]{:S(2)}, u32[]{:S(2)}) collective-permute-start(bf16[128,1024]{1,0:T(8,128)(2,1)} %get-tuple-element.88), channel_id=1, source_target_pairs={{0,4},{1,5},{2,6},{3,7},{4,0},{5,1},{6,2},{7,3},{8,12},{9,13},{10,... | collective-permute-start | bytes 786440 | tf_op jit(solution)/shard_map/ppermute | solution.py:402
  98.6 25.5 %collective-permute-start.22 = (bf16[128,1024]{1,0:T(8,128)(2,1)}, bf16[128,1024]{1,0:T(8,128)(2,1)}, u32[]{:S(2)}, u32[]{:S(2)}) collective-permute-start(bf16[128,1024]{1,0:T(8,128)(2,1)} %get-tuple-element.87), channel_id=1, source_target_pairs={{0,6},{1,7},{2,4},{3,5},{4,2},{5,3},{6,0},{7,1},{8,14},{9,15},{10,... | collective-permute-start | bytes 786440 | tf_op jit(solution)/shard_map/ppermute | solution.py:402
  122.5 3.3 %collective-permute-start.18 = (f32[16,256]{1,0:T(8,128)S(1)}, f32[16,256]{1,0:T(8,128)S(1)}, u32[]{:S(2)}, u32[]{:S(2)}) collective-permute-start(f32[16,256]{1,0:T(8,128)S(1)} %get-tuple-element.56), channel_id=1, source_target_pairs={{0,8},{8,0},{16,24},{24,16},{1,9},{9,1},{17,25},{25,17},{2,10},{10... | collective-permute-start | bytes 49160 | tf_op jit(solution)/shard_map/ppermute | solution.py:439
  123.9 2.7 %collective-permute-start.19 = (f32[16,256]{1,0:T(8,128)S(1)}, f32[16,256]{1,0:T(8,128)S(1)}, u32[]{:S(2)}, u32[]{:S(2)}) collective-permute-start(f32[16,256]{1,0:T(8,128)S(1)} %get-tuple-element.56), channel_id=1, source_target_pairs={{0,16},{8,24},{16,0},{24,8},{1,17},{9,25},{17,1},{25,9},{2,18},{10... | collective-permute-start | bytes 49160 | tf_op jit(solution)/shard_map/ppermute | solution.py:439
  124.1 3.5 %collective-permute-start.20 = (f32[16,256]{1,0:T(8,128)S(1)}, f32[16,256]{1,0:T(8,128)S(1)}, u32[]{:S(2)}, u32[]{:S(2)}) collective-permute-start(f32[16,256]{1,0:T(8,128)S(1)} %get-tuple-element.56), channel_id=1, source_target_pairs={{0,24},{8,16},{16,8},{24,0},{1,25},{9,17},{17,9},{25,1},{2,26},{10... | collective-permute-start | bytes 49160 | tf_op jit(solution)/shard_map/ppermute | solution.py:439
  128.8 17.4 %collective-permute-start.25 = (bf16[512,768]{1,0:T(8,128)(2,1)S(1)}, bf16[512,768]{1,0:T(8,128)(2,1)S(1)}, u32[]{:S(2)}, u32[]{:S(2)}) collective-permute-start(bf16[512,768]{1,0:T(8,128)(2,1)S(1)} %slice.132), channel_id=1, source_target_pairs={{0,8},{8,0},{16,24},{24,16},{1,9},{9,1},{17,25},{25,17},{2,10},{10... | collective-permute-start | bytes 2359304 | tf_op jit(solution)/shard_map/ppermute | solution.py:27
  130.3 16.0 %collective-permute-start.26 = (bf16[512,768]{1,0:T(8,128)(2,1)S(1)}, bf16[512,768]{1,0:T(8,128)(2,1)S(1)}, u32[]{:S(2)}, u32[]{:S(2)}) collective-permute-start(bf16[512,768]{1,0:T(8,128)(2,1)S(1)} %slice.133), channel_id=1, source_target_pairs={{0,16},{8,24},{16,0},{24,8},{1,17},{9,25},{17,1},{25,9},{2,18},{10... | collective-permute-start | bytes 2359304 | tf_op jit(solution)/shard_map/ppermute | solution.py:27
  133.1 7.1 %collective-permute-start.27 = (bf16[1024,128]{1,0:T(8,128)(2,1)S(1)}, bf16[1024,128]{1,0:T(8,128)(2,1)S(1)}, u32[]{:S(2)}, u32[]{:S(2)}) collective-permute-start(bf16[1024,128]{1,0:T(8,128)(2,1)S(1)} %gated_signal.4.refs_0_), channel_id=1, source_target_pairs={{0,2},{1,3},{2,4},{3,5},{4,6},{5,7},{6,0},{7,1},{8,10},{9,11},{10,... | collective-permute-start | bytes 786440 | tf_op jit(solution)/shard_map/ppermute | solution.py:459
  135.0 8.9 %collective-permute-start.28 = (bf16[1024,128]{1,0:T(8,128)(2,1)S(1)}, bf16[1024,128]{1,0:T(8,128)(2,1)S(1)}, u32[]{:S(2)}, u32[]{:S(2)}) collective-permute-start(bf16[1024,128]{1,0:T(8,128)(2,1)S(1)} %gated_signal.5.refs_1_), channel_id=1, source_target_pairs={{0,2},{1,3},{2,4},{3,5},{4,6},{5,7},{6,0},{7,1},{8,10},{9,11},{10,... | collective-permute-start | bytes 786440 | tf_op jit(solution)/shard_map/ppermute | solution.py:459
  140.2 16.6 %collective-permute-start.29 = (bf16[1024,128]{1,0:T(8,128)(2,1)S(1)}, bf16[1024,128]{1,0:T(8,128)(2,1)S(1)}, u32[]{:S(2)}, u32[]{:S(2)}) collective-permute-start(bf16[1024,128]{1,0:T(8,128)(2,1)S(1)} %collective-permute-done.27.refs_2_), channel_id=1, source_target_pairs={{0,2},{1,3},{2,4},{3,5},{4,6},{5,7},{6,0},{7,1},{8,10},{9,11},{10,... | collective-permute-start | bytes 786440 | tf_op jit(solution)/shard_map/ppermute | solution.py:459
  143.9 12.9 %collective-permute-start.30 = (bf16[1024,128]{1,0:T(8,128)(2,1)S(1)}, bf16[1024,128]{1,0:T(8,128)(2,1)S(1)}, u32[]{:S(2)}, u32[]{:S(2)}) collective-permute-start(bf16[1024,128]{1,0:T(8,128)(2,1)S(1)} %collective-permute-done.28.refs_3_), channel_id=1, source_target_pairs={{0,2},{1,3},{2,4},{3,5},{4,6},{5,7},{6,0},{7,1},{8,10},{9,11},{10,... | collective-permute-start | bytes 786440 | tf_op jit(solution)/shard_map/ppermute | solution.py:459
  144.9 21.6 %copy-start.33 = (bf16[2,128,1024]{2,1,0:T(8,128)(2,1)}, bf16[2,128,1024]{2,1,0:T(8,128)(2,1)S(1)}, u32[]{:S(2)}) copy-start(bf16[2,128,1024]{2,1,0:T(8,128)(2,1)S(1)} %pad_maximum_fusion.1) | copy-start | bytes 1572868
  146.2 22.7 %copy-start.31 = (bf16[2,128,1024]{2,1,0:T(8,128)(2,1)}, bf16[2,128,1024]{2,1,0:T(8,128)(2,1)S(1)}, u32[]{:S(2)}) copy-start(bf16[2,128,1024]{2,1,0:T(8,128)(2,1)S(1)} %pad_maximum_fusion.2) | copy-start | bytes 1572868
  146.2 12.4 %copy-start.15 = (f32[128,256]{1,0:T(8,128)S(1)}, f32[128,256]{1,0:T(8,128)}, u32[]{:S(2)}) copy-start(f32[128,256]{1,0:T(8,128)} %get-tuple-element.96.reach_ref) | copy-start | bytes 393220
  156.8 12.1 %collective-permute-start.34 = (bf16[1024,128]{1,0:T(8,128)(2,1)S(1)}, bf16[1024,128]{1,0:T(8,128)(2,1)S(1)}, u32[]{:S(2)}, u32[]{:S(2)}) collective-permute-start(bf16[1024,128]{1,0:T(8,128)(2,1)S(1)} %collective-permute-done.29.refs_4_), channel_id=1, source_target_pairs={{0,2},{1,3},{2,4},{3,5},{4,6},{5,7},{6,0},{7,1},{8,10},{9,11},{10,... | collective-permute-start | bytes 786440 | tf_op jit(solution)/shard_map/ppermute | solution.py:27
  158.1 10.7 %collective-permute-start.35 = (bf16[1024,128]{1,0:T(8,128)(2,1)S(1)}, bf16[1024,128]{1,0:T(8,128)(2,1)S(1)}, u32[]{:S(2)}, u32[]{:S(2)}) collective-permute-start(bf16[1024,128]{1,0:T(8,128)(2,1)S(1)} %collective-permute-done.30.refs_5_), channel_id=1, source_target_pairs={{0,2},{1,3},{2,4},{3,5},{4,6},{5,7},{6,0},{7,1},{8,10},{9,11},{10,... | collective-permute-start | bytes 786440 | tf_op jit(solution)/shard_map/ppermute | solution.py:27
  163.8 2.7 %collective-permute-start.31 = (f32[16,256]{1,0:T(8,128)S(1)}, f32[16,256]{1,0:T(8,128)S(1)}, u32[]{:S(2)}, u32[]{:S(2)}) collective-permute-start(f32[16,256]{1,0:T(8,128)S(1)} %get-tuple-element.70), channel_id=1, source_target_pairs={{0,8},{8,0},{16,24},{24,16},{1,9},{9,1},{17,25},{25,17},{2,10},{10... | collective-permute-start | bytes 49160 | tf_op jit(solution)/shard_map/ppermute | solution.py:439
  165.1 2.6 %collective-permute-start.32 = (f32[16,256]{1,0:T(8,128)S(1)}, f32[16,256]{1,0:T(8,128)S(1)}, u32[]{:S(2)}, u32[]{:S(2)}) collective-permute-start(f32[16,256]{1,0:T(8,128)S(1)} %get-tuple-element.70), channel_id=1, source_target_pairs={{0,16},{8,24},{16,0},{24,8},{1,17},{9,25},{17,1},{25,9},{2,18},{10... | collective-permute-start | bytes 49160 | tf_op jit(solution)/shard_map/ppermute | solution.py:439
  165.4 3.5 %collective-permute-start.33 = (f32[16,256]{1,0:T(8,128)S(1)}, f32[16,256]{1,0:T(8,128)S(1)}, u32[]{:S(2)}, u32[]{:S(2)}) collective-permute-start(f32[16,256]{1,0:T(8,128)S(1)} %get-tuple-element.70), channel_id=1, source_target_pairs={{0,24},{8,16},{16,8},{24,0},{1,25},{9,17},{17,9},{25,1},{2,26},{10... | collective-permute-start | bytes 49160 | tf_op jit(solution)/shard_map/ppermute | solution.py:439
  166.5 8.4 %collective-permute-start.42 = (bf16[2,128,1024]{2,1,0:T(8,128)(2,1)S(1)}, bf16[2,128,1024]{2,1,0:T(8,128)(2,1)}, u32[]{:S(2)}, u32[]{:S(2)}) collective-permute-start(bf16[2,128,1024]{2,1,0:T(8,128)(2,1)S(1)} %pad_maximum_fusion.1), channel_id=1, source_target_pairs={{0,16},{8,24},{16,0},{24,8},{1,17},{9,25},{17,1},{25,9},{2,18},{10... | collective-permute-start | bytes 1572872 | tf_op jit(solution)/shard_map/ppermute | solution.py:27
  168.9 13.4 %collective-permute-start.43 = (bf16[2,128,1024]{2,1,0:T(8,128)(2,1)S(1)}, bf16[2,128,1024]{2,1,0:T(8,128)(2,1)S(1)}, u32[]{:S(2)}, u32[]{:S(2)}) collective-permute-start(bf16[2,128,1024]{2,1,0:T(8,128)(2,1)S(1)} %pad_maximum_fusion.2), channel_id=1, source_target_pairs={{0,8},{8,0},{16,24},{24,16},{1,9},{9,1},{17,25},{25,17},{2,10},{10... | collective-permute-start | bytes 1572872 | tf_op jit(solution)/shard_map/ppermute | solution.py:27
  172.2 7.3 %collective-permute-start.36 = (bf16[1024,128]{1,0:T(8,128)(2,1)S(1)}, bf16[1024,128]{1,0:T(8,128)(2,1)S(1)}, u32[]{:S(2)}, u32[]{:S(2)}) collective-permute-start(bf16[1024,128]{1,0:T(8,128)(2,1)S(1)} %gated_signal.6.refs_0_), channel_id=1, source_target_pairs={{0,2},{1,3},{2,4},{3,5},{4,6},{5,7},{6,0},{7,1},{8,10},{9,11},{10,... | collective-permute-start | bytes 786440 | tf_op jit(solution)/shard_map/ppermute | solution.py:459
  174.2 8.1 %collective-permute-start.39 = (bf16[1024,128]{1,0:T(8,128)(2,1)S(1)}, bf16[1024,128]{1,0:T(8,128)(2,1)S(1)}, u32[]{:S(2)}, u32[]{:S(2)}) collective-permute-start(bf16[1024,128]{1,0:T(8,128)(2,1)S(1)} %gated_signal.7.refs_1_), channel_id=1, source_target_pairs={{0,2},{1,3},{2,4},{3,5},{4,6},{5,7},{6,0},{7,1},{8,10},{9,11},{10,... | collective-permute-start | bytes 786440 | tf_op jit(solution)/shard_map/ppermute | solution.py:459
  183.1 15.2 %collective-permute-start.44 = (bf16[2,128,1024]{2,1,0:T(8,128)(2,1)}, bf16[2,128,1024]{2,1,0:T(8,128)(2,1)}, u32[]{:S(2)}, u32[]{:S(2)}) collective-permute-start(bf16[2,128,1024]{2,1,0:T(8,128)(2,1)} %collective-permute-done.42), channel_id=1, source_target_pairs={{0,8},{8,0},{16,24},{24,16},{1,9},{9,1},{17,25},{25,17},{2,10},{10... | collective-permute-start | bytes 1572872 | tf_op jit(solution)/shard_map/ppermute | solution.py:27
  184.3 8.4 %collective-permute-start.37 = (bf16[1024,128]{1,0:T(8,128)(2,1)S(1)}, bf16[1024,128]{1,0:T(8,128)(2,1)S(1)}, u32[]{:S(2)}, u32[]{:S(2)}) collective-permute-start(bf16[1024,128]{1,0:T(8,128)(2,1)S(1)} %collective-permute-done.36.refs_2_), channel_id=1, source_target_pairs={{0,2},{1,3},{2,4},{3,5},{4,6},{5,7},{6,0},{7,1},{8,10},{9,11},{10,... | collective-permute-start | bytes 786440 | tf_op jit(solution)/shard_map/ppermute | solution.py:459
  184.3 14.0 %collective-permute-start.40 = (bf16[1024,128]{1,0:T(8,128)(2,1)S(1)}, bf16[1024,128]{1,0:T(8,128)(2,1)S(1)}, u32[]{:S(2)}, u32[]{:S(2)}) collective-permute-start(bf16[1024,128]{1,0:T(8,128)(2,1)S(1)} %collective-permute-done.39.refs_3_), channel_id=1, source_target_pairs={{0,2},{1,3},{2,4},{3,5},{4,6},{5,7},{6,0},{7,1},{8,10},{9,11},{10,... | collective-permute-start | bytes 786440 | tf_op jit(solution)/shard_map/ppermute | solution.py:459
  186.3 14.6 %collective-permute-start.45 = (bf16[2,128,1024]{2,1,0:T(8,128)(2,1)}, bf16[2,128,1024]{2,1,0:T(8,128)(2,1)}, u32[]{:S(2)}, u32[]{:S(2)}) collective-permute-start(bf16[2,128,1024]{2,1,0:T(8,128)(2,1)} %copy-done.34), channel_id=1, source_target_pairs={{0,16},{8,24},{16,0},{24,8},{1,17},{9,25},{17,1},{25,9},{2,18},{10... | collective-permute-start | bytes 1572872 | tf_op jit(solution)/shard_map/ppermute | solution.py:27
  186.6 15.4 %collective-permute-start.46 = (bf16[2,128,1024]{2,1,0:T(8,128)(2,1)}, bf16[2,128,1024]{2,1,0:T(8,128)(2,1)S(1)}, u32[]{:S(2)}, u32[]{:S(2)}) collective-permute-start(bf16[2,128,1024]{2,1,0:T(8,128)(2,1)} %copy-done.33), channel_id=1, source_target_pairs={{0,8},{8,0},{16,24},{24,16},{1,9},{9,1},{17,25},{25,17},{2,10},{10... | collective-permute-start | bytes 1572872 | tf_op jit(solution)/shard_map/ppermute | solution.py:27
  188.9 14.4 %copy-start.35 = (bf16[2,128,1024]{2,1,0:T(8,128)(2,1)S(1)}, bf16[2,128,1024]{2,1,0:T(8,128)(2,1)}, u32[]{:S(2)}) copy-start(bf16[2,128,1024]{2,1,0:T(8,128)(2,1)} %copy-done.34) | copy-start | bytes 1572868
  192.7 10.6 %collective-permute-start.47 = (bf16[2,128,1024]{2,1,0:T(8,128)(2,1)S(1)}, bf16[2,128,1024]{2,1,0:T(8,128)(2,1)S(1)}, u32[]{:S(2)}, u32[]{:S(2)}) collective-permute-start(bf16[2,128,1024]{2,1,0:T(8,128)(2,1)S(1)} %copy-done.32), channel_id=1, source_target_pairs={{0,16},{8,24},{16,0},{24,8},{1,17},{9,25},{17,1},{25,9},{2,18},{10... | collective-permute-start | bytes 1572872 | tf_op jit(solution)/shard_map/ppermute | solution.py:27
  198.3 14.4 %collective-permute-start.38 = (bf16[1024,128]{1,0:T(8,128)(2,1)S(1)}, bf16[1024,128]{1,0:T(8,128)(2,1)S(1)}, u32[]{:S(2)}, u32[]{:S(2)}) collective-permute-start(bf16[1024,128]{1,0:T(8,128)(2,1)S(1)} %collective-permute-done.37.refs_4_), channel_id=1, source_target_pairs={{0,2},{1,3},{2,4},{3,5},{4,6},{5,7},{6,0},{7,1},{8,10},{9,11},{10,... | collective-permute-start | bytes 786440 | tf_op jit(solution)/shard_map/ppermute | solution.py:459
  198.3 14.4 %collective-permute-start.41 = (bf16[1024,128]{1,0:T(8,128)(2,1)S(1)}, bf16[1024,128]{1,0:T(8,128)(2,1)S(1)}, u32[]{:S(2)}, u32[]{:S(2)}) collective-permute-start(bf16[1024,128]{1,0:T(8,128)(2,1)S(1)} %collective-permute-done.40.refs_5_), channel_id=1, source_target_pairs={{0,2},{1,3},{2,4},{3,5},{4,6},{5,7},{6,0},{7,1},{8,10},{9,11},{10,... | collective-permute-start | bytes 786440 | tf_op jit(solution)/shard_map/ppermute | solution.py:459
  212.6 18.7 %copy-start.7 = (f32[5,16,256]{2,1,0:T(8,128)S(1)}, f32[5,16,256]{2,1,0:T(8,128)}, u32[]{:S(2)}) copy-start(f32[5,16,256]{2,1,0:T(8,128)} %copy-done.6) | copy-start | bytes 245764
  212.7 18.7 %copy-start.36 = (f32[4,16,512]{2,1,0:T(8,128)S(1)}, f32[4,16,512]{2,1,0:T(8,128)}, u32[]{:S(2)}) copy-start(f32[4,16,512]{2,1,0:T(8,128)} %get-tuple-element.105) | copy-start | bytes 393220
  212.7 18.7 %copy-start.45 = (f32[1,16,512]{2,1,0:T(8,128)S(1)}, f32[1,16,512]{2,1,0:T(8,128)}, u32[]{:S(2)}) copy-start(f32[1,16,512]{2,1,0:T(8,128)} %get-tuple-element.100) | copy-start | bytes 98308
  213.8 19.8 %collective-permute-start.48 = (bf16[1024,512]{1,0:T(8,128)(2,1)S(1)}, bf16[1024,512]{1,0:T(8,128)(2,1)S(1)}, u32[]{:S(2)}, u32[]{:S(2)}) collective-permute-start(bf16[1024,512]{1,0:T(8,128)(2,1)S(1)} %add_outputs.11), channel_id=1, source_target_pairs={{0,1},{1,0},{2,3},{3,2},{4,5},{5,4},{6,7},{7,6},{8,9},{9,8},{10,11... | collective-permute-start | bytes 3145736 | tf_op jit(solution)/shard_map/ppermute | solution.py:293
  (41 other events, 257.3 us)
Sparse Core Ops, SparseCore 0:
  10.2 87.5 all-gather.2

commit v5 on v4

--- a/solution.py
+++ b/solution.py
@@ -71,7 +71,7 @@
         shifted_start(v_ref, tail_v_ref, 2, segment),
         (zero,) * modes,
     )
-    state = lax.fori_loop(0, segment, step, carry, unroll=4)[4]
+    state = lax.fori_loop(0, segment, step, carry, unroll=16)[4]
     for n in range(modes):
         end = wide(scale_ref[n : n + 1, :]) * state[n]
         rows = slice(n * SEGMENTS, (n + 1) * SEGMENTS)
@@ -111,7 +111,7 @@
         return (q, q1, tuple(lam[n] * carried[n] for n in range(modes)))
 
     start = (shifted_start(q_ref, tail_q_ref, 1, segment), shifted_start(q_ref, tail_q_ref, 2, segment), carried)
-    lax.fori_loop(0, segment, step, start, unroll=4)
+    lax.fori_loop(0, segment, step, start, unroll=8)
     gated_ref[...] = wide_ref[...].astype(gated_ref.dtype)
 
 
@@ -213,7 +213,7 @@
         out_ref[...] = total(False) * inverse_ref[...]
 
 
-def project(everything, tails, units, order, inverse, tail_inverse):
+def project(everything, tails, units, order, inverse, tail_inverse, streamed):
     mp, tokens, features = everything.shape
     width = units[0].shape[1]
     tile = math.gcd(tokens, 256)
@@ -232,7 +232,10 @@
             in_specs=[
                 pl.BlockSpec((mp, tile, features), lambda m, order: (0, m, 0)),
                 pl.BlockSpec((mp, TAIL, features), lambda m, order: (0, 0, 0)),
-                *[pl.BlockSpec(memory_space=pltpu.VMEM) for _ in units],
+                *[
+                    pl.BlockSpec(unit.shape, lambda m, order: (0, 0)) if n < streamed else pl.BlockSpec(memory_space=pltpu.VMEM)
+                    for n, unit in enumerate(units)
+                ],
                 pl.BlockSpec((tile, 1), lambda m, order: (m, 0)),
                 pl.BlockSpec((TAIL, 1), lambda m, order: (0, 0)),
             ],
@@ -242,7 +245,7 @@
             ],
         ),
         out_shape=[jax.ShapeDtypeStruct((tokens, width), f32), jax.ShapeDtypeStruct((TAIL, width), f32)],
-        compiler_params=pltpu.CompilerParams(vmem_limit_bytes=40 * 2**20),
+        compiler_params=pltpu.CompilerParams(vmem_limit_bytes=(56 if streamed == len(units) else 40) * 2**20),
         name="project",
     )(order, everything, tails, *units, inverse, tail_inverse)
 
@@ -427,12 +430,12 @@
         taps = short_filter[:, :, span].reshape(3, 3 * share)
         if rings:
             order = lax.optimization_barrier((order, gated))[0]
-        projected, before = project(everything, tails_all, units[g], order, inverse, tail_inverse)
+        projected, before = project(everything, tails_all, units[g], order, inverse, tail_inverse, len(units[g]) if g == 0 else 1)
         if special and g > 0:
             rings[0].append(send([(block, *along_z) for block in rings[0][-1]], [before]))
         tails = jnp.where(me == 0, tails_in[:, :, span].reshape(2, 3 * share), before[TAIL - 2 :])
         if special and g > 0:
-            tails = lax.optimization_barrier((tails, rings[0][1]))[0]
+            tails = lax.optimization_barrier((tails, (*rings[0][1], *panel_top)))[0]
         response, ends, last = local_filter(projected, tails, taps, own)
         if special:
             shared = lax.optimization_barrier((last, by_chip[0] if g == 0 else rings[0][2]))[0]
@@ -463,7 +466,7 @@
                 top, bottom = rows[: chips // 2], rows[chips // 2 :]
                 panel_top = send([(top, *along_x), (top, *along_y)], gated)
             else:
-                panel_far = send([(panel_top[1], *along_x), (panel_bottom[0], *along_y)], blocks[1])
+                panel_far = send([(panel_top[1], *along_x), (panel_bottom[0], *along_y)], [*blocks[1][:1], panel_bottom[1]])
         else:
             gathered = [lax.all_gather(block, "mp", axis=0, axis_index_groups=groups_of_core) for block in gated]
             rings.append([[block[n] for block in gathered] for n in range(chips)])
@@ -477,16 +480,14 @@
         panel = panel.reshape(chips, channels, 2 * columns)
     mine, other = core[None].astype(jnp.int32), (1 - core)[None].astype(jnp.int32)
     kept, given = [activations], []
-    for g in range(groups):
-        final = g == groups - 1
-        steps = [slice(0, chips - 1), slice(chips - 1, chips)] if final else [slice(0, chips)]
-        for n, step in enumerate(steps):
-            dtype = bf16 if final and n == len(steps) - 1 else f32
-            last_step = rings[g][step]
-            if final and n == len(steps) - 1:
-                last_step = lax.optimization_barrier((last_step, (kept[0], given[0])))[0]
-            given = [add_outputs(last_step, panel_order[step], panel, g, other, given, dtype)]
-            kept = [add_outputs(last_step, panel_order[step], panel, g, mine, kept, f32)]
+    for g in range(groups - 1):
+        kept = [add_outputs(rings[g], panel_order, panel, g, mine, kept, f32)]
+    for g in range(groups - 1):
+        given = [add_outputs(rings[g], panel_order, panel, g, other, given, f32)]
+    given = [add_outputs(rings[-1][:-1], panel_order[:-1], panel, groups - 1, other, given, f32)]
+    rings[-1][-1] = lax.optimization_barrier((rings[-1][-1], (kept, given)))[0]
+    given = [add_outputs(rings[-1][-1:], panel_order[-1:], panel, groups - 1, other, given, bf16)]
+    kept = [add_outputs(rings[-1], panel_order, panel, groups - 1, mine, kept, f32)]
     total = (kept[0] + core_swap(given[0]).astype(f32)).astype(bf16)
     return (total, jnp.concatenate(finals, axis=1).T)
 

time: 243 us -> 232 us (0.955)
  local copies, waits for them, and re-layouts: 37.9 us -> 30.1 us
  starting transfers between devices: 69.7 us -> 62.4 us
  waiting for transfers between devices: 60.6 us -> 64.6 us
    unnamed x127 -> x125, local copies, waits for them, and re-layouts: 14.2 us -> 7.68 us
    ppermute x3, starting transfers between devices: 20.4 us -> 16.7 us  [core_swap(): return lax.ppermute(block, 'mp', swap_route(lax.axis_size('mp'), 1))]
    ppermute x6, waiting for transfers between devices: 4.24 us -> 7.12 us  [local(): lax.ppermute(shared, *route)]
    pallas_call x6 -> x5, Pallas kernels: 11.3 us -> 10.5 us  [add_outputs(): pl.pallas_call(functools.partial(output_kernel, [[0] * len(chip) for chip...]
  transfers between devices with their start and end apart: 50 -> 50, of which waited for: 19 -> 17; matrix products, arithmetic and copies ran while one was open for 14% -> 14% of each run, Pallas kernels for 19% -> 20%
where the time goes in v5:
time: 232 us; the launch traced here: 231 us
  waiting for transfers between devices  64.6 us (28%)
  starting transfers between devices  62.4 us (27%)
  Pallas kernels  46.8 us (20%)
  local copies, waits for them, and re-layouts  30.1 us (13%)
  between operations  15.1 us (7%)
  other arithmetic  11.7 us (5%)
    pallas_call x2, Pallas kernels, project(): pl.pallas_call(functools.partial(project_kernel, chunks), grid_spec=pltpu...  22.7 us
    ppermute x10, waiting for transfers between devices, local(): blocks.append([lax.ppermute(block, *along_z) for block in blocks[-1]])  22.4 us
    ppermute x19, waiting for transfers between devices, send(): lax.ppermute(arrays[id(array)], axis, route)  20.5 us
    ppermute x19, starting transfers between devices, send(): lax.ppermute(arrays[id(array)], axis, route)  18.8 us
    ppermute x3, starting transfers between devices, core_swap(): return lax.ppermute(block, 'mp', swap_route(lax.axis_size('mp'), 1))  16.7 us
    ppermute x1, waiting for transfers between devices, local(): tails_all = lax.ppermute(scaled[-TAIL:], *next_on)[None]  12.3 us
    pallas_call x5, Pallas kernels, add_outputs(): pl.pallas_call(functools.partial(output_kernel, [[0] * len(chip) for chip...  10.5 us
    pallas_call x2, Pallas kernels, local_filter(): pl.pallas_call(functools.partial(local_kernel, tokens // SEGMENTS, modes)...  8.63 us
  transfers between devices with their start and end apart: 50, of which 17 were waited for; matrix products, arithmetic and copies ran while one was open for 14% of the time, Pallas kernels for 20%

profile of v5, /device:TPU:1, one launch (start us, length us, event | category | flops | bytes accessed | tf_op | source)
XLA Modules:
  0.0 230.7 jit_solution(12653146581971908222)
XLA Ops:
  7.2 2.5 %fusion.1 = (f32[1024]{0:T(1024)S(1)}, bf16[1024,512]{1,0:T(8,128)(2,1)}) fusion(bf16[1024,512]{1,0:T(8,128)(2,1)} %refs_9_.1, f32[512]{0:T(512)} %param.11), kind=kLoop, calls=%fused_computation.3 | loop fusion | flops 2620416 | bytes 2103296 | tf_op jit(solution)/shard_map/reduce_sum | solution.py:372
  9.7 3.2 %fusion.11 = (bf16[1024,3,256]{2,0,1:T(8,128)(2,1)}, bf16[1024,3,256]{2,0,1:T(8,128)(2,1)S(1)}) fusion(bf16[1024,3,512]{2,0,1:T(8,128)(2,1)} %param.12), kind=kLoop, calls=%fused_computation.78 | loop fusion | bytes 6291456 | tf_op jit(solution)/shard_map/slice | solution.py:369
  14.6 2.1 collective-permute-start.5
  16.7 1.2 collective-permute-start.6
  18.0 1.2 collective-permute-start.7
  25.5 3.4 %collective-permute-start.10 = (f32[1,1024]{1,0:T(1,128)S(1)}, f32[1,1024]{1,0:T(1,128)S(1)}, u32[]{:S(2)}, u32[]{:S(2)}) collective-permute-start(f32[1,1024]{1,0:T(1,128)S(1)} %add.108), channel_id=1, source_target_pairs={{0,6},{1,7},{2,4},{3,5},{4,2},{5,3},{6,0},{7,1},{8,14},{9,15},{10,... | collective-permute-start | bytes 12296 | tf_op jit(solution)/shard_map/ppermute | solution.py:387
  30.0 1.7 copy.39
  32.4 2.1 collective-permute-start
  34.8 3.1 %collective-permute-start.13 = (f32[16,1]{1,0:T(8,128)S(1)}, f32[16,1]{1,0:T(8,128)S(1)}, u32[]{:S(2)}, u32[]{:S(2)}) collective-permute-start(f32[16,1]{1,0:T(8,128)S(1)} %copy.24), channel_id=1, source_target_pairs={{0,8},{8,16},{16,24},{1,9},{9,17},{17,25},{2,10},{10,18},{18,26},{... | collective-permute-start | bytes 200 | tf_op jit(solution)/shard_map/ppermute | solution.py:389
  37.8 12.3 %collective-permute-done = bf16[16,512]{1,0:T(8,128)(2,1)S(1)} collective-permute-done((bf16[16,512]{1,0:T(8,128)(2,1)S(1)}, bf16[16,512]{1,0:T(8,128)(2,1)S(1)}, u32[]{:S(2)}, u32[]{:S(2)}) %collective-permute-start) | collective-permute-done | bytes 16416 | tf_op jit(solution)/shard_map/ppermute | solution.py:371
  50.1 1.6 collective-permute-start.1
  51.8 1.2 slice.114
  53.0 2.3 collective-permute-start.11
  55.2 1.2 slice.115
  56.5 1.3 collective-permute-start.12
  57.8 1.3 collective-permute-start.2
  59.1 2.3 %collective-permute-start.3 = (bf16[2,16,512]{2,1,0:T(8,128)(2,1)S(1)}, bf16[2,16,512]{2,1,0:T(8,128)(2,1)S(1)}, u32[]{:S(2)}, u32[]{:S(2)}) collective-permute-start(bf16[2,16,512]{2,1,0:T(8,128)(2,1)S(1)} %pad_maximum_fusion.5), channel_id=1, source_target_pairs={{0,4},{1,5},{2,6},{3,7},{4,0},{5,1},{6,2},{7,3},{8,12},{9,13},{10,... | collective-permute-start | bytes 98312 | tf_op jit(solution)/shard_map/ppermute | solution.py:397
  61.7 1.4 collective-permute-start.16
  63.9 1.5 collective-permute-start.15
  65.4 1.3 collective-permute-done.4
  67.4 10.6 %collective-permute-done.16 = bf16[128,1024]{1,0:T(8,128)(2,1)S(1)} collective-permute-done((bf16[128,1024]{1,0:T(8,128)(2,1)}, bf16[128,1024]{1,0:T(8,128)(2,1)S(1)}, u32[]{:S(2)}, u32[]{:S(2)}) %collective-permute-start.16) | collective-permute-done | bytes 262176 | tf_op jit(solution)/shard_map/ppermute | solution.py:27
  78.0 8.8 %collective-permute-done.15 = bf16[128,1024]{1,0:T(8,128)(2,1)S(1)} collective-permute-done((bf16[128,1024]{1,0:T(8,128)(2,1)}, bf16[128,1024]{1,0:T(8,128)(2,1)S(1)}, u32[]{:S(2)}, u32[]{:S(2)}) %collective-permute-start.15) | collective-permute-done | bytes 262176 | tf_op jit(solution)/shard_map/ppermute | solution.py:27
  89.5 1.3 collective-permute-start.24
  91.6 1.3 pad_maximum_fusion
  94.0 1.2 collective-permute-start.17
  95.2 2.3 collective-permute-start.21
  99.2 12.7 %project.2 = (f32[1024,768]{1,0:T(8,128)}, f32[16,768]{1,0:T(8,128)}) custom-call(s32[16]{0:T(128)} %concatenate.29.order_ref, bf16[8,1024,512]{2,1,0:T(8,128)(2,1)} %bitcast.156, bf16[8,16,512]{2,1,0:T(8,128)(2,1)} %copy-done.15, bf16[1024,768]{1,0:T(8,128)(2,1)} %copy-done.26, bf16[1024,768]{1,0:T(8,128)(2,1)} %collective-permute-done.5.refs_1_, ...), custom_call_target="tpu_custom_call" | custom-call | tf_op jit(solution)/shard_map/project/pallas_call | solution.py:227
  112.6 1.9 copy-done
  114.5 4.3 %local_filter.2 = (f32[1024,256]{1,0:T(8,128)S(1)}, f32[128,256]{1,0:T(8,128)S(1)}, f32[16,256]{1,0:T(8,128)S(1)}) custom-call(f32[1024,768]{1,0:T(8,128)S(1)} %copy-done, f32[1024,768]{1,0:T(8,128)S(1)} %copy-done, f32[2,768]{1,0:T(2,128)S(1)} %slice_select_fusion.1.tail_k_ref.tail_v_ref.tail_q_ref, ...), custom_call_target="tpu_custom_call" | custom-call | bytes 3145728 | tf_op jit(solution)/shard_map/local_filter/pallas_call | solution.py:127
  118.9 1.5 collective-permute-start.18
  121.6 3.3 %collective-permute-done.18 = f32[16,256]{1,0:T(8,128)S(1)} collective-permute-done((f32[16,256]{1,0:T(8,128)S(1)}, f32[16,256]{1,0:T(8,128)S(1)}, u32[]{:S(2)}, u32[]{:S(2)}) %collective-permute-start.18) | collective-permute-done | bytes 16416 | tf_op jit(solution)/shard_map/ppermute | solution.py:442
  125.8 1.2 slice.131
  127.6 1.3 collective-permute-start.26
  128.9 1.2 gated_signal.4.refs_0_
  130.2 1.2 collective-permute-start.27
  131.4 1.2 gated_signal.5.refs_1_
  132.7 1.3 collective-permute-start.28
  135.2 2.0 collective-permute-done.27.refs_2_
  137.5 5.1 %collective-permute-done.28.refs_3_ = bf16[1024,128]{1,0:T(8,128)(2,1)S(1)} collective-permute-done((bf16[1024,128]{1,0:T(8,128)(2,1)S(1)}, bf16[1024,128]{1,0:T(8,128)(2,1)S(1)}, u32[]{:S(2)}, u32[]{:S(2)}) %collective-permute-start.28) | collective-permute-done | bytes 262176 | tf_op jit(solution)/shard_map/ppermute | solution.py:462
  143.7 1.3 collective-permute-start.32
  145.0 1.1 pad_maximum_fusion.2
  146.2 10.0 %project.3 = (f32[1024,768]{1,0:T(8,128)S(1)}, f32[16,768]{1,0:T(8,128)S(1)}) custom-call(s32[16]{0:T(128)S(1)} %copy-done.25, bf16[8,1024,512]{2,1,0:T(8,128)(2,1)} %bitcast.157, bf16[8,16,512]{2,1,0:T(8,128)(2,1)S(1)} %copy-done.16, bf16[1024,768]{1,0:T(8,128)(2,1)S(1)} %copy.30.refs_0_, bf16[1024,768]{1,0:T(8,128)(2,1)S(1)} %collective-permute-done.23.refs_1_, ...), custom_call_target="tpu_custom_call" | custom-call | tf_op jit(solution)/shard_map/project/pallas_call | solution.py:227
  156.2 1.3 collective-permute-start.36
  158.7 4.3 %local_filter.3 = (f32[1024,256]{1,0:T(8,128)S(1)}, f32[128,256]{1,0:T(8,128)S(1)}, f32[16,256]{1,0:T(8,128)S(1)}) custom-call(f32[1024,768]{1,0:T(8,128)S(1)} %get-tuple-element.64.k_ref.v_ref.q_ref, f32[1024,768]{1,0:T(8,128)S(1)} %get-tuple-element.64.k_ref.v_ref.q_ref, f32[2,768]{1,0:T(2,128)S(1)} %slice_select_fusion.tail_k_ref.tail_v_ref.tail_q_ref, ...), custom_call_target="tpu_custom_call" | custom-call | bytes 3145728 | tf_op jit(solution)/shard_map/local_filter/pallas_call | solution.py:127
  163.9 1.2 collective-permute-start.34
  166.4 2.4 %collective-permute-done.35 = f32[16,256]{1,0:T(8,128)S(1)} collective-permute-done((f32[16,256]{1,0:T(8,128)S(1)}, f32[16,256]{1,0:T(8,128)S(1)}, u32[]{:S(2)}, u32[]{:S(2)}) %collective-permute-start.35) | collective-permute-done | bytes 16416 | tf_op jit(solution)/shard_map/ppermute | solution.py:442
  169.9 1.2 gated_signal.6.refs_0_
  171.3 1.2 gated_signal.7.refs_1_
  172.5 1.2 collective-permute-start.39
  173.7 4.5 %collective-permute-done.38.refs_2_ = bf16[1024,128]{1,0:T(8,128)(2,1)S(1)} collective-permute-done((bf16[1024,128]{1,0:T(8,128)(2,1)S(1)}, bf16[1024,128]{1,0:T(8,128)(2,1)S(1)}, u32[]{:S(2)}, u32[]{:S(2)}) %collective-permute-start.38) | collective-permute-done | bytes 262176 | tf_op jit(solution)/shard_map/ppermute | solution.py:462
  179.1 2.0 collective-permute-done.39.refs_3_
  182.6 1.3 fusion.2
  183.9 3.1 %collective-permute-done.40.refs_4_ = bf16[1024,128]{1,0:T(8,128)(2,1)S(1)} collective-permute-done((bf16[1024,128]{1,0:T(8,128)(2,1)S(1)}, bf16[1024,128]{1,0:T(8,128)(2,1)S(1)}, u32[]{:S(2)}, u32[]{:S(2)}) %collective-permute-start.40) | collective-permute-done | bytes 262176 | tf_op jit(solution)/shard_map/ppermute | solution.py:462
  187.0 5.6 %collective-permute-done.41.refs_5_ = bf16[1024,128]{1,0:T(8,128)(2,1)S(1)} collective-permute-done((bf16[1024,128]{1,0:T(8,128)(2,1)S(1)}, bf16[1024,128]{1,0:T(8,128)(2,1)S(1)}, u32[]{:S(2)}, u32[]{:S(2)}) %collective-permute-start.41) | collective-permute-done | bytes 262176 | tf_op jit(solution)/shard_map/ppermute | solution.py:462
  192.6 1.1 bitcast_dynamic-update-slice_fusion.4
  193.7 1.1 bitcast_dynamic-update-slice_fusion.3
  195.0 1.2 bitcast_dynamic-update-slice_fusion.1
  196.2 1.1 bitcast_dynamic-update-slice_fusion
  197.4 2.4 %add_outputs.6.refs_7_ = f32[1024,512]{1,0:T(8,128)S(1)} custom-call(s32[4]{0:T(128)S(1)} %pad_add_fusion.order_ref, s32[1]{0:T(128)} %bitcast.72.half_ref, bf16[1024,128]{1,0:T(8,128)(2,1)S(1)} %gated_signal.4.refs_0_, bf16[1024,128]{1,0:T(8,128)(2,1)S(1)} %copy-done.4, bf16[1024,128]{1,0:T(8,128)(2,1)S(1)} %copy-done.6, bf16[1024,128]{1,0:T(8,128)(2,1)S(1)} %copy-done.8, ...), custom_call_target="tpu_custom_call" | custom-call | flops 2147483648 | bytes 2097152 | tf_op jit(solution)/shard_map/add_outputs/pallas_call | solution.py:274
  199.8 2.2 add_outputs.7.refs_3_
  202.0 2.4 %add_outputs.5.refs_9_ = f32[1024,512]{1,0:T(8,128)S(1)} custom-call(s32[4]{0:T(128)S(1)} %pad_add_fusion.order_ref, s32[1]{0:T(128)} %bitcast.4.half_ref, bf16[1024,128]{1,0:T(8,128)(2,1)S(1)} %gated_signal.4.refs_0_, bf16[1024,128]{1,0:T(8,128)(2,1)S(1)} %copy-done.4, bf16[1024,128]{1,0:T(8,128)(2,1)S(1)} %copy-done.6, bf16[1024,128]{1,0:T(8,128)(2,1)S(1)} %copy-done.8, ...), custom_call_target="tpu_custom_call" | custom-call | flops 2147483648 | bytes 2097152 | tf_op jit(solution)/shard_map/add_outputs/pallas_call | solution.py:274
  205.6 13.9 %collective-permute-start.48 = (bf16[1024,512]{1,0:T(8,128)(2,1)S(1)}, bf16[1024,512]{1,0:T(8,128)(2,1)S(1)}, u32[]{:S(2)}, u32[]{:S(2)}) collective-permute-start(bf16[1024,512]{1,0:T(8,128)(2,1)S(1)} %add_outputs.9), channel_id=1, source_target_pairs={{0,1},{1,0},{2,3},{3,2},{4,5},{5,4},{6,7},{7,6},{8,9},{9,8},{10,11... | collective-permute-start | bytes 3145736 | tf_op jit(solution)/shard_map/ppermute | solution.py:296
  220.1 2.4 %add_outputs.8 = f32[1024,512]{1,0:T(8,128)S(1)} custom-call(s32[4]{0:T(128)S(1)} %pad_add_fusion.order_ref, s32[1]{0:T(128)} %bitcast.4.half_ref, bf16[1024,128]{1,0:T(8,128)(2,1)S(1)} %gated_signal.6.refs_0_, bf16[1024,128]{1,0:T(8,128)(2,1)S(1)} %gated_signal.7.refs_1_, bf16[1024,128]{1,0:T(8,128)(2,1)S(1)} %collective-permute-done.38.refs_2_, ...), custom_call_target="tpu_custom_call" | custom-call | flops 2147483648 | bytes 2097152 | tf_op jit(solution)/shard_map/add_outputs/pallas_call | solution.py:274
  222.5 1.3 add_convert_fusion
  (234 shorter events, 32.5 us)
Async XLA Ops:
  7.2 92.0 %all-gather.3.cloned.1.call-start = ((), (), s32[]{:S(2)}) async-start(), calls=%async_computation | async-start | bytes 9437184 | tf_op jit(solution)/shard_map/all_gather | solution.py:368
  14.6 17.2 %copy-start.26 = (bf16[1024,768]{1,0:T(8,128)(2,1)}, bf16[1024,768]{1,0:T(8,128)(2,1)S(1)}, u32[]{:S(2)}) copy-start(bf16[1024,768]{1,0:T(8,128)(2,1)S(1)} %copy.25.refs_0_) | copy-start | bytes 4718596
  14.6 37.2 %collective-permute-start.5 = (bf16[1024,768]{1,0:T(8,128)(2,1)S(1)}, bf16[1024,768]{1,0:T(8,128)(2,1)}, u32[]{:S(2)}, u32[]{:S(2)}) collective-permute-start(bf16[1024,768]{1,0:T(8,128)(2,1)S(1)} %copy.25.refs_0_), channel_id=1, source_target_pairs={{0,8},{8,0},{16,24},{24,16},{1,9},{9,1},{17,25},{25,17},{2,10},{10... | collective-permute-start | bytes 4718600 | tf_op jit(solution)/shard_map/ppermute | solution.py:27
  16.7 35.1 %collective-permute-start.6 = (bf16[1024,768]{1,0:T(8,128)(2,1)S(1)}, bf16[1024,768]{1,0:T(8,128)(2,1)}, u32[]{:S(2)}, u32[]{:S(2)}) collective-permute-start(bf16[1024,768]{1,0:T(8,128)(2,1)S(1)} %copy.25.refs_0_), channel_id=1, source_target_pairs={{0,16},{8,24},{16,0},{24,8},{1,17},{9,25},{17,1},{25,9},{2,18},{10... | collective-permute-start | bytes 4718600 | tf_op jit(solution)/shard_map/ppermute | solution.py:27
  18.0 7.5 %collective-permute-start.7 = (f32[1,1024]{1,0:T(1,128)S(1)}, f32[1,1024]{1,0:T(1,128)S(1)}, u32[]{:S(2)}, u32[]{:S(2)}) collective-permute-start(f32[1,1024]{1,0:T(1,128)S(1)} %bitcast.174), channel_id=1, source_target_pairs={{0,1},{1,0},{2,3},{3,2},{4,5},{5,4},{6,7},{7,6},{8,9},{9,8},{10,11... | collective-permute-start | bytes 12296 | tf_op jit(solution)/shard_map/ppermute | solution.py:296
  25.5 6.9 %collective-permute-start.10 = (f32[1,1024]{1,0:T(1,128)S(1)}, f32[1,1024]{1,0:T(1,128)S(1)}, u32[]{:S(2)}, u32[]{:S(2)}) collective-permute-start(f32[1,1024]{1,0:T(1,128)S(1)} %add.108), channel_id=1, source_target_pairs={{0,6},{1,7},{2,4},{3,5},{4,2},{5,3},{6,0},{7,1},{8,14},{9,15},{10,... | collective-permute-start | bytes 12296 | tf_op jit(solution)/shard_map/ppermute | solution.py:387
  28.9 5.7 %collective-permute-start.8 = (f32[1,1024]{1,0:T(1,128)S(1)}, f32[1,1024]{1,0:T(1,128)S(1)}, u32[]{:S(2)}, u32[]{:S(2)}) collective-permute-start(f32[1,1024]{1,0:T(1,128)S(1)} %add.108), channel_id=1, source_target_pairs={{0,2},{1,3},{2,0},{3,1},{4,6},{5,7},{6,4},{7,5},{8,10},{9,11},{10,... | collective-permute-start | bytes 12296 | tf_op jit(solution)/shard_map/ppermute | solution.py:387
  28.9 5.7 %collective-permute-start.9 = (f32[1,1024]{1,0:T(1,128)S(1)}, f32[1,1024]{1,0:T(1,128)S(1)}, u32[]{:S(2)}, u32[]{:S(2)}) collective-permute-start(f32[1,1024]{1,0:T(1,128)S(1)} %add.108), channel_id=1, source_target_pairs={{0,4},{1,5},{2,6},{3,7},{4,0},{5,1},{6,2},{7,3},{8,12},{9,13},{10,... | collective-permute-start | bytes 12296 | tf_op jit(solution)/shard_map/ppermute | solution.py:387
  32.4 17.7 %collective-permute-start = (bf16[16,512]{1,0:T(8,128)(2,1)S(1)}, bf16[16,512]{1,0:T(8,128)(2,1)S(1)}, u32[]{:S(2)}, u32[]{:S(2)}) collective-permute-start(bf16[16,512]{1,0:T(8,128)(2,1)S(1)} %slice.147), channel_id=1, source_target_pairs={{0,8},{8,16},{16,24},{1,9},{9,17},{17,25},{2,10},{10,18},{18,26},{... | collective-permute-start | bytes 49160 | tf_op jit(solution)/shard_map/ppermute | solution.py:371
  34.6 54.8 %copy-start.49 = (f32[1,1024]{1,0:T(1,128)}, f32[1,1024]{1,0:T(1,128)S(1)}, u32[]{:S(2)}) copy-start(f32[1,1024]{1,0:T(1,128)S(1)} %add_rsqrt_fusion) | copy-start | bytes 12292
  34.8 26.6 %collective-permute-start.13 = (f32[16,1]{1,0:T(8,128)S(1)}, f32[16,1]{1,0:T(8,128)S(1)}, u32[]{:S(2)}, u32[]{:S(2)}) collective-permute-start(f32[16,1]{1,0:T(8,128)S(1)} %copy.24), channel_id=1, source_target_pairs={{0,8},{8,16},{16,24},{1,9},{9,17},{17,25},{2,10},{10,18},{18,26},{... | collective-permute-start | bytes 200 | tf_op jit(solution)/shard_map/ppermute | solution.py:389
  50.1 7.6 %collective-permute-start.1 = (bf16[1,16,512]{2,1,0:T(8,128)(2,1)S(1)}, bf16[1,16,512]{2,1,0:T(8,128)(2,1)S(1)}, u32[]{:S(2)}, u32[]{:S(2)}) collective-permute-start(bf16[1,16,512]{2,1,0:T(8,128)(2,1)S(1)} %bitcast.167), channel_id=1, source_target_pairs={{0,1},{1,0},{2,3},{3,2},{4,5},{5,4},{6,7},{7,6},{8,9},{9,8},{10,11... | collective-permute-start | bytes 49160 | tf_op jit(solution)/shard_map/ppermute | solution.py:296
  53.0 33.8 %collective-permute-start.11 = (bf16[512,768]{1,0:T(8,128)(2,1)S(1)}, bf16[512,768]{1,0:T(8,128)(2,1)S(1)}, u32[]{:S(2)}, u32[]{:S(2)}) collective-permute-start(bf16[512,768]{1,0:T(8,128)(2,1)S(1)} %slice.114), channel_id=1, source_target_pairs={{0,8},{8,0},{16,24},{24,16},{1,9},{9,1},{17,25},{25,17},{2,10},{10... | collective-permute-start | bytes 2359304 | tf_op jit(solution)/shard_map/ppermute | solution.py:27
  56.5 34.3 %copy-start.52 = (f32[512]{0:T(512)S(1)}, f32[512]{0:T(512)}, u32[]{:S(2)}) copy-start(f32[512]{0:T(512)} %param.17) | copy-start | bytes 6148
  56.5 30.3 %collective-permute-start.12 = (bf16[512,768]{1,0:T(8,128)(2,1)S(1)}, bf16[512,768]{1,0:T(8,128)(2,1)S(1)}, u32[]{:S(2)}, u32[]{:S(2)}) collective-permute-start(bf16[512,768]{1,0:T(8,128)(2,1)S(1)} %slice.115), channel_id=1, source_target_pairs={{0,16},{8,24},{16,0},{24,8},{1,17},{9,25},{17,1},{25,9},{2,18},{10... | collective-permute-start | bytes 2359304 | tf_op jit(solution)/shard_map/ppermute | solution.py:27
  57.8 3.9 %collective-permute-start.2 = (bf16[2,16,512]{2,1,0:T(8,128)(2,1)S(1)}, bf16[2,16,512]{2,1,0:T(8,128)(2,1)S(1)}, u32[]{:S(2)}, u32[]{:S(2)}) collective-permute-start(bf16[2,16,512]{2,1,0:T(8,128)(2,1)S(1)} %pad_maximum_fusion.5), channel_id=1, source_target_pairs={{0,2},{1,3},{2,0},{3,1},{4,6},{5,7},{6,4},{7,5},{8,10},{9,11},{10,... | collective-permute-start | bytes 98312 | tf_op jit(solution)/shard_map/ppermute | solution.py:397
  59.1 4.8 %collective-permute-start.3 = (bf16[2,16,512]{2,1,0:T(8,128)(2,1)S(1)}, bf16[2,16,512]{2,1,0:T(8,128)(2,1)S(1)}, u32[]{:S(2)}, u32[]{:S(2)}) collective-permute-start(bf16[2,16,512]{2,1,0:T(8,128)(2,1)S(1)} %pad_maximum_fusion.5), channel_id=1, source_target_pairs={{0,4},{1,5},{2,6},{3,7},{4,0},{5,1},{6,2},{7,3},{8,12},{9,13},{10,... | collective-permute-start | bytes 98312 | tf_op jit(solution)/shard_map/ppermute | solution.py:397
  61.4 30.2 %copy-start.23 = (f32[16,1]{1,0:T(8,128)}, f32[16,1]{1,0:T(8,128)S(1)}, u32[]{:S(2)}) copy-start(f32[16,1]{1,0:T(8,128)S(1)} %collective-permute-done.13.refs_6_) | copy-start | bytes 196
  61.4 5.3 %collective-permute-start.4 = (bf16[2,16,512]{2,1,0:T(8,128)(2,1)S(1)}, bf16[2,16,512]{2,1,0:T(8,128)(2,1)S(1)}, u32[]{:S(2)}, u32[]{:S(2)}) collective-permute-start(bf16[2,16,512]{2,1,0:T(8,128)(2,1)S(1)} %pad_maximum_fusion.5), channel_id=1, source_target_pairs={{0,6},{1,7},{2,4},{3,5},{4,2},{5,3},{6,0},{7,1},{8,14},{9,15},{10,... | collective-permute-start | bytes 98312 | tf_op jit(solution)/shard_map/ppermute | solution.py:397
  61.7 16.3 %collective-permute-start.16 = (bf16[128,1024]{1,0:T(8,128)(2,1)}, bf16[128,1024]{1,0:T(8,128)(2,1)S(1)}, u32[]{:S(2)}, u32[]{:S(2)}) collective-permute-start(bf16[128,1024]{1,0:T(8,128)(2,1)} %get-tuple-element.55), channel_id=1, source_target_pairs={{0,24},{8,16},{16,8},{24,0},{1,25},{9,17},{17,9},{25,1},{2,26},{10... | collective-permute-start | bytes 786440 | tf_op jit(solution)/shard_map/ppermute | solution.py:27
  63.9 22.9 %collective-permute-start.15 = (bf16[128,1024]{1,0:T(8,128)(2,1)}, bf16[128,1024]{1,0:T(8,128)(2,1)S(1)}, u32[]{:S(2)}, u32[]{:S(2)}) collective-permute-start(bf16[128,1024]{1,0:T(8,128)(2,1)} %get-tuple-element.54), channel_id=1, source_target_pairs={{0,16},{8,24},{16,0},{24,8},{1,17},{9,25},{17,1},{25,9},{2,18},{10... | collective-permute-start | bytes 786440 | tf_op jit(solution)/shard_map/ppermute | solution.py:27
  66.7 20.1 %collective-permute-start.14 = (bf16[128,1024]{1,0:T(8,128)(2,1)}, bf16[128,1024]{1,0:T(8,128)(2,1)S(1)}, u32[]{:S(2)}, u32[]{:S(2)}) collective-permute-start(bf16[128,1024]{1,0:T(8,128)(2,1)} %get-tuple-element.53), channel_id=1, source_target_pairs={{0,8},{8,0},{16,24},{24,16},{1,9},{9,1},{17,25},{25,17},{2,10},{10... | collective-permute-start | bytes 786440 | tf_op jit(solution)/shard_map/ppermute | solution.py:27
  67.4 25.6 %copy-start.15 = (bf16[8,16,512]{2,1,0:T(8,128)(2,1)}, bf16[8,16,512]{2,1,0:T(8,128)(2,1)S(1)}, u32[]{:S(2)}) copy-start(bf16[8,16,512]{2,1,0:T(8,128)(2,1)S(1)} %constant_dynamic-update-slice_fusion.tails_ref) | copy-start | bytes 393220
  89.4 36.3 %collective-permute-start.23 = (bf16[1024,768]{1,0:T(8,128)(2,1)S(1)}, bf16[1024,768]{1,0:T(8,128)(2,1)S(1)}, u32[]{:S(2)}, u32[]{:S(2)}) collective-permute-start(bf16[1024,768]{1,0:T(8,128)(2,1)S(1)} %copy.30.refs_0_), channel_id=1, source_target_pairs={{0,8},{8,0},{16,24},{24,16},{1,9},{9,1},{17,25},{25,17},{2,10},{10... | collective-permute-start | bytes 4718600 | tf_op jit(solution)/shard_map/ppermute | solution.py:27
  89.5 36.3 %collective-permute-start.24 = (bf16[1024,768]{1,0:T(8,128)(2,1)S(1)}, bf16[1024,768]{1,0:T(8,128)(2,1)}, u32[]{:S(2)}, u32[]{:S(2)}) collective-permute-start(bf16[1024,768]{1,0:T(8,128)(2,1)S(1)} %copy.30.refs_0_), channel_id=1, source_target_pairs={{0,16},{8,24},{16,0},{24,8},{1,17},{9,25},{17,1},{25,9},{2,18},{10... | collective-permute-start | bytes 4718600 | tf_op jit(solution)/shard_map/ppermute | solution.py:27
  94.0 24.9 %collective-permute-start.17 = (bf16[128,1024]{1,0:T(8,128)(2,1)}, bf16[128,1024]{1,0:T(8,128)(2,1)}, u32[]{:S(2)}, u32[]{:S(2)}) collective-permute-start(bf16[128,1024]{1,0:T(8,128)(2,1)} %get-tuple-element.89), channel_id=1, source_target_pairs={{0,2},{1,3},{2,0},{3,1},{4,6},{5,7},{6,4},{7,5},{8,10},{9,11},{10,... | collective-permute-start | bytes 786440 | tf_op jit(solution)/shard_map/ppermute | solution.py:405
  95.2 25.1 %collective-permute-start.21 = (bf16[128,1024]{1,0:T(8,128)(2,1)}, bf16[128,1024]{1,0:T(8,128)(2,1)}, u32[]{:S(2)}, u32[]{:S(2)}) collective-permute-start(bf16[128,1024]{1,0:T(8,128)(2,1)} %get-tuple-element.88), channel_id=1, source_target_pairs={{0,4},{1,5},{2,6},{3,7},{4,0},{5,1},{6,2},{7,3},{8,12},{9,13},{10,... | collective-permute-start | bytes 786440 | tf_op jit(solution)/shard_map/ppermute | solution.py:405
  97.5 23.2 %collective-permute-start.22 = (bf16[128,1024]{1,0:T(8,128)(2,1)}, bf16[128,1024]{1,0:T(8,128)(2,1)}, u32[]{:S(2)}, u32[]{:S(2)}) collective-permute-start(bf16[128,1024]{1,0:T(8,128)(2,1)} %get-tuple-element.87), channel_id=1, source_target_pairs={{0,6},{1,7},{2,4},{3,5},{4,2},{5,3},{6,0},{7,1},{8,14},{9,15},{10,... | collective-permute-start | bytes 786440 | tf_op jit(solution)/shard_map/ppermute | solution.py:405
  118.9 6.0 %collective-permute-start.18 = (f32[16,256]{1,0:T(8,128)S(1)}, f32[16,256]{1,0:T(8,128)S(1)}, u32[]{:S(2)}, u32[]{:S(2)}) collective-permute-start(f32[16,256]{1,0:T(8,128)S(1)} %get-tuple-element.56), channel_id=1, source_target_pairs={{0,8},{8,0},{16,24},{24,16},{1,9},{9,1},{17,25},{25,17},{2,10},{10... | collective-permute-start | bytes 49160 | tf_op jit(solution)/shard_map/ppermute | solution.py:442
  120.3 4.5 %collective-permute-start.19 = (f32[16,256]{1,0:T(8,128)S(1)}, f32[16,256]{1,0:T(8,128)S(1)}, u32[]{:S(2)}, u32[]{:S(2)}) collective-permute-start(f32[16,256]{1,0:T(8,128)S(1)} %get-tuple-element.56), channel_id=1, source_target_pairs={{0,16},{8,24},{16,0},{24,8},{1,17},{9,25},{17,1},{25,9},{2,18},{10... | collective-permute-start | bytes 49160 | tf_op jit(solution)/shard_map/ppermute | solution.py:442
  120.7 5.1 %collective-permute-start.20 = (f32[16,256]{1,0:T(8,128)S(1)}, f32[16,256]{1,0:T(8,128)S(1)}, u32[]{:S(2)}, u32[]{:S(2)}) collective-permute-start(f32[16,256]{1,0:T(8,128)S(1)} %get-tuple-element.56), channel_id=1, source_target_pairs={{0,24},{8,16},{16,8},{24,0},{1,25},{9,17},{17,9},{25,1},{2,26},{10... | collective-permute-start | bytes 49160 | tf_op jit(solution)/shard_map/ppermute | solution.py:442
  127.0 16.7 %collective-permute-start.25 = (bf16[512,768]{1,0:T(8,128)(2,1)S(1)}, bf16[512,768]{1,0:T(8,128)(2,1)S(1)}, u32[]{:S(2)}, u32[]{:S(2)}) collective-permute-start(bf16[512,768]{1,0:T(8,128)(2,1)S(1)} %slice.131), channel_id=1, source_target_pairs={{0,8},{8,0},{16,24},{24,16},{1,9},{9,1},{17,25},{25,17},{2,10},{10... | collective-permute-start | bytes 2359304 | tf_op jit(solution)/shard_map/ppermute | solution.py:27
  127.6 18.6 %collective-permute-start.26 = (bf16[512,768]{1,0:T(8,128)(2,1)S(1)}, bf16[512,768]{1,0:T(8,128)(2,1)S(1)}, u32[]{:S(2)}, u32[]{:S(2)}) collective-permute-start(bf16[512,768]{1,0:T(8,128)(2,1)S(1)} %slice.132), channel_id=1, source_target_pairs={{0,16},{8,24},{16,0},{24,8},{1,17},{9,25},{17,1},{25,9},{2,18},{10... | collective-permute-start | bytes 2359304 | tf_op jit(solution)/shard_map/ppermute | solution.py:27
  130.1 14.8 %copy-start.43 = (f32[1,3,3,256]{3,2,1,0:T(4,128)S(1)}, f32[1,3,3,256]{3,2,1,0:T(4,128)}, u32[]{:S(2)}) copy-start(f32[1,3,3,256]{3,2,1,0:T(4,128)} %get-tuple-element.119) | copy-start | bytes 27652
  130.2 7.1 %collective-permute-start.27 = (bf16[1024,128]{1,0:T(8,128)(2,1)S(1)}, bf16[1024,128]{1,0:T(8,128)(2,1)S(1)}, u32[]{:S(2)}, u32[]{:S(2)}) collective-permute-start(bf16[1024,128]{1,0:T(8,128)(2,1)S(1)} %gated_signal.4.refs_0_), channel_id=1, source_target_pairs={{0,2},{1,3},{2,4},{3,5},{4,6},{5,7},{6,0},{7,1},{8,10},{9,11},{10,... | collective-permute-start | bytes 786440 | tf_op jit(solution)/shard_map/ppermute | solution.py:462
  132.7 13.5 %copy-start.1 = (f32[1024,1]{1,0:T(8,128)S(1)}, f32[1024,1]{1,0:T(8,128)}, u32[]{:S(2)}) copy-start(f32[1024,1]{1,0:T(8,128)} %copy.26.refs_5_) | copy-start | bytes 12292
  132.7 13.5 %copy-start.16 = (bf16[8,16,512]{2,1,0:T(8,128)(2,1)S(1)}, bf16[8,16,512]{2,1,0:T(8,128)(2,1)}, u32[]{:S(2)}) copy-start(bf16[8,16,512]{2,1,0:T(8,128)(2,1)} %copy-done.15) | copy-start | bytes 393220
  132.7 13.5 %copy-start.24 = (f32[16,1]{1,0:T(8,128)S(1)}, f32[16,1]{1,0:T(8,128)}, u32[]{:S(2)}) copy-start(f32[16,1]{1,0:T(8,128)} %copy-done.23) | copy-start | bytes 196
  132.7 13.5 %copy-start.25 = (s32[16]{0:T(128)S(1)}, s32[16]{0:T(128)}, u32[]{:S(2)}) copy-start(s32[16]{0:T(128)} %concatenate.29.order_ref) | copy-start | bytes 196
  132.7 9.9 %collective-permute-start.28 = (bf16[1024,128]{1,0:T(8,128)(2,1)S(1)}, bf16[1024,128]{1,0:T(8,128)(2,1)S(1)}, u32[]{:S(2)}, u32[]{:S(2)}) collective-permute-start(bf16[1024,128]{1,0:T(8,128)(2,1)S(1)} %gated_signal.5.refs_1_), channel_id=1, source_target_pairs={{0,2},{1,3},{2,4},{3,5},{4,6},{5,7},{6,0},{7,1},{8,10},{9,11},{10,... | collective-permute-start | bytes 786440 | tf_op jit(solution)/shard_map/ppermute | solution.py:462
  135.0 23.6 %collective-permute-start.29 = (bf16[2,128,1024]{2,1,0:T(8,128)(2,1)S(1)}, bf16[2,128,1024]{2,1,0:T(8,128)(2,1)S(1)}, u32[]{:S(2)}, u32[]{:S(2)}) collective-permute-start(bf16[2,128,1024]{2,1,0:T(8,128)(2,1)S(1)} %pad_maximum_fusion.1), channel_id=1, source_target_pairs={{0,8},{8,0},{16,24},{24,16},{1,9},{9,1},{17,25},{25,17},{2,10},{10... | collective-permute-start | bytes 1572872 | tf_op jit(solution)/shard_map/ppermute | solution.py:27
  137.2 19.0 %copy-start.5 = (bf16[1024,128]{1,0:T(8,128)(2,1)}, bf16[1024,128]{1,0:T(8,128)(2,1)S(1)}, u32[]{:S(2)}) copy-start(bf16[1024,128]{1,0:T(8,128)(2,1)S(1)} %collective-permute-done.27.refs_2_) | copy-start | bytes 786436
  137.2 21.4 %collective-permute-start.30 = (bf16[2,128,1024]{2,1,0:T(8,128)(2,1)S(1)}, bf16[2,128,1024]{2,1,0:T(8,128)(2,1)}, u32[]{:S(2)}, u32[]{:S(2)}) collective-permute-start(bf16[2,128,1024]{2,1,0:T(8,128)(2,1)S(1)} %pad_maximum_fusion.1), channel_id=1, source_target_pairs={{0,16},{8,24},{16,0},{24,8},{1,17},{9,25},{17,1},{25,9},{2,18},{10... | collective-permute-start | bytes 1572872 | tf_op jit(solution)/shard_map/ppermute | solution.py:27
  142.6 13.6 %copy-start.7 = (bf16[1024,128]{1,0:T(8,128)(2,1)}, bf16[1024,128]{1,0:T(8,128)(2,1)S(1)}, u32[]{:S(2)}) copy-start(bf16[1024,128]{1,0:T(8,128)(2,1)S(1)} %collective-permute-done.28.refs_3_) | copy-start | bytes 786436
  142.6 13.6 %collective-permute-start.31 = (bf16[1024,128]{1,0:T(8,128)(2,1)S(1)}, bf16[1024,128]{1,0:T(8,128)(2,1)S(1)}, u32[]{:S(2)}, u32[]{:S(2)}) collective-permute-start(bf16[1024,128]{1,0:T(8,128)(2,1)S(1)} %collective-permute-done.27.refs_2_), channel_id=1, source_target_pairs={{0,2},{1,3},{2,4},{3,5},{4,6},{5,7},{6,0},{7,1},{8,10},{9,11},{10,... | collective-permute-start | bytes 786440 | tf_op jit(solution)/shard_map/ppermute | solution.py:462
  143.7 12.6 %collective-permute-start.32 = (bf16[1024,128]{1,0:T(8,128)(2,1)S(1)}, bf16[1024,128]{1,0:T(8,128)(2,1)S(1)}, u32[]{:S(2)}, u32[]{:S(2)}) collective-permute-start(bf16[1024,128]{1,0:T(8,128)(2,1)S(1)} %collective-permute-done.28.refs_3_), channel_id=1, source_target_pairs={{0,2},{1,3},{2,4},{3,5},{4,6},{5,7},{6,0},{7,1},{8,10},{9,11},{10,... | collective-permute-start | bytes 786440 | tf_op jit(solution)/shard_map/ppermute | solution.py:462
  156.2 12.6 %collective-permute-start.36 = (bf16[1024,128]{1,0:T(8,128)(2,1)S(1)}, bf16[1024,128]{1,0:T(8,128)(2,1)S(1)}, u32[]{:S(2)}, u32[]{:S(2)}) collective-permute-start(bf16[1024,128]{1,0:T(8,128)(2,1)S(1)} %collective-permute-done.31.refs_4_), channel_id=1, source_target_pairs={{0,2},{1,3},{2,4},{3,5},{4,6},{5,7},{6,0},{7,1},{8,10},{9,11},{10,... | collective-permute-start | bytes 786440 | tf_op jit(solution)/shard_map/ppermute | solution.py:27
  157.6 11.2 %collective-permute-start.37 = (bf16[1024,128]{1,0:T(8,128)(2,1)S(1)}, bf16[1024,128]{1,0:T(8,128)(2,1)S(1)}, u32[]{:S(2)}, u32[]{:S(2)}) collective-permute-start(bf16[1024,128]{1,0:T(8,128)(2,1)S(1)} %collective-permute-done.32.refs_5_), channel_id=1, source_target_pairs={{0,2},{1,3},{2,4},{3,5},{4,6},{5,7},{6,0},{7,1},{8,10},{9,11},{10,... | collective-permute-start | bytes 786440 | tf_op jit(solution)/shard_map/ppermute | solution.py:27
  163.1 2.7 %collective-permute-start.33 = (f32[16,256]{1,0:T(8,128)S(1)}, f32[16,256]{1,0:T(8,128)S(1)}, u32[]{:S(2)}, u32[]{:S(2)}) collective-permute-start(f32[16,256]{1,0:T(8,128)S(1)} %get-tuple-element.71), channel_id=1, source_target_pairs={{0,8},{8,0},{16,24},{24,16},{1,9},{9,1},{17,25},{25,17},{2,10},{10... | collective-permute-start | bytes 49160 | tf_op jit(solution)/shard_map/ppermute | solution.py:442
  163.9 2.6 %collective-permute-start.34 = (f32[16,256]{1,0:T(8,128)S(1)}, f32[16,256]{1,0:T(8,128)S(1)}, u32[]{:S(2)}, u32[]{:S(2)}) collective-permute-start(f32[16,256]{1,0:T(8,128)S(1)} %get-tuple-element.71), channel_id=1, source_target_pairs={{0,16},{8,24},{16,0},{24,8},{1,17},{9,25},{17,1},{25,9},{2,18},{10... | collective-permute-start | bytes 49160 | tf_op jit(solution)/shard_map/ppermute | solution.py:442
  165.0 3.8 %collective-permute-start.35 = (f32[16,256]{1,0:T(8,128)S(1)}, f32[16,256]{1,0:T(8,128)S(1)}, u32[]{:S(2)}, u32[]{:S(2)}) collective-permute-start(f32[16,256]{1,0:T(8,128)S(1)} %get-tuple-element.71), channel_id=1, source_target_pairs={{0,24},{8,16},{16,8},{24,0},{1,25},{9,17},{17,9},{25,1},{2,26},{10... | collective-permute-start | bytes 49160 | tf_op jit(solution)/shard_map/ppermute | solution.py:442
  168.8 9.4 %collective-permute-start.44 = (bf16[2,128,1024]{2,1,0:T(8,128)(2,1)S(1)}, bf16[2,128,1024]{2,1,0:T(8,128)(2,1)}, u32[]{:S(2)}, u32[]{:S(2)}) collective-permute-start(bf16[2,128,1024]{2,1,0:T(8,128)(2,1)S(1)} %pad_maximum_fusion.2), channel_id=1, source_target_pairs={{0,8},{8,0},{16,24},{24,16},{1,9},{9,1},{17,25},{25,17},{2,10},{10... | collective-permute-start | bytes 1572872 | tf_op jit(solution)/shard_map/ppermute | solution.py:27
  168.9 9.4 %collective-permute-start.45 = (bf16[2,128,1024]{2,1,0:T(8,128)(2,1)S(1)}, bf16[2,128,1024]{2,1,0:T(8,128)(2,1)S(1)}, u32[]{:S(2)}, u32[]{:S(2)}) collective-permute-start(bf16[2,128,1024]{2,1,0:T(8,128)(2,1)S(1)} %pad_maximum_fusion.2), channel_id=1, source_target_pairs={{0,16},{8,24},{16,0},{24,8},{1,17},{9,25},{17,1},{25,9},{2,18},{10... | collective-permute-start | bytes 1572872 | tf_op jit(solution)/shard_map/ppermute | solution.py:27
  171.2 7.1 %collective-permute-start.38 = (bf16[1024,128]{1,0:T(8,128)(2,1)S(1)}, bf16[1024,128]{1,0:T(8,128)(2,1)S(1)}, u32[]{:S(2)}, u32[]{:S(2)}) collective-permute-start(bf16[1024,128]{1,0:T(8,128)(2,1)S(1)} %gated_signal.6.refs_0_), channel_id=1, source_target_pairs={{0,2},{1,3},{2,4},{3,5},{4,6},{5,7},{6,0},{7,1},{8,10},{9,11},{10,... | collective-permute-start | bytes 786440 | tf_op jit(solution)/shard_map/ppermute | solution.py:462
  172.5 8.6 %collective-permute-start.39 = (bf16[1024,128]{1,0:T(8,128)(2,1)S(1)}, bf16[1024,128]{1,0:T(8,128)(2,1)S(1)}, u32[]{:S(2)}, u32[]{:S(2)}) collective-permute-start(bf16[1024,128]{1,0:T(8,128)(2,1)S(1)} %gated_signal.7.refs_1_), channel_id=1, source_target_pairs={{0,2},{1,3},{2,4},{3,5},{4,6},{5,7},{6,0},{7,1},{8,10},{9,11},{10,... | collective-permute-start | bytes 786440 | tf_op jit(solution)/shard_map/ppermute | solution.py:462
  178.3 14.4 %collective-permute-start.46 = (bf16[2,128,1024]{2,1,0:T(8,128)(2,1)}, bf16[2,128,1024]{2,1,0:T(8,128)(2,1)}, u32[]{:S(2)}, u32[]{:S(2)}) collective-permute-start(bf16[2,128,1024]{2,1,0:T(8,128)(2,1)} %collective-permute-done.30), channel_id=1, source_target_pairs={{0,8},{8,0},{16,24},{24,16},{1,9},{9,1},{17,25},{25,17},{2,10},{10... | collective-permute-start | bytes 1572872 | tf_op jit(solution)/shard_map/ppermute | solution.py:27
  179.1 8.0 %collective-permute-start.40 = (bf16[1024,128]{1,0:T(8,128)(2,1)S(1)}, bf16[1024,128]{1,0:T(8,128)(2,1)S(1)}, u32[]{:S(2)}, u32[]{:S(2)}) collective-permute-start(bf16[1024,128]{1,0:T(8,128)(2,1)S(1)} %collective-permute-done.38.refs_2_), channel_id=1, source_target_pairs={{0,2},{1,3},{2,4},{3,5},{4,6},{5,7},{6,0},{7,1},{8,10},{9,11},{10,... | collective-permute-start | bytes 786440 | tf_op jit(solution)/shard_map/ppermute | solution.py:462
  181.1 11.6 %collective-permute-start.41 = (bf16[1024,128]{1,0:T(8,128)(2,1)S(1)}, bf16[1024,128]{1,0:T(8,128)(2,1)S(1)}, u32[]{:S(2)}, u32[]{:S(2)}) collective-permute-start(bf16[1024,128]{1,0:T(8,128)(2,1)S(1)} %collective-permute-done.39.refs_3_), channel_id=1, source_target_pairs={{0,2},{1,3},{2,4},{3,5},{4,6},{5,7},{6,0},{7,1},{8,10},{9,11},{10,... | collective-permute-start | bytes 786440 | tf_op jit(solution)/shard_map/ppermute | solution.py:462
  181.1 12.7 %collective-permute-start.47 = (bf16[2,128,1024]{2,1,0:T(8,128)(2,1)}, bf16[2,128,1024]{2,1,0:T(8,128)(2,1)}, u32[]{:S(2)}, u32[]{:S(2)}) collective-permute-start(bf16[2,128,1024]{2,1,0:T(8,128)(2,1)} %collective-permute-done.44), channel_id=1, source_target_pairs={{0,16},{8,24},{16,0},{24,8},{1,17},{9,25},{17,1},{25,9},{2,18},{10... | collective-permute-start | bytes 1572872 | tf_op jit(solution)/shard_map/ppermute | solution.py:27
  187.0 17.5 %collective-permute-start.42 = (bf16[1024,128]{1,0:T(8,128)(2,1)S(1)}, bf16[1024,128]{1,0:T(8,128)(2,1)S(1)}, u32[]{:S(2)}, u32[]{:S(2)}) collective-permute-start(bf16[1024,128]{1,0:T(8,128)(2,1)S(1)} %collective-permute-done.40.refs_4_), channel_id=1, source_target_pairs={{0,2},{1,3},{2,4},{3,5},{4,6},{5,7},{6,0},{7,1},{8,10},{9,11},{10,... | collective-permute-start | bytes 786440 | tf_op jit(solution)/shard_map/ppermute | solution.py:462
  192.6 11.9 %collective-permute-start.43 = (bf16[1024,128]{1,0:T(8,128)(2,1)S(1)}, bf16[1024,128]{1,0:T(8,128)(2,1)S(1)}, u32[]{:S(2)}, u32[]{:S(2)}) collective-permute-start(bf16[1024,128]{1,0:T(8,128)(2,1)S(1)} %collective-permute-done.41.refs_5_), channel_id=1, source_target_pairs={{0,2},{1,3},{2,4},{3,5},{4,6},{5,7},{6,0},{7,1},{8,10},{9,11},{10,... | collective-permute-start | bytes 786440 | tf_op jit(solution)/shard_map/ppermute | solution.py:462
  204.4 15.0 %copy-start.36 = (f32[4,16,512]{2,1,0:T(8,128)S(1)}, f32[4,16,512]{2,1,0:T(8,128)}, u32[]{:S(2)}) copy-start(f32[4,16,512]{2,1,0:T(8,128)} %get-tuple-element.105) | copy-start | bytes 393220
  204.5 15.0 %copy-start.42 = (f32[1,16,512]{2,1,0:T(8,128)S(1)}, f32[1,16,512]{2,1,0:T(8,128)}, u32[]{:S(2)}) copy-start(f32[1,16,512]{2,1,0:T(8,128)} %get-tuple-element.100) | copy-start | bytes 98308
  205.6 17.0 %collective-permute-start.48 = (bf16[1024,512]{1,0:T(8,128)(2,1)S(1)}, bf16[1024,512]{1,0:T(8,128)(2,1)S(1)}, u32[]{:S(2)}, u32[]{:S(2)}) collective-permute-start(bf16[1024,512]{1,0:T(8,128)(2,1)S(1)} %add_outputs.9), channel_id=1, source_target_pairs={{0,1},{1,0},{2,3},{3,2},{4,5},{5,4},{6,7},{7,6},{8,9},{9,8},{10,11... | collective-permute-start | bytes 3145736 | tf_op jit(solution)/shard_map/ppermute | solution.py:296
  (40 other events, 260.3 us)
Sparse Core Ops, SparseCore 0:
  10.2 87.5 all-gather.2

commit v6 on v5

--- a/solution.py
+++ b/solution.py
@@ -388,14 +388,16 @@
         inverse = lax.rsqrt(squares[0] / model_width + 1e-06)[:, None]
         tail_inverse = lax.ppermute(inverse[-TAIL:], *next_on)
         first_near = near
-        near, sent = lax.optimization_barrier(((near, sent), inverse))[0]
+        opposite = send([(sent[3], *across)], [squares])
+        near, sent = lax.optimization_barrier(((near, sent), (inverse, opposite)))[0]
         far = send([(near[1][:middle], *along_x), (near[0][middle:], *along_y)])
         units = [[w_units[0], *near, *far]]
-        got = send([(sent[1], *along_x), (sent[2], *along_y), (sent[3], *across)], first_near)
+        got = send([(sent[1], *along_x), (sent[2], *along_y)], first_near) + opposite
         by_owner = jnp.stack([sent[0], *got])
         tails_all = jnp.concatenate([tails_all, core_swap(tails_all)])
         tails_all = jnp.concatenate([tails_all, *[lax.ppermute(tails_all, *route) for route in others]])
-        w_second = lax.optimization_barrier((w_units[1], (*far, *got, tails_all, tail_inverse)))[0]
+        second = lax.optimization_barrier((w_in, inverse))[0][:, :, share:].reshape(-1, 3 * share)
+        w_second = lax.optimization_barrier((second, (*far, *got, tails_all, tail_inverse)))[0]
         near = send([(w_second, *along_x), (w_second, *along_y)])
         order = jnp.stack([(me ^ (n // per)) * per + n % per for n in range(mp)]).astype(jnp.int32)
         order = jnp.concatenate([order, order ^ here])

time: 232 us -> 229 us (0.987)
  waiting for transfers between devices: 64.6 us -> 59.5 us
  local copies, waits for them, and re-layouts: 30.1 us -> 34.5 us
    ppermute x19, waiting for transfers between devices: 20.5 us -> 14 us  [send(): lax.ppermute(arrays[id(array)], axis, route)]
    ppermute x19, starting transfers between devices: 18.8 us -> 15.5 us  [send(): lax.ppermute(arrays[id(array)], axis, route)]
    slice x1 -> x2, local copies, waits for them, and re-layouts: 3.23 us -> 0.01 us  [local(): w_in[:, :, g * share:(g + 1) * share].reshape(-1, 3 * share)]
    ppermute x3, starting transfers between devices: 3.64 us -> 6.8 us  [local(): lax.ppermute(tails_all, *route)]
    ppermute x1, waiting for transfers between devices: 0.01 us -> 3.16 us  [local(): tail_inverse = lax.ppermute(inverse[-TAIL:], *next_on)]
    optimization_barrier x1 -> x2, local copies, waits for them, and re-layouts: 0.69 us -> 3.75 us  [the longest x1 3.06 us: local(): lax.optimization_barrier((w_in, inverse))[0][:, :, share:]]
    ppermute x10, starting transfers between devices: 5.19 us -> 2.22 us  [local(): blocks.append([lax.ppermute(block, *along_z) for block in blocks[-1]])]
    ppermute x10, waiting for transfers between devices: 22.4 us -> 20 us  [local(): blocks.append([lax.ppermute(block, *along_z) for block in blocks[-1]])]
  transfers between devices with their start and end apart: 50 -> 50, of which waited for: 17 -> 22; matrix products, arithmetic and copies ran while one was open for 14% -> 16% of each run, Pallas kernels for 20% -> 20%
where the time goes in v6:
time: 229 us; the launch traced here: 228 us
  starting transfers between devices  60.6 us (26%)
  waiting for transfers between devices  59.5 us (26%)
  Pallas kernels  46.8 us (20%)
  local copies, waits for them, and re-layouts  34.5 us (15%)
  between operations  15.2 us (7%)
  other arithmetic  11.8 us (5%)
    pallas_call x2, Pallas kernels, project(): pl.pallas_call(functools.partial(project_kernel, chunks), grid_spec=pltpu...  22.7 us
    ppermute x10, waiting for transfers between devices, local(): blocks.append([lax.ppermute(block, *along_z) for block in blocks[-1]])  20 us
    ppermute x3, starting transfers between devices, core_swap(): return lax.ppermute(block, 'mp', swap_route(lax.axis_size('mp'), 1))  17.9 us
    ppermute x19, starting transfers between devices, send(): lax.ppermute(arrays[id(array)], axis, route)  15.5 us
    ppermute x19, waiting for transfers between devices, send(): lax.ppermute(arrays[id(array)], axis, route)  14 us
    ppermute x1, waiting for transfers between devices, local(): tails_all = lax.ppermute(scaled[-TAIL:], *next_on)[None]  11.2 us
    pallas_call x5, Pallas kernels, add_outputs(): pl.pallas_call(functools.partial(output_kernel, [[0] * len(chip) for chip...  10.5 us
    pallas_call x2, Pallas kernels, local_filter(): pl.pallas_call(functools.partial(local_kernel, tokens // SEGMENTS, modes)...  8.63 us
  transfers between devices with their start and end apart: 50, of which 22 were waited for; matrix products, arithmetic and copies ran while one was open for 16% of the time, Pallas kernels for 20%

profile of v6, /device:TPU:1, one launch (start us, length us, event | category | flops | bytes accessed | tf_op | source)
XLA Modules:
  0.0 228.4 jit_solution(13964634791228351257)
XLA Ops:
  7.2 2.6 %fusion.1 = (f32[1024]{0:T(1024)S(1)}, bf16[1024,512]{1,0:T(8,128)(2,1)}) fusion(bf16[1024,512]{1,0:T(8,128)(2,1)} %refs_9_.1, f32[512]{0:T(512)} %param.11), kind=kLoop, calls=%fused_computation.3 | loop fusion | flops 2620416 | bytes 2103296 | tf_op jit(solution)/shard_map/reduce_sum | solution.py:372
  9.9 1.8 copy.38
  11.7 2.7 %copy.25.refs_0_ = bf16[1024,768]{1,0:T(8,128)(2,1)} copy(bf16[1024,768]{0,1:T(8,128)(2,1)} %bitcast.159) | data formatting | bytes 3145728 | tf_op jit(solution)/shard_map/reshape | solution.py:369
  14.4 2.0 collective-permute-start.5
  16.5 1.2 collective-permute-start.6
  17.7 1.2 collective-permute-start.7
  24.2 3.4 %collective-permute-start.10 = (f32[1,1024]{1,0:T(1,128)S(1)}, f32[1,1024]{1,0:T(1,128)S(1)}, u32[]{:S(2)}, u32[]{:S(2)}) collective-permute-start(f32[1,1024]{1,0:T(1,128)S(1)} %add.108), channel_id=1, source_target_pairs={{0,6},{1,7},{2,4},{3,5},{4,2},{5,3},{6,0},{7,1},{8,14},{9,15},{10,... | collective-permute-start | bytes 12296 | tf_op jit(solution)/shard_map/ppermute | solution.py:387
  27.9 2.2 dynamic-slice_bitcast_fusion.3
  30.1 1.3 slice.147
  31.4 2.2 collective-permute-start
  35.8 3.1 %copy.27 = bf16[1024,3,512]{0,2,1:T(8,128)(2,1)} copy(bf16[1024,3,512]{2,0,1:T(8,128)(2,1)S(1)} %copy-done.26) | data formatting | bytes 6291456 | tf_op jit(solution)/shard_map/optimization_barrier | solution.py:399
  38.9 11.2 %collective-permute-done = bf16[16,512]{1,0:T(8,128)(2,1)S(1)} collective-permute-done((bf16[16,512]{1,0:T(8,128)(2,1)}, bf16[16,512]{1,0:T(8,128)(2,1)S(1)}, u32[]{:S(2)}, u32[]{:S(2)}) %collective-permute-start) | collective-permute-done | bytes 16416 | tf_op jit(solution)/shard_map/ppermute | solution.py:371
  50.1 2.7 %collective-permute-start.1 = (bf16[1,16,512]{2,1,0:T(8,128)(2,1)S(1)}, bf16[1,16,512]{2,1,0:T(8,128)(2,1)S(1)}, u32[]{:S(2)}, u32[]{:S(2)}) collective-permute-start(bf16[1,16,512]{2,1,0:T(8,128)(2,1)S(1)} %bitcast.166), channel_id=1, source_target_pairs={{0,1},{1,0},{2,3},{3,2},{4,5},{5,4},{6,7},{7,6},{8,9},{9,8},{10,11... | collective-permute-start | bytes 49160 | tf_op jit(solution)/shard_map/ppermute | solution.py:296
  52.8 4.7 %collective-permute-done.11 = bf16[128,1024]{1,0:T(8,128)(2,1)} collective-permute-done((bf16[128,1024]{1,0:T(8,128)(2,1)S(1)}, bf16[128,1024]{1,0:T(8,128)(2,1)}, u32[]{:S(2)}, u32[]{:S(2)}) %collective-permute-start.11) | collective-permute-done | bytes 262176 | tf_op jit(solution)/shard_map/ppermute | solution.py:27
  57.5 1.2 slice.114
  58.7 1.6 collective-permute-start.12
  60.2 1.2 slice.115
  61.7 1.4 collective-permute-start.2
  63.2 2.3 %collective-permute-start.3 = (bf16[2,16,512]{2,1,0:T(8,128)(2,1)S(1)}, bf16[2,16,512]{2,1,0:T(8,128)(2,1)S(1)}, u32[]{:S(2)}, u32[]{:S(2)}) collective-permute-start(bf16[2,16,512]{2,1,0:T(8,128)(2,1)S(1)} %pad_maximum_fusion.5), channel_id=1, source_target_pairs={{0,4},{1,5},{2,6},{3,7},{4,0},{5,1},{6,2},{7,3},{8,12},{9,13},{10,... | collective-permute-start | bytes 98312 | tf_op jit(solution)/shard_map/ppermute | solution.py:398
  65.5 1.2 collective-permute-start.16
  66.7 1.3 collective-permute-start.15
  68.0 1.7 collective-permute-done.3
  69.8 3.1 %collective-permute-start.4 = (bf16[2,16,512]{2,1,0:T(8,128)(2,1)S(1)}, bf16[2,16,512]{2,1,0:T(8,128)(2,1)S(1)}, u32[]{:S(2)}, u32[]{:S(2)}) collective-permute-start(bf16[2,16,512]{2,1,0:T(8,128)(2,1)S(1)} %pad_maximum_fusion.5), channel_id=1, source_target_pairs={{0,6},{1,7},{2,4},{3,5},{4,2},{5,3},{6,0},{7,1},{8,14},{9,15},{10,... | collective-permute-start | bytes 98312 | tf_op jit(solution)/shard_map/ppermute | solution.py:398
  72.8 2.2 collective-permute-done.4
  75.0 3.1 %collective-permute-start.14 = (f32[16,1]{1,0:T(8,128)S(1)}, f32[16,1]{1,0:T(8,128)S(1)}, u32[]{:S(2)}, u32[]{:S(2)}) collective-permute-start(f32[16,1]{1,0:T(8,128)S(1)} %copy-done.50), channel_id=1, source_target_pairs={{0,8},{8,16},{16,24},{1,9},{9,17},{17,25},{2,10},{10,18},{18,26},{... | collective-permute-start | bytes 200 | tf_op jit(solution)/shard_map/ppermute | solution.py:389
  78.2 3.2 %collective-permute-done.14.refs_6_ = f32[16,1]{1,0:T(8,128)S(1)} collective-permute-done((f32[16,1]{1,0:T(8,128)S(1)}, f32[16,1]{1,0:T(8,128)S(1)}, u32[]{:S(2)}, u32[]{:S(2)}) %collective-permute-start.14) | collective-permute-done | bytes 96 | tf_op jit(solution)/shard_map/ppermute | solution.py:389
  81.3 3.1 %collective-permute-done.16 = bf16[128,1024]{1,0:T(8,128)(2,1)S(1)} collective-permute-done((bf16[128,1024]{1,0:T(8,128)(2,1)S(1)}, bf16[128,1024]{1,0:T(8,128)(2,1)S(1)}, u32[]{:S(2)}, u32[]{:S(2)}) %collective-permute-start.16) | collective-permute-done | bytes 262176 | tf_op jit(solution)/shard_map/ppermute | solution.py:27
  88.4 1.3 pad_maximum_fusion
  90.7 1.3 collective-permute-start.17
  92.1 2.4 %collective-permute-start.21 = (bf16[128,1024]{1,0:T(8,128)(2,1)}, bf16[128,1024]{1,0:T(8,128)(2,1)}, u32[]{:S(2)}, u32[]{:S(2)}) collective-permute-start(bf16[128,1024]{1,0:T(8,128)(2,1)} %get-tuple-element.88), channel_id=1, source_target_pairs={{0,4},{1,5},{2,6},{3,7},{4,0},{5,1},{6,2},{7,3},{8,12},{9,13},{10,... | collective-permute-start | bytes 786440 | tf_op jit(solution)/shard_map/ppermute | solution.py:407
  96.8 1.4 all-gather.3.cloned.1.call-done
  98.2 12.7 %project.2 = (f32[1024,768]{1,0:T(8,128)}, f32[16,768]{1,0:T(8,128)}) custom-call(s32[16]{0:T(128)} %concatenate.29.order_ref, bf16[8,1024,512]{2,1,0:T(8,128)(2,1)} %bitcast.156, bf16[8,16,512]{2,1,0:T(8,128)(2,1)} %copy-done.15, bf16[1024,768]{1,0:T(8,128)(2,1)} %copy.25.refs_0_, bf16[1024,768]{1,0:T(8,128)(2,1)} %collective-permute-done.5.refs_1_, ...), custom_call_target="tpu_custom_call" | custom-call | tf_op jit(solution)/shard_map/project/pallas_call | solution.py:227
  111.6 1.9 copy-done
  113.5 4.3 %local_filter.2 = (f32[1024,256]{1,0:T(8,128)S(1)}, f32[128,256]{1,0:T(8,128)S(1)}, f32[16,256]{1,0:T(8,128)S(1)}) custom-call(f32[1024,768]{1,0:T(8,128)S(1)} %copy-done, f32[1024,768]{1,0:T(8,128)S(1)} %copy-done, f32[2,768]{1,0:T(2,128)S(1)} %slice_select_fusion.1.tail_k_ref.tail_v_ref.tail_q_ref, ...), custom_call_target="tpu_custom_call" | custom-call | bytes 3145728 | tf_op jit(solution)/shard_map/local_filter/pallas_call | solution.py:127
  118.9 1.3 collective-permute-start.19
  122.1 1.6 collective-permute-done.20
  123.7 1.2 slice.131
  126.1 1.2 gated_signal.4.refs_0_
  127.4 1.2 gated_signal.5.refs_1_
  130.0 1.3 collective-permute-start.29
  131.3 3.1 %collective-permute-done.27.refs_2_ = bf16[1024,128]{1,0:T(8,128)(2,1)S(1)} collective-permute-done((bf16[1024,128]{1,0:T(8,128)(2,1)S(1)}, bf16[1024,128]{1,0:T(8,128)(2,1)S(1)}, u32[]{:S(2)}, u32[]{:S(2)}) %collective-permute-start.27) | collective-permute-done | bytes 262176 | tf_op jit(solution)/shard_map/ppermute | solution.py:464
  135.5 2.4 %collective-permute-done.28.refs_3_ = bf16[1024,128]{1,0:T(8,128)(2,1)S(1)} collective-permute-done((bf16[1024,128]{1,0:T(8,128)(2,1)S(1)}, bf16[1024,128]{1,0:T(8,128)(2,1)S(1)}, u32[]{:S(2)}, u32[]{:S(2)}) %collective-permute-start.28) | collective-permute-done | bytes 262176 | tf_op jit(solution)/shard_map/ppermute | solution.py:464
  137.9 1.6 collective-permute-done.25.refs_3_
  140.7 10.0 %project.3 = (f32[1024,768]{1,0:T(8,128)S(1)}, f32[16,768]{1,0:T(8,128)S(1)}) custom-call(s32[16]{0:T(128)S(1)} %copy-done.25, bf16[8,1024,512]{2,1,0:T(8,128)(2,1)} %bitcast.157, bf16[8,16,512]{2,1,0:T(8,128)(2,1)S(1)} %copy-done.16, bf16[1024,768]{1,0:T(8,128)(2,1)S(1)} %copy.30.refs_0_, bf16[1024,768]{1,0:T(8,128)(2,1)S(1)} %collective-permute-done.23.refs_1_, ...), custom_call_target="tpu_custom_call" | custom-call | tf_op jit(solution)/shard_map/project/pallas_call | solution.py:227
  150.9 2.2 collective-permute-start.37
  153.1 4.3 %local_filter.3 = (f32[1024,256]{1,0:T(8,128)S(1)}, f32[128,256]{1,0:T(8,128)S(1)}, f32[16,256]{1,0:T(8,128)S(1)}) custom-call(f32[1024,768]{1,0:T(8,128)S(1)} %get-tuple-element.64.k_ref.v_ref.q_ref, f32[1024,768]{1,0:T(8,128)S(1)} %get-tuple-element.64.k_ref.v_ref.q_ref, f32[2,768]{1,0:T(2,128)S(1)} %slice_select_fusion.tail_k_ref.tail_v_ref.tail_q_ref, ...), custom_call_target="tpu_custom_call" | custom-call | bytes 3145728 | tf_op jit(solution)/shard_map/local_filter/pallas_call | solution.py:127
  158.2 1.1 collective-permute-start.34
  160.8 2.0 collective-permute-done.35
  164.0 1.2 gated_signal.6.refs_0_
  165.3 1.7 collective-permute-start.38
  167.0 1.2 gated_signal.7.refs_1_
  168.4 6.4 %collective-permute-done.38.refs_2_ = bf16[1024,128]{1,0:T(8,128)(2,1)S(1)} collective-permute-done((bf16[1024,128]{1,0:T(8,128)(2,1)S(1)}, bf16[1024,128]{1,0:T(8,128)(2,1)S(1)}, u32[]{:S(2)}, u32[]{:S(2)}) %collective-permute-start.38) | collective-permute-done | bytes 262176 | tf_op jit(solution)/shard_map/ppermute | solution.py:464
  175.6 2.0 collective-permute-done.39.refs_3_
  178.6 1.3 fusion.2
  180.0 2.6 %collective-permute-done.40.refs_4_ = bf16[1024,128]{1,0:T(8,128)(2,1)S(1)} collective-permute-done((bf16[1024,128]{1,0:T(8,128)(2,1)S(1)}, bf16[1024,128]{1,0:T(8,128)(2,1)S(1)}, u32[]{:S(2)}, u32[]{:S(2)}) %collective-permute-start.40) | collective-permute-done | bytes 262176 | tf_op jit(solution)/shard_map/ppermute | solution.py:464
  182.6 3.5 %collective-permute-done.41.refs_5_ = bf16[1024,128]{1,0:T(8,128)(2,1)S(1)} collective-permute-done((bf16[1024,128]{1,0:T(8,128)(2,1)S(1)}, bf16[1024,128]{1,0:T(8,128)(2,1)S(1)}, u32[]{:S(2)}, u32[]{:S(2)}) %collective-permute-start.41) | collective-permute-done | bytes 262176 | tf_op jit(solution)/shard_map/ppermute | solution.py:464
  186.1 1.6 collective-permute-done.46
  188.8 2.7 %collective-permute-done.47 = bf16[2,128,1024]{2,1,0:T(8,128)(2,1)} collective-permute-done((bf16[2,128,1024]{2,1,0:T(8,128)(2,1)}, bf16[2,128,1024]{2,1,0:T(8,128)(2,1)}, u32[]{:S(2)}, u32[]{:S(2)}) %collective-permute-start.47) | collective-permute-done | bytes 524320 | tf_op jit(solution)/shard_map/ppermute | solution.py:27
  194.9 2.4 %add_outputs.6.refs_7_ = f32[1024,512]{1,0:T(8,128)S(1)} custom-call(s32[4]{0:T(128)S(1)} %pad_add_fusion.order_ref, s32[1]{0:T(128)} %bitcast.72.half_ref, bf16[1024,128]{1,0:T(8,128)(2,1)S(1)} %gated_signal.4.refs_0_, bf16[1024,128]{1,0:T(8,128)(2,1)S(1)} %copy-done.4, bf16[1024,128]{1,0:T(8,128)(2,1)S(1)} %copy-done.6, bf16[1024,128]{1,0:T(8,128)(2,1)S(1)} %copy-done.8, ...), custom_call_target="tpu_custom_call" | custom-call | flops 2147483648 | bytes 2097152 | tf_op jit(solution)/shard_map/add_outputs/pallas_call | solution.py:274
  197.4 2.2 add_outputs.7.refs_3_
  199.6 2.4 %add_outputs.5.refs_9_ = f32[1024,512]{1,0:T(8,128)S(1)} custom-call(s32[4]{0:T(128)S(1)} %pad_add_fusion.order_ref, s32[1]{0:T(128)} %bitcast.4.half_ref, bf16[1024,128]{1,0:T(8,128)(2,1)S(1)} %gated_signal.4.refs_0_, bf16[1024,128]{1,0:T(8,128)(2,1)S(1)} %copy-done.4, bf16[1024,128]{1,0:T(8,128)(2,1)S(1)} %copy-done.6, bf16[1024,128]{1,0:T(8,128)(2,1)S(1)} %copy-done.8, ...), custom_call_target="tpu_custom_call" | custom-call | flops 2147483648 | bytes 2097152 | tf_op jit(solution)/shard_map/add_outputs/pallas_call | solution.py:274
  203.1 14.0 %collective-permute-start.48 = (bf16[1024,512]{1,0:T(8,128)(2,1)S(1)}, bf16[1024,512]{1,0:T(8,128)(2,1)S(1)}, u32[]{:S(2)}, u32[]{:S(2)}) collective-permute-start(bf16[1024,512]{1,0:T(8,128)(2,1)S(1)} %add_outputs.9), channel_id=1, source_target_pairs={{0,1},{1,0},{2,3},{3,2},{4,5},{5,4},{6,7},{7,6},{8,9},{9,8},{10,11... | collective-permute-start | bytes 3145736 | tf_op jit(solution)/shard_map/ppermute | solution.py:296
  217.7 2.4 %add_outputs.8 = f32[1024,512]{1,0:T(8,128)S(1)} custom-call(s32[4]{0:T(128)S(1)} %pad_add_fusion.order_ref, s32[1]{0:T(128)} %bitcast.4.half_ref, bf16[1024,128]{1,0:T(8,128)(2,1)S(1)} %gated_signal.6.refs_0_, bf16[1024,128]{1,0:T(8,128)(2,1)S(1)} %gated_signal.7.refs_1_, bf16[1024,128]{1,0:T(8,128)(2,1)S(1)} %collective-permute-done.38.refs_2_, ...), custom_call_target="tpu_custom_call" | custom-call | flops 2147483648 | bytes 2097152 | tf_op jit(solution)/shard_map/add_outputs/pallas_call | solution.py:274
  220.2 1.3 add_convert_fusion
  (239 shorter events, 35.4 us)
Async XLA Ops:
  7.2 91.0 %all-gather.3.cloned.1.call-start = ((), (), s32[]{:S(2)}) async-start(), calls=%async_computation | async-start | bytes 9437184 | tf_op jit(solution)/shard_map/all_gather | solution.py:368
  11.7 24.1 %copy-start.26 = (bf16[1024,3,512]{2,0,1:T(8,128)(2,1)S(1)}, bf16[1024,3,512]{2,0,1:T(8,128)(2,1)}, u32[]{:S(2)}) copy-start(bf16[1024,3,512]{2,0,1:T(8,128)(2,1)} %param.12) | copy-start | bytes 9437188
  14.4 43.0 %collective-permute-start.5 = (bf16[1024,768]{1,0:T(8,128)(2,1)}, bf16[1024,768]{1,0:T(8,128)(2,1)}, u32[]{:S(2)}, u32[]{:S(2)}) collective-permute-start(bf16[1024,768]{1,0:T(8,128)(2,1)} %copy.25.refs_0_), channel_id=1, source_target_pairs={{0,8},{8,0},{16,24},{24,16},{1,9},{9,1},{17,25},{25,17},{2,10},{10... | collective-permute-start | bytes 4718600 | tf_op jit(solution)/shard_map/ppermute | solution.py:27
  16.5 41.0 %collective-permute-start.6 = (bf16[1024,768]{1,0:T(8,128)(2,1)}, bf16[1024,768]{1,0:T(8,128)(2,1)}, u32[]{:S(2)}, u32[]{:S(2)}) collective-permute-start(bf16[1024,768]{1,0:T(8,128)(2,1)} %copy.25.refs_0_), channel_id=1, source_target_pairs={{0,16},{8,24},{16,0},{24,8},{1,17},{9,25},{17,1},{25,9},{2,18},{10... | collective-permute-start | bytes 4718600 | tf_op jit(solution)/shard_map/ppermute | solution.py:27
  17.7 6.5 %collective-permute-start.7 = (f32[1,1024]{1,0:T(1,128)S(1)}, f32[1,1024]{1,0:T(1,128)S(1)}, u32[]{:S(2)}, u32[]{:S(2)}) collective-permute-start(f32[1,1024]{1,0:T(1,128)S(1)} %bitcast.173), channel_id=1, source_target_pairs={{0,1},{1,0},{2,3},{3,2},{4,5},{5,4},{6,7},{7,6},{8,9},{9,8},{10,11... | collective-permute-start | bytes 12296 | tf_op jit(solution)/shard_map/ppermute | solution.py:296
  24.2 7.2 %collective-permute-start.10 = (f32[1,1024]{1,0:T(1,128)S(1)}, f32[1,1024]{1,0:T(1,128)S(1)}, u32[]{:S(2)}, u32[]{:S(2)}) collective-permute-start(f32[1,1024]{1,0:T(1,128)S(1)} %add.108), channel_id=1, source_target_pairs={{0,6},{1,7},{2,4},{3,5},{4,2},{5,3},{6,0},{7,1},{8,14},{9,15},{10,... | collective-permute-start | bytes 12296 | tf_op jit(solution)/shard_map/ppermute | solution.py:387
  27.6 6.0 %collective-permute-start.8 = (f32[1,1024]{1,0:T(1,128)S(1)}, f32[1,1024]{1,0:T(1,128)S(1)}, u32[]{:S(2)}, u32[]{:S(2)}) collective-permute-start(f32[1,1024]{1,0:T(1,128)S(1)} %add.108), channel_id=1, source_target_pairs={{0,2},{1,3},{2,0},{3,1},{4,6},{5,7},{6,4},{7,5},{8,10},{9,11},{10,... | collective-permute-start | bytes 12296 | tf_op jit(solution)/shard_map/ppermute | solution.py:387
  27.6 6.0 %collective-permute-start.9 = (f32[1,1024]{1,0:T(1,128)S(1)}, f32[1,1024]{1,0:T(1,128)S(1)}, u32[]{:S(2)}, u32[]{:S(2)}) collective-permute-start(f32[1,1024]{1,0:T(1,128)S(1)} %add.108), channel_id=1, source_target_pairs={{0,4},{1,5},{2,6},{3,7},{4,0},{5,1},{6,2},{7,3},{8,12},{9,13},{10,... | collective-permute-start | bytes 12296 | tf_op jit(solution)/shard_map/ppermute | solution.py:387
  31.4 18.7 %collective-permute-start = (bf16[16,512]{1,0:T(8,128)(2,1)}, bf16[16,512]{1,0:T(8,128)(2,1)S(1)}, u32[]{:S(2)}, u32[]{:S(2)}) collective-permute-start(bf16[16,512]{1,0:T(8,128)(2,1)} %slice.147), channel_id=1, source_target_pairs={{0,8},{8,16},{16,24},{1,9},{9,17},{17,25},{2,10},{10,18},{18,26},{... | collective-permute-start | bytes 49160 | tf_op jit(solution)/shard_map/ppermute | solution.py:371
  33.6 23.8 %collective-permute-start.11 = (bf16[128,1024]{1,0:T(8,128)(2,1)S(1)}, bf16[128,1024]{1,0:T(8,128)(2,1)}, u32[]{:S(2)}, u32[]{:S(2)}) collective-permute-start(bf16[128,1024]{1,0:T(8,128)(2,1)S(1)} %get-tuple-element.42), channel_id=1, source_target_pairs={{0,24},{8,16},{16,8},{24,0},{1,25},{9,17},{17,9},{25,1},{2,26},{10... | collective-permute-start | bytes 786440 | tf_op jit(solution)/shard_map/ppermute | solution.py:27
  38.8 26.6 %copy-start.37 = (bf16[128,1024]{1,0:T(8,128)(2,1)S(1)}, bf16[128,1024]{1,0:T(8,128)(2,1)}, u32[]{:S(2)}) copy-start(bf16[128,1024]{1,0:T(8,128)(2,1)} %get-tuple-element.54) | copy-start | bytes 786436
  38.8 27.8 %copy-start.36 = (bf16[128,1024]{1,0:T(8,128)(2,1)S(1)}, bf16[128,1024]{1,0:T(8,128)(2,1)}, u32[]{:S(2)}) copy-start(bf16[128,1024]{1,0:T(8,128)(2,1)} %get-tuple-element.53) | copy-start | bytes 786436
  38.8 36.2 %copy-start.50 = (f32[16,1]{1,0:T(8,128)S(1)}, f32[16,1]{1,0:T(8,128)}, u32[]{:S(2)}) copy-start(f32[16,1]{1,0:T(8,128)} %copy.24) | copy-start | bytes 196
  38.9 47.5 %slice-start.1 = ((bf16[1024,3,512]{0,2,1:T(8,128)(2,1)}), bf16[1024,3,256]{0,2,1:T(8,128)(2,1)S(1)}, s32[]{:S(2)}) async-start(bf16[1024,3,512]{0,2,1:T(8,128)(2,1)} %copy.27), calls=%async_computation.2 | async-start | bytes 3145728 | tf_op jit(solution)/shard_map/slice | solution.py:399
  50.1 11.6 %collective-permute-start.1 = (bf16[1,16,512]{2,1,0:T(8,128)(2,1)S(1)}, bf16[1,16,512]{2,1,0:T(8,128)(2,1)S(1)}, u32[]{:S(2)}, u32[]{:S(2)}) collective-permute-start(bf16[1,16,512]{2,1,0:T(8,128)(2,1)S(1)} %bitcast.166), channel_id=1, source_target_pairs={{0,1},{1,0},{2,3},{3,2},{4,5},{5,4},{6,7},{7,6},{8,9},{9,8},{10,11... | collective-permute-start | bytes 49160 | tf_op jit(solution)/shard_map/ppermute | solution.py:296
  57.5 30.1 %copy-start.53 = (f32[512]{0:T(512)S(1)}, f32[512]{0:T(512)}, u32[]{:S(2)}) copy-start(f32[512]{0:T(512)} %param.17) | copy-start | bytes 6148
  57.5 30.1 %copy-start.52 = (f32[128]{0:T(128)S(1)}, f32[128]{0:T(128)}, u32[]{:S(2)}) copy-start(f32[128]{0:T(128)} %mul.145) | copy-start | bytes 1540
  58.7 25.8 %collective-permute-start.12 = (bf16[512,768]{1,0:T(8,128)(2,1)S(1)}, bf16[512,768]{1,0:T(8,128)(2,1)S(1)}, u32[]{:S(2)}, u32[]{:S(2)}) collective-permute-start(bf16[512,768]{1,0:T(8,128)(2,1)S(1)} %slice.114), channel_id=1, source_target_pairs={{0,8},{8,0},{16,24},{24,16},{1,9},{9,1},{17,25},{25,17},{2,10},{10... | collective-permute-start | bytes 2359304 | tf_op jit(solution)/shard_map/ppermute | solution.py:27
  61.4 23.0 %collective-permute-start.13 = (bf16[512,768]{1,0:T(8,128)(2,1)S(1)}, bf16[512,768]{1,0:T(8,128)(2,1)S(1)}, u32[]{:S(2)}, u32[]{:S(2)}) collective-permute-start(bf16[512,768]{1,0:T(8,128)(2,1)S(1)} %slice.115), channel_id=1, source_target_pairs={{0,16},{8,24},{16,0},{24,8},{1,17},{9,25},{17,1},{25,9},{2,18},{10... | collective-permute-start | bytes 2359304 | tf_op jit(solution)/shard_map/ppermute | solution.py:27
  61.7 4.9 %collective-permute-start.2 = (bf16[2,16,512]{2,1,0:T(8,128)(2,1)S(1)}, bf16[2,16,512]{2,1,0:T(8,128)(2,1)S(1)}, u32[]{:S(2)}, u32[]{:S(2)}) collective-permute-start(bf16[2,16,512]{2,1,0:T(8,128)(2,1)S(1)} %pad_maximum_fusion.5), channel_id=1, source_target_pairs={{0,2},{1,3},{2,0},{3,1},{4,6},{5,7},{6,4},{7,5},{8,10},{9,11},{10,... | collective-permute-start | bytes 98312 | tf_op jit(solution)/shard_map/ppermute | solution.py:398
  63.2 6.6 %collective-permute-start.3 = (bf16[2,16,512]{2,1,0:T(8,128)(2,1)S(1)}, bf16[2,16,512]{2,1,0:T(8,128)(2,1)S(1)}, u32[]{:S(2)}, u32[]{:S(2)}) collective-permute-start(bf16[2,16,512]{2,1,0:T(8,128)(2,1)S(1)} %pad_maximum_fusion.5), channel_id=1, source_target_pairs={{0,4},{1,5},{2,6},{3,7},{4,0},{5,1},{6,2},{7,3},{8,12},{9,13},{10,... | collective-permute-start | bytes 98312 | tf_op jit(solution)/shard_map/ppermute | solution.py:398
  65.5 19.0 %collective-permute-start.16 = (bf16[128,1024]{1,0:T(8,128)(2,1)S(1)}, bf16[128,1024]{1,0:T(8,128)(2,1)S(1)}, u32[]{:S(2)}, u32[]{:S(2)}) collective-permute-start(bf16[128,1024]{1,0:T(8,128)(2,1)S(1)} %copy-done.37), channel_id=1, source_target_pairs={{0,16},{8,24},{16,0},{24,8},{1,17},{9,25},{17,1},{25,9},{2,18},{10... | collective-permute-start | bytes 786440 | tf_op jit(solution)/shard_map/ppermute | solution.py:27
  66.7 17.8 %collective-permute-start.15 = (bf16[128,1024]{1,0:T(8,128)(2,1)S(1)}, bf16[128,1024]{1,0:T(8,128)(2,1)S(1)}, u32[]{:S(2)}, u32[]{:S(2)}) collective-permute-start(bf16[128,1024]{1,0:T(8,128)(2,1)S(1)} %copy-done.36), channel_id=1, source_target_pairs={{0,8},{8,0},{16,24},{24,16},{1,9},{9,1},{17,25},{25,17},{2,10},{10... | collective-permute-start | bytes 786440 | tf_op jit(solution)/shard_map/ppermute | solution.py:27
  69.8 5.3 %collective-permute-start.4 = (bf16[2,16,512]{2,1,0:T(8,128)(2,1)S(1)}, bf16[2,16,512]{2,1,0:T(8,128)(2,1)S(1)}, u32[]{:S(2)}, u32[]{:S(2)}) collective-permute-start(bf16[2,16,512]{2,1,0:T(8,128)(2,1)S(1)} %pad_maximum_fusion.5), channel_id=1, source_target_pairs={{0,6},{1,7},{2,4},{3,5},{4,2},{5,3},{6,0},{7,1},{8,14},{9,15},{10,... | collective-permute-start | bytes 98312 | tf_op jit(solution)/shard_map/ppermute | solution.py:398
  75.0 6.3 %collective-permute-start.14 = (f32[16,1]{1,0:T(8,128)S(1)}, f32[16,1]{1,0:T(8,128)S(1)}, u32[]{:S(2)}, u32[]{:S(2)}) collective-permute-start(f32[16,1]{1,0:T(8,128)S(1)} %copy-done.50), channel_id=1, source_target_pairs={{0,8},{8,16},{16,24},{1,9},{9,17},{17,25},{2,10},{10,18},{18,26},{... | collective-permute-start | bytes 200 | tf_op jit(solution)/shard_map/ppermute | solution.py:389
  87.1 36.6 %collective-permute-start.23 = (bf16[1024,768]{1,0:T(8,128)(2,1)S(1)}, bf16[1024,768]{1,0:T(8,128)(2,1)S(1)}, u32[]{:S(2)}, u32[]{:S(2)}) collective-permute-start(bf16[1024,768]{1,0:T(8,128)(2,1)S(1)} %copy.30.refs_0_), channel_id=1, source_target_pairs={{0,8},{8,0},{16,24},{24,16},{1,9},{9,1},{17,25},{25,17},{2,10},{10... | collective-permute-start | bytes 4718600 | tf_op jit(solution)/shard_map/ppermute | solution.py:27
  87.2 36.5 %collective-permute-start.24 = (bf16[1024,768]{1,0:T(8,128)(2,1)S(1)}, bf16[1024,768]{1,0:T(8,128)(2,1)}, u32[]{:S(2)}, u32[]{:S(2)}) collective-permute-start(bf16[1024,768]{1,0:T(8,128)(2,1)S(1)} %copy.30.refs_0_), channel_id=1, source_target_pairs={{0,16},{8,24},{16,0},{24,8},{1,17},{9,25},{17,1},{25,9},{2,18},{10... | collective-permute-start | bytes 4718600 | tf_op jit(solution)/shard_map/ppermute | solution.py:27
  90.7 27.1 %collective-permute-start.17 = (bf16[128,1024]{1,0:T(8,128)(2,1)}, bf16[128,1024]{1,0:T(8,128)(2,1)}, u32[]{:S(2)}, u32[]{:S(2)}) collective-permute-start(bf16[128,1024]{1,0:T(8,128)(2,1)} %get-tuple-element.89), channel_id=1, source_target_pairs={{0,2},{1,3},{2,0},{3,1},{4,6},{5,7},{6,4},{7,5},{8,10},{9,11},{10,... | collective-permute-start | bytes 786440 | tf_op jit(solution)/shard_map/ppermute | solution.py:407
  92.1 26.9 %collective-permute-start.21 = (bf16[128,1024]{1,0:T(8,128)(2,1)}, bf16[128,1024]{1,0:T(8,128)(2,1)}, u32[]{:S(2)}, u32[]{:S(2)}) collective-permute-start(bf16[128,1024]{1,0:T(8,128)(2,1)} %get-tuple-element.88), channel_id=1, source_target_pairs={{0,4},{1,5},{2,6},{3,7},{4,0},{5,1},{6,2},{7,3},{8,12},{9,13},{10,... | collective-permute-start | bytes 786440 | tf_op jit(solution)/shard_map/ppermute | solution.py:407
  94.4 25.7 %collective-permute-start.22 = (bf16[128,1024]{1,0:T(8,128)(2,1)}, bf16[128,1024]{1,0:T(8,128)(2,1)}, u32[]{:S(2)}, u32[]{:S(2)}) collective-permute-start(bf16[128,1024]{1,0:T(8,128)(2,1)} %get-tuple-element.87), channel_id=1, source_target_pairs={{0,6},{1,7},{2,4},{3,5},{4,2},{5,3},{6,0},{7,1},{8,14},{9,15},{10,... | collective-permute-start | bytes 786440 | tf_op jit(solution)/shard_map/ppermute | solution.py:407
  117.9 3.3 %collective-permute-start.18 = (f32[16,256]{1,0:T(8,128)S(1)}, f32[16,256]{1,0:T(8,128)S(1)}, u32[]{:S(2)}, u32[]{:S(2)}) collective-permute-start(f32[16,256]{1,0:T(8,128)S(1)} %get-tuple-element.55), channel_id=1, source_target_pairs={{0,8},{8,0},{16,24},{24,16},{1,9},{9,1},{17,25},{25,17},{2,10},{10... | collective-permute-start | bytes 49160 | tf_op jit(solution)/shard_map/ppermute | solution.py:444
  118.9 3.2 %collective-permute-start.19 = (f32[16,256]{1,0:T(8,128)S(1)}, f32[16,256]{1,0:T(8,128)S(1)}, u32[]{:S(2)}, u32[]{:S(2)}) collective-permute-start(f32[16,256]{1,0:T(8,128)S(1)} %get-tuple-element.55), channel_id=1, source_target_pairs={{0,16},{8,24},{16,0},{24,8},{1,17},{9,25},{17,1},{25,9},{2,18},{10... | collective-permute-start | bytes 49160 | tf_op jit(solution)/shard_map/ppermute | solution.py:444
  120.2 3.6 %collective-permute-start.20 = (f32[16,256]{1,0:T(8,128)S(1)}, f32[16,256]{1,0:T(8,128)S(1)}, u32[]{:S(2)}, u32[]{:S(2)}) collective-permute-start(f32[16,256]{1,0:T(8,128)S(1)} %get-tuple-element.55), channel_id=1, source_target_pairs={{0,24},{8,16},{16,8},{24,0},{1,25},{9,17},{17,9},{25,1},{2,26},{10... | collective-permute-start | bytes 49160 | tf_op jit(solution)/shard_map/ppermute | solution.py:444
  124.9 14.6 %collective-permute-start.25 = (bf16[512,768]{1,0:T(8,128)(2,1)S(1)}, bf16[512,768]{1,0:T(8,128)(2,1)S(1)}, u32[]{:S(2)}, u32[]{:S(2)}) collective-permute-start(bf16[512,768]{1,0:T(8,128)(2,1)S(1)} %slice.131), channel_id=1, source_target_pairs={{0,8},{8,0},{16,24},{24,16},{1,9},{9,1},{17,25},{25,17},{2,10},{10... | collective-permute-start | bytes 2359304 | tf_op jit(solution)/shard_map/ppermute | solution.py:27
  125.5 15.2 %collective-permute-start.26 = (bf16[512,768]{1,0:T(8,128)(2,1)S(1)}, bf16[512,768]{1,0:T(8,128)(2,1)S(1)}, u32[]{:S(2)}, u32[]{:S(2)}) collective-permute-start(bf16[512,768]{1,0:T(8,128)(2,1)S(1)} %slice.132), channel_id=1, source_target_pairs={{0,16},{8,24},{16,0},{24,8},{1,17},{9,25},{17,1},{25,9},{2,18},{10... | collective-permute-start | bytes 2359304 | tf_op jit(solution)/shard_map/ppermute | solution.py:27
  127.4 7.1 %collective-permute-start.27 = (bf16[1024,128]{1,0:T(8,128)(2,1)S(1)}, bf16[1024,128]{1,0:T(8,128)(2,1)S(1)}, u32[]{:S(2)}, u32[]{:S(2)}) collective-permute-start(bf16[1024,128]{1,0:T(8,128)(2,1)S(1)} %gated_signal.4.refs_0_), channel_id=1, source_target_pairs={{0,2},{1,3},{2,4},{3,5},{4,6},{5,7},{6,0},{7,1},{8,10},{9,11},{10,... | collective-permute-start | bytes 786440 | tf_op jit(solution)/shard_map/ppermute | solution.py:464
  128.7 9.2 %collective-permute-start.28 = (bf16[1024,128]{1,0:T(8,128)(2,1)S(1)}, bf16[1024,128]{1,0:T(8,128)(2,1)S(1)}, u32[]{:S(2)}, u32[]{:S(2)}) collective-permute-start(bf16[1024,128]{1,0:T(8,128)(2,1)S(1)} %gated_signal.5.refs_1_), channel_id=1, source_target_pairs={{0,2},{1,3},{2,4},{3,5},{4,6},{5,7},{6,0},{7,1},{8,10},{9,11},{10,... | collective-permute-start | bytes 786440 | tf_op jit(solution)/shard_map/ppermute | solution.py:464
  130.0 23.0 %collective-permute-start.29 = (bf16[2,128,1024]{2,1,0:T(8,128)(2,1)S(1)}, bf16[2,128,1024]{2,1,0:T(8,128)(2,1)S(1)}, u32[]{:S(2)}, u32[]{:S(2)}) collective-permute-start(bf16[2,128,1024]{2,1,0:T(8,128)(2,1)S(1)} %pad_maximum_fusion.1), channel_id=1, source_target_pairs={{0,8},{8,0},{16,24},{24,16},{1,9},{9,1},{17,25},{25,17},{2,10},{10... | collective-permute-start | bytes 1572872 | tf_op jit(solution)/shard_map/ppermute | solution.py:27
  134.4 16.3 %copy-start.5 = (bf16[1024,128]{1,0:T(8,128)(2,1)}, bf16[1024,128]{1,0:T(8,128)(2,1)S(1)}, u32[]{:S(2)}) copy-start(bf16[1024,128]{1,0:T(8,128)(2,1)S(1)} %collective-permute-done.27.refs_2_) | copy-start | bytes 786436
  134.4 18.6 %collective-permute-start.30 = (bf16[2,128,1024]{2,1,0:T(8,128)(2,1)S(1)}, bf16[2,128,1024]{2,1,0:T(8,128)(2,1)}, u32[]{:S(2)}, u32[]{:S(2)}) collective-permute-start(bf16[2,128,1024]{2,1,0:T(8,128)(2,1)S(1)} %pad_maximum_fusion.1), channel_id=1, source_target_pairs={{0,16},{8,24},{16,0},{24,8},{1,17},{9,25},{17,1},{25,9},{2,18},{10... | collective-permute-start | bytes 1572872 | tf_op jit(solution)/shard_map/ppermute | solution.py:27
  137.9 12.9 %collective-permute-start.31 = (bf16[1024,128]{1,0:T(8,128)(2,1)S(1)}, bf16[1024,128]{1,0:T(8,128)(2,1)S(1)}, u32[]{:S(2)}, u32[]{:S(2)}) collective-permute-start(bf16[1024,128]{1,0:T(8,128)(2,1)S(1)} %collective-permute-done.27.refs_2_), channel_id=1, source_target_pairs={{0,2},{1,3},{2,4},{3,5},{4,6},{5,7},{6,0},{7,1},{8,10},{9,11},{10,... | collective-permute-start | bytes 786440 | tf_op jit(solution)/shard_map/ppermute | solution.py:464
  139.6 11.2 %collective-permute-start.32 = (bf16[1024,128]{1,0:T(8,128)(2,1)S(1)}, bf16[1024,128]{1,0:T(8,128)(2,1)S(1)}, u32[]{:S(2)}, u32[]{:S(2)}) collective-permute-start(bf16[1024,128]{1,0:T(8,128)(2,1)S(1)} %collective-permute-done.28.refs_3_), channel_id=1, source_target_pairs={{0,2},{1,3},{2,4},{3,5},{4,6},{5,7},{6,0},{7,1},{8,10},{9,11},{10,... | collective-permute-start | bytes 786440 | tf_op jit(solution)/shard_map/ppermute | solution.py:464
  150.8 12.0 %collective-permute-start.36 = (bf16[1024,128]{1,0:T(8,128)(2,1)S(1)}, bf16[1024,128]{1,0:T(8,128)(2,1)S(1)}, u32[]{:S(2)}, u32[]{:S(2)}) collective-permute-start(bf16[1024,128]{1,0:T(8,128)(2,1)S(1)} %collective-permute-done.31.refs_4_), channel_id=1, source_target_pairs={{0,2},{1,3},{2,4},{3,5},{4,6},{5,7},{6,0},{7,1},{8,10},{9,11},{10,... | collective-permute-start | bytes 786440 | tf_op jit(solution)/shard_map/ppermute | solution.py:27
  150.9 12.2 %collective-permute-start.37 = (bf16[1024,128]{1,0:T(8,128)(2,1)S(1)}, bf16[1024,128]{1,0:T(8,128)(2,1)S(1)}, u32[]{:S(2)}, u32[]{:S(2)}) collective-permute-start(bf16[1024,128]{1,0:T(8,128)(2,1)S(1)} %collective-permute-done.32.refs_5_), channel_id=1, source_target_pairs={{0,2},{1,3},{2,4},{3,5},{4,6},{5,7},{6,0},{7,1},{8,10},{9,11},{10,... | collective-permute-start | bytes 786440 | tf_op jit(solution)/shard_map/ppermute | solution.py:27
  157.5 2.7 %collective-permute-start.33 = (f32[16,256]{1,0:T(8,128)S(1)}, f32[16,256]{1,0:T(8,128)S(1)}, u32[]{:S(2)}, u32[]{:S(2)}) collective-permute-start(f32[16,256]{1,0:T(8,128)S(1)} %get-tuple-element.71), channel_id=1, source_target_pairs={{0,8},{8,0},{16,24},{24,16},{1,9},{9,1},{17,25},{25,17},{2,10},{10... | collective-permute-start | bytes 49160 | tf_op jit(solution)/shard_map/ppermute | solution.py:444
  158.2 2.6 %collective-permute-start.34 = (f32[16,256]{1,0:T(8,128)S(1)}, f32[16,256]{1,0:T(8,128)S(1)}, u32[]{:S(2)}, u32[]{:S(2)}) collective-permute-start(f32[16,256]{1,0:T(8,128)S(1)} %get-tuple-element.71), channel_id=1, source_target_pairs={{0,16},{8,24},{16,0},{24,8},{1,17},{9,25},{17,1},{25,9},{2,18},{10... | collective-permute-start | bytes 49160 | tf_op jit(solution)/shard_map/ppermute | solution.py:444
  159.3 3.5 %collective-permute-start.35 = (f32[16,256]{1,0:T(8,128)S(1)}, f32[16,256]{1,0:T(8,128)S(1)}, u32[]{:S(2)}, u32[]{:S(2)}) collective-permute-start(f32[16,256]{1,0:T(8,128)S(1)} %get-tuple-element.71), channel_id=1, source_target_pairs={{0,24},{8,16},{16,8},{24,0},{1,25},{9,17},{17,9},{25,1},{2,26},{10... | collective-permute-start | bytes 49160 | tf_op jit(solution)/shard_map/ppermute | solution.py:444
  163.1 11.7 %collective-permute-start.44 = (bf16[2,128,1024]{2,1,0:T(8,128)(2,1)S(1)}, bf16[2,128,1024]{2,1,0:T(8,128)(2,1)}, u32[]{:S(2)}, u32[]{:S(2)}) collective-permute-start(bf16[2,128,1024]{2,1,0:T(8,128)(2,1)S(1)} %pad_maximum_fusion.2), channel_id=1, source_target_pairs={{0,8},{8,0},{16,24},{24,16},{1,9},{9,1},{17,25},{25,17},{2,10},{10... | collective-permute-start | bytes 1572872 | tf_op jit(solution)/shard_map/ppermute | solution.py:27
  163.7 11.1 %collective-permute-start.45 = (bf16[2,128,1024]{2,1,0:T(8,128)(2,1)S(1)}, bf16[2,128,1024]{2,1,0:T(8,128)(2,1)S(1)}, u32[]{:S(2)}, u32[]{:S(2)}) collective-permute-start(bf16[2,128,1024]{2,1,0:T(8,128)(2,1)S(1)} %pad_maximum_fusion.2), channel_id=1, source_target_pairs={{0,16},{8,24},{16,0},{24,8},{1,17},{9,25},{17,1},{25,9},{2,18},{10... | collective-permute-start | bytes 1572872 | tf_op jit(solution)/shard_map/ppermute | solution.py:27
  165.3 9.5 %collective-permute-start.38 = (bf16[1024,128]{1,0:T(8,128)(2,1)S(1)}, bf16[1024,128]{1,0:T(8,128)(2,1)S(1)}, u32[]{:S(2)}, u32[]{:S(2)}) collective-permute-start(bf16[1024,128]{1,0:T(8,128)(2,1)S(1)} %gated_signal.6.refs_0_), channel_id=1, source_target_pairs={{0,2},{1,3},{2,4},{3,5},{4,6},{5,7},{6,0},{7,1},{8,10},{9,11},{10,... | collective-permute-start | bytes 786440 | tf_op jit(solution)/shard_map/ppermute | solution.py:464
  168.2 9.4 %collective-permute-start.39 = (bf16[1024,128]{1,0:T(8,128)(2,1)S(1)}, bf16[1024,128]{1,0:T(8,128)(2,1)S(1)}, u32[]{:S(2)}, u32[]{:S(2)}) collective-permute-start(bf16[1024,128]{1,0:T(8,128)(2,1)S(1)} %gated_signal.7.refs_1_), channel_id=1, source_target_pairs={{0,2},{1,3},{2,4},{3,5},{4,6},{5,7},{6,0},{7,1},{8,10},{9,11},{10,... | collective-permute-start | bytes 786440 | tf_op jit(solution)/shard_map/ppermute | solution.py:464
  174.8 12.9 %collective-permute-start.46 = (bf16[2,128,1024]{2,1,0:T(8,128)(2,1)}, bf16[2,128,1024]{2,1,0:T(8,128)(2,1)}, u32[]{:S(2)}, u32[]{:S(2)}) collective-permute-start(bf16[2,128,1024]{2,1,0:T(8,128)(2,1)} %collective-permute-done.30), channel_id=1, source_target_pairs={{0,8},{8,0},{16,24},{24,16},{1,9},{9,1},{17,25},{25,17},{2,10},{10... | collective-permute-start | bytes 1572872 | tf_op jit(solution)/shard_map/ppermute | solution.py:27
  175.6 7.0 %collective-permute-start.40 = (bf16[1024,128]{1,0:T(8,128)(2,1)S(1)}, bf16[1024,128]{1,0:T(8,128)(2,1)S(1)}, u32[]{:S(2)}, u32[]{:S(2)}) collective-permute-start(bf16[1024,128]{1,0:T(8,128)(2,1)S(1)} %collective-permute-done.38.refs_2_), channel_id=1, source_target_pairs={{0,2},{1,3},{2,4},{3,5},{4,6},{5,7},{6,0},{7,1},{8,10},{9,11},{10,... | collective-permute-start | bytes 786440 | tf_op jit(solution)/shard_map/ppermute | solution.py:464
  177.6 8.5 %collective-permute-start.41 = (bf16[1024,128]{1,0:T(8,128)(2,1)S(1)}, bf16[1024,128]{1,0:T(8,128)(2,1)S(1)}, u32[]{:S(2)}, u32[]{:S(2)}) collective-permute-start(bf16[1024,128]{1,0:T(8,128)(2,1)S(1)} %collective-permute-done.39.refs_3_), channel_id=1, source_target_pairs={{0,2},{1,3},{2,4},{3,5},{4,6},{5,7},{6,0},{7,1},{8,10},{9,11},{10,... | collective-permute-start | bytes 786440 | tf_op jit(solution)/shard_map/ppermute | solution.py:464
  177.6 13.9 %collective-permute-start.47 = (bf16[2,128,1024]{2,1,0:T(8,128)(2,1)}, bf16[2,128,1024]{2,1,0:T(8,128)(2,1)}, u32[]{:S(2)}, u32[]{:S(2)}) collective-permute-start(bf16[2,128,1024]{2,1,0:T(8,128)(2,1)} %collective-permute-done.44), channel_id=1, source_target_pairs={{0,16},{8,24},{16,0},{24,8},{1,17},{9,25},{17,1},{25,9},{2,18},{10... | collective-permute-start | bytes 1572872 | tf_op jit(solution)/shard_map/ppermute | solution.py:27
  179.9 14.9 %copy-start.4 = (bf16[1024,128]{1,0:T(8,128)(2,1)S(1)}, bf16[1024,128]{1,0:T(8,128)(2,1)}, u32[]{:S(2)}) copy-start(bf16[1024,128]{1,0:T(8,128)(2,1)} %copy-done.3) | copy-start | bytes 786436
  179.9 14.9 %copy-start.6 = (bf16[1024,128]{1,0:T(8,128)(2,1)S(1)}, bf16[1024,128]{1,0:T(8,128)(2,1)}, u32[]{:S(2)}) copy-start(bf16[1024,128]{1,0:T(8,128)(2,1)} %copy-done.5) | copy-start | bytes 786436
  179.9 14.9 %copy-start.8 = (bf16[1024,128]{1,0:T(8,128)(2,1)S(1)}, bf16[1024,128]{1,0:T(8,128)(2,1)}, u32[]{:S(2)}) copy-start(bf16[1024,128]{1,0:T(8,128)(2,1)} %copy-done.7) | copy-start | bytes 786436
  180.0 14.9 %copy-start.10 = (bf16[1024,128]{1,0:T(8,128)(2,1)S(1)}, bf16[1024,128]{1,0:T(8,128)(2,1)}, u32[]{:S(2)}) copy-start(bf16[1024,128]{1,0:T(8,128)(2,1)} %copy-done.9) | copy-start | bytes 786436
  182.6 19.4 %collective-permute-start.42 = (bf16[1024,128]{1,0:T(8,128)(2,1)S(1)}, bf16[1024,128]{1,0:T(8,128)(2,1)S(1)}, u32[]{:S(2)}, u32[]{:S(2)}) collective-permute-start(bf16[1024,128]{1,0:T(8,128)(2,1)S(1)} %collective-permute-done.40.refs_4_), channel_id=1, source_target_pairs={{0,2},{1,3},{2,4},{3,5},{4,6},{5,7},{6,0},{7,1},{8,10},{9,11},{10,... | collective-permute-start | bytes 786440 | tf_op jit(solution)/shard_map/ppermute | solution.py:464
  186.1 16.0 %collective-permute-start.43 = (bf16[1024,128]{1,0:T(8,128)(2,1)S(1)}, bf16[1024,128]{1,0:T(8,128)(2,1)S(1)}, u32[]{:S(2)}, u32[]{:S(2)}) collective-permute-start(bf16[1024,128]{1,0:T(8,128)(2,1)S(1)} %collective-permute-done.41.refs_5_), channel_id=1, source_target_pairs={{0,2},{1,3},{2,4},{3,5},{4,6},{5,7},{6,0},{7,1},{8,10},{9,11},{10,... | collective-permute-start | bytes 786440 | tf_op jit(solution)/shard_map/ppermute | solution.py:464
  202.0 15.1 %copy-start.35 = (f32[4,16,512]{2,1,0:T(8,128)S(1)}, f32[4,16,512]{2,1,0:T(8,128)}, u32[]{:S(2)}) copy-start(f32[4,16,512]{2,1,0:T(8,128)} %get-tuple-element.105) | copy-start | bytes 393220
  202.0 15.1 %copy-start.42 = (f32[1,16,512]{2,1,0:T(8,128)S(1)}, f32[1,16,512]{2,1,0:T(8,128)}, u32[]{:S(2)}) copy-start(f32[1,16,512]{2,1,0:T(8,128)} %get-tuple-element.100) | copy-start | bytes 98308
  203.1 17.1 %collective-permute-start.48 = (bf16[1024,512]{1,0:T(8,128)(2,1)S(1)}, bf16[1024,512]{1,0:T(8,128)(2,1)S(1)}, u32[]{:S(2)}, u32[]{:S(2)}) collective-permute-start(bf16[1024,512]{1,0:T(8,128)(2,1)S(1)} %add_outputs.9), channel_id=1, source_target_pairs={{0,1},{1,0},{2,3},{3,2},{4,5},{5,4},{6,7},{7,6},{8,9},{9,8},{10,11... | collective-permute-start | bytes 3145736 | tf_op jit(solution)/shard_map/ppermute | solution.py:296
  (43 other events, 376.5 us)
Sparse Core Ops, SparseCore 0:
  10.2 87.9 all-gather.2

commit v7 on v6

--- a/solution.py
+++ b/solution.py
@@ -269,7 +269,7 @@
     tokens = gated[0][0].shape[0]
     share = len(gated[0]) * LANES
     chips, columns = panel.shape[0], panel.shape[2] // 2
-    tile = math.gcd(tokens, 256)
+    tile = math.gcd(tokens, 512)
     blocks = [block for chip in gated for block in chip]
     return pl.pallas_call(
         functools.partial(output_kernel, [[0] * len(chip) for chip in gated]),

time: 229 us -> 228 us (level)
  no operation moved by 1% of the time
where the time goes in v7:
time: 228 us; the launch traced here: 227 us
  starting transfers between devices  60.6 us (27%)
  waiting for transfers between devices  59.5 us (26%)
  Pallas kernels  45 us (20%)
  local copies, waits for them, and re-layouts  34.5 us (15%)
  between operations  15.2 us (7%)
  other arithmetic  11.8 us (5%)
    pallas_call x2, Pallas kernels, project(): pl.pallas_call(functools.partial(project_kernel, chunks), grid_spec=pltpu...  22.7 us
    ppermute x10, waiting for transfers between devices, local(): blocks.append([lax.ppermute(block, *along_z) for block in blocks[-1]])  20 us
    ppermute x3, starting transfers between devices, core_swap(): return lax.ppermute(block, 'mp', swap_route(lax.axis_size('mp'), 1))  17.9 us
    ppermute x19, starting transfers between devices, send(): lax.ppermute(arrays[id(array)], axis, route)  15.5 us
    ppermute x19, waiting for transfers between devices, send(): lax.ppermute(arrays[id(array)], axis, route)  14 us
    ppermute x1, waiting for transfers between devices, local(): tails_all = lax.ppermute(scaled[-TAIL:], *next_on)[None]  11.2 us
    pallas_call x5, Pallas kernels, add_outputs(): pl.pallas_call(functools.partial(output_kernel, [[0] * len(chip) for chip...  8.79 us
    pallas_call x2, Pallas kernels, local_filter(): pl.pallas_call(functools.partial(local_kernel, tokens // SEGMENTS, modes)...  8.63 us
  transfers between devices with their start and end apart: 50, of which 22 were waited for; matrix products, arithmetic and copies ran while one was open for 16% of the time, Pallas kernels for 20%

profile of v7, /device:TPU:1, one launch (start us, length us, event | category | flops | bytes accessed | tf_op | source)
XLA Modules:
  0.0 226.6 jit_solution(14027961788118275572)
XLA Ops:
  7.2 2.6 %fusion.1 = (f32[1024]{0:T(1024)S(1)}, bf16[1024,512]{1,0:T(8,128)(2,1)}) fusion(bf16[1024,512]{1,0:T(8,128)(2,1)} %refs_9_.1, f32[512]{0:T(512)} %param.11), kind=kLoop, calls=%fused_computation.3 | loop fusion | flops 2620416 | bytes 2103296 | tf_op jit(solution)/shard_map/reduce_sum | solution.py:372
  9.9 1.8 copy.38
  11.7 2.7 %copy.25.refs_0_ = bf16[1024,768]{1,0:T(8,128)(2,1)} copy(bf16[1024,768]{0,1:T(8,128)(2,1)} %bitcast.159) | data formatting | bytes 3145728 | tf_op jit(solution)/shard_map/reshape | solution.py:369
  14.4 2.0 collective-permute-start.5
  16.5 1.2 collective-permute-start.6
  17.7 1.2 collective-permute-start.7
  24.2 3.4 %collective-permute-start.10 = (f32[1,1024]{1,0:T(1,128)S(1)}, f32[1,1024]{1,0:T(1,128)S(1)}, u32[]{:S(2)}, u32[]{:S(2)}) collective-permute-start(f32[1,1024]{1,0:T(1,128)S(1)} %add.108), channel_id=1, source_target_pairs={{0,6},{1,7},{2,4},{3,5},{4,2},{5,3},{6,0},{7,1},{8,14},{9,15},{10,... | collective-permute-start | bytes 12296 | tf_op jit(solution)/shard_map/ppermute | solution.py:387
  27.9 2.2 dynamic-slice_bitcast_fusion.3
  30.1 1.3 slice.147
  31.4 2.2 collective-permute-start
  35.8 3.1 %copy.27 = bf16[1024,3,512]{0,2,1:T(8,128)(2,1)} copy(bf16[1024,3,512]{2,0,1:T(8,128)(2,1)S(1)} %copy-done.26) | data formatting | bytes 6291456 | tf_op jit(solution)/shard_map/optimization_barrier | solution.py:399
  38.9 11.2 %collective-permute-done = bf16[16,512]{1,0:T(8,128)(2,1)S(1)} collective-permute-done((bf16[16,512]{1,0:T(8,128)(2,1)}, bf16[16,512]{1,0:T(8,128)(2,1)S(1)}, u32[]{:S(2)}, u32[]{:S(2)}) %collective-permute-start) | collective-permute-done | bytes 16416 | tf_op jit(solution)/shard_map/ppermute | solution.py:371
  50.1 2.7 %collective-permute-start.1 = (bf16[1,16,512]{2,1,0:T(8,128)(2,1)S(1)}, bf16[1,16,512]{2,1,0:T(8,128)(2,1)S(1)}, u32[]{:S(2)}, u32[]{:S(2)}) collective-permute-start(bf16[1,16,512]{2,1,0:T(8,128)(2,1)S(1)} %bitcast.166), channel_id=1, source_target_pairs={{0,1},{1,0},{2,3},{3,2},{4,5},{5,4},{6,7},{7,6},{8,9},{9,8},{10,11... | collective-permute-start | bytes 49160 | tf_op jit(solution)/shard_map/ppermute | solution.py:296
  52.8 4.7 %collective-permute-done.11 = bf16[128,1024]{1,0:T(8,128)(2,1)} collective-permute-done((bf16[128,1024]{1,0:T(8,128)(2,1)S(1)}, bf16[128,1024]{1,0:T(8,128)(2,1)}, u32[]{:S(2)}, u32[]{:S(2)}) %collective-permute-start.11) | collective-permute-done | bytes 262176 | tf_op jit(solution)/shard_map/ppermute | solution.py:27
  57.5 1.2 slice.114
  58.7 1.6 collective-permute-start.12
  60.2 1.2 slice.115
  61.7 1.4 collective-permute-start.2
  63.2 2.3 %collective-permute-start.3 = (bf16[2,16,512]{2,1,0:T(8,128)(2,1)S(1)}, bf16[2,16,512]{2,1,0:T(8,128)(2,1)S(1)}, u32[]{:S(2)}, u32[]{:S(2)}) collective-permute-start(bf16[2,16,512]{2,1,0:T(8,128)(2,1)S(1)} %pad_maximum_fusion.5), channel_id=1, source_target_pairs={{0,4},{1,5},{2,6},{3,7},{4,0},{5,1},{6,2},{7,3},{8,12},{9,13},{10,... | collective-permute-start | bytes 98312 | tf_op jit(solution)/shard_map/ppermute | solution.py:398
  65.5 1.2 collective-permute-start.16
  66.7 1.3 collective-permute-start.15
  68.0 1.7 collective-permute-done.3
  69.8 3.1 %collective-permute-start.4 = (bf16[2,16,512]{2,1,0:T(8,128)(2,1)S(1)}, bf16[2,16,512]{2,1,0:T(8,128)(2,1)S(1)}, u32[]{:S(2)}, u32[]{:S(2)}) collective-permute-start(bf16[2,16,512]{2,1,0:T(8,128)(2,1)S(1)} %pad_maximum_fusion.5), channel_id=1, source_target_pairs={{0,6},{1,7},{2,4},{3,5},{4,2},{5,3},{6,0},{7,1},{8,14},{9,15},{10,... | collective-permute-start | bytes 98312 | tf_op jit(solution)/shard_map/ppermute | solution.py:398
  72.8 2.2 collective-permute-done.4
  75.0 3.1 %collective-permute-start.14 = (f32[16,1]{1,0:T(8,128)S(1)}, f32[16,1]{1,0:T(8,128)S(1)}, u32[]{:S(2)}, u32[]{:S(2)}) collective-permute-start(f32[16,1]{1,0:T(8,128)S(1)} %copy-done.50), channel_id=1, source_target_pairs={{0,8},{8,16},{16,24},{1,9},{9,17},{17,25},{2,10},{10,18},{18,26},{... | collective-permute-start | bytes 200 | tf_op jit(solution)/shard_map/ppermute | solution.py:389
  78.2 3.2 %collective-permute-done.14.refs_6_ = f32[16,1]{1,0:T(8,128)S(1)} collective-permute-done((f32[16,1]{1,0:T(8,128)S(1)}, f32[16,1]{1,0:T(8,128)S(1)}, u32[]{:S(2)}, u32[]{:S(2)}) %collective-permute-start.14) | collective-permute-done | bytes 96 | tf_op jit(solution)/shard_map/ppermute | solution.py:389
  81.3 3.1 %collective-permute-done.16 = bf16[128,1024]{1,0:T(8,128)(2,1)S(1)} collective-permute-done((bf16[128,1024]{1,0:T(8,128)(2,1)S(1)}, bf16[128,1024]{1,0:T(8,128)(2,1)S(1)}, u32[]{:S(2)}, u32[]{:S(2)}) %collective-permute-start.16) | collective-permute-done | bytes 262176 | tf_op jit(solution)/shard_map/ppermute | solution.py:27
  88.4 1.3 pad_maximum_fusion
  90.7 1.3 collective-permute-start.17
  92.1 2.4 %collective-permute-start.21 = (bf16[128,1024]{1,0:T(8,128)(2,1)}, bf16[128,1024]{1,0:T(8,128)(2,1)}, u32[]{:S(2)}, u32[]{:S(2)}) collective-permute-start(bf16[128,1024]{1,0:T(8,128)(2,1)} %get-tuple-element.88), channel_id=1, source_target_pairs={{0,4},{1,5},{2,6},{3,7},{4,0},{5,1},{6,2},{7,3},{8,12},{9,13},{10,... | collective-permute-start | bytes 786440 | tf_op jit(solution)/shard_map/ppermute | solution.py:407
  96.8 1.4 all-gather.3.cloned.1.call-done
  98.2 12.7 %project.2 = (f32[1024,768]{1,0:T(8,128)}, f32[16,768]{1,0:T(8,128)}) custom-call(s32[16]{0:T(128)} %concatenate.29.order_ref, bf16[8,1024,512]{2,1,0:T(8,128)(2,1)} %bitcast.156, bf16[8,16,512]{2,1,0:T(8,128)(2,1)} %copy-done.15, bf16[1024,768]{1,0:T(8,128)(2,1)} %copy.25.refs_0_, bf16[1024,768]{1,0:T(8,128)(2,1)} %collective-permute-done.5.refs_1_, ...), custom_call_target="tpu_custom_call" | custom-call | tf_op jit(solution)/shard_map/project/pallas_call | solution.py:227
  111.6 1.9 copy-done
  113.5 4.3 %local_filter.2 = (f32[1024,256]{1,0:T(8,128)S(1)}, f32[128,256]{1,0:T(8,128)S(1)}, f32[16,256]{1,0:T(8,128)S(1)}) custom-call(f32[1024,768]{1,0:T(8,128)S(1)} %copy-done, f32[1024,768]{1,0:T(8,128)S(1)} %copy-done, f32[2,768]{1,0:T(2,128)S(1)} %slice_select_fusion.1.tail_k_ref.tail_v_ref.tail_q_ref, ...), custom_call_target="tpu_custom_call" | custom-call | bytes 3145728 | tf_op jit(solution)/shard_map/local_filter/pallas_call | solution.py:127
  118.9 1.3 collective-permute-start.19
  122.1 1.6 collective-permute-done.20
  123.7 1.2 slice.131
  126.1 1.2 gated_signal.4.refs_0_
  127.4 1.2 gated_signal.5.refs_1_
  130.0 1.3 collective-permute-start.29
  131.3 3.1 %collective-permute-done.27.refs_2_ = bf16[1024,128]{1,0:T(8,128)(2,1)S(1)} collective-permute-done((bf16[1024,128]{1,0:T(8,128)(2,1)S(1)}, bf16[1024,128]{1,0:T(8,128)(2,1)S(1)}, u32[]{:S(2)}, u32[]{:S(2)}) %collective-permute-start.27) | collective-permute-done | bytes 262176 | tf_op jit(solution)/shard_map/ppermute | solution.py:464
  135.5 2.4 %collective-permute-done.28.refs_3_ = bf16[1024,128]{1,0:T(8,128)(2,1)S(1)} collective-permute-done((bf16[1024,128]{1,0:T(8,128)(2,1)S(1)}, bf16[1024,128]{1,0:T(8,128)(2,1)S(1)}, u32[]{:S(2)}, u32[]{:S(2)}) %collective-permute-start.28) | collective-permute-done | bytes 262176 | tf_op jit(solution)/shard_map/ppermute | solution.py:464
  137.9 1.6 collective-permute-done.25.refs_3_
  140.7 10.0 %project.3 = (f32[1024,768]{1,0:T(8,128)S(1)}, f32[16,768]{1,0:T(8,128)S(1)}) custom-call(s32[16]{0:T(128)S(1)} %copy-done.25, bf16[8,1024,512]{2,1,0:T(8,128)(2,1)} %bitcast.157, bf16[8,16,512]{2,1,0:T(8,128)(2,1)S(1)} %copy-done.16, bf16[1024,768]{1,0:T(8,128)(2,1)S(1)} %copy.30.refs_0_, bf16[1024,768]{1,0:T(8,128)(2,1)S(1)} %collective-permute-done.23.refs_1_, ...), custom_call_target="tpu_custom_call" | custom-call | tf_op jit(solution)/shard_map/project/pallas_call | solution.py:227
  150.9 2.2 collective-permute-start.37
  153.1 4.3 %local_filter.3 = (f32[1024,256]{1,0:T(8,128)S(1)}, f32[128,256]{1,0:T(8,128)S(1)}, f32[16,256]{1,0:T(8,128)S(1)}) custom-call(f32[1024,768]{1,0:T(8,128)S(1)} %get-tuple-element.64.k_ref.v_ref.q_ref, f32[1024,768]{1,0:T(8,128)S(1)} %get-tuple-element.64.k_ref.v_ref.q_ref, f32[2,768]{1,0:T(2,128)S(1)} %slice_select_fusion.tail_k_ref.tail_v_ref.tail_q_ref, ...), custom_call_target="tpu_custom_call" | custom-call | bytes 3145728 | tf_op jit(solution)/shard_map/local_filter/pallas_call | solution.py:127
  158.2 1.1 collective-permute-start.34
  160.8 2.0 collective-permute-done.35
  164.0 1.2 gated_signal.6.refs_0_
  165.3 1.7 collective-permute-start.38
  167.0 1.2 gated_signal.7.refs_1_
  168.4 6.4 %collective-permute-done.38.refs_2_ = bf16[1024,128]{1,0:T(8,128)(2,1)S(1)} collective-permute-done((bf16[1024,128]{1,0:T(8,128)(2,1)S(1)}, bf16[1024,128]{1,0:T(8,128)(2,1)S(1)}, u32[]{:S(2)}, u32[]{:S(2)}) %collective-permute-start.38) | collective-permute-done | bytes 262176 | tf_op jit(solution)/shard_map/ppermute | solution.py:464
  175.6 2.0 collective-permute-done.39.refs_3_
  178.6 1.3 fusion.2
  180.0 2.6 %collective-permute-done.40.refs_4_ = bf16[1024,128]{1,0:T(8,128)(2,1)S(1)} collective-permute-done((bf16[1024,128]{1,0:T(8,128)(2,1)S(1)}, bf16[1024,128]{1,0:T(8,128)(2,1)S(1)}, u32[]{:S(2)}, u32[]{:S(2)}) %collective-permute-start.40) | collective-permute-done | bytes 262176 | tf_op jit(solution)/shard_map/ppermute | solution.py:464
  182.6 3.5 %collective-permute-done.41.refs_5_ = bf16[1024,128]{1,0:T(8,128)(2,1)S(1)} collective-permute-done((bf16[1024,128]{1,0:T(8,128)(2,1)S(1)}, bf16[1024,128]{1,0:T(8,128)(2,1)S(1)}, u32[]{:S(2)}, u32[]{:S(2)}) %collective-permute-start.41) | collective-permute-done | bytes 262176 | tf_op jit(solution)/shard_map/ppermute | solution.py:464
  186.1 1.6 collective-permute-done.46
  188.8 2.7 %collective-permute-done.47 = bf16[2,128,1024]{2,1,0:T(8,128)(2,1)} collective-permute-done((bf16[2,128,1024]{2,1,0:T(8,128)(2,1)}, bf16[2,128,1024]{2,1,0:T(8,128)(2,1)}, u32[]{:S(2)}, u32[]{:S(2)}) %collective-permute-start.47) | collective-permute-done | bytes 524320 | tf_op jit(solution)/shard_map/ppermute | solution.py:27
  194.9 2.1 add_outputs.6.refs_7_
  197.0 1.8 add_outputs.7.refs_3_
  198.9 2.1 add_outputs.5.refs_9_
  201.7 14.0 %collective-permute-start.48 = (bf16[1024,512]{1,0:T(8,128)(2,1)S(1)}, bf16[1024,512]{1,0:T(8,128)(2,1)S(1)}, u32[]{:S(2)}, u32[]{:S(2)}) collective-permute-start(bf16[1024,512]{1,0:T(8,128)(2,1)S(1)} %add_outputs.9), channel_id=1, source_target_pairs={{0,1},{1,0},{2,3},{3,2},{4,5},{5,4},{6,7},{7,6},{8,9},{9,8},{10,11... | collective-permute-start | bytes 3145736 | tf_op jit(solution)/shard_map/ppermute | solution.py:296
  216.4 2.1 add_outputs.8
  218.4 1.3 add_convert_fusion
  (239 shorter events, 35.0 us)
Async XLA Ops:
  7.2 91.0 %all-gather.3.cloned.1.call-start = ((), (), s32[]{:S(2)}) async-start(), calls=%async_computation | async-start | bytes 9437184 | tf_op jit(solution)/shard_map/all_gather | solution.py:368
  11.7 24.1 %copy-start.26 = (bf16[1024,3,512]{2,0,1:T(8,128)(2,1)S(1)}, bf16[1024,3,512]{2,0,1:T(8,128)(2,1)}, u32[]{:S(2)}) copy-start(bf16[1024,3,512]{2,0,1:T(8,128)(2,1)} %param.12) | copy-start | bytes 9437188
  14.4 43.0 %collective-permute-start.5 = (bf16[1024,768]{1,0:T(8,128)(2,1)}, bf16[1024,768]{1,0:T(8,128)(2,1)}, u32[]{:S(2)}, u32[]{:S(2)}) collective-permute-start(bf16[1024,768]{1,0:T(8,128)(2,1)} %copy.25.refs_0_), channel_id=1, source_target_pairs={{0,8},{8,0},{16,24},{24,16},{1,9},{9,1},{17,25},{25,17},{2,10},{10... | collective-permute-start | bytes 4718600 | tf_op jit(solution)/shard_map/ppermute | solution.py:27
  16.5 41.0 %collective-permute-start.6 = (bf16[1024,768]{1,0:T(8,128)(2,1)}, bf16[1024,768]{1,0:T(8,128)(2,1)}, u32[]{:S(2)}, u32[]{:S(2)}) collective-permute-start(bf16[1024,768]{1,0:T(8,128)(2,1)} %copy.25.refs_0_), channel_id=1, source_target_pairs={{0,16},{8,24},{16,0},{24,8},{1,17},{9,25},{17,1},{25,9},{2,18},{10... | collective-permute-start | bytes 4718600 | tf_op jit(solution)/shard_map/ppermute | solution.py:27
  17.7 6.5 %collective-permute-start.7 = (f32[1,1024]{1,0:T(1,128)S(1)}, f32[1,1024]{1,0:T(1,128)S(1)}, u32[]{:S(2)}, u32[]{:S(2)}) collective-permute-start(f32[1,1024]{1,0:T(1,128)S(1)} %bitcast.173), channel_id=1, source_target_pairs={{0,1},{1,0},{2,3},{3,2},{4,5},{5,4},{6,7},{7,6},{8,9},{9,8},{10,11... | collective-permute-start | bytes 12296 | tf_op jit(solution)/shard_map/ppermute | solution.py:296
  24.2 7.2 %collective-permute-start.10 = (f32[1,1024]{1,0:T(1,128)S(1)}, f32[1,1024]{1,0:T(1,128)S(1)}, u32[]{:S(2)}, u32[]{:S(2)}) collective-permute-start(f32[1,1024]{1,0:T(1,128)S(1)} %add.108), channel_id=1, source_target_pairs={{0,6},{1,7},{2,4},{3,5},{4,2},{5,3},{6,0},{7,1},{8,14},{9,15},{10,... | collective-permute-start | bytes 12296 | tf_op jit(solution)/shard_map/ppermute | solution.py:387
  27.6 6.0 %collective-permute-start.8 = (f32[1,1024]{1,0:T(1,128)S(1)}, f32[1,1024]{1,0:T(1,128)S(1)}, u32[]{:S(2)}, u32[]{:S(2)}) collective-permute-start(f32[1,1024]{1,0:T(1,128)S(1)} %add.108), channel_id=1, source_target_pairs={{0,2},{1,3},{2,0},{3,1},{4,6},{5,7},{6,4},{7,5},{8,10},{9,11},{10,... | collective-permute-start | bytes 12296 | tf_op jit(solution)/shard_map/ppermute | solution.py:387
  27.6 6.0 %collective-permute-start.9 = (f32[1,1024]{1,0:T(1,128)S(1)}, f32[1,1024]{1,0:T(1,128)S(1)}, u32[]{:S(2)}, u32[]{:S(2)}) collective-permute-start(f32[1,1024]{1,0:T(1,128)S(1)} %add.108), channel_id=1, source_target_pairs={{0,4},{1,5},{2,6},{3,7},{4,0},{5,1},{6,2},{7,3},{8,12},{9,13},{10,... | collective-permute-start | bytes 12296 | tf_op jit(solution)/shard_map/ppermute | solution.py:387
  31.4 18.7 %collective-permute-start = (bf16[16,512]{1,0:T(8,128)(2,1)}, bf16[16,512]{1,0:T(8,128)(2,1)S(1)}, u32[]{:S(2)}, u32[]{:S(2)}) collective-permute-start(bf16[16,512]{1,0:T(8,128)(2,1)} %slice.147), channel_id=1, source_target_pairs={{0,8},{8,16},{16,24},{1,9},{9,17},{17,25},{2,10},{10,18},{18,26},{... | collective-permute-start | bytes 49160 | tf_op jit(solution)/shard_map/ppermute | solution.py:371
  33.6 23.8 %collective-permute-start.11 = (bf16[128,1024]{1,0:T(8,128)(2,1)S(1)}, bf16[128,1024]{1,0:T(8,128)(2,1)}, u32[]{:S(2)}, u32[]{:S(2)}) collective-permute-start(bf16[128,1024]{1,0:T(8,128)(2,1)S(1)} %get-tuple-element.42), channel_id=1, source_target_pairs={{0,24},{8,16},{16,8},{24,0},{1,25},{9,17},{17,9},{25,1},{2,26},{10... | collective-permute-start | bytes 786440 | tf_op jit(solution)/shard_map/ppermute | solution.py:27
  38.8 26.6 %copy-start.37 = (bf16[128,1024]{1,0:T(8,128)(2,1)S(1)}, bf16[128,1024]{1,0:T(8,128)(2,1)}, u32[]{:S(2)}) copy-start(bf16[128,1024]{1,0:T(8,128)(2,1)} %get-tuple-element.54) | copy-start | bytes 786436
  38.8 27.8 %copy-start.36 = (bf16[128,1024]{1,0:T(8,128)(2,1)S(1)}, bf16[128,1024]{1,0:T(8,128)(2,1)}, u32[]{:S(2)}) copy-start(bf16[128,1024]{1,0:T(8,128)(2,1)} %get-tuple-element.53) | copy-start | bytes 786436
  38.8 36.2 %copy-start.50 = (f32[16,1]{1,0:T(8,128)S(1)}, f32[16,1]{1,0:T(8,128)}, u32[]{:S(2)}) copy-start(f32[16,1]{1,0:T(8,128)} %copy.24) | copy-start | bytes 196
  38.9 47.5 %slice-start.1 = ((bf16[1024,3,512]{0,2,1:T(8,128)(2,1)}), bf16[1024,3,256]{0,2,1:T(8,128)(2,1)S(1)}, s32[]{:S(2)}) async-start(bf16[1024,3,512]{0,2,1:T(8,128)(2,1)} %copy.27), calls=%async_computation.2 | async-start | bytes 3145728 | tf_op jit(solution)/shard_map/slice | solution.py:399
  50.1 11.6 %collective-permute-start.1 = (bf16[1,16,512]{2,1,0:T(8,128)(2,1)S(1)}, bf16[1,16,512]{2,1,0:T(8,128)(2,1)S(1)}, u32[]{:S(2)}, u32[]{:S(2)}) collective-permute-start(bf16[1,16,512]{2,1,0:T(8,128)(2,1)S(1)} %bitcast.166), channel_id=1, source_target_pairs={{0,1},{1,0},{2,3},{3,2},{4,5},{5,4},{6,7},{7,6},{8,9},{9,8},{10,11... | collective-permute-start | bytes 49160 | tf_op jit(solution)/shard_map/ppermute | solution.py:296
  57.5 30.1 %copy-start.53 = (f32[512]{0:T(512)S(1)}, f32[512]{0:T(512)}, u32[]{:S(2)}) copy-start(f32[512]{0:T(512)} %param.17) | copy-start | bytes 6148
  57.5 30.1 %copy-start.52 = (f32[128]{0:T(128)S(1)}, f32[128]{0:T(128)}, u32[]{:S(2)}) copy-start(f32[128]{0:T(128)} %mul.145) | copy-start | bytes 1540
  58.7 25.8 %collective-permute-start.12 = (bf16[512,768]{1,0:T(8,128)(2,1)S(1)}, bf16[512,768]{1,0:T(8,128)(2,1)S(1)}, u32[]{:S(2)}, u32[]{:S(2)}) collective-permute-start(bf16[512,768]{1,0:T(8,128)(2,1)S(1)} %slice.114), channel_id=1, source_target_pairs={{0,8},{8,0},{16,24},{24,16},{1,9},{9,1},{17,25},{25,17},{2,10},{10... | collective-permute-start | bytes 2359304 | tf_op jit(solution)/shard_map/ppermute | solution.py:27
  61.4 23.0 %collective-permute-start.13 = (bf16[512,768]{1,0:T(8,128)(2,1)S(1)}, bf16[512,768]{1,0:T(8,128)(2,1)S(1)}, u32[]{:S(2)}, u32[]{:S(2)}) collective-permute-start(bf16[512,768]{1,0:T(8,128)(2,1)S(1)} %slice.115), channel_id=1, source_target_pairs={{0,16},{8,24},{16,0},{24,8},{1,17},{9,25},{17,1},{25,9},{2,18},{10... | collective-permute-start | bytes 2359304 | tf_op jit(solution)/shard_map/ppermute | solution.py:27
  61.7 4.9 %collective-permute-start.2 = (bf16[2,16,512]{2,1,0:T(8,128)(2,1)S(1)}, bf16[2,16,512]{2,1,0:T(8,128)(2,1)S(1)}, u32[]{:S(2)}, u32[]{:S(2)}) collective-permute-start(bf16[2,16,512]{2,1,0:T(8,128)(2,1)S(1)} %pad_maximum_fusion.5), channel_id=1, source_target_pairs={{0,2},{1,3},{2,0},{3,1},{4,6},{5,7},{6,4},{7,5},{8,10},{9,11},{10,... | collective-permute-start | bytes 98312 | tf_op jit(solution)/shard_map/ppermute | solution.py:398
  63.2 6.6 %collective-permute-start.3 = (bf16[2,16,512]{2,1,0:T(8,128)(2,1)S(1)}, bf16[2,16,512]{2,1,0:T(8,128)(2,1)S(1)}, u32[]{:S(2)}, u32[]{:S(2)}) collective-permute-start(bf16[2,16,512]{2,1,0:T(8,128)(2,1)S(1)} %pad_maximum_fusion.5), channel_id=1, source_target_pairs={{0,4},{1,5},{2,6},{3,7},{4,0},{5,1},{6,2},{7,3},{8,12},{9,13},{10,... | collective-permute-start | bytes 98312 | tf_op jit(solution)/shard_map/ppermute | solution.py:398
  65.5 19.0 %collective-permute-start.16 = (bf16[128,1024]{1,0:T(8,128)(2,1)S(1)}, bf16[128,1024]{1,0:T(8,128)(2,1)S(1)}, u32[]{:S(2)}, u32[]{:S(2)}) collective-permute-start(bf16[128,1024]{1,0:T(8,128)(2,1)S(1)} %copy-done.37), channel_id=1, source_target_pairs={{0,16},{8,24},{16,0},{24,8},{1,17},{9,25},{17,1},{25,9},{2,18},{10... | collective-permute-start | bytes 786440 | tf_op jit(solution)/shard_map/ppermute | solution.py:27
  66.7 17.8 %collective-permute-start.15 = (bf16[128,1024]{1,0:T(8,128)(2,1)S(1)}, bf16[128,1024]{1,0:T(8,128)(2,1)S(1)}, u32[]{:S(2)}, u32[]{:S(2)}) collective-permute-start(bf16[128,1024]{1,0:T(8,128)(2,1)S(1)} %copy-done.36), channel_id=1, source_target_pairs={{0,8},{8,0},{16,24},{24,16},{1,9},{9,1},{17,25},{25,17},{2,10},{10... | collective-permute-start | bytes 786440 | tf_op jit(solution)/shard_map/ppermute | solution.py:27
  69.8 5.3 %collective-permute-start.4 = (bf16[2,16,512]{2,1,0:T(8,128)(2,1)S(1)}, bf16[2,16,512]{2,1,0:T(8,128)(2,1)S(1)}, u32[]{:S(2)}, u32[]{:S(2)}) collective-permute-start(bf16[2,16,512]{2,1,0:T(8,128)(2,1)S(1)} %pad_maximum_fusion.5), channel_id=1, source_target_pairs={{0,6},{1,7},{2,4},{3,5},{4,2},{5,3},{6,0},{7,1},{8,14},{9,15},{10,... | collective-permute-start | bytes 98312 | tf_op jit(solution)/shard_map/ppermute | solution.py:398
  75.0 6.3 %collective-permute-start.14 = (f32[16,1]{1,0:T(8,128)S(1)}, f32[16,1]{1,0:T(8,128)S(1)}, u32[]{:S(2)}, u32[]{:S(2)}) collective-permute-start(f32[16,1]{1,0:T(8,128)S(1)} %copy-done.50), channel_id=1, source_target_pairs={{0,8},{8,16},{16,24},{1,9},{9,17},{17,25},{2,10},{10,18},{18,26},{... | collective-permute-start | bytes 200 | tf_op jit(solution)/shard_map/ppermute | solution.py:389
  87.1 36.6 %collective-permute-start.23 = (bf16[1024,768]{1,0:T(8,128)(2,1)S(1)}, bf16[1024,768]{1,0:T(8,128)(2,1)S(1)}, u32[]{:S(2)}, u32[]{:S(2)}) collective-permute-start(bf16[1024,768]{1,0:T(8,128)(2,1)S(1)} %copy.30.refs_0_), channel_id=1, source_target_pairs={{0,8},{8,0},{16,24},{24,16},{1,9},{9,1},{17,25},{25,17},{2,10},{10... | collective-permute-start | bytes 4718600 | tf_op jit(solution)/shard_map/ppermute | solution.py:27
  87.2 36.5 %collective-permute-start.24 = (bf16[1024,768]{1,0:T(8,128)(2,1)S(1)}, bf16[1024,768]{1,0:T(8,128)(2,1)}, u32[]{:S(2)}, u32[]{:S(2)}) collective-permute-start(bf16[1024,768]{1,0:T(8,128)(2,1)S(1)} %copy.30.refs_0_), channel_id=1, source_target_pairs={{0,16},{8,24},{16,0},{24,8},{1,17},{9,25},{17,1},{25,9},{2,18},{10... | collective-permute-start | bytes 4718600 | tf_op jit(solution)/shard_map/ppermute | solution.py:27
  90.7 27.1 %collective-permute-start.17 = (bf16[128,1024]{1,0:T(8,128)(2,1)}, bf16[128,1024]{1,0:T(8,128)(2,1)}, u32[]{:S(2)}, u32[]{:S(2)}) collective-permute-start(bf16[128,1024]{1,0:T(8,128)(2,1)} %get-tuple-element.89), channel_id=1, source_target_pairs={{0,2},{1,3},{2,0},{3,1},{4,6},{5,7},{6,4},{7,5},{8,10},{9,11},{10,... | collective-permute-start | bytes 786440 | tf_op jit(solution)/shard_map/ppermute | solution.py:407
  92.1 26.9 %collective-permute-start.21 = (bf16[128,1024]{1,0:T(8,128)(2,1)}, bf16[128,1024]{1,0:T(8,128)(2,1)}, u32[]{:S(2)}, u32[]{:S(2)}) collective-permute-start(bf16[128,1024]{1,0:T(8,128)(2,1)} %get-tuple-element.88), channel_id=1, source_target_pairs={{0,4},{1,5},{2,6},{3,7},{4,0},{5,1},{6,2},{7,3},{8,12},{9,13},{10,... | collective-permute-start | bytes 786440 | tf_op jit(solution)/shard_map/ppermute | solution.py:407
  94.4 25.7 %collective-permute-start.22 = (bf16[128,1024]{1,0:T(8,128)(2,1)}, bf16[128,1024]{1,0:T(8,128)(2,1)}, u32[]{:S(2)}, u32[]{:S(2)}) collective-permute-start(bf16[128,1024]{1,0:T(8,128)(2,1)} %get-tuple-element.87), channel_id=1, source_target_pairs={{0,6},{1,7},{2,4},{3,5},{4,2},{5,3},{6,0},{7,1},{8,14},{9,15},{10,... | collective-permute-start | bytes 786440 | tf_op jit(solution)/shard_map/ppermute | solution.py:407
  117.9 3.3 %collective-permute-start.18 = (f32[16,256]{1,0:T(8,128)S(1)}, f32[16,256]{1,0:T(8,128)S(1)}, u32[]{:S(2)}, u32[]{:S(2)}) collective-permute-start(f32[16,256]{1,0:T(8,128)S(1)} %get-tuple-element.55), channel_id=1, source_target_pairs={{0,8},{8,0},{16,24},{24,16},{1,9},{9,1},{17,25},{25,17},{2,10},{10... | collective-permute-start | bytes 49160 | tf_op jit(solution)/shard_map/ppermute | solution.py:444
  118.9 3.2 %collective-permute-start.19 = (f32[16,256]{1,0:T(8,128)S(1)}, f32[16,256]{1,0:T(8,128)S(1)}, u32[]{:S(2)}, u32[]{:S(2)}) collective-permute-start(f32[16,256]{1,0:T(8,128)S(1)} %get-tuple-element.55), channel_id=1, source_target_pairs={{0,16},{8,24},{16,0},{24,8},{1,17},{9,25},{17,1},{25,9},{2,18},{10... | collective-permute-start | bytes 49160 | tf_op jit(solution)/shard_map/ppermute | solution.py:444
  120.2 3.6 %collective-permute-start.20 = (f32[16,256]{1,0:T(8,128)S(1)}, f32[16,256]{1,0:T(8,128)S(1)}, u32[]{:S(2)}, u32[]{:S(2)}) collective-permute-start(f32[16,256]{1,0:T(8,128)S(1)} %get-tuple-element.55), channel_id=1, source_target_pairs={{0,24},{8,16},{16,8},{24,0},{1,25},{9,17},{17,9},{25,1},{2,26},{10... | collective-permute-start | bytes 49160 | tf_op jit(solution)/shard_map/ppermute | solution.py:444
  124.9 14.6 %collective-permute-start.25 = (bf16[512,768]{1,0:T(8,128)(2,1)S(1)}, bf16[512,768]{1,0:T(8,128)(2,1)S(1)}, u32[]{:S(2)}, u32[]{:S(2)}) collective-permute-start(bf16[512,768]{1,0:T(8,128)(2,1)S(1)} %slice.131), channel_id=1, source_target_pairs={{0,8},{8,0},{16,24},{24,16},{1,9},{9,1},{17,25},{25,17},{2,10},{10... | collective-permute-start | bytes 2359304 | tf_op jit(solution)/shard_map/ppermute | solution.py:27
  125.5 15.2 %collective-permute-start.26 = (bf16[512,768]{1,0:T(8,128)(2,1)S(1)}, bf16[512,768]{1,0:T(8,128)(2,1)S(1)}, u32[]{:S(2)}, u32[]{:S(2)}) collective-permute-start(bf16[512,768]{1,0:T(8,128)(2,1)S(1)} %slice.132), channel_id=1, source_target_pairs={{0,16},{8,24},{16,0},{24,8},{1,17},{9,25},{17,1},{25,9},{2,18},{10... | collective-permute-start | bytes 2359304 | tf_op jit(solution)/shard_map/ppermute | solution.py:27
  127.4 7.1 %collective-permute-start.27 = (bf16[1024,128]{1,0:T(8,128)(2,1)S(1)}, bf16[1024,128]{1,0:T(8,128)(2,1)S(1)}, u32[]{:S(2)}, u32[]{:S(2)}) collective-permute-start(bf16[1024,128]{1,0:T(8,128)(2,1)S(1)} %gated_signal.4.refs_0_), channel_id=1, source_target_pairs={{0,2},{1,3},{2,4},{3,5},{4,6},{5,7},{6,0},{7,1},{8,10},{9,11},{10,... | collective-permute-start | bytes 786440 | tf_op jit(solution)/shard_map/ppermute | solution.py:464
  128.7 9.2 %collective-permute-start.28 = (bf16[1024,128]{1,0:T(8,128)(2,1)S(1)}, bf16[1024,128]{1,0:T(8,128)(2,1)S(1)}, u32[]{:S(2)}, u32[]{:S(2)}) collective-permute-start(bf16[1024,128]{1,0:T(8,128)(2,1)S(1)} %gated_signal.5.refs_1_), channel_id=1, source_target_pairs={{0,2},{1,3},{2,4},{3,5},{4,6},{5,7},{6,0},{7,1},{8,10},{9,11},{10,... | collective-permute-start | bytes 786440 | tf_op jit(solution)/shard_map/ppermute | solution.py:464
  130.0 23.0 %collective-permute-start.29 = (bf16[2,128,1024]{2,1,0:T(8,128)(2,1)S(1)}, bf16[2,128,1024]{2,1,0:T(8,128)(2,1)S(1)}, u32[]{:S(2)}, u32[]{:S(2)}) collective-permute-start(bf16[2,128,1024]{2,1,0:T(8,128)(2,1)S(1)} %pad_maximum_fusion.1), channel_id=1, source_target_pairs={{0,8},{8,0},{16,24},{24,16},{1,9},{9,1},{17,25},{25,17},{2,10},{10... | collective-permute-start | bytes 1572872 | tf_op jit(solution)/shard_map/ppermute | solution.py:27
  134.4 16.3 %copy-start.5 = (bf16[1024,128]{1,0:T(8,128)(2,1)}, bf16[1024,128]{1,0:T(8,128)(2,1)S(1)}, u32[]{:S(2)}) copy-start(bf16[1024,128]{1,0:T(8,128)(2,1)S(1)} %collective-permute-done.27.refs_2_) | copy-start | bytes 786436
  134.4 18.6 %collective-permute-start.30 = (bf16[2,128,1024]{2,1,0:T(8,128)(2,1)S(1)}, bf16[2,128,1024]{2,1,0:T(8,128)(2,1)}, u32[]{:S(2)}, u32[]{:S(2)}) collective-permute-start(bf16[2,128,1024]{2,1,0:T(8,128)(2,1)S(1)} %pad_maximum_fusion.1), channel_id=1, source_target_pairs={{0,16},{8,24},{16,0},{24,8},{1,17},{9,25},{17,1},{25,9},{2,18},{10... | collective-permute-start | bytes 1572872 | tf_op jit(solution)/shard_map/ppermute | solution.py:27
  137.9 12.9 %collective-permute-start.31 = (bf16[1024,128]{1,0:T(8,128)(2,1)S(1)}, bf16[1024,128]{1,0:T(8,128)(2,1)S(1)}, u32[]{:S(2)}, u32[]{:S(2)}) collective-permute-start(bf16[1024,128]{1,0:T(8,128)(2,1)S(1)} %collective-permute-done.27.refs_2_), channel_id=1, source_target_pairs={{0,2},{1,3},{2,4},{3,5},{4,6},{5,7},{6,0},{7,1},{8,10},{9,11},{10,... | collective-permute-start | bytes 786440 | tf_op jit(solution)/shard_map/ppermute | solution.py:464
  139.6 11.2 %collective-permute-start.32 = (bf16[1024,128]{1,0:T(8,128)(2,1)S(1)}, bf16[1024,128]{1,0:T(8,128)(2,1)S(1)}, u32[]{:S(2)}, u32[]{:S(2)}) collective-permute-start(bf16[1024,128]{1,0:T(8,128)(2,1)S(1)} %collective-permute-done.28.refs_3_), channel_id=1, source_target_pairs={{0,2},{1,3},{2,4},{3,5},{4,6},{5,7},{6,0},{7,1},{8,10},{9,11},{10,... | collective-permute-start | bytes 786440 | tf_op jit(solution)/shard_map/ppermute | solution.py:464
  150.8 12.0 %collective-permute-start.36 = (bf16[1024,128]{1,0:T(8,128)(2,1)S(1)}, bf16[1024,128]{1,0:T(8,128)(2,1)S(1)}, u32[]{:S(2)}, u32[]{:S(2)}) collective-permute-start(bf16[1024,128]{1,0:T(8,128)(2,1)S(1)} %collective-permute-done.31.refs_4_), channel_id=1, source_target_pairs={{0,2},{1,3},{2,4},{3,5},{4,6},{5,7},{6,0},{7,1},{8,10},{9,11},{10,... | collective-permute-start | bytes 786440 | tf_op jit(solution)/shard_map/ppermute | solution.py:27
  150.9 12.2 %collective-permute-start.37 = (bf16[1024,128]{1,0:T(8,128)(2,1)S(1)}, bf16[1024,128]{1,0:T(8,128)(2,1)S(1)}, u32[]{:S(2)}, u32[]{:S(2)}) collective-permute-start(bf16[1024,128]{1,0:T(8,128)(2,1)S(1)} %collective-permute-done.32.refs_5_), channel_id=1, source_target_pairs={{0,2},{1,3},{2,4},{3,5},{4,6},{5,7},{6,0},{7,1},{8,10},{9,11},{10,... | collective-permute-start | bytes 786440 | tf_op jit(solution)/shard_map/ppermute | solution.py:27
  157.5 2.7 %collective-permute-start.33 = (f32[16,256]{1,0:T(8,128)S(1)}, f32[16,256]{1,0:T(8,128)S(1)}, u32[]{:S(2)}, u32[]{:S(2)}) collective-permute-start(f32[16,256]{1,0:T(8,128)S(1)} %get-tuple-element.71), channel_id=1, source_target_pairs={{0,8},{8,0},{16,24},{24,16},{1,9},{9,1},{17,25},{25,17},{2,10},{10... | collective-permute-start | bytes 49160 | tf_op jit(solution)/shard_map/ppermute | solution.py:444
  158.2 2.6 %collective-permute-start.34 = (f32[16,256]{1,0:T(8,128)S(1)}, f32[16,256]{1,0:T(8,128)S(1)}, u32[]{:S(2)}, u32[]{:S(2)}) collective-permute-start(f32[16,256]{1,0:T(8,128)S(1)} %get-tuple-element.71), channel_id=1, source_target_pairs={{0,16},{8,24},{16,0},{24,8},{1,17},{9,25},{17,1},{25,9},{2,18},{10... | collective-permute-start | bytes 49160 | tf_op jit(solution)/shard_map/ppermute | solution.py:444
  159.3 3.5 %collective-permute-start.35 = (f32[16,256]{1,0:T(8,128)S(1)}, f32[16,256]{1,0:T(8,128)S(1)}, u32[]{:S(2)}, u32[]{:S(2)}) collective-permute-start(f32[16,256]{1,0:T(8,128)S(1)} %get-tuple-element.71), channel_id=1, source_target_pairs={{0,24},{8,16},{16,8},{24,0},{1,25},{9,17},{17,9},{25,1},{2,26},{10... | collective-permute-start | bytes 49160 | tf_op jit(solution)/shard_map/ppermute | solution.py:444
  163.1 11.7 %collective-permute-start.44 = (bf16[2,128,1024]{2,1,0:T(8,128)(2,1)S(1)}, bf16[2,128,1024]{2,1,0:T(8,128)(2,1)}, u32[]{:S(2)}, u32[]{:S(2)}) collective-permute-start(bf16[2,128,1024]{2,1,0:T(8,128)(2,1)S(1)} %pad_maximum_fusion.2), channel_id=1, source_target_pairs={{0,8},{8,0},{16,24},{24,16},{1,9},{9,1},{17,25},{25,17},{2,10},{10... | collective-permute-start | bytes 1572872 | tf_op jit(solution)/shard_map/ppermute | solution.py:27
  163.7 11.1 %collective-permute-start.45 = (bf16[2,128,1024]{2,1,0:T(8,128)(2,1)S(1)}, bf16[2,128,1024]{2,1,0:T(8,128)(2,1)S(1)}, u32[]{:S(2)}, u32[]{:S(2)}) collective-permute-start(bf16[2,128,1024]{2,1,0:T(8,128)(2,1)S(1)} %pad_maximum_fusion.2), channel_id=1, source_target_pairs={{0,16},{8,24},{16,0},{24,8},{1,17},{9,25},{17,1},{25,9},{2,18},{10... | collective-permute-start | bytes 1572872 | tf_op jit(solution)/shard_map/ppermute | solution.py:27
  165.3 9.5 %collective-permute-start.38 = (bf16[1024,128]{1,0:T(8,128)(2,1)S(1)}, bf16[1024,128]{1,0:T(8,128)(2,1)S(1)}, u32[]{:S(2)}, u32[]{:S(2)}) collective-permute-start(bf16[1024,128]{1,0:T(8,128)(2,1)S(1)} %gated_signal.6.refs_0_), channel_id=1, source_target_pairs={{0,2},{1,3},{2,4},{3,5},{4,6},{5,7},{6,0},{7,1},{8,10},{9,11},{10,... | collective-permute-start | bytes 786440 | tf_op jit(solution)/shard_map/ppermute | solution.py:464
  168.2 9.4 %collective-permute-start.39 = (bf16[1024,128]{1,0:T(8,128)(2,1)S(1)}, bf16[1024,128]{1,0:T(8,128)(2,1)S(1)}, u32[]{:S(2)}, u32[]{:S(2)}) collective-permute-start(bf16[1024,128]{1,0:T(8,128)(2,1)S(1)} %gated_signal.7.refs_1_), channel_id=1, source_target_pairs={{0,2},{1,3},{2,4},{3,5},{4,6},{5,7},{6,0},{7,1},{8,10},{9,11},{10,... | collective-permute-start | bytes 786440 | tf_op jit(solution)/shard_map/ppermute | solution.py:464
  174.8 12.9 %collective-permute-start.46 = (bf16[2,128,1024]{2,1,0:T(8,128)(2,1)}, bf16[2,128,1024]{2,1,0:T(8,128)(2,1)}, u32[]{:S(2)}, u32[]{:S(2)}) collective-permute-start(bf16[2,128,1024]{2,1,0:T(8,128)(2,1)} %collective-permute-done.30), channel_id=1, source_target_pairs={{0,8},{8,0},{16,24},{24,16},{1,9},{9,1},{17,25},{25,17},{2,10},{10... | collective-permute-start | bytes 1572872 | tf_op jit(solution)/shard_map/ppermute | solution.py:27
  175.6 7.0 %collective-permute-start.40 = (bf16[1024,128]{1,0:T(8,128)(2,1)S(1)}, bf16[1024,128]{1,0:T(8,128)(2,1)S(1)}, u32[]{:S(2)}, u32[]{:S(2)}) collective-permute-start(bf16[1024,128]{1,0:T(8,128)(2,1)S(1)} %collective-permute-done.38.refs_2_), channel_id=1, source_target_pairs={{0,2},{1,3},{2,4},{3,5},{4,6},{5,7},{6,0},{7,1},{8,10},{9,11},{10,... | collective-permute-start | bytes 786440 | tf_op jit(solution)/shard_map/ppermute | solution.py:464
  177.6 8.5 %collective-permute-start.41 = (bf16[1024,128]{1,0:T(8,128)(2,1)S(1)}, bf16[1024,128]{1,0:T(8,128)(2,1)S(1)}, u32[]{:S(2)}, u32[]{:S(2)}) collective-permute-start(bf16[1024,128]{1,0:T(8,128)(2,1)S(1)} %collective-permute-done.39.refs_3_), channel_id=1, source_target_pairs={{0,2},{1,3},{2,4},{3,5},{4,6},{5,7},{6,0},{7,1},{8,10},{9,11},{10,... | collective-permute-start | bytes 786440 | tf_op jit(solution)/shard_map/ppermute | solution.py:464
  177.6 13.9 %collective-permute-start.47 = (bf16[2,128,1024]{2,1,0:T(8,128)(2,1)}, bf16[2,128,1024]{2,1,0:T(8,128)(2,1)}, u32[]{:S(2)}, u32[]{:S(2)}) collective-permute-start(bf16[2,128,1024]{2,1,0:T(8,128)(2,1)} %collective-permute-done.44), channel_id=1, source_target_pairs={{0,16},{8,24},{16,0},{24,8},{1,17},{9,25},{17,1},{25,9},{2,18},{10... | collective-permute-start | bytes 1572872 | tf_op jit(solution)/shard_map/ppermute | solution.py:27
  179.9 14.9 %copy-start.34 = (bf16[2,128,1024]{2,1,0:T(8,128)(2,1)S(1)}, bf16[2,128,1024]{2,1,0:T(8,128)(2,1)}, u32[]{:S(2)}) copy-start(bf16[2,128,1024]{2,1,0:T(8,128)(2,1)} %copy-done.33) | copy-start | bytes 1572868
  179.9 14.9 %copy-start.4 = (bf16[1024,128]{1,0:T(8,128)(2,1)S(1)}, bf16[1024,128]{1,0:T(8,128)(2,1)}, u32[]{:S(2)}) copy-start(bf16[1024,128]{1,0:T(8,128)(2,1)} %copy-done.3) | copy-start | bytes 786436
  179.9 14.9 %copy-start.6 = (bf16[1024,128]{1,0:T(8,128)(2,1)S(1)}, bf16[1024,128]{1,0:T(8,128)(2,1)}, u32[]{:S(2)}) copy-start(bf16[1024,128]{1,0:T(8,128)(2,1)} %copy-done.5) | copy-start | bytes 786436
  179.9 14.9 %copy-start.8 = (bf16[1024,128]{1,0:T(8,128)(2,1)S(1)}, bf16[1024,128]{1,0:T(8,128)(2,1)}, u32[]{:S(2)}) copy-start(bf16[1024,128]{1,0:T(8,128)(2,1)} %copy-done.7) | copy-start | bytes 786436
  180.0 14.9 %copy-start.10 = (bf16[1024,128]{1,0:T(8,128)(2,1)S(1)}, bf16[1024,128]{1,0:T(8,128)(2,1)}, u32[]{:S(2)}) copy-start(bf16[1024,128]{1,0:T(8,128)(2,1)} %copy-done.9) | copy-start | bytes 786436
  180.0 14.9 %copy-start.12 = (bf16[1024,128]{1,0:T(8,128)(2,1)S(1)}, bf16[1024,128]{1,0:T(8,128)(2,1)}, u32[]{:S(2)}) copy-start(bf16[1024,128]{1,0:T(8,128)(2,1)} %copy-done.11) | copy-start | bytes 786436
  182.6 18.4 %collective-permute-start.42 = (bf16[1024,128]{1,0:T(8,128)(2,1)S(1)}, bf16[1024,128]{1,0:T(8,128)(2,1)S(1)}, u32[]{:S(2)}, u32[]{:S(2)}) collective-permute-start(bf16[1024,128]{1,0:T(8,128)(2,1)S(1)} %collective-permute-done.40.refs_4_), channel_id=1, source_target_pairs={{0,2},{1,3},{2,4},{3,5},{4,6},{5,7},{6,0},{7,1},{8,10},{9,11},{10,... | collective-permute-start | bytes 786440 | tf_op jit(solution)/shard_map/ppermute | solution.py:464
  186.1 14.9 %collective-permute-start.43 = (bf16[1024,128]{1,0:T(8,128)(2,1)S(1)}, bf16[1024,128]{1,0:T(8,128)(2,1)S(1)}, u32[]{:S(2)}, u32[]{:S(2)}) collective-permute-start(bf16[1024,128]{1,0:T(8,128)(2,1)S(1)} %collective-permute-done.41.refs_5_), channel_id=1, source_target_pairs={{0,2},{1,3},{2,4},{3,5},{4,6},{5,7},{6,0},{7,1},{8,10},{9,11},{10,... | collective-permute-start | bytes 786440 | tf_op jit(solution)/shard_map/ppermute | solution.py:464
  201.7 16.7 %collective-permute-start.48 = (bf16[1024,512]{1,0:T(8,128)(2,1)S(1)}, bf16[1024,512]{1,0:T(8,128)(2,1)S(1)}, u32[]{:S(2)}, u32[]{:S(2)}) collective-permute-start(bf16[1024,512]{1,0:T(8,128)(2,1)S(1)} %add_outputs.9), channel_id=1, source_target_pairs={{0,1},{1,0},{2,3},{3,2},{4,5},{5,4},{6,7},{7,6},{8,9},{9,8},{10,11... | collective-permute-start | bytes 3145736 | tf_op jit(solution)/shard_map/ppermute | solution.py:296
  (43 other events, 375.8 us)
Sparse Core Ops, SparseCore 0:
  10.2 87.9 all-gather.2
